TPU v7x, 32 devices: a whole 2x2x4 slice. The times are simulated.
32 devices in a mesh: ctx: 8 (over z, x), exp: 4 (over y, core).
Axes of the slice: x: 2, y: 2, z: 4, core: 2. Of those that a mesh axis runs over, the one named last changes fastest.
Arguments:
- inputs: bfloat16 [2560, 2048], P(('ctx', 'exp')), may hold values from -6 to 6
- attn_gain: float32 [2048], replicated, may hold values from 0.1 to 1.9
- w_query: bfloat16 [2048, 2048], P(None, 'exp'), as said below
- w_key: bfloat16 [2048, 2048], P(None, 'exp'), as said below
- w_value: bfloat16 [2048, 2048], P(None, 'exp'), may hold values from -0.125 to 0.125
- w_out: bfloat16 [2048, 2048], P('exp'), may hold values from -0.125 to 0.125
- sel_blocks: int32 [2560, 16, 3], P('ctx', 'exp'), may hold values from 0 to 6, as said below
- ffn_gain: float32 [2048], replicated, may hold values from 0.1 to 1.9
- w_gate: bfloat16 [32, 2048, 704], P(('ctx', 'exp')), may hold values from -0.125 to 0.125
- w_up: bfloat16 [32, 2048, 704], P(('ctx', 'exp')), may hold values from -0.125 to 0.125
- w_down: bfloat16 [32, 704, 2048], P(('ctx', 'exp')), may hold values from -0.15625 to 0.15625
- routes: int32 [2560, 6], P(('ctx', 'exp')), may hold values from 0 to 15, all different within a row; in each aligned block of 80 rows (0 to 79, 80 to 159, ...) at most 40 rows name the same one
- gate_weights: float32 [2560, 6], P(('ctx', 'exp')), may hold values from 0.05 to 0.5
Outputs:
- layer_out: bfloat16 [2560, 2048], P(('ctx', 'exp'))
Inputs may be any that keep to these rules, and one draw needn't show every extreme that they name: `sel_blocks`: for a query in block b = t // 320, the 3 entries of a head are distinct and lie below max(b, 3); entries below b name selected earlier blocks, and block b - 1 is always among them when b >= 1. `routes`: each row names 6 different experts; within the 80 rows of one device no expert is named by more than 40 rows. `w_query`: entries are bounded in magnitude by 8 * 2048 ** -0.5. `w_key`: entries are bounded in magnitude by 130 * 2048 ** -0.5.
All inputs are finite; a program needn't handle non-finite values.
Results may differ from a plain program's by a relative error of at most 0.014.
Values may be sent and summed in bfloat16 or wider, within the bound.
No kernel may reach another device: no remote copies, remote signals or barrier semaphores. Data moves between devices by JAX's collectives and lax.ppermute only.
A program may use at most 128 MiB of HBM per device.

v0:
```python
import math

import jax
import jax.numpy as jnp
from jax import lax
from jax.sharding import PartitionSpec as P


def partner_2(block, axis, stride):
    count = lax.axis_size(axis)
    route = []
    for low in range(count):
        high = low | 1 << stride
        if high != low and high < count:
            route += [(low, high), (high, low)]
    return lax.ppermute(block, axis, route)


def normalize(values, gain_vec):
    floats = values.astype(jnp.float32)
    factor = lax.rsqrt(jnp.mean(floats * floats, axis=-1, keepdims=True) + 1e-06)
    return (floats * factor * gain_vec).astype(jnp.bfloat16)


def shards(
    inputs,
    attn_gain,
    w_query,
    w_key,
    w_value,
    w_out,
    sel_blocks,
    ffn_gain,
    w_gate,
    w_up,
    w_down,
    routes,
    gate_weights,
):
    tok_rows, model_width = inputs.shape
    block_len, heads_here, pick_count = sel_blocks.shape
    head_dim = w_query.shape[1] // heads_here
    hidden_cols = heads_here * head_dim
    ctx_count = lax.axis_size("ctx")
    exp_count = lax.axis_size("exp")
    ctx_index = lax.axis_index("ctx")
    normed = normalize(inputs, attn_gain)
    shard_piece = lax.all_gather(normed, "exp", axis=0, tiled=True)
    query_part = jnp.dot(shard_piece, w_query, preferred_element_type=jnp.float32).astype(
        jnp.bfloat16
    )
    key_part = jnp.dot(shard_piece, w_key, preferred_element_type=jnp.float32).astype(jnp.bfloat16)
    value_part = jnp.dot(shard_piece, w_value, preferred_element_type=jnp.float32).astype(
        jnp.bfloat16
    )
    projected = jnp.stack([query_part, key_part, value_part], axis=1)
    queries = projected[:, 0].reshape(block_len, heads_here, head_dim)
    keys_values = projected[:, 1:]
    block_ids = jnp.arange(ctx_count, dtype=jnp.int32)
    chosen = jnp.any(sel_blocks[:, :, :, None] == block_ids, axis=2) & (block_ids < ctx_index)
    chosen_table = chosen.astype(jnp.bfloat16)
    query_pos = ctx_index * block_len + jnp.arange(block_len, dtype=jnp.int32)
    scaling = 1.0 / math.sqrt(head_dim)

    def attend_rows(running, shard_piece, first_row):
        run_max, run_sum, totals = running
        piece_rows = shard_piece.shape[0]
        key_rows = shard_piece[:, 0].reshape(piece_rows, heads_here, head_dim)
        value_rows = shard_piece[:, 1].reshape(piece_rows, heads_here, head_dim)
        scores = (
            jnp.einsum("qhd,khd->hqk", queries, key_rows, preferred_element_type=jnp.float32)
            * scaling
        )
        key_pos = first_row + jnp.arange(piece_rows, dtype=jnp.int32)
        key_block = key_pos // block_len
        onehot = (key_block[None, :] == block_ids[:, None]).astype(jnp.bfloat16)
        picked = (
            jnp.einsum("qhb,bk->hqk", chosen_table, onehot, preferred_element_type=jnp.float32)
            > 0.5
        )
        own_block = (key_block[None, :] == ctx_index) & (key_pos[None, :] <= query_pos[:, None])
        allowed = picked | own_block[None]
        new_max = jnp.maximum(run_max, jnp.max(jnp.where(allowed, scores, -jnp.inf), axis=-1))
        weights = jnp.where(allowed, jnp.exp(scores - new_max[..., None]), 0.0)
        rescale = jnp.exp(run_max - new_max)
        run_sum = run_sum * rescale + jnp.sum(weights, axis=-1)
        totals = totals * rescale[..., None] + jnp.einsum(
            "hqk,khd->hqd",
            weights.astype(jnp.bfloat16),
            value_rows,
            preferred_element_type=jnp.float32,
        )
        return (new_max, run_sum, totals)

    initial = (
        jnp.full((heads_here, block_len), -1e30, jnp.float32),
        jnp.zeros((heads_here, block_len), jnp.float32),
        jnp.zeros((heads_here, block_len, head_dim), jnp.float32),
    )
    shard_piece = lax.all_gather(keys_values, "ctx", axis=0, tiled=True)
    piece_rows = shard_piece.shape[0]
    shard_group = 4
    step_rows = shard_group * block_len
    turn_count = piece_rows // step_rows
    stacked = shard_piece.reshape(turn_count, step_rows, 2, hidden_cols)
    offsets = jnp.arange(turn_count, dtype=jnp.int32) * step_rows

    def fold_step(carry, operands):
        row_block, offset = operands
        return (attend_rows(carry, row_block, offset), None)

    result, _ = lax.scan(fold_step, initial, (stacked, offsets))
    run_max, run_sum, totals = result
    attended = (
        (totals / run_sum[..., None])
        .transpose(1, 0, 2)
        .reshape(block_len, hidden_cols)
        .astype(jnp.bfloat16)
    )
    row_data = attended
    head_mixed = lax.psum_scatter(
        jnp.dot(row_data, w_out, preferred_element_type=jnp.float32).astype(jnp.bfloat16),
        "exp",
        scatter_dimension=0,
        tiled=True,
    ).astype(jnp.float32)
    residual = (inputs.astype(jnp.float32) + head_mixed).astype(jnp.bfloat16)
    ffn_in = normalize(residual, ffn_gain)
    top_count = routes.shape[1]
    experts = ctx_count * exp_count // 2
    capacity = 2 * max(1, (tok_rows * top_count + experts - 1) // experts * 2 // 3)
    flat_routes = routes.reshape(-1)
    expert_ids = jnp.arange(experts, dtype=jnp.int32)
    member = (flat_routes[:, None] == expert_ids[None, :]).astype(jnp.int32)
    before = jnp.cumsum(member, axis=0) - member
    position = jnp.sum(before * member, axis=1)
    slot_index = flat_routes * capacity + position
    slot_ids = jnp.arange(experts * capacity, dtype=jnp.int32)
    placing = jnp.any(
        slot_index.reshape(tok_rows, top_count)[None, :, :] == slot_ids[:, None, None], axis=2
    ).astype(jnp.bfloat16)
    packed = jnp.dot(placing, ffn_in, preferred_element_type=jnp.float32).astype(jnp.bfloat16)
    half_index = lax.axis_index("exp") % 2
    slot_halves = packed.reshape(experts * 2, capacity // 2, model_width)
    mine = lax.all_to_all(slot_halves, ("ctx", "exp"), split_axis=0, concat_axis=0, tiled=True)
    partner = partner_2(mine, "exp", 0)
    lower_first = jnp.concatenate([mine, partner], axis=1)
    upper_first = jnp.concatenate([partner, mine], axis=1)
    arrived = jnp.where(half_index == 0, lower_first, upper_first)
    sources, slot_count, _ = arrived.shape
    row_data = arrived.reshape(sources * slot_count, model_width)
    gate_part = jnp.dot(row_data, w_gate[0], preferred_element_type=jnp.float32)
    up_part = jnp.dot(row_data, w_up[0], preferred_element_type=jnp.float32)
    hidden = (jax.nn.silu(gate_part) * up_part).astype(jnp.bfloat16)
    partial_value = jnp.dot(hidden, w_down[0], preferred_element_type=jnp.float32).reshape(
        sources, slot_count, model_width
    )
    handed = lax.all_to_all(
        partial_value.astype(jnp.bfloat16), ("ctx", "exp"), split_axis=0, concat_axis=0, tiled=True
    ).astype(partial_value.dtype)
    results = handed.reshape(experts, 2, capacity, model_width).sum(axis=1).astype(jnp.bfloat16)
    picked_rows = results.reshape(experts * capacity, model_width)[slot_index].reshape(
        tok_rows, top_count, model_width
    )
    expert_mix = jnp.sum(picked_rows.astype(jnp.float32) * gate_weights[:, :, None], axis=1)
    return (residual.astype(jnp.float32) + expert_mix).astype(jnp.bfloat16)


def solution(mesh):
    placed = (
        P(("ctx", "exp"), None),
        P(),
        P(None, "exp"),
        P(None, "exp"),
        P(None, "exp"),
        P("exp", None),
        P("ctx", "exp", None),
        P(),
        P(("ctx", "exp"), None, None),
        P(("ctx", "exp"), None, None),
        P(("ctx", "exp"), None, None),
        P(("ctx", "exp"), None),
        P(("ctx", "exp"), None),
    )
    return jax.shard_map(
        shards, mesh=mesh, in_specs=placed, out_specs=P(("ctx", "exp"), None), check_vma=False
    )
```

profile of v0, /device:TPU:0, one launch (start us, length us, event | category | flops | bytes accessed | tf_op | source)
XLA Modules:
  0.0 480.8 jit_solution(6081359266340250535)
XLA Ops:
  6.5 1.3 fusion.32
  7.8 1.9 fusion.34
  9.8 21.0 %all-gather.3.cloned.1.call-done = bf16[320,2048]{1,0:T(8,128)(2,1)} async-done(((bf16[80,2048]{1,0:T(8,128)(2,1)}), bf16[320,2048]{1,0:T(8,128)(2,1)}) %all-gather.3.cloned.1.call-update) | async-done | bytes 1310736 | tf_op jit(solution)/shard_map/all_gather | solution.py:48
  30.8 3.0 fusion.29
  33.8 0.8 fusion.30
  34.6 0.9 pad_maximum_fusion
  35.8 2.8 fusion.31
  38.7 83.3 %all-gather.5.cloned.1.call-done = bf16[2560,2,512]{2,0,1:T(8,128)(2,1)} async-done(((bf16[320,2,512]{2,0,1:T(8,128)(2,1)}), bf16[2560,2,512]{2,0,1:T(8,128)(2,1)}) %all-gather.5.cloned.1.call-update) | async-done | bytes 5242896 | tf_op jit(solution)/shard_map/all_gather | solution.py:100
  122.0 57.5 %while.17 = (s32[]{:T(128)}, f32[4,320]{1,0:T(4,128)S(1)}, f32[4,320]{1,0:T(4,128)S(1)}, f32[4,320,128]{2,1,0:T(8,128)}, s32[2]{0:T(128)S(1)}, /*index=5*/bf16[3...) while((s32[]{:T(128)}, f32[4,320]{1,0:T(4,128)S(1)}, ...), condition=%wide.region_5.6_spmd.clone, body=%wide.region_2.5_spmd.clone.sunk | while | flops 887726400 | bytes 112686352 | solution.py:112
  122.0 0.6 dynamic_slice.20
  123.9 1.1 compare_and_fusion.2
  125.0 3.4 constant_dynamic-slice_fusion.2
  128.4 4.4 copy.79
  132.8 2.9 fusion.86
  135.8 1.0 fusion.87
  136.8 4.0 fusion.88
  140.8 5.1 %fusion.89 = f32[4,320]{1,0:T(4,128)S(1)} fusion(pred[4,320,1280]{2,1,0:T(32,128)(4,1)} %get-tuple-element.327, f32[4,1280,320]{1,2,0:T(8,128)} %copy-done.1, f32[4,320]{1,0:T(4,128)S(1)} %select_maximum_fusion.2), kind=kLoop, calls=%fused_computation.10.clone.1 | loop fusion | flops 6552320 | bytes 8202240 | tf_op jit(solution)/shard_map/while/body/eval_jaxpr/reduce_sum | solution.py:86
  146.5 4.1 fusion.91
  152.6 1.1 compare_and_fusion.2
  153.7 3.4 constant_dynamic-slice_fusion.2
  157.1 4.4 copy.79
  161.5 2.9 fusion.86
  164.4 1.0 fusion.87
  165.5 4.0 fusion.88
  169.5 5.1 %fusion.89 = f32[4,320]{1,0:T(4,128)S(1)} fusion(pred[4,320,1280]{2,1,0:T(32,128)(4,1)} %get-tuple-element.327, f32[4,1280,320]{1,2,0:T(8,128)} %copy-done.1, f32[4,320]{1,0:T(4,128)S(1)} %select_maximum_fusion.2), kind=kLoop, calls=%fused_computation.10.clone.1 | loop fusion | flops 6552320 | bytes 8202240 | tf_op jit(solution)/shard_map/while/body/eval_jaxpr/reduce_sum | solution.py:86
  175.2 4.3 fusion.91
  179.4 3.8 convolution_convert_fusion.2
  183.5 1.2 reduce-window.6
  185.6 22.6 %reduce-scatter.2.cloned.1.call-done = bf16[80,2048]{1,0:T(8,128)(2,1)} async-done(((bf16[320,2048]{1,0:T(8,128)(2,1)}), bf16[80,2048]{1,0:T(8,128)(2,1)}) %reduce-scatter.2.cloned.1.call-update) | async-done | bytes 327696 | tf_op jit(solution)/shard_map/reduce_scatter | solution.py:121
  208.2 1.2 fusion.36
  209.4 3.4 convolution_convert_fusion.1
  212.8 5.2 %reshape.178 = bf16[32,20,2048]{2,1,0:T(8,128)(2,1)} reshape(bf16[640,2048]{1,0:T(8,128)(2,1)} %convolution_convert_fusion.1) | data formatting | bytes 5242880 | tf_op jit(solution)/shard_map/reshape | solution.py:144
  218.0 75.8 %all_to_all.10 = bf16[32,20,2048]{2,1,0:T(8,128)(2,1)S(1)} all-to-all(bf16[32,20,2048]{2,1,0:T(8,128)(2,1)} %reshape.178), channel_id=1, replica_groups=mesh['ctx'=8,'exp'=4] {'ctx','exp'}, dimensions={0} | all-to-all | bytes 5242880 | tf_op jit(solution)/shard_map/all_to_all | solution.py:145
  293.7 3.0 copy.58
  296.7 5.2 %collective-permute-done = bf16[32,20,2048]{2,0,1:T(8,128)(2,1)} collective-permute-done((bf16[32,20,2048]{2,0,1:T(8,128)(2,1)}, bf16[32,20,2048]{2,0,1:T(8,128)(2,1)}, u32[]{:S(2)}, u32[]{:S(2)}) %collective-permute-start) | collective-permute-done | bytes 2621472 | tf_op jit(solution)/shard_map/ppermute | solution.py:16
  302.0 3.2 copy.59
  305.2 4.0 maximum_select_fusion
  309.2 3.9 fusion.26
  313.2 5.4 %multiply_convert_fusion = bf16[1280,704]{0,1:T(8,128)(2,1)} fusion(f32[1280,704]{0,1:T(8,128)S(1)} %fusion.26, bf16[1280,2048]{1,0:T(8,128)(2,1)S(1)} %bitcast.122, bf16[1,2048,704]{1,2,0:T(8,128)(2,1)S(1)} %copy-done.14), kind=kOutput, calls=%fused_computation.36 | convolution fusion | flops 3696394240 | bytes 13533184 | tf_op jit(solution)/shard_map/dot_general | solution.py:153
  318.6 3.9 copy.61
  322.5 7.6 %convolution_convert_fusion = bf16[32,40,2048]{2,1,0:T(8,128)(2,1)} fusion(bf16[32,40,704]{2,1,0:T(8,128)(2,1)} %bitcast.123, bf16[1,704,2048]{2,1,0:T(8,128)(2,1)S(1)} %copy-done), kind=kOutput, calls=%fused_computation.35 | convolution fusion | flops 3693608960 | bytes 9928704 | tf_op jit(solution)/shard_map/dot_general | solution.py:155
  330.1 4.0 all-to-all-start.1
  334.3 116.7 %all-to-all-done.1 = bf16[32,40,2048]{2,1,0:T(8,128)(2,1)} async-done(((bf16[32,40,2048]{2,1,0:T(8,128)(2,1)}), bf16[32,40,2048]{2,1,0:T(8,128)(2,1)}, u32[]{:S(2)}, u32[]{:S(2)}) %all-to-all-start.1) | async-done | bytes 5242912 | tf_op jit(solution)/shard_map/all_to_all | solution.py:158
  451.0 6.0 %bitcast_reduce_fusion = bf16[16,40,2048]{2,1,0:T(8,128)(2,1)} fusion(bf16[32,40,2048]{2,1,0:T(8,128)(2,1)} %all-to-all-done.1), kind=kLoop, calls=%fused_computation.33 | loop fusion | flops 1310720 | bytes 7864320 | tf_op jit(solution)/shard_map/reduce_sum | solution.py:161
  457.0 7.3 %gather_fusion = bf16[480,2048]{1,0:T(8,128)(2,1)} fusion(bf16[640,2048]{1,0:T(8,128)(2,1)} %bitcast.117, s32[1024]{0:T(1024)S(1)} %pad_clamp_fusion), kind=kCustom, calls=%fused_computation | custom fusion | bytes 3934080 | tf_op jit(solution)/shard_map/gather | solution.py:162
  464.4 4.5 reshape.182
  468.9 4.5 multiply_reduce_fusion
  473.4 0.8 fusion.39
  (90 shorter events, 6.1 us)
Async XLA Ops:
  6.5 315.9 %copy-start = (bf16[1,704,2048]{2,1,0:T(8,128)(2,1)S(1)}, bf16[1,704,2048]{2,1,0:T(8,128)(2,1)}, u32[]{:S(2)}) copy-start(bf16[1,704,2048]{2,1,0:T(8,128)(2,1)} %param.25) | copy-start | bytes 8650756
  6.5 24.2 %all-gather.3.cloned.1.call-start = ((), (), s32[]{:S(2)}) async-start(), calls=%async_computation.3 | async-start | bytes 1638400 | tf_op jit(solution)/shard_map/all_gather | solution.py:48
  9.7 112.2 %all-gather.5.cloned.1.call-start = ((), (), s32[]{:S(2)}) async-start(), calls=%async_computation.4 | async-start | bytes 5898240 | tf_op jit(solution)/shard_map/all_gather | solution.py:100
  30.8 3.0 copy-start.15
  30.8 3.0 copy-start.16
  33.8 1.9 copy-start.9
  35.5 172.6 %reduce-scatter.2.cloned.1.call-start = ((), (), s32[]{:S(2)}) async-start(), calls=%async_computation.5 | async-start | bytes 1638400 | tf_op jit(solution)/shard_map/reduce_scatter | solution.py:121
  135.8 1.0 copy-start.6
  136.8 4.0 copy-start.1
  140.8 5.3 %copy-start.2 = (f32[4,1280,320]{1,2,0:T(8,128)S(1)}, f32[4,1280,320]{1,2,0:T(8,128)}, u32[]{:S(2)}) copy-start(f32[4,1280,320]{1,2,0:T(8,128)} %copy-done.1) | copy-start | bytes 19660804 | tf_op jit(solution)/shard_map/while
  140.8 5.7 %copy-start.3 = (pred[4,320,1280]{2,1,0:T(32,128)(4,1)S(1)}, pred[4,320,1280]{2,1,0:T(32,128)(4,1)}, u32[]{:S(2)}) copy-start(pred[4,320,1280]{2,1,0:T(32,128)(4,1)} %get-tuple-element.327) | copy-start | bytes 4915204 | tf_op jit(solution)/shard_map/while
  164.4 1.0 copy-start.6
  165.4 4.0 copy-start.1
  169.4 5.3 %copy-start.2 = (f32[4,1280,320]{1,2,0:T(8,128)S(1)}, f32[4,1280,320]{1,2,0:T(8,128)}, u32[]{:S(2)}) copy-start(f32[4,1280,320]{1,2,0:T(8,128)} %copy-done.1) | copy-start | bytes 19660804 | tf_op jit(solution)/shard_map/while
  169.4 5.7 %copy-start.3 = (pred[4,320,1280]{2,1,0:T(32,128)(4,1)S(1)}, pred[4,320,1280]{2,1,0:T(32,128)(4,1)}, u32[]{:S(2)}) copy-start(pred[4,320,1280]{2,1,0:T(32,128)(4,1)} %get-tuple-element.327) | copy-start | bytes 4915204 | tf_op jit(solution)/shard_map/while
  179.4 3.9 copy-start.11
  179.4 28.7 %copy-start.7 = (bf16[80,2048]{1,0:T(8,128)(2,1)S(1)}, bf16[80,2048]{1,0:T(8,128)(2,1)}, u32[]{:S(2)}) copy-start(bf16[80,2048]{1,0:T(8,128)(2,1)} %param.15) | copy-start | bytes 983044
  179.4 29.9 %copy-start.10 = (f32[2048]{0:T(1024)S(1)}, f32[2048]{0:T(1024)}, u32[]{:S(2)}) copy-start(f32[2048]{0:T(1024)} %param.22) | copy-start | bytes 24580
  293.7 3.0 copy-start.4
  296.7 5.3 %collective-permute-start = (bf16[32,20,2048]{2,0,1:T(8,128)(2,1)}, bf16[32,20,2048]{2,0,1:T(8,128)(2,1)}, u32[]{:S(2)}, u32[]{:S(2)}) collective-permute-start(bf16[32,20,2048]{2,0,1:T(8,128)(2,1)} %copy.58), channel_id=1, source_target_pairs={{0,1},{1,0},{2,3},{3,2},{4,5},{5,4},{6,7},{7,6},{8,9},{9,8},{10,11... | collective-permute-start | bytes 7864328 | tf_op jit(solution)/shard_map/ppermute | solution.py:16
  296.7 8.5 %copy-start.5 = (bf16[32,20,2048]{2,1,0:T(8,128)(2,1)S(1)}, bf16[32,20,2048]{2,1,0:T(8,128)(2,1)}, u32[]{:S(2)}) copy-start(bf16[32,20,2048]{2,1,0:T(8,128)(2,1)} %copy-done.4) | copy-start | bytes 7864324
  305.2 4.0 copy-start.13
  309.2 4.0 copy-start.14
  330.1 4.1 copy-start.12
  330.1 121.0 %all-to-all-start.1 = ((bf16[32,40,2048]{2,1,0:T(8,128)(2,1)}), bf16[32,40,2048]{2,1,0:T(8,128)(2,1)}, u32[]{:S(2)}, u32[]{:S(2)}) async-start(bf16[32,40,2048]{2,1,0:T(8,128)(2,1)} %convolution_convert_fusion), calls=%async_computation.2 | async-start | bytes 10485760 | tf_op jit(solution)/shard_map/all_to_all | solution.py:158
  468.9 4.5 copy-start.8
Sparse Core Ops, SparseCore 0:
  9.8 20.8 all-gather.2
  35.7 86.2 all-gather.4
  183.4 24.7 reduce-scatter.1
where the time goes:
time: 482 us; the launch traced here: 481 us
  waiting for transfers between devices  249 us (52%)
  blocking collectives  75.8 us (16%)
  local copies, waits for them, and re-layouts  52 us (11%)
  matrix products  49.1 us (10%)
  other arithmetic  37.3 us (8%)
  between operations  13.4 us (3%)
    all_to_all x1, waiting for transfers between devices, shards(): lax.all_to_all(partial_value.astype(jnp.bfloat16), ('ctx', 'exp'), split_...  117 us
    all_gather x1, waiting for transfers between devices, shards(): shard_piece = lax.all_gather(keys_values, 'ctx', axis=0, tiled=True)  83.3 us
    all_to_all x1, blocking collectives, shards(): lax.all_to_all(slot_halves, ('ctx', 'exp'), split_axis=0, concat_axis=0,...  75.8 us
    reduce_scatter x1, waiting for transfers between devices, shards(): lax.psum_scatter(jnp.dot(row_data, w_out, preferred_element_type=jnp.floa...  22.6 us
    all_gather x1, waiting for transfers between devices, shards(): shard_piece = lax.all_gather(normed, 'exp', axis=0, tiled=True)  21 us
    dynamic_slice x6, local copies, waits for them, and re-layouts, shards(): result, _ = lax.scan(fold_step, initial, (stacked, offsets))  16.9 us
    reduce_sum x2, other arithmetic, attend_rows(): run_sum = run_sum * rescale + jnp.sum(weights, axis=-1)  10.3 us
  transfers between devices with their start and end apart: 5, of which 5 were waited for; matrix products, arithmetic and copies ran while one was open for 1% of the time, Pallas kernels for 0%

commit v1 on v0

v1 whole, which is shorter than its diff:
```python
import functools
import math

import jax
import jax.numpy as jnp
from jax import lax
from jax.experimental import pallas as pl
from jax.experimental.pallas import tpu as pltpu
from jax.sharding import PartitionSpec as P

AXES = ("ctx", "exp")
PARAMS = pltpu.CompilerParams(vmem_limit_bytes=56 * 1024 * 1024)
VMEM = pl.BlockSpec(memory_space=pltpu.VMEM)
SMEM = pl.BlockSpec(memory_space=pltpu.SMEM)
PAD_ROWS = 16
LANES = 128


def move(block, target):
    ctx_count, exp_count = lax.axis_size("ctx"), lax.axis_size("exp")
    route = []
    for ctx in range(ctx_count):
        for exp in range(exp_count):
            z, x, y, c = target(ctx // 2, ctx % 2, exp // 2, exp % 2)
            route.append((ctx * exp_count + exp, (z * 2 + x) * exp_count + y * 2 + c))
    return lax.ppermute(block, AXES, route)


def swap_core(block):
    return move(block, lambda z, x, y, c: (z, x, y, c ^ 1))


def swap_layer(block, hop):
    return move(block, lambda z, x, y, c: (z, x ^ (hop >> 1), y ^ (hop & 1), c))


def turn_z(block, turn):
    depth = lax.axis_size("ctx") // 2
    return move(block, lambda z, x, y, c: ((z + turn) % depth, x, y, c))


def head_out(block, turn):
    depth = lax.axis_size("ctx") // 2
    return move(block, lambda z, x, y, c: ((z + turn) % depth, c, y, x))


def head_back(block, turn):
    depth = lax.axis_size("ctx") // 2
    return move(block, lambda z, x, y, c: ((z - turn) % depth, c, y, x))


def normalize(values, gain_vec):
    floats = values.astype(jnp.float32)
    factor = lax.rsqrt(jnp.mean(floats * floats, axis=-1, keepdims=True) + 1e-06)
    return (floats * factor * gain_vec).astype(jnp.bfloat16)


def f32_dot(left, right):
    return jnp.dot(left, right, preferred_element_type=jnp.float32)


def struct(*shape, dtype=jnp.bfloat16):
    return jax.ShapeDtypeStruct(shape, dtype)


def call(kernel, outs, operands, scratch=(), flops=0, smem=1):
    return pl.pallas_call(
        kernel,
        out_shape=outs,
        in_specs=[SMEM] * smem + [VMEM] * (len(operands) - smem),
        out_specs=jax.tree.map(lambda _: VMEM, outs),
        scratch_shapes=list(scratch),
        compiler_params=PARAMS,
        cost_estimate=pl.CostEstimate(
            flops=flops,
            bytes_accessed=sum(a.size * a.dtype.itemsize for a in operands),
            transcendentals=0,
        ),
    )(*operands)


def project_kernel(hops, depth, head_dim, place, *refs):
    row_refs, (gain, w_query, w_key, w_value, marks) = refs[:hops], refs[hops : hops + 5]
    outs, (rows, mixed) = refs[hops + 5 : hops + 5 + depth], refs[hops + 5 + depth :]
    exp_index, z_index = place[0], place[1]
    tok_rows = row_refs[0].shape[0]
    block_len = hops * tok_rows
    for hop, row_ref in enumerate(row_refs):
        start = pl.multiple_of((exp_index ^ hop) * tok_rows, 16)
        rows[pl.ds(start, tok_rows), :] = normalize(row_ref[...], gain[...])
    for part, weight in enumerate((w_query, w_key, w_value)):
        mixed[part] = f32_dot(rows[...], weight[...]).astype(jnp.bfloat16)
    for turn in range(depth):
        head = lax.rem(z_index + turn, depth)
        columns = pl.ds(pl.multiple_of(head * head_dim, head_dim), head_dim)
        for part in range(3):
            outs[turn][0:block_len, part * head_dim : (part + 1) * head_dim] = mixed[part, :, columns]
        outs[turn][block_len : block_len + PAD_ROWS, :] = marks[head]


def attend_kernel(depth, block_len, head_dim, place, *refs):
    own_refs, near_refs = refs[:depth], refs[depth : 2 * depth]
    outs, (own, near, mixed) = refs[2 * depth : 3 * depth], refs[3 * depth :]
    z_index, core = place[1], place[2]
    scaling = 1.0 / math.sqrt(head_dim)
    for turn in range(depth):
        source = lax.rem(z_index + depth - turn, depth)
        own[source] = own_refs[turn][...]
        near[source] = near_refs[turn][0:block_len, head_dim : 3 * head_dim]
    key_pos = lax.broadcasted_iota(jnp.int32, (block_len, block_len), 0)
    query_pos = lax.broadcasted_iota(jnp.int32, (block_len, block_len), 1)
    causal = jnp.where(key_pos <= query_pos, 0.0, -1e30)
    for level in range(depth):
        query = own[level, 0:block_len, 0:head_dim]
        marks = own[level, block_len : block_len + PAD_ROWS, 0:block_len].astype(jnp.float32)
        marks = marks[0:1].astype(jnp.int32)
        run_max = run_sum = total = None
        order = [(level, True)] + [(c, True) for c in range(level)] + [(c, False) for c in range(level + 1)]
        for c, mine in order:
            if mine:
                key = own[c, 0:block_len, head_dim : 2 * head_dim]
                value = own[c, 0:block_len, 2 * head_dim : 3 * head_dim]
            else:
                key, value = near[c, :, 0:head_dim], near[c, :, head_dim : 2 * head_dim]
            scores = scaling * lax.dot_general(
                key, query, (((1,), (1,)), ((), ())), preferred_element_type=jnp.float32
            )
            if mine and c == level:
                scores = scores + causal
            else:
                bit = 2 * c + (core if mine else 1 - core)
                chosen = lax.shift_right_logical(marks, jnp.broadcast_to(bit, marks.shape)) & 1
                scores = jnp.where(chosen == 1, scores, -1e30)
            top = jnp.max(scores, axis=0, keepdims=True)
            new_max = top if run_max is None else jnp.maximum(run_max, top)
            weights = jnp.exp(scores - new_max)
            added = jnp.sum(weights, axis=0, keepdims=True)
            product = lax.dot_general(
                value,
                weights.astype(jnp.bfloat16),
                (((0,), (0,)), ((), ())),
                preferred_element_type=jnp.float32,
            )
            if run_max is None:
                run_sum, total = added, product
            else:
                rescale = jnp.exp(run_max - new_max)
                run_sum, total = run_sum * rescale + added, total * rescale + product
            run_max = new_max
        mixed[level] = (total / run_sum).T.astype(jnp.bfloat16)
    for turn in range(depth):
        outs[turn][...] = mixed[lax.rem(z_index + depth - turn, depth)]


def attend_gathered(normed_block, w_query, w_key, w_value, sel_blocks):
    block_len, heads_here, _ = sel_blocks.shape
    hidden_cols = w_query.shape[1]
    head_dim = hidden_cols // heads_here
    ctx_count, ctx_index = lax.axis_size("ctx"), lax.axis_index("ctx")
    query_part, key_part, value_part = (
        f32_dot(normed_block, weight).astype(jnp.bfloat16) for weight in (w_query, w_key, w_value)
    )
    queries = query_part.reshape(block_len, heads_here, head_dim)
    keys_values = jnp.stack([key_part, value_part], axis=1)
    block_ids = jnp.arange(ctx_count, dtype=jnp.int32)
    chosen = jnp.any(sel_blocks[:, :, :, None] == block_ids, axis=2) & (block_ids < ctx_index)
    position = jnp.arange(block_len, dtype=jnp.int32)
    causal = position[None, :] <= position[:, None]
    scaling = 1.0 / math.sqrt(head_dim)

    def fold_step(running, operands):
        run_max, run_sum, totals = running
        piece, block = operands
        key_rows = piece[:, 0].reshape(block_len, heads_here, head_dim)
        value_rows = piece[:, 1].reshape(block_len, heads_here, head_dim)
        scores = (
            jnp.einsum("qhd,khd->hqk", queries, key_rows, preferred_element_type=jnp.float32)
            * scaling
        )
        picked = jnp.take(chosen, block, axis=2).T[:, :, None]
        allowed = picked | ((block == ctx_index) & causal)[None]
        new_max = jnp.maximum(run_max, jnp.max(jnp.where(allowed, scores, -jnp.inf), axis=-1))
        weights = jnp.where(allowed, jnp.exp(scores - new_max[..., None]), 0.0)
        rescale = jnp.exp(run_max - new_max)
        run_sum = run_sum * rescale + jnp.sum(weights, axis=-1)
        totals = totals * rescale[..., None] + jnp.einsum(
            "hqk,khd->hqd",
            weights.astype(jnp.bfloat16),
            value_rows,
            preferred_element_type=jnp.float32,
        )
        return (new_max, run_sum, totals), None

    initial = (
        jnp.full((heads_here, block_len), -1e30, jnp.float32),
        jnp.zeros((heads_here, block_len), jnp.float32),
        jnp.zeros((heads_here, block_len, head_dim), jnp.float32),
    )
    gathered = lax.all_gather(keys_values, "ctx", axis=0)
    (_, run_sum, totals), _ = lax.scan(fold_step, initial, (gathered, block_ids))
    attended = (totals / run_sum[..., None]).astype(jnp.bfloat16)
    return [attended[head] for head in range(heads_here)]


def mix_kernel(hops, heads, head_dim, place, *refs):
    head_refs, w_out = refs[:heads], refs[heads]
    kept, given, attended, mixed = refs[heads + 1 :]
    exp_index, turned = place[0], place[3]
    tok_rows = kept.shape[1]
    for turn, head_ref in enumerate(head_refs):
        head = lax.rem(turned + turn, heads)
        attended[:, pl.ds(pl.multiple_of(head * head_dim, head_dim), head_dim)] = head_ref[...]
    mixed[...] = f32_dot(attended[...], w_out[...]).astype(jnp.bfloat16)
    for hop in range(hops):
        start = pl.multiple_of((exp_index ^ hop) * tok_rows, 16)
        (given if hop & 1 else kept)[hop >> 1] = mixed[pl.ds(start, tok_rows), :]


def residual_kernel(inputs, kept, given, far, gain, residual, ffn_in):
    summed = kept[0].astype(jnp.float32) + given[0].astype(jnp.float32) + far[...].astype(jnp.float32)
    rounded = (inputs[...].astype(jnp.float32) + summed).astype(jnp.bfloat16)
    residual[...] = rounded
    ffn_in[...] = normalize(rounded, gain[...])


def pack_kernel(depth, capacity, place, routes, *refs):
    sources, outs, (rows,) = refs[:depth], refs[depth : depth + 4], refs[depth + 4 :]
    expert = place[4]
    tok_rows = sources[0].shape[0]
    total = depth * tok_rows
    for turn in range(depth):
        rows[turn * tok_rows : (turn + 1) * tok_rows, :] = sources[turn][...]
    earlier = lax.broadcasted_iota(jnp.int32, (total, total), 0)
    later = lax.broadcasted_iota(jnp.int32, (total, total), 1)
    before = ((earlier < later) & (earlier // tok_rows == later // tok_rows)).astype(jnp.bfloat16)
    first_slot = lax.broadcasted_iota(jnp.int32, (1, total), 1) // tok_rows * capacity
    slot = lax.broadcasted_iota(jnp.int32, (depth * capacity, total), 0)
    for hop in range(4):
        hit = jnp.where(routes[...] == (expert ^ hop).astype(jnp.float32), 1.0, 0.0)
        member = jnp.sum(hit, axis=0, keepdims=True)
        place_in = f32_dot(jnp.broadcast_to(member, (16, total)).astype(jnp.bfloat16), before)[0:1]
        target = jnp.where(member > 0.5, place_in.astype(jnp.int32) + first_slot, -1)
        placing = jnp.where(slot == target, 1.0, 0.0).astype(jnp.bfloat16)
        outs[hop][...] = f32_dot(placing, rows[...]).astype(jnp.bfloat16)


def expert_kernel(parts, *refs):
    row_refs, (w_gate, w_up, w_down), outs = refs[:parts], refs[parts : parts + 3], refs[parts + 3 :]
    across = (((1,), (1,)), ((), ()))
    for first in range(0, parts, 2):
        rows = jnp.concatenate([row_refs[first][...], row_refs[first + 1][...]], axis=0)
        gate_part = lax.dot_general(rows, w_gate[...], across, preferred_element_type=jnp.float32)
        up_part = lax.dot_general(rows, w_up[...], across, preferred_element_type=jnp.float32)
        hidden = (gate_part / (1.0 + jnp.exp(-gate_part)) * up_part).astype(jnp.bfloat16)
        result = f32_dot(hidden, w_down[...]).astype(jnp.bfloat16)
        half = row_refs[first].shape[0]
        outs[first][...] = result[:half]
        outs[first + 1][...] = result[half:]


def combine_kernel(depth, capacity, place, routes, gates, *refs):
    returned, outs = refs[:4], refs[4 : 4 + depth]
    expert = place[4]
    total = routes.shape[0]
    tok_rows = total // depth
    later = lax.broadcasted_iota(jnp.int32, (total, total), 0)
    earlier = lax.broadcasted_iota(jnp.int32, (total, total), 1)
    before = ((earlier < later) & (earlier // tok_rows == later // tok_rows)).astype(jnp.bfloat16)
    first_slot = lax.broadcasted_iota(jnp.int32, (total, 1), 0) // tok_rows * capacity
    slot = lax.broadcasted_iota(jnp.int32, (total, depth * capacity), 1)
    mixed = jnp.zeros((total, returned[0].shape[1]), jnp.float32)
    for hop in range(4):
        hit = routes[...] == (expert ^ hop).astype(jnp.float32)
        member = jnp.sum(jnp.where(hit, 1.0, 0.0), axis=1, keepdims=True)
        factor = jnp.sum(jnp.where(hit, gates[...], 0.0), axis=1, keepdims=True)
        place_in = f32_dot(before, jnp.broadcast_to(member, (total, LANES)).astype(jnp.bfloat16))[:, 0:1]
        target = jnp.where(member > 0.5, place_in.astype(jnp.int32) + first_slot, -1)
        placing = jnp.where(slot == target, factor, 0.0)
        upper = placing.astype(jnp.bfloat16)
        lower = (placing - upper.astype(jnp.float32)).astype(jnp.bfloat16)
        mixed = mixed + f32_dot(upper, returned[hop][...]) + f32_dot(lower, returned[hop][...])
    for turn in range(depth):
        outs[turn][...] = mixed[turn * tok_rows : (turn + 1) * tok_rows].astype(jnp.bfloat16)


def shards(
    inputs,
    attn_gain,
    w_query,
    w_key,
    w_value,
    w_out,
    sel_blocks,
    ffn_gain,
    w_gate,
    w_up,
    w_down,
    routes,
    gate_weights,
):
    tok_rows, model_width = inputs.shape
    block_len, heads_here, pick_count = sel_blocks.shape
    hidden_cols = w_query.shape[1]
    head_dim = hidden_cols // heads_here
    ctx_count, exp_count = lax.axis_size("ctx"), lax.axis_size("exp")
    depth = ctx_count // 2
    ctx_index, exp_index = lax.axis_index("ctx"), lax.axis_index("exp")
    z_index, x_index = ctx_index // 2, ctx_index % 2
    expert = (ctx_index * exp_count + exp_index) // 2
    by_head = heads_here == depth and block_len <= 3 * head_dim and head_dim == LANES
    place = jnp.stack(
        [exp_index, z_index, exp_index % 2, z_index if by_head else jnp.zeros_like(z_index), expert]
    ).astype(jnp.int32)

    noted = jnp.concatenate([routes.astype(jnp.float32), gate_weights], axis=1)
    noted = lax.all_gather(noted, "ctx", axis=0).reshape(depth, 2, tok_rows, -1)
    noted = lax.dynamic_index_in_dim(noted, x_index, 1, keepdims=False)
    sources = (z_index - jnp.arange(depth)) % depth
    noted = noted[sources].reshape(depth * tok_rows, -1)
    top_count = routes.shape[1]
    near_routes, near_gates = noted[:, :top_count], noted[:, top_count:]

    near = swap_core(inputs)
    far = move(inputs, lambda z, x, y, c: (z, x, y ^ 1, c))
    far_near = swap_core(far)
    if by_head:
        marks = jnp.sum(
            jnp.where(sel_blocks < ctx_index, jnp.left_shift(1, jnp.minimum(sel_blocks, 30)), 0), axis=2
        )
        marks = jnp.pad(marks.T.astype(jnp.bfloat16), ((0, 0), (0, 3 * head_dim - block_len)))
        marks = jnp.broadcast_to(marks[:, None], (heads_here, PAD_ROWS, 3 * head_dim))
        payload = struct(block_len + PAD_ROWS, 3 * head_dim)
        sent = call(
            functools.partial(project_kernel, exp_count, depth, head_dim),
            [payload] * depth,
            [place, inputs, near, far, far_near, attn_gain.reshape(1, -1), w_query, w_key, w_value, marks],
            [
                pltpu.VMEM((block_len, model_width), jnp.bfloat16),
                pltpu.VMEM((3, block_len, hidden_cols), jnp.bfloat16),
            ],
            flops=6 * block_len * model_width * hidden_cols,
        )
        own = [head_out(sent[turn], turn) for turn in range(depth)]
        beside = [swap_core(block) for block in own]
        mixed = call(
            functools.partial(attend_kernel, depth, block_len, head_dim),
            [struct(block_len, head_dim)] * depth,
            [place, *own, *beside],
            [
                pltpu.VMEM((depth, block_len + PAD_ROWS, 3 * head_dim), jnp.bfloat16),
                pltpu.VMEM((depth, block_len, 2 * head_dim), jnp.bfloat16),
                pltpu.VMEM((depth, block_len, head_dim), jnp.bfloat16),
            ],
            flops=4 * depth * ctx_count * block_len * block_len * head_dim,
        )
        heads = [head_back(mixed[turn], turn) for turn in range(depth)]
    else:
        block = jnp.stack([inputs, near, far, far_near])[exp_index ^ jnp.arange(exp_count)]
        normed = normalize(block.reshape(block_len, model_width), attn_gain)
        heads = attend_gathered(normed, w_query, w_key, w_value, sel_blocks)

    halves = struct(exp_count // 2, tok_rows, model_width)
    kept, given = call(
        functools.partial(mix_kernel, exp_count, heads_here, head_dim),
        [halves, halves],
        [place, *heads, w_out],
        [
            pltpu.VMEM((block_len, hidden_cols), jnp.bfloat16),
            pltpu.VMEM((block_len, model_width), jnp.bfloat16),
        ],
        flops=2 * block_len * model_width * hidden_cols,
    )
    given = swap_core(given)
    beyond = (kept[1].astype(jnp.float32) + given[1].astype(jnp.float32)).astype(jnp.bfloat16)
    beyond = move(beyond, lambda z, x, y, c: (z, x, y ^ 1, c))
    residual, ffn_in = call(
        residual_kernel,
        [struct(tok_rows, model_width)] * 2,
        [inputs, kept, given, beyond, ffn_gain.reshape(1, -1)],
        smem=0,
    )

    experts = ctx_count * exp_count // 2
    capacity = 2 * max(1, (tok_rows * top_count + experts - 1) // experts * 2 // 3)
    slots = depth * capacity
    column = [ffn_in] + [turn_z(ffn_in, turn) for turn in range(1, depth)]
    packed = call(
        functools.partial(pack_kernel, depth, capacity),
        [struct(slots, model_width)] * 4,
        [place, near_routes.T, *column],
        [pltpu.VMEM((depth * tok_rows, model_width), jnp.bfloat16)],
        flops=8 * slots * depth * tok_rows * model_width,
    )
    arrived = [packed[0]] + [swap_layer(packed[hop], hop) for hop in range(1, 4)]
    beside = [swap_core(rows) for rows in arrived]
    weights = [w_gate[0].T, w_up[0].T, w_down[0]]

    def expert_rows(rows):
        return call(
            functools.partial(expert_kernel, len(rows)),
            [struct(slots, model_width)] * len(rows),
            [*rows, *weights],
            flops=6 * len(rows) * slots * model_width * w_gate.shape[2],
            smem=0,
        )

    own_part = expert_rows(arrived)
    beside_part = expert_rows(beside)
    other_part = [swap_core(rows) for rows in beside_part]
    results = [
        (own.astype(jnp.float32) + other.astype(jnp.float32)).astype(jnp.bfloat16)
        for own, other in zip(own_part, other_part)
    ]
    returned = [results[0]] + [swap_layer(results[hop], hop) for hop in range(1, 4)]
    sums = call(
        functools.partial(combine_kernel, depth, capacity),
        [struct(tok_rows, model_width)] * depth,
        [place, near_routes, near_gates, *returned],
        flops=16 * slots * depth * tok_rows * model_width,
    )
    layer_out = residual.astype(jnp.float32) + sums[0].astype(jnp.float32)
    for turn in range(1, depth):
        layer_out = layer_out + turn_z(sums[turn], -turn).astype(jnp.float32)
    return layer_out.astype(jnp.bfloat16)


def solution(mesh):
    placed = (
        P(("ctx", "exp"), None),
        P(),
        P(None, "exp"),
        P(None, "exp"),
        P(None, "exp"),
        P("exp", None),
        P("ctx", "exp", None),
        P(),
        P(("ctx", "exp"), None, None),
        P(("ctx", "exp"), None, None),
        P(("ctx", "exp"), None, None),
        P(("ctx", "exp"), None),
        P(("ctx", "exp"), None),
    )
    return jax.shard_map(
        shards, mesh=mesh, in_specs=placed, out_specs=P(("ctx", "exp"), None), check_vma=False
    )
```

time: 482 us -> 281 us (0.58)
  waiting for transfers between devices: 249 us -> 126 us
  Pallas kernels: 0 us -> 58.1 us
  matrix products: 49.1 us -> 0 us
  blocking collectives: 75.8 us -> 30.5 us
  starting transfers between devices: 4.07 us -> 49.1 us
  local copies, waits for them, and re-layouts: 52 us -> 9.76 us
  other arithmetic: 37.3 us -> 6.77 us
  between operations: 13.4 us -> 0.28 us
    ppermute x1 -> x37, waiting for transfers between devices: 5.25 us -> 126 us  [move(): return lax.ppermute(block, AXES, route)]
    all_to_all x1 -> x0, waiting for transfers between devices: 117 us -> none  [shards(): lax.all_to_all(partial_value.astype(jnp.bfloat16), ('ctx', 'exp'), split_...]
    all_gather x2 -> x0, waiting for transfers between devices: 104 us -> none  [the longest x1 83.3 us: shards(): shard_piece = lax.all_gather(keys_values, 'ctx', axis=0, tiled=True)]
    all_to_all x1 -> x0, blocking collectives: 75.8 us -> none  [shards(): lax.all_to_all(slot_halves, ('ctx', 'exp'), split_axis=0, concat_axis=0,...]
    pallas_call x0 -> x8, Pallas kernels: none -> 58.1 us  [call(): pl.pallas_call(kernel, out_shape=outs, in_specs=[SMEM] * smem + [VMEM] *...]
    dot_general x14 -> x0, matrix products: 49.1 us -> none  [the longest x2 8.41 us: attend_rows(): jnp.einsum('hqk,khd->hqd', weights.astype(jnp.bfloat16), value_rows, pref...]
    ppermute x1 -> x37, starting transfers between devices: 0.01 us -> 49.1 us  [move(): return lax.ppermute(block, AXES, route)]
    all_gather x0 -> x1, blocking collectives: none -> 30.5 us  [shards(): noted = lax.all_gather(noted, 'ctx', axis=0).reshape(depth, 2, tok_rows, -1)]
  transfers between devices with their start and end apart: 5 -> 37, of which waited for: 5 -> 20; matrix products, arithmetic and copies ran while one was open for 1% -> 2% of each run, Pallas kernels for 0% -> 4%
where the time goes in v1:
time: 281 us
  waiting for transfers between devices  126 us (45%)
  Pallas kernels  58.1 us (21%)
  starting transfers between devices  49.1 us (17%)
  blocking collectives  30.5 us (11%)
  local copies, waits for them, and re-layouts  9.76 us (3%)
  other arithmetic  6.77 us (2%)
    ppermute x37, waiting for transfers between devices, move(): return lax.ppermute(block, AXES, route)  126 us
    pallas_call x8, Pallas kernels, call(): pl.pallas_call(kernel, out_shape=outs, in_specs=[SMEM] * smem + [VMEM] *...  58.1 us
    ppermute x37, starting transfers between devices, move(): return lax.ppermute(block, AXES, route)  49.1 us
    all_gather x1, blocking collectives, shards(): noted = lax.all_gather(noted, 'ctx', axis=0).reshape(depth, 2, tok_rows, -1)  30.5 us
    unnamed x76, local copies, waits for them, and re-layouts  6.28 us
  transfers between devices with their start and end apart: 37, of which 20 were waited for; matrix products, arithmetic and copies ran while one was open for 2% of the time, Pallas kernels for 4%

profile of v1, /device:TPU:0, one launch (start us, length us, event | category | flops | bytes accessed | tf_op | source)
XLA Modules:
  0.0 280.8 jit_solution(12751325606411475162)
XLA Ops:
  0.0 3.0 %collective-permute-start.1 = (bf16[80,2048]{1,0:T(8,128)(2,1)}, bf16[80,2048]{1,0:T(8,128)(2,1)S(1)}, u32[]{:S(2)}, u32[]{:S(2)}) collective-permute-start(bf16[80,2048]{1,0:T(8,128)(2,1)} %inputs.1), channel_id=1, source_target_pairs={{0,2},{1,3},{2,0},{3,1},{4,6},{5,7},{6,4},{7,5},{8,10},{9,11},{10,... | collective-permute-start | bytes 983048 | tf_op jit(solution)/shard_map/ppermute | solution.py:26
  3.0 7.9 %collective-permute-done.1.refs_2_ = bf16[80,2048]{1,0:T(8,128)(2,1)S(1)} collective-permute-done((bf16[80,2048]{1,0:T(8,128)(2,1)}, bf16[80,2048]{1,0:T(8,128)(2,1)S(1)}, u32[]{:S(2)}, u32[]{:S(2)}) %collective-permute-start.1) | collective-permute-done | bytes 327712 | tf_op jit(solution)/shard_map/ppermute | solution.py:26
  13.2 7.3 %shard_map.127 = (bf16[336,384]{1,0:T(8,128)(2,1)}, bf16[336,384]{1,0:T(8,128)(2,1)}, bf16[336,384]{1,0:T(8,128)(2,1)}, bf16[336,384]{1,0:T(8,128)(2,1)}) custom-call(s32[5]{0:T(128)} %stack.20.place, bf16[80,2048]{1,0:T(8,128)(2,1)} %inputs.1, bf16[80,2048]{1,0:T(8,128)(2,1)} %copy-done.5, bf16[80,2048]{1,0:T(8,128)(2,1)} %copy-done.4, ...), custom_call_target="tpu_custom_call" | custom-call | flops 2013265920 | bytes 7659540 | tf_op jit(solution)/shard_map/pallas_call | solution.py:67
  20.6 1.6 collective-permute-start.3
  22.2 1.8 collective-permute-start.4
  24.0 2.6 collective-permute-start.5
  26.6 1.3 collective-permute-start.6
  27.9 2.6 collective-permute-start.7
  30.5 1.7 collective-permute-done.4.refs_1_
  32.2 3.8 %collective-permute-start.8 = (bf16[336,384]{1,0:T(8,128)(2,1)S(1)}, bf16[336,384]{1,0:T(8,128)(2,1)S(1)}, u32[]{:S(2)}, u32[]{:S(2)}) collective-permute-start(bf16[336,384]{1,0:T(8,128)(2,1)S(1)} %collective-permute-done.4.refs_1_), channel_id=1, source_target_pairs={{0,1},{1,0},{2,3},{3,2},{4,5},{5,4},{6,7},{7,6},{8,9},{9,8},{10,11... | collective-permute-start | bytes 774152 | tf_op jit(solution)/shard_map/ppermute | solution.py:26
  36.0 8.3 %collective-permute-done.5.refs_2_ = bf16[336,384]{1,0:T(8,128)(2,1)S(1)} collective-permute-done((bf16[336,384]{1,0:T(8,128)(2,1)}, bf16[336,384]{1,0:T(8,128)(2,1)S(1)}, u32[]{:S(2)}, u32[]{:S(2)}) %collective-permute-start.5) | collective-permute-done | bytes 258080 | tf_op jit(solution)/shard_map/ppermute | solution.py:26
  47.5 9.7 %shard_map.128 = (bf16[320,128]{1,0:T(8,128)(2,1)}, bf16[320,128]{1,0:T(8,128)(2,1)}, bf16[320,128]{1,0:T(8,128)(2,1)}, bf16[320,128]{1,0:T(8,128)(2,1)}) custom-call(s32[5]{0:T(128)} %stack.20.place, bf16[336,384]{1,0:T(8,128)(2,1)} %copy-done.26, bf16[336,384]{1,0:T(8,128)(2,1)} %copy-done.27, bf16[336,384]{1,0:T(8,128)(2,1)} %copy-done.28, ...), custom_call_target="tpu_custom_call" | custom-call | flops 1677721600 | bytes 2064404 | tf_op jit(solution)/shard_map/pallas_call | solution.py:67
  57.2 1.7 collective-permute-start.11
  58.9 7.0 %collective-permute-start.12 = (bf16[320,128]{1,0:T(8,128)(2,1)}, bf16[320,128]{1,0:T(8,128)(2,1)S(1)}, u32[]{:S(2)}, u32[]{:S(2)}) collective-permute-start(bf16[320,128]{1,0:T(8,128)(2,1)} %get-tuple-element.38), channel_id=1, source_target_pairs={{0,24},{1,28},{2,26},{3,30},{4,25},{5,29},{6,27},{7,31},{8,0},{9,4... | collective-permute-start | bytes 245768 | tf_op jit(solution)/shard_map/ppermute | solution.py:26
  66.5 1.8 collective-permute-done.12.refs_1_
  68.3 4.8 %collective-permute-done.13.refs_2_ = bf16[320,128]{1,0:T(8,128)(2,1)S(1)} collective-permute-done((bf16[320,128]{1,0:T(8,128)(2,1)}, bf16[320,128]{1,0:T(8,128)(2,1)S(1)}, u32[]{:S(2)}, u32[]{:S(2)}) %collective-permute-start.13) | collective-permute-done | bytes 81952 | tf_op jit(solution)/shard_map/ppermute | solution.py:26
  74.4 3.8 %shard_map.129 = (bf16[2,80,2048]{2,1,0:T(8,128)(2,1)}, bf16[2,80,2048]{2,1,0:T(8,128)(2,1)}) custom-call(s32[5]{0:T(128)} %stack.20.place, bf16[320,128]{1,0:T(8,128)(2,1)} %copy-done.34, bf16[320,128]{1,0:T(8,128)(2,1)} %copy-done.35, bf16[320,128]{1,0:T(8,128)(2,1)} %copy-done.36, bf16[320,128]{1,0:T(8,128)(2,1)} %copy-done.37, bf16[512,2048]{1,0:T(8,128)(2,1)} %refs_4_.1), custom_call_target="tpu_custom_call" | custom-call | flops 671088640 | bytes 2424852 | tf_op jit(solution)/shard_map/pallas_call | solution.py:67
  78.2 2.1 collective-permute-start.15
  80.3 1.9 collective-permute-done.15.given
  82.2 1.3 fusion
  83.5 1.1 collective-permute-start.16
  84.6 30.5 %all-gather.1 = f32[8,80,12]{1,2,0:T(8,128)S(1)} all-gather(f32[1,80,12]{1,2,0:T(8,128)S(1)} %maximum_bitcast_fusion), channel_id=2, replica_groups=mesh['ctx'=8,'exp'=4] {'ctx'}, dimensions={0}, use_global_device_ids=true | all-gather | bytes 34560 | tf_op jit(solution)/shard_map/all_gather | solution.py:316
  115.9 2.6 shard_map.130
  119.0 1.5 collective-permute-start.17
  122.7 7.3 %collective-permute-done.19.refs_3_ = bf16[80,2048]{1,0:T(8,128)(2,1)S(1)} collective-permute-done((bf16[80,2048]{1,0:T(8,128)(2,1)}, bf16[80,2048]{1,0:T(8,128)(2,1)S(1)}, u32[]{:S(2)}, u32[]{:S(2)}) %collective-permute-start.19) | collective-permute-done | bytes 327712 | tf_op jit(solution)/shard_map/ppermute | solution.py:26
  130.0 11.5 %collective-permute-done.18.refs_2_ = bf16[80,2048]{1,0:T(8,128)(2,1)S(1)} collective-permute-done((bf16[80,2048]{1,0:T(8,128)(2,1)}, bf16[80,2048]{1,0:T(8,128)(2,1)S(1)}, u32[]{:S(2)}, u32[]{:S(2)}) %collective-permute-start.18) | collective-permute-done | bytes 327712 | tf_op jit(solution)/shard_map/ppermute | solution.py:26
  142.9 4.3 %shard_map.131 = (bf16[160,2048]{1,0:T(8,128)(2,1)}, bf16[160,2048]{1,0:T(8,128)(2,1)}, bf16[160,2048]{1,0:T(8,128)(2,1)}, bf16[160,2048]{1,0:T(8,128)(2,1)}) custom-call(s32[5]{0:T(128)} %stack.20.place, f32[6,320]{1,0:T(8,128)} %copy.20.routes, bf16[80,2048]{1,0:T(8,128)(2,1)} %get-tuple-element.44.refs_0_, bf16[80,2048]{1,0:T(8,128)(2,1)} %copy-done.25, ...), custom_call_target="tpu_custom_call" | custom-call | flops 838860800 | bytes 1318420 | tf_op jit(solution)/shard_map/pallas_call | solution.py:67
  148.3 1.6 collective-permute-start.21
  149.9 1.2 collective-permute-start.22
  151.1 13.5 %collective-permute-done.20.refs_1_ = bf16[160,2048]{1,0:T(8,128)(2,1)S(1)} collective-permute-done((bf16[160,2048]{1,0:T(8,128)(2,1)}, bf16[160,2048]{1,0:T(8,128)(2,1)S(1)}, u32[]{:S(2)}, u32[]{:S(2)}) %collective-permute-start.20) | collective-permute-done | bytes 655392 | tf_op jit(solution)/shard_map/ppermute | solution.py:26
  164.6 1.6 collective-permute-done.21.refs_2_
  166.2 8.9 %collective-permute-done.22.refs_3_ = bf16[160,2048]{1,0:T(8,128)(2,1)S(1)} collective-permute-done((bf16[160,2048]{1,0:T(8,128)(2,1)}, bf16[160,2048]{1,0:T(8,128)(2,1)S(1)}, u32[]{:S(2)}, u32[]{:S(2)}) %collective-permute-start.22) | collective-permute-done | bytes 655392 | tf_op jit(solution)/shard_map/ppermute | solution.py:26
  175.1 2.0 collective-permute-done.26.refs_3_
  178.1 11.6 %shard_map.133 = (bf16[160,2048]{1,0:T(8,128)(2,1)}, bf16[160,2048]{1,0:T(8,128)(2,1)}, bf16[160,2048]{1,0:T(8,128)(2,1)}, bf16[160,2048]{1,0:T(8,128)(2,1)}) custom-call(bf16[160,2048]{1,0:T(8,128)(2,1)} %copy-done.17, bf16[160,2048]{1,0:T(8,128)(2,1)} %copy-done.19, bf16[160,2048]{1,0:T(8,128)(2,1)} %copy-done.21, bf16[160,2048]{1,0:T(8,128)(2,1)} %copy-done.22, ...), custom_call_target="tpu_custom_call" | custom-call | flops 5536481280 | bytes 11272192 | tf_op jit(solution)/shard_map/pallas_call | solution.py:67
  190.3 11.9 %shard_map.132 = (bf16[160,2048]{1,0:T(8,128)(2,1)}, bf16[160,2048]{1,0:T(8,128)(2,1)}, bf16[160,2048]{1,0:T(8,128)(2,1)}, bf16[160,2048]{1,0:T(8,128)(2,1)}) custom-call(bf16[160,2048]{1,0:T(8,128)(2,1)} %get-tuple-element.45.refs_0_, bf16[160,2048]{1,0:T(8,128)(2,1)} %copy-done.11, bf16[160,2048]{1,0:T(8,128)(2,1)} %copy-done.12, ...), custom_call_target="tpu_custom_call" | custom-call | flops 5536481280 | bytes 11272192 | tf_op jit(solution)/shard_map/pallas_call | solution.py:67
  202.8 1.3 add_convert_fusion.2
  205.0 1.4 collective-permute-start.31
  206.6 1.6 collective-permute-start.33
  208.2 1.1 add_convert_fusion.3.refs_0_
  209.3 11.7 %collective-permute-done.29.refs_1_ = bf16[160,2048]{1,0:T(8,128)(2,1)S(1)} collective-permute-done((bf16[160,2048]{1,0:T(8,128)(2,1)S(1)}, bf16[160,2048]{1,0:T(8,128)(2,1)S(1)}, u32[]{:S(2)}, u32[]{:S(2)}) %collective-permute-start.29) | collective-permute-done | bytes 655392 | tf_op jit(solution)/shard_map/ppermute | solution.py:26
  221.0 1.7 collective-permute-done.31.refs_2_
  222.7 13.8 %collective-permute-done.33.refs_3_ = bf16[160,2048]{1,0:T(8,128)(2,1)S(1)} collective-permute-done((bf16[160,2048]{1,0:T(8,128)(2,1)S(1)}, bf16[160,2048]{1,0:T(8,128)(2,1)S(1)}, u32[]{:S(2)}, u32[]{:S(2)}) %collective-permute-start.33) | collective-permute-done | bytes 655392 | tf_op jit(solution)/shard_map/ppermute | solution.py:26
  237.3 6.9 %shard_map.134 = (bf16[80,2048]{1,0:T(8,128)(2,1)}, bf16[80,2048]{1,0:T(8,128)(2,1)}, bf16[80,2048]{1,0:T(8,128)(2,1)}, bf16[80,2048]{1,0:T(8,128)(2,1)}) custom-call(s32[5]{0:T(128)} %stack.20.place, f32[320,6]{1,0:T(8,128)} %get-tuple-element.63.routes, f32[320,6]{1,0:T(8,128)} %get-tuple-element.62.gates, bf16[160,2048]{1,0:T(8,128)(2,1)} %add_convert_fusion.3.refs_0_, ...), custom_call_target="tpu_custom_call" | custom-call | flops 1677721600 | bytes 2636820 | tf_op jit(solution)/shard_map/pallas_call | solution.py:67
  245.3 5.4 %collective-permute-start.35 = (bf16[80,2048]{1,0:T(8,128)(2,1)}, bf16[80,2048]{1,0:T(8,128)(2,1)S(1)}, u32[]{:S(2)}, u32[]{:S(2)}) collective-permute-start(bf16[80,2048]{1,0:T(8,128)(2,1)} %get-tuple-element.59), channel_id=1, source_target_pairs={{0,16},{1,17},{2,18},{3,19},{4,20},{5,21},{6,22},{7,23},{8,24},{9,... | collective-permute-start | bytes 983048 | tf_op jit(solution)/shard_map/ppermute | solution.py:26
  250.7 2.0 collective-permute-start.36
  252.7 3.3 %collective-permute-done.34 = bf16[80,2048]{1,0:T(8,128)(2,1)S(1)} collective-permute-done((bf16[80,2048]{1,0:T(8,128)(2,1)}, bf16[80,2048]{1,0:T(8,128)(2,1)S(1)}, u32[]{:S(2)}, u32[]{:S(2)}) %collective-permute-start.34) | collective-permute-done | bytes 327712 | tf_op jit(solution)/shard_map/ppermute | solution.py:26
  256.0 22.9 %collective-permute-done.35 = bf16[80,2048]{1,0:T(8,128)(2,1)S(1)} collective-permute-done((bf16[80,2048]{1,0:T(8,128)(2,1)}, bf16[80,2048]{1,0:T(8,128)(2,1)S(1)}, u32[]{:S(2)}, u32[]{:S(2)}) %collective-permute-start.35) | collective-permute-done | bytes 327712 | tf_op jit(solution)/shard_map/ppermute | solution.py:26
  278.9 1.9 add_convert_fusion.4
  (131 shorter events, 18.4 us)
Async XLA Ops:
  0.0 10.9 %collective-permute-start.1 = (bf16[80,2048]{1,0:T(8,128)(2,1)}, bf16[80,2048]{1,0:T(8,128)(2,1)S(1)}, u32[]{:S(2)}, u32[]{:S(2)}) collective-permute-start(bf16[80,2048]{1,0:T(8,128)(2,1)} %inputs.1), channel_id=1, source_target_pairs={{0,2},{1,3},{2,0},{3,1},{4,6},{5,7},{6,4},{7,5},{8,10},{9,11},{10,... | collective-permute-start | bytes 983048 | tf_op jit(solution)/shard_map/ppermute | solution.py:26
  3.0 9.4 %collective-permute-start = (bf16[80,2048]{1,0:T(8,128)(2,1)}, bf16[80,2048]{1,0:T(8,128)(2,1)S(1)}, u32[]{:S(2)}, u32[]{:S(2)}) collective-permute-start(bf16[80,2048]{1,0:T(8,128)(2,1)} %inputs.1), channel_id=1, source_target_pairs={{0,1},{1,0},{2,3},{3,2},{4,5},{5,4},{6,7},{7,6},{8,9},{9,8},{10,11... | collective-permute-start | bytes 983048 | tf_op jit(solution)/shard_map/ppermute | solution.py:26
  10.9 1.6 collective-permute-start.2
  20.6 7.3 %collective-permute-start.3 = (bf16[336,384]{1,0:T(8,128)(2,1)}, bf16[336,384]{1,0:T(8,128)(2,1)S(1)}, u32[]{:S(2)}, u32[]{:S(2)}) collective-permute-start(bf16[336,384]{1,0:T(8,128)(2,1)} %get-tuple-element.33), channel_id=1, source_target_pairs={{0,0},{1,4},{2,2},{3,6},{4,1},{5,5},{6,3},{7,7},{8,8},{9,12},{10,1... | collective-permute-start | bytes 774152 | tf_op jit(solution)/shard_map/ppermute | solution.py:26
  22.2 10.0 %collective-permute-start.4 = (bf16[336,384]{1,0:T(8,128)(2,1)}, bf16[336,384]{1,0:T(8,128)(2,1)S(1)}, u32[]{:S(2)}, u32[]{:S(2)}) collective-permute-start(bf16[336,384]{1,0:T(8,128)(2,1)} %get-tuple-element.34), channel_id=1, source_target_pairs={{0,8},{1,12},{2,10},{3,14},{4,9},{5,13},{6,11},{7,15},{8,16},{9,20... | collective-permute-start | bytes 774152 | tf_op jit(solution)/shard_map/ppermute | solution.py:26
  24.0 20.3 %collective-permute-start.5 = (bf16[336,384]{1,0:T(8,128)(2,1)}, bf16[336,384]{1,0:T(8,128)(2,1)S(1)}, u32[]{:S(2)}, u32[]{:S(2)}) collective-permute-start(bf16[336,384]{1,0:T(8,128)(2,1)} %get-tuple-element.35), channel_id=1, source_target_pairs={{0,16},{1,20},{2,18},{3,22},{4,17},{5,21},{6,19},{7,23},{8,24},{9,... | collective-permute-start | bytes 774152 | tf_op jit(solution)/shard_map/ppermute | solution.py:26
  26.6 18.4 %collective-permute-start.6 = (bf16[336,384]{1,0:T(8,128)(2,1)}, bf16[336,384]{1,0:T(8,128)(2,1)S(1)}, u32[]{:S(2)}, u32[]{:S(2)}) collective-permute-start(bf16[336,384]{1,0:T(8,128)(2,1)} %get-tuple-element.36), channel_id=1, source_target_pairs={{0,24},{1,28},{2,26},{3,30},{4,25},{5,29},{6,27},{7,31},{8,0},{9,4... | collective-permute-start | bytes 774152 | tf_op jit(solution)/shard_map/ppermute | solution.py:26
  27.9 18.5 %copy-start.26 = (bf16[336,384]{1,0:T(8,128)(2,1)}, bf16[336,384]{1,0:T(8,128)(2,1)S(1)}, u32[]{:S(2)}) copy-start(bf16[336,384]{1,0:T(8,128)(2,1)S(1)} %collective-permute-done.3.refs_0_) | copy-start | bytes 774148
  27.9 17.1 %collective-permute-start.7 = (bf16[336,384]{1,0:T(8,128)(2,1)S(1)}, bf16[336,384]{1,0:T(8,128)(2,1)S(1)}, u32[]{:S(2)}, u32[]{:S(2)}) collective-permute-start(bf16[336,384]{1,0:T(8,128)(2,1)S(1)} %collective-permute-done.3.refs_0_), channel_id=1, source_target_pairs={{0,1},{1,0},{2,3},{3,2},{4,5},{5,4},{6,7},{7,6},{8,9},{9,8},{10,11... | collective-permute-start | bytes 774152 | tf_op jit(solution)/shard_map/ppermute | solution.py:26
  32.2 14.3 %copy-start.27 = (bf16[336,384]{1,0:T(8,128)(2,1)}, bf16[336,384]{1,0:T(8,128)(2,1)S(1)}, u32[]{:S(2)}) copy-start(bf16[336,384]{1,0:T(8,128)(2,1)S(1)} %collective-permute-done.4.refs_1_) | copy-start | bytes 774148
  32.2 12.9 %collective-permute-start.8 = (bf16[336,384]{1,0:T(8,128)(2,1)S(1)}, bf16[336,384]{1,0:T(8,128)(2,1)S(1)}, u32[]{:S(2)}, u32[]{:S(2)}) collective-permute-start(bf16[336,384]{1,0:T(8,128)(2,1)S(1)} %collective-permute-done.4.refs_1_), channel_id=1, source_target_pairs={{0,1},{1,0},{2,3},{3,2},{4,5},{5,4},{6,7},{7,6},{8,9},{9,8},{10,11... | collective-permute-start | bytes 774152 | tf_op jit(solution)/shard_map/ppermute | solution.py:26
  44.3 1.8 collective-permute-start.9
  44.9 1.5 collective-permute-start.10
  57.2 23.0 %copy-start.9 = (s32[80,6]{0,1:T(8,128)S(1)}, s32[80,6]{0,1:T(8,128)}, u32[]{:S(2)}) copy-start(s32[80,6]{0,1:T(8,128)} %param.24) | copy-start | bytes 5764
  57.2 9.3 %collective-permute-start.11 = (bf16[320,128]{1,0:T(8,128)(2,1)}, bf16[320,128]{1,0:T(8,128)(2,1)S(1)}, u32[]{:S(2)}, u32[]{:S(2)}) collective-permute-start(bf16[320,128]{1,0:T(8,128)(2,1)} %get-tuple-element.37), channel_id=1, source_target_pairs={{0,0},{1,4},{2,2},{3,6},{4,1},{5,5},{6,3},{7,7},{8,8},{9,12},{10,1... | collective-permute-start | bytes 245768 | tf_op jit(solution)/shard_map/ppermute | solution.py:26
  58.9 9.4 %collective-permute-start.12 = (bf16[320,128]{1,0:T(8,128)(2,1)}, bf16[320,128]{1,0:T(8,128)(2,1)S(1)}, u32[]{:S(2)}, u32[]{:S(2)}) collective-permute-start(bf16[320,128]{1,0:T(8,128)(2,1)} %get-tuple-element.38), channel_id=1, source_target_pairs={{0,24},{1,28},{2,26},{3,30},{4,25},{5,29},{6,27},{7,31},{8,0},{9,4... | collective-permute-start | bytes 245768 | tf_op jit(solution)/shard_map/ppermute | solution.py:26
  65.9 7.2 %collective-permute-start.13 = (bf16[320,128]{1,0:T(8,128)(2,1)}, bf16[320,128]{1,0:T(8,128)(2,1)S(1)}, u32[]{:S(2)}, u32[]{:S(2)}) collective-permute-start(bf16[320,128]{1,0:T(8,128)(2,1)} %get-tuple-element.39), channel_id=1, source_target_pairs={{0,16},{1,20},{2,18},{3,22},{4,17},{5,21},{6,19},{7,23},{8,24},{9,... | collective-permute-start | bytes 245768 | tf_op jit(solution)/shard_map/ppermute | solution.py:26
  65.9 18.6 %copy-start.10 = (f32[80,6]{0,1:T(8,128)S(1)}, f32[80,6]{0,1:T(8,128)}, u32[]{:S(2)}) copy-start(f32[80,6]{0,1:T(8,128)} %param.25) | copy-start | bytes 5764
  65.9 7.2 %collective-permute-start.14 = (bf16[320,128]{1,0:T(8,128)(2,1)}, bf16[320,128]{1,0:T(8,128)(2,1)S(1)}, u32[]{:S(2)}, u32[]{:S(2)}) collective-permute-start(bf16[320,128]{1,0:T(8,128)(2,1)} %get-tuple-element.40), channel_id=1, source_target_pairs={{0,8},{1,12},{2,10},{3,14},{4,9},{5,13},{6,11},{7,15},{8,16},{9,20... | collective-permute-start | bytes 245768 | tf_op jit(solution)/shard_map/ppermute | solution.py:26
  78.2 4.0 %collective-permute-start.15 = (bf16[2,80,2048]{2,1,0:T(8,128)(2,1)}, bf16[2,80,2048]{2,1,0:T(8,128)(2,1)S(1)}, u32[]{:S(2)}, u32[]{:S(2)}) collective-permute-start(bf16[2,80,2048]{2,1,0:T(8,128)(2,1)} %get-tuple-element.42), channel_id=1, source_target_pairs={{0,1},{1,0},{2,3},{3,2},{4,5},{5,4},{6,7},{7,6},{8,9},{9,8},{10,11... | collective-permute-start | bytes 1966088 | tf_op jit(solution)/shard_map/ppermute | solution.py:26
  82.2 33.0 %copy-start = (bf16[2,80,2048]{2,1,0:T(8,128)(2,1)}, bf16[2,80,2048]{2,1,0:T(8,128)(2,1)S(1)}, u32[]{:S(2)}) copy-start(bf16[2,80,2048]{2,1,0:T(8,128)(2,1)S(1)} %collective-permute-done.15.given) | copy-start | bytes 1966084
  83.5 31.7 %collective-permute-start.16 = (bf16[80,2048]{1,0:T(8,128)(2,1)S(1)}, bf16[80,2048]{1,0:T(8,128)(2,1)S(1)}, u32[]{:S(2)}, u32[]{:S(2)}) collective-permute-start(bf16[80,2048]{1,0:T(8,128)(2,1)S(1)} %fusion), channel_id=1, source_target_pairs={{0,2},{1,3},{2,0},{3,1},{4,6},{5,7},{6,4},{7,5},{8,10},{9,11},{10,... | collective-permute-start | bytes 983048 | tf_op jit(solution)/shard_map/ppermute | solution.py:26
  118.4 11.5 %collective-permute-start.19 = (bf16[80,2048]{1,0:T(8,128)(2,1)}, bf16[80,2048]{1,0:T(8,128)(2,1)S(1)}, u32[]{:S(2)}, u32[]{:S(2)}) collective-permute-start(bf16[80,2048]{1,0:T(8,128)(2,1)} %get-tuple-element.44.refs_0_), channel_id=1, source_target_pairs={{0,24},{1,25},{2,26},{3,27},{4,28},{5,29},{6,30},{7,31},{8,0},{9,1... | collective-permute-start | bytes 983048 | tf_op jit(solution)/shard_map/ppermute | solution.py:26
  119.0 22.5 %collective-permute-start.18 = (bf16[80,2048]{1,0:T(8,128)(2,1)}, bf16[80,2048]{1,0:T(8,128)(2,1)S(1)}, u32[]{:S(2)}, u32[]{:S(2)}) collective-permute-start(bf16[80,2048]{1,0:T(8,128)(2,1)} %get-tuple-element.44.refs_0_), channel_id=1, source_target_pairs={{0,16},{1,17},{2,18},{3,19},{4,20},{5,21},{6,22},{7,23},{8,24},{9,... | collective-permute-start | bytes 983048 | tf_op jit(solution)/shard_map/ppermute | solution.py:26
  119.0 22.5 %collective-permute-start.17 = (bf16[80,2048]{1,0:T(8,128)(2,1)}, bf16[80,2048]{1,0:T(8,128)(2,1)S(1)}, u32[]{:S(2)}, u32[]{:S(2)}) collective-permute-start(bf16[80,2048]{1,0:T(8,128)(2,1)} %get-tuple-element.44.refs_0_), channel_id=1, source_target_pairs={{0,8},{1,9},{2,10},{3,11},{4,12},{5,13},{6,14},{7,15},{8,16},{9,17... | collective-permute-start | bytes 983048 | tf_op jit(solution)/shard_map/ppermute | solution.py:26
  147.2 17.4 %collective-permute-start.20 = (bf16[160,2048]{1,0:T(8,128)(2,1)}, bf16[160,2048]{1,0:T(8,128)(2,1)S(1)}, u32[]{:S(2)}, u32[]{:S(2)}) collective-permute-start(bf16[160,2048]{1,0:T(8,128)(2,1)} %get-tuple-element.46), channel_id=1, source_target_pairs={{0,2},{1,3},{2,0},{3,1},{4,6},{5,7},{6,4},{7,5},{8,10},{9,11},{10,... | collective-permute-start | bytes 1966088 | tf_op jit(solution)/shard_map/ppermute | solution.py:26
  148.3 17.9 %collective-permute-start.21 = (bf16[160,2048]{1,0:T(8,128)(2,1)}, bf16[160,2048]{1,0:T(8,128)(2,1)S(1)}, u32[]{:S(2)}, u32[]{:S(2)}) collective-permute-start(bf16[160,2048]{1,0:T(8,128)(2,1)} %get-tuple-element.47), channel_id=1, source_target_pairs={{0,4},{1,5},{2,6},{3,7},{4,0},{5,1},{6,2},{7,3},{8,12},{9,13},{10,... | collective-permute-start | bytes 1966088 | tf_op jit(solution)/shard_map/ppermute | solution.py:26
  149.9 25.2 %collective-permute-start.22 = (bf16[160,2048]{1,0:T(8,128)(2,1)}, bf16[160,2048]{1,0:T(8,128)(2,1)S(1)}, u32[]{:S(2)}, u32[]{:S(2)}) collective-permute-start(bf16[160,2048]{1,0:T(8,128)(2,1)} %get-tuple-element.48), channel_id=1, source_target_pairs={{0,6},{1,7},{2,4},{3,5},{4,2},{5,3},{6,0},{7,1},{8,14},{9,15},{10,... | collective-permute-start | bytes 1966088 | tf_op jit(solution)/shard_map/ppermute | solution.py:26
  151.1 24.0 %collective-permute-start.23 = (bf16[160,2048]{1,0:T(8,128)(2,1)}, bf16[160,2048]{1,0:T(8,128)(2,1)S(1)}, u32[]{:S(2)}, u32[]{:S(2)}) collective-permute-start(bf16[160,2048]{1,0:T(8,128)(2,1)} %get-tuple-element.45.refs_0_), channel_id=1, source_target_pairs={{0,1},{1,0},{2,3},{3,2},{4,5},{5,4},{6,7},{7,6},{8,9},{9,8},{10,11... | collective-permute-start | bytes 1966088 | tf_op jit(solution)/shard_map/ppermute | solution.py:26
  164.6 25.1 %copy-start.11 = (bf16[160,2048]{1,0:T(8,128)(2,1)}, bf16[160,2048]{1,0:T(8,128)(2,1)S(1)}, u32[]{:S(2)}) copy-start(bf16[160,2048]{1,0:T(8,128)(2,1)S(1)} %collective-permute-done.20.refs_1_) | copy-start | bytes 1966084
  164.6 10.5 %collective-permute-start.24 = (bf16[160,2048]{1,0:T(8,128)(2,1)S(1)}, bf16[160,2048]{1,0:T(8,128)(2,1)S(1)}, u32[]{:S(2)}, u32[]{:S(2)}) collective-permute-start(bf16[160,2048]{1,0:T(8,128)(2,1)S(1)} %collective-permute-done.20.refs_1_), channel_id=1, source_target_pairs={{0,1},{1,0},{2,3},{3,2},{4,5},{5,4},{6,7},{7,6},{8,9},{9,8},{10,11... | collective-permute-start | bytes 1966088 | tf_op jit(solution)/shard_map/ppermute | solution.py:26
  166.2 23.5 %copy-start.12 = (bf16[160,2048]{1,0:T(8,128)(2,1)}, bf16[160,2048]{1,0:T(8,128)(2,1)S(1)}, u32[]{:S(2)}) copy-start(bf16[160,2048]{1,0:T(8,128)(2,1)S(1)} %collective-permute-done.21.refs_2_) | copy-start | bytes 1966084
  166.2 8.9 %collective-permute-start.25 = (bf16[160,2048]{1,0:T(8,128)(2,1)S(1)}, bf16[160,2048]{1,0:T(8,128)(2,1)S(1)}, u32[]{:S(2)}, u32[]{:S(2)}) collective-permute-start(bf16[160,2048]{1,0:T(8,128)(2,1)S(1)} %collective-permute-done.21.refs_2_), channel_id=1, source_target_pairs={{0,1},{1,0},{2,3},{3,2},{4,5},{5,4},{6,7},{7,6},{8,9},{9,8},{10,11... | collective-permute-start | bytes 1966088 | tf_op jit(solution)/shard_map/ppermute | solution.py:26
  175.1 14.6 %copy-start.13 = (bf16[160,2048]{1,0:T(8,128)(2,1)}, bf16[160,2048]{1,0:T(8,128)(2,1)S(1)}, u32[]{:S(2)}) copy-start(bf16[160,2048]{1,0:T(8,128)(2,1)S(1)} %collective-permute-done.22.refs_3_) | copy-start | bytes 1966084
  175.1 2.1 collective-permute-start.26
  189.7 13.1 %collective-permute-start.28 = (bf16[160,2048]{1,0:T(8,128)(2,1)}, bf16[160,2048]{1,0:T(8,128)(2,1)S(1)}, u32[]{:S(2)}, u32[]{:S(2)}) collective-permute-start(bf16[160,2048]{1,0:T(8,128)(2,1)} %get-tuple-element.52), channel_id=1, source_target_pairs={{0,1},{1,0},{2,3},{3,2},{4,5},{5,4},{6,7},{7,6},{8,9},{9,8},{10,11... | collective-permute-start | bytes 1966088 | tf_op jit(solution)/shard_map/ppermute | solution.py:26
  189.9 14.9 %collective-permute-start.30 = (bf16[160,2048]{1,0:T(8,128)(2,1)}, bf16[160,2048]{1,0:T(8,128)(2,1)S(1)}, u32[]{:S(2)}, u32[]{:S(2)}) collective-permute-start(bf16[160,2048]{1,0:T(8,128)(2,1)} %get-tuple-element.54), channel_id=1, source_target_pairs={{0,1},{1,0},{2,3},{3,2},{4,5},{5,4},{6,7},{7,6},{8,9},{9,8},{10,11... | collective-permute-start | bytes 1966088 | tf_op jit(solution)/shard_map/ppermute | solution.py:26
  202.2 6.0 %collective-permute-start.27 = (bf16[160,2048]{1,0:T(8,128)(2,1)S(1)}, bf16[160,2048]{1,0:T(8,128)(2,1)S(1)}, u32[]{:S(2)}, u32[]{:S(2)}) collective-permute-start(bf16[160,2048]{1,0:T(8,128)(2,1)S(1)} %copy-done.14), channel_id=1, source_target_pairs={{0,1},{1,0},{2,3},{3,2},{4,5},{5,4},{6,7},{7,6},{8,9},{9,8},{10,11... | collective-permute-start | bytes 1966088 | tf_op jit(solution)/shard_map/ppermute | solution.py:26
  202.5 3.9 %collective-permute-start.32 = (bf16[160,2048]{1,0:T(8,128)(2,1)S(1)}, bf16[160,2048]{1,0:T(8,128)(2,1)S(1)}, u32[]{:S(2)}, u32[]{:S(2)}) collective-permute-start(bf16[160,2048]{1,0:T(8,128)(2,1)S(1)} %copy-done.15), channel_id=1, source_target_pairs={{0,1},{1,0},{2,3},{3,2},{4,5},{5,4},{6,7},{7,6},{8,9},{9,8},{10,11... | collective-permute-start | bytes 1966088 | tf_op jit(solution)/shard_map/ppermute | solution.py:26
  204.1 16.9 %collective-permute-start.29 = (bf16[160,2048]{1,0:T(8,128)(2,1)S(1)}, bf16[160,2048]{1,0:T(8,128)(2,1)S(1)}, u32[]{:S(2)}, u32[]{:S(2)}) collective-permute-start(bf16[160,2048]{1,0:T(8,128)(2,1)S(1)} %add_convert_fusion.2), channel_id=1, source_target_pairs={{0,2},{1,3},{2,0},{3,1},{4,6},{5,7},{6,4},{7,5},{8,10},{9,11},{10,... | collective-permute-start | bytes 1966088 | tf_op jit(solution)/shard_map/ppermute | solution.py:26
  205.0 17.7 %collective-permute-start.31 = (bf16[160,2048]{1,0:T(8,128)(2,1)S(1)}, bf16[160,2048]{1,0:T(8,128)(2,1)S(1)}, u32[]{:S(2)}, u32[]{:S(2)}) collective-permute-start(bf16[160,2048]{1,0:T(8,128)(2,1)S(1)} %add_convert_fusion.1), channel_id=1, source_target_pairs={{0,4},{1,5},{2,6},{3,7},{4,0},{5,1},{6,2},{7,3},{8,12},{9,13},{10,... | collective-permute-start | bytes 1966088 | tf_op jit(solution)/shard_map/ppermute | solution.py:26
  206.6 29.9 %collective-permute-start.33 = (bf16[160,2048]{1,0:T(8,128)(2,1)S(1)}, bf16[160,2048]{1,0:T(8,128)(2,1)S(1)}, u32[]{:S(2)}, u32[]{:S(2)}) collective-permute-start(bf16[160,2048]{1,0:T(8,128)(2,1)S(1)} %add_convert_fusion), channel_id=1, source_target_pairs={{0,6},{1,7},{2,4},{3,5},{4,2},{5,3},{6,0},{7,1},{8,14},{9,15},{10,... | collective-permute-start | bytes 1966088 | tf_op jit(solution)/shard_map/ppermute | solution.py:26
  221.0 15.5 %copy-start.16 = (bf16[160,2048]{1,0:T(8,128)(2,1)}, bf16[160,2048]{1,0:T(8,128)(2,1)S(1)}, u32[]{:S(2)}) copy-start(bf16[160,2048]{1,0:T(8,128)(2,1)S(1)} %collective-permute-done.29.refs_1_) | copy-start | bytes 1966084
  222.7 13.8 %copy-start.18 = (bf16[160,2048]{1,0:T(8,128)(2,1)}, bf16[160,2048]{1,0:T(8,128)(2,1)S(1)}, u32[]{:S(2)}) copy-start(bf16[160,2048]{1,0:T(8,128)(2,1)S(1)} %collective-permute-done.31.refs_2_) | copy-start | bytes 1966084
  237.3 41.5 %copy-start.7 = (bf16[80,2048]{1,0:T(8,128)(2,1)S(1)}, bf16[80,2048]{1,0:T(8,128)(2,1)}, u32[]{:S(2)}) copy-start(bf16[80,2048]{1,0:T(8,128)(2,1)} %get-tuple-element.43) | copy-start | bytes 983044
  244.2 11.8 %collective-permute-start.34 = (bf16[80,2048]{1,0:T(8,128)(2,1)}, bf16[80,2048]{1,0:T(8,128)(2,1)S(1)}, u32[]{:S(2)}, u32[]{:S(2)}) collective-permute-start(bf16[80,2048]{1,0:T(8,128)(2,1)} %get-tuple-element.58), channel_id=1, source_target_pairs={{0,24},{1,25},{2,26},{3,27},{4,28},{5,29},{6,30},{7,31},{8,0},{9,1... | collective-permute-start | bytes 983048 | tf_op jit(solution)/shard_map/ppermute | solution.py:26
  245.3 33.6 %collective-permute-start.35 = (bf16[80,2048]{1,0:T(8,128)(2,1)}, bf16[80,2048]{1,0:T(8,128)(2,1)S(1)}, u32[]{:S(2)}, u32[]{:S(2)}) collective-permute-start(bf16[80,2048]{1,0:T(8,128)(2,1)} %get-tuple-element.59), channel_id=1, source_target_pairs={{0,16},{1,17},{2,18},{3,19},{4,20},{5,21},{6,22},{7,23},{8,24},{9,... | collective-permute-start | bytes 983048 | tf_op jit(solution)/shard_map/ppermute | solution.py:26
  250.7 28.2 %collective-permute-start.36 = (bf16[80,2048]{1,0:T(8,128)(2,1)}, bf16[80,2048]{1,0:T(8,128)(2,1)S(1)}, u32[]{:S(2)}, u32[]{:S(2)}) collective-permute-start(bf16[80,2048]{1,0:T(8,128)(2,1)} %get-tuple-element.60), channel_id=1, source_target_pairs={{0,8},{1,9},{2,10},{3,11},{4,12},{5,13},{6,14},{7,15},{8,16},{9,17... | collective-permute-start | bytes 983048 | tf_op jit(solution)/shard_map/ppermute | solution.py:26
  (27 other events, 79.2 us)

commit v2 on v1

--- a/solution.py
+++ b/solution.py
@@ -9,7 +9,7 @@
 from jax.sharding import PartitionSpec as P
 
 AXES = ("ctx", "exp")
-PARAMS = pltpu.CompilerParams(vmem_limit_bytes=56 * 1024 * 1024)
+PARAMS = pltpu.CompilerParams(vmem_limit_bytes=24 * 1024 * 1024)
 VMEM = pl.BlockSpec(memory_space=pltpu.VMEM)
 SMEM = pl.BlockSpec(memory_space=pltpu.SMEM)
 PAD_ROWS = 16
@@ -39,6 +39,30 @@
     return move(block, lambda z, x, y, c: ((z + turn) % depth, x, y, c))
 
 
+def gather_z(block):
+    depth = lax.axis_size("ctx") // 2
+    column = [block] + [None] * (depth - 1)
+    for turn in range(1, depth // 2 + 1):
+        column[turn] = turn_z(column[turn - 1], 1)
+    for turn in range(depth - 1, depth // 2, -1):
+        column[turn] = turn_z(column[(turn + 1) % depth], -1)
+    return column
+
+
+def scatter_z(sums):
+    depth = len(sums)
+
+    def added(left, right):
+        return (left.astype(jnp.float32) + right.astype(jnp.float32)).astype(left.dtype)
+
+    below, above = None, None
+    for turn in range(depth // 2, 0, -1):
+        below = turn_z(sums[turn] if below is None else added(below, sums[turn]), -1)
+    for turn in range(depth // 2 + 1, depth):
+        above = turn_z(sums[turn] if above is None else added(above, sums[turn]), 1)
+    return [part for part in (below, above) if part is not None]
+
+
 def head_out(block, turn):
     depth = lax.axis_size("ctx") // 2
     return move(block, lambda z, x, y, c: ((z + turn) % depth, c, y, x))
@@ -60,10 +84,13 @@
 
 
 def struct(*shape, dtype=jnp.bfloat16):
-    return jax.ShapeDtypeStruct(shape, dtype)
+    return pltpu.VMEM(shape, dtype)
 
 
 def call(kernel, outs, operands, scratch=(), flops=0, smem=1):
+    operands = operands[:smem] + [
+        pltpu.with_memory_space_constraint(a, pltpu.VMEM) for a in operands[smem:]
+    ]
     return pl.pallas_call(
         kernel,
         out_shape=outs,
@@ -245,17 +272,19 @@
 
 
 def expert_kernel(parts, *refs):
-    row_refs, (w_gate, w_up, w_down), outs = refs[:parts], refs[parts : parts + 3], refs[parts + 3 :]
+    row_refs, weights, outs = refs[:parts], refs[parts : parts + 6], refs[parts + 6 :]
     across = (((1,), (1,)), ((), ()))
-    for first in range(0, parts, 2):
-        rows = jnp.concatenate([row_refs[first][...], row_refs[first + 1][...]], axis=0)
+    rows = jnp.concatenate([row_ref[...] for row_ref in row_refs], axis=0)
+    result = None
+    for w_gate, w_up, w_down in (weights[:3], weights[3:]):
         gate_part = lax.dot_general(rows, w_gate[...], across, preferred_element_type=jnp.float32)
         up_part = lax.dot_general(rows, w_up[...], across, preferred_element_type=jnp.float32)
         hidden = (gate_part / (1.0 + jnp.exp(-gate_part)) * up_part).astype(jnp.bfloat16)
-        result = f32_dot(hidden, w_down[...]).astype(jnp.bfloat16)
-        half = row_refs[first].shape[0]
-        outs[first][...] = result[:half]
-        outs[first + 1][...] = result[half:]
+        product = f32_dot(hidden, w_down[...])
+        result = product if result is None else result + product
+    count = row_refs[0].shape[0]
+    for part, out in enumerate(outs):
+        out[...] = result[part * count : (part + 1) * count].astype(jnp.bfloat16)
 
 
 def combine_kernel(depth, capacity, place, routes, gates, *refs):
@@ -312,16 +341,15 @@
         [exp_index, z_index, exp_index % 2, z_index if by_head else jnp.zeros_like(z_index), expert]
     ).astype(jnp.int32)
 
-    noted = jnp.concatenate([routes.astype(jnp.float32), gate_weights], axis=1)
-    noted = lax.all_gather(noted, "ctx", axis=0).reshape(depth, 2, tok_rows, -1)
-    noted = lax.dynamic_index_in_dim(noted, x_index, 1, keepdims=False)
-    sources = (z_index - jnp.arange(depth)) % depth
-    noted = noted[sources].reshape(depth * tok_rows, -1)
+    noted = gather_z(jnp.concatenate([routes.astype(jnp.float32), gate_weights], axis=1))
     top_count = routes.shape[1]
-    near_routes, near_gates = noted[:, :top_count], noted[:, top_count:]
+
+    weights = (w_gate, w_up, w_down)
+    other_weights = tuple(swap_core(weight) for weight in weights)
 
     near = swap_core(inputs)
     far = move(inputs, lambda z, x, y, c: (z, x, y ^ 1, c))
+    far, noted = lax.optimization_barrier((far, noted))
     far_near = swap_core(far)
     if by_head:
         marks = jnp.sum(
@@ -359,6 +387,8 @@
         normed = normalize(block.reshape(block_len, model_width), attn_gain)
         heads = attend_gathered(normed, w_query, w_key, w_value, sel_blocks)
 
+    heads, other_weights = lax.optimization_barrier((heads, other_weights))
+
     halves = struct(exp_count // 2, tok_rows, model_width)
     kept, given = call(
         functools.partial(mix_kernel, exp_count, heads_here, head_dim),
@@ -382,45 +412,50 @@
 
     experts = ctx_count * exp_count // 2
     capacity = 2 * max(1, (tok_rows * top_count + experts - 1) // experts * 2 // 3)
-    slots = depth * capacity
-    column = [ffn_in] + [turn_z(ffn_in, turn) for turn in range(1, depth)]
-    packed = call(
-        functools.partial(pack_kernel, depth, capacity),
-        [struct(slots, model_width)] * 4,
-        [place, near_routes.T, *column],
-        [pltpu.VMEM((depth * tok_rows, model_width), jnp.bfloat16)],
-        flops=8 * slots * depth * tok_rows * model_width,
-    )
-    arrived = [packed[0]] + [swap_layer(packed[hop], hop) for hop in range(1, 4)]
-    beside = [swap_core(rows) for rows in arrived]
-    weights = [w_gate[0].T, w_up[0].T, w_down[0]]
-
-    def expert_rows(rows):
-        return call(
-            functools.partial(expert_kernel, len(rows)),
-            [struct(slots, model_width)] * len(rows),
-            [*rows, *weights],
-            flops=6 * len(rows) * slots * model_width * w_gate.shape[2],
+    column = gather_z(ffn_in)
+    nearest = sorted(range(depth), key=lambda turn: min(turn, depth - turn))
+    group_size = depth // 2
+    groups = [nearest[first : first + group_size] for first in range(0, depth, group_size)]
+    notes = [jnp.concatenate([noted[turn] for turn in group], axis=0) for group in groups]
+    slots = group_size * capacity
+    expert_weights = [
+        array
+        for gate, up, down in (weights, other_weights)
+        for array in (gate[0].T, up[0].T, down[0])
+    ]
+    arrived = []
+    for group, note in zip(groups, notes):
+        packed = call(
+            functools.partial(pack_kernel, group_size, capacity),
+            [struct(slots, model_width)] * 4,
+            [place, note[:, :top_count].T, *[column[turn] for turn in group]],
+            [pltpu.VMEM((group_size * tok_rows, model_width), jnp.bfloat16)],
+            flops=8 * slots * group_size * tok_rows * model_width,
+        )
+        arrived.append([packed[0]] + [swap_layer(packed[hop], hop) for hop in range(1, 4)])
+    sums = [None] * depth
+    returned = []
+    for rows in arrived:
+        results = call(
+            functools.partial(expert_kernel, 4),
+            [struct(slots, model_width)] * 4,
+            [*rows, *expert_weights],
+            flops=48 * slots * model_width * w_gate.shape[2],
             smem=0,
         )
-
-    own_part = expert_rows(arrived)
-    beside_part = expert_rows(beside)
-    other_part = [swap_core(rows) for rows in beside_part]
-    results = [
-        (own.astype(jnp.float32) + other.astype(jnp.float32)).astype(jnp.bfloat16)
-        for own, other in zip(own_part, other_part)
-    ]
-    returned = [results[0]] + [swap_layer(results[hop], hop) for hop in range(1, 4)]
-    sums = call(
-        functools.partial(combine_kernel, depth, capacity),
-        [struct(tok_rows, model_width)] * depth,
-        [place, near_routes, near_gates, *returned],
-        flops=16 * slots * depth * tok_rows * model_width,
-    )
+        returned.append([results[0]] + [swap_layer(results[hop], hop) for hop in range(1, 4)])
+    for group, note, rows in zip(groups, notes, returned):
+        parts = call(
+            functools.partial(combine_kernel, group_size, capacity),
+            [struct(tok_rows, model_width)] * group_size,
+            [place, note[:, :top_count], note[:, top_count:], *rows],
+            flops=16 * slots * group_size * tok_rows * model_width,
+        )
+        for turn, part in zip(group, parts):
+            sums[turn] = part
     layer_out = residual.astype(jnp.float32) + sums[0].astype(jnp.float32)
-    for turn in range(1, depth):
-        layer_out = layer_out + turn_z(sums[turn], -turn).astype(jnp.float32)
+    for part in scatter_z(sums):
+        layer_out = layer_out + part.astype(jnp.float32)
     return layer_out.astype(jnp.bfloat16)
 
 

time: 281 us -> 207 us (0.74)
  waiting for transfers between devices: 126 us -> 92.6 us
  blocking collectives: 30.5 us -> 0 us
  Pallas kernels: 58.1 us -> 42.8 us
  local copies, waits for them, and re-layouts: 9.76 us -> 15.1 us
    ppermute x37 -> x41, waiting for transfers between devices: 126 us -> 92.6 us  [move(): return lax.ppermute(block, AXES, route)]
    all_gather x1 -> x0, blocking collectives: 30.5 us -> none  [shards(): noted = lax.all_gather(noted, 'ctx', axis=0).reshape(depth, 2, tok_rows, -1)]
    pallas_call x8 -> x10, Pallas kernels: 58.1 us -> 42.8 us  [call(): pl.pallas_call(kernel, out_shape=outs, in_specs=[SMEM] * smem + [VMEM] *...]
    unnamed x76 -> x40, local copies, waits for them, and re-layouts: 6.28 us -> 15 us
    ppermute x37 -> x41, starting transfers between devices: 49.1 us -> 51.6 us  [move(): return lax.ppermute(block, AXES, route)]
  transfers between devices with their start and end apart: 37 -> 41, of which waited for: 20 -> 22; matrix products, arithmetic and copies ran while one was open for 2% -> 2% of each run, Pallas kernels for 4% -> 19%
where the time goes in v2:
time: 207 us
  waiting for transfers between devices  92.6 us (45%)
  starting transfers between devices  51.6 us (25%)
  Pallas kernels  42.8 us (21%)
  local copies, waits for them, and re-layouts  15.1 us (7%)
  other arithmetic  4.25 us (2%)
    ppermute x41, waiting for transfers between devices, move(): return lax.ppermute(block, AXES, route)  92.6 us
    ppermute x41, starting transfers between devices, move(): return lax.ppermute(block, AXES, route)  51.6 us
    pallas_call x10, Pallas kernels, call(): pl.pallas_call(kernel, out_shape=outs, in_specs=[SMEM] * smem + [VMEM] *...  42.8 us
    unnamed x40, local copies, waits for them, and re-layouts  15 us
  transfers between devices with their start and end apart: 41, of which 22 were waited for; matrix products, arithmetic and copies ran while one was open for 2% of the time, Pallas kernels for 19%

profile of v2, /device:TPU:0, one launch (start us, length us, event | category | flops | bytes accessed | tf_op | source)
XLA Modules:
  0.0 206.7 jit_solution(16284466018697396003)
XLA Ops:
  1.0 2.5 %collective-permute-start.1 = (bf16[80,2048]{1,0:T(8,128)(2,1)}, bf16[80,2048]{1,0:T(8,128)(2,1)S(1)}, u32[]{:S(2)}, u32[]{:S(2)}) collective-permute-start(bf16[80,2048]{1,0:T(8,128)(2,1)} %inputs.1), channel_id=1, source_target_pairs={{0,2},{1,3},{2,0},{3,1},{4,6},{5,7},{6,4},{7,5},{8,10},{9,11},{10,... | collective-permute-start | bytes 983048 | tf_op jit(solution)/shard_map/ppermute | solution.py:26
  4.9 1.6 collective-permute-start.2
  6.4 3.9 %collective-permute-done.2 = f32[80,12]{0,1:T(8,128)S(1)} collective-permute-done((f32[80,12]{0,1:T(8,128)S(1)}, f32[80,12]{0,1:T(8,128)S(1)}, u32[]{:S(2)}, u32[]{:S(2)}) %collective-permute-start.2) | collective-permute-done | bytes 3872 | tf_op jit(solution)/shard_map/ppermute | solution.py:26
  10.3 1.8 collective-permute-start.4
  12.1 1.8 collective-permute-done.4
  14.0 5.4 %collective-permute-done.3 = f32[80,12]{0,1:T(8,128)S(1)} collective-permute-done((f32[80,12]{0,1:T(8,128)S(1)}, f32[80,12]{0,1:T(8,128)S(1)}, u32[]{:S(2)}, u32[]{:S(2)}) %collective-permute-start.3) | collective-permute-done | bytes 3872 | tf_op jit(solution)/shard_map/ppermute | solution.py:26
  21.7 1.6 copy-done
  23.3 1.6 copy-done.1
  24.8 1.6 copy-done.2
  28.1 3.7 %shard_map.127 = (bf16[336,384]{1,0:T(8,128)(2,1)S(1)}, bf16[336,384]{1,0:T(8,128)(2,1)S(1)}, bf16[336,384]{1,0:T(8,128)(2,1)S(1)}, bf16[336,384]{1,0:T(8,128)(2,1)S(1)}) custom-call(s32[5]{0:T(128)S(1)} %stack.20.place, bf16[80,2048]{1,0:T(8,128)(2,1)S(1)} %copy-done.3, bf16[80,2048]{1,0:T(8,128)(2,1)S(1)} %collective-permute-done.refs_1_, ...), custom_call_target="tpu_custom_call" | custom-call | flops 2013265920 | bytes 7659540 | tf_op jit(solution)/shard_map/pallas_call | solution.py:94
  32.6 2.3 %collective-permute-start.8 = (bf16[336,384]{1,0:T(8,128)(2,1)S(1)}, bf16[336,384]{1,0:T(8,128)(2,1)S(1)}, u32[]{:S(2)}, u32[]{:S(2)}) collective-permute-start(bf16[336,384]{1,0:T(8,128)(2,1)S(1)} %get-tuple-element.52), channel_id=1, source_target_pairs={{0,16},{1,20},{2,18},{3,22},{4,17},{5,21},{6,19},{7,23},{8,24},{9,... | collective-permute-start | bytes 774152 | tf_op jit(solution)/shard_map/ppermute | solution.py:26
  35.0 6.7 %collective-permute-done.7.refs_1_ = bf16[336,384]{1,0:T(8,128)(2,1)S(1)} collective-permute-done((bf16[336,384]{1,0:T(8,128)(2,1)S(1)}, bf16[336,384]{1,0:T(8,128)(2,1)S(1)}, u32[]{:S(2)}, u32[]{:S(2)}) %collective-permute-start.7) | collective-permute-done | bytes 258080 | tf_op jit(solution)/shard_map/ppermute | solution.py:26
  41.9 10.9 %collective-permute-done.8.refs_2_ = bf16[336,384]{1,0:T(8,128)(2,1)S(1)} collective-permute-done((bf16[336,384]{1,0:T(8,128)(2,1)S(1)}, bf16[336,384]{1,0:T(8,128)(2,1)S(1)}, u32[]{:S(2)}, u32[]{:S(2)}) %collective-permute-start.8) | collective-permute-done | bytes 258080 | tf_op jit(solution)/shard_map/ppermute | solution.py:26
  52.7 1.9 collective-permute-start.10
  54.6 3.5 %collective-permute-start.11 = (bf16[336,384]{1,0:T(8,128)(2,1)S(1)}, bf16[336,384]{1,0:T(8,128)(2,1)S(1)}, u32[]{:S(2)}, u32[]{:S(2)}) collective-permute-start(bf16[336,384]{1,0:T(8,128)(2,1)S(1)} %collective-permute-done.7.refs_1_), channel_id=1, source_target_pairs={{0,1},{1,0},{2,3},{3,2},{4,5},{5,4},{6,7},{7,6},{8,9},{9,8},{10,11... | collective-permute-start | bytes 774152 | tf_op jit(solution)/shard_map/ppermute | solution.py:26
  60.8 7.9 %shard_map.128 = (bf16[320,128]{1,0:T(8,128)(2,1)S(1)}, bf16[320,128]{1,0:T(8,128)(2,1)S(1)}, bf16[320,128]{1,0:T(8,128)(2,1)S(1)}, bf16[320,128]{1,0:T(8,128)(2,1)S(1)}) custom-call(s32[5]{0:T(128)S(1)} %stack.20.place, bf16[336,384]{1,0:T(8,128)(2,1)S(1)} %collective-permute-done.6.refs_0_, bf16[336,384]{1,0:T(8,128)(2,1)S(1)} %collective-permute-done.7.refs_1_, ...), custom_call_target="tpu_custom_call" | custom-call | flops 1677721600 | bytes 2064404 | tf_op jit(solution)/shard_map/pallas_call | solution.py:94
  69.6 2.2 %collective-permute-start.15 = (bf16[320,128]{1,0:T(8,128)(2,1)S(1)}, bf16[320,128]{1,0:T(8,128)(2,1)S(1)}, u32[]{:S(2)}, u32[]{:S(2)}) collective-permute-start(bf16[320,128]{1,0:T(8,128)(2,1)S(1)} %get-tuple-element.55), channel_id=1, source_target_pairs={{0,24},{1,28},{2,26},{3,30},{4,25},{5,29},{6,27},{7,31},{8,0},{9,4... | collective-permute-start | bytes 245768 | tf_op jit(solution)/shard_map/ppermute | solution.py:26
  71.8 2.2 %collective-permute-start.16 = (bf16[320,128]{1,0:T(8,128)(2,1)S(1)}, bf16[320,128]{1,0:T(8,128)(2,1)S(1)}, u32[]{:S(2)}, u32[]{:S(2)}) collective-permute-start(bf16[320,128]{1,0:T(8,128)(2,1)S(1)} %get-tuple-element.56), channel_id=1, source_target_pairs={{0,16},{1,20},{2,18},{3,22},{4,17},{5,21},{6,19},{7,23},{8,24},{9,... | collective-permute-start | bytes 245768 | tf_op jit(solution)/shard_map/ppermute | solution.py:26
  74.1 2.8 %collective-permute-start.17 = (bf16[320,128]{1,0:T(8,128)(2,1)S(1)}, bf16[320,128]{1,0:T(8,128)(2,1)S(1)}, u32[]{:S(2)}, u32[]{:S(2)}) collective-permute-start(bf16[320,128]{1,0:T(8,128)(2,1)S(1)} %get-tuple-element.57), channel_id=1, source_target_pairs={{0,8},{1,12},{2,10},{3,14},{4,9},{5,13},{6,11},{7,15},{8,16},{9,20... | collective-permute-start | bytes 245768 | tf_op jit(solution)/shard_map/ppermute | solution.py:26
  77.6 3.2 %collective-permute-done.17.refs_3_ = bf16[320,128]{1,0:T(8,128)(2,1)S(1)} collective-permute-done((bf16[320,128]{1,0:T(8,128)(2,1)S(1)}, bf16[320,128]{1,0:T(8,128)(2,1)S(1)}, u32[]{:S(2)}, u32[]{:S(2)}) %collective-permute-start.17) | collective-permute-done | bytes 81952 | tf_op jit(solution)/shard_map/ppermute | solution.py:26
  80.8 1.5 shard_map.129
  82.3 4.9 %collective-permute-start.21 = (bf16[2,80,2048]{2,1,0:T(8,128)(2,1)S(1)}, bf16[2,80,2048]{2,1,0:T(8,128)(2,1)S(1)}, u32[]{:S(2)}, u32[]{:S(2)}) collective-permute-start(bf16[2,80,2048]{2,1,0:T(8,128)(2,1)S(1)} %get-tuple-element.63), channel_id=1, source_target_pairs={{0,1},{1,0},{2,3},{3,2},{4,5},{5,4},{6,7},{7,6},{8,9},{9,8},{10,11... | collective-permute-start | bytes 1966088 | tf_op jit(solution)/shard_map/ppermute | solution.py:26
  87.3 1.7 collective-permute-done.21.given
  89.9 9.3 %collective-permute-done.22.far = bf16[80,2048]{1,0:T(8,128)(2,1)S(1)} collective-permute-done((bf16[80,2048]{1,0:T(8,128)(2,1)S(1)}, bf16[80,2048]{1,0:T(8,128)(2,1)S(1)}, u32[]{:S(2)}, u32[]{:S(2)}) %collective-permute-start.22) | collective-permute-done | bytes 327712 | tf_op jit(solution)/shard_map/ppermute | solution.py:26
  99.6 3.8 %collective-permute-start.30 = (bf16[80,2048]{1,0:T(8,128)(2,1)S(1)}, bf16[80,2048]{1,0:T(8,128)(2,1)S(1)}, u32[]{:S(2)}, u32[]{:S(2)}) collective-permute-start(bf16[80,2048]{1,0:T(8,128)(2,1)S(1)} %get-tuple-element.67.refs_0_), channel_id=1, source_target_pairs={{0,24},{1,25},{2,26},{3,27},{4,28},{5,29},{6,30},{7,31},{8,0},{9,1... | collective-permute-start | bytes 983048 | tf_op jit(solution)/shard_map/ppermute | solution.py:26
  103.4 8.6 %collective-permute-done.23.refs_1_ = bf16[80,2048]{1,0:T(8,128)(2,1)S(1)} collective-permute-done((bf16[80,2048]{1,0:T(8,128)(2,1)S(1)}, bf16[80,2048]{1,0:T(8,128)(2,1)S(1)}, u32[]{:S(2)}, u32[]{:S(2)}) %collective-permute-start.23) | collective-permute-done | bytes 327712 | tf_op jit(solution)/shard_map/ppermute | solution.py:26
  112.1 3.7 %collective-permute-done.30.refs_0_ = bf16[80,2048]{1,0:T(8,128)(2,1)S(1)} collective-permute-done((bf16[80,2048]{1,0:T(8,128)(2,1)S(1)}, bf16[80,2048]{1,0:T(8,128)(2,1)S(1)}, u32[]{:S(2)}, u32[]{:S(2)}) %collective-permute-start.30) | collective-permute-done | bytes 327712 | tf_op jit(solution)/shard_map/ppermute | solution.py:26
  115.8 8.8 %collective-permute-done.31.refs_1_ = bf16[80,2048]{1,0:T(8,128)(2,1)S(1)} collective-permute-done((bf16[80,2048]{1,0:T(8,128)(2,1)S(1)}, bf16[80,2048]{1,0:T(8,128)(2,1)S(1)}, u32[]{:S(2)}, u32[]{:S(2)}) %collective-permute-start.31) | collective-permute-done | bytes 327712 | tf_op jit(solution)/shard_map/ppermute | solution.py:26
  124.6 1.6 shard_map.134
  128.9 1.5 collective-permute-start.34
  130.7 1.6 shard_map.131
  134.3 8.8 %collective-permute-done.32.refs_1_ = bf16[80,2048]{1,0:T(8,128)(2,1)S(1)} collective-permute-done((bf16[80,2048]{1,0:T(8,128)(2,1)S(1)}, bf16[80,2048]{1,0:T(8,128)(2,1)S(1)}, u32[]{:S(2)}, u32[]{:S(2)}) %collective-permute-start.32) | collective-permute-done | bytes 327712 | tf_op jit(solution)/shard_map/ppermute | solution.py:26
  144.1 2.0 collective-permute-done.34.refs_3_
  146.1 1.8 copy-done.7
  148.0 1.8 copy-done.9
  149.8 1.8 copy-done.11
  152.6 10.0 %shard_map.135 = (bf16[80,2048]{1,0:T(8,128)(2,1)S(1)}, bf16[80,2048]{1,0:T(8,128)(2,1)S(1)}, bf16[80,2048]{1,0:T(8,128)(2,1)S(1)}, bf16[80,2048]{1,0:T(8,128)(2,1)S(1)}) custom-call(bf16[80,2048]{1,0:T(8,128)(2,1)S(1)} %copy-done.17, bf16[80,2048]{1,0:T(8,128)(2,1)S(1)} %collective-permute-done.32.refs_1_, ...), custom_call_target="tpu_custom_call" | custom-call | flops 5536481280 | bytes 18612224 | tf_op jit(solution)/shard_map/pallas_call | solution.py:94
  163.3 1.3 collective-permute-start.36
  164.6 1.5 collective-permute-start.37
  166.2 10.1 %shard_map.132 = (bf16[80,2048]{1,0:T(8,128)(2,1)S(1)}, bf16[80,2048]{1,0:T(8,128)(2,1)S(1)}, bf16[80,2048]{1,0:T(8,128)(2,1)S(1)}, bf16[80,2048]{1,0:T(8,128)(2,1)S(1)}) custom-call(bf16[80,2048]{1,0:T(8,128)(2,1)S(1)} %get-tuple-element.68.refs_0_, bf16[80,2048]{1,0:T(8,128)(2,1)S(1)} %collective-permute-done.24.refs_1_, ...), custom_call_target="tpu_custom_call" | custom-call | flops 5536481280 | bytes 18612224 | tf_op jit(solution)/shard_map/pallas_call | solution.py:94
  178.3 1.5 collective-permute-start.29
  179.8 3.0 %shard_map.136 = (bf16[80,2048]{1,0:T(8,128)(2,1)S(1)}, bf16[80,2048]{1,0:T(8,128)(2,1)S(1)}) custom-call(s32[5]{0:T(128)S(1)} %stack.20.place, f32[160,6]{1,0:T(8,128)S(1)} %copy.26.routes, f32[160,6]{1,0:T(8,128)S(1)} %copy.27.gates, bf16[80,2048]{1,0:T(8,128)(2,1)S(1)} %get-tuple-element.86.refs_0_, bf16[80,2048]{1,0:T(8,128)(2,1)S(1)} %collective-permute-done.35.refs_1_, ...), custom_call_target="tpu_custom_call" | custom-call | flops 419430400 | bytes 1318420 | tf_op jit(solution)/shard_map/pallas_call | solution.py:94
  183.1 2.7 %collective-permute-done.27.refs_1_ = bf16[80,2048]{1,0:T(8,128)(2,1)S(1)} collective-permute-done((bf16[80,2048]{1,0:T(8,128)(2,1)S(1)}, bf16[80,2048]{1,0:T(8,128)(2,1)S(1)}, u32[]{:S(2)}, u32[]{:S(2)}) %collective-permute-start.27) | collective-permute-done | bytes 327712 | tf_op jit(solution)/shard_map/ppermute | solution.py:26
  185.9 3.5 %collective-permute-done.29.refs_3_ = bf16[80,2048]{1,0:T(8,128)(2,1)S(1)} collective-permute-done((bf16[80,2048]{1,0:T(8,128)(2,1)S(1)}, bf16[80,2048]{1,0:T(8,128)(2,1)S(1)}, u32[]{:S(2)}, u32[]{:S(2)}) %collective-permute-start.29) | collective-permute-done | bytes 327712 | tf_op jit(solution)/shard_map/ppermute | solution.py:26
  190.3 3.0 %shard_map.133 = (bf16[80,2048]{1,0:T(8,128)(2,1)S(1)}, bf16[80,2048]{1,0:T(8,128)(2,1)S(1)}) custom-call(s32[5]{0:T(128)S(1)} %stack.20.place, f32[160,6]{1,0:T(8,128)S(1)} %copy.24.routes, f32[160,6]{1,0:T(8,128)S(1)} %copy.25.gates, bf16[80,2048]{1,0:T(8,128)(2,1)S(1)} %copy-done.15, bf16[80,2048]{1,0:T(8,128)(2,1)S(1)} %collective-permute-done.27.refs_1_, ...), custom_call_target="tpu_custom_call" | custom-call | flops 419430400 | bytes 1318420 | tf_op jit(solution)/shard_map/pallas_call | solution.py:94
  194.5 3.9 %collective-permute-start.39 = (bf16[80,2048]{1,0:T(8,128)(2,1)S(1)}, bf16[80,2048]{1,0:T(8,128)(2,1)S(1)}, u32[]{:S(2)}, u32[]{:S(2)}) collective-permute-start(bf16[80,2048]{1,0:T(8,128)(2,1)S(1)} %add_convert_fusion.1), channel_id=1, source_target_pairs={{0,24},{1,25},{2,26},{3,27},{4,28},{5,29},{6,30},{7,31},{8,0},{9,1... | collective-permute-start | bytes 983048 | tf_op jit(solution)/shard_map/ppermute | solution.py:26
  198.4 4.1 %collective-permute-done.40 = bf16[80,2048]{1,0:T(8,128)(2,1)S(1)} collective-permute-done((bf16[80,2048]{1,0:T(8,128)(2,1)S(1)}, bf16[80,2048]{1,0:T(8,128)(2,1)S(1)}, u32[]{:S(2)}, u32[]{:S(2)}) %collective-permute-start.40) | collective-permute-done | bytes 327712 | tf_op jit(solution)/shard_map/ppermute | solution.py:26
  202.5 3.3 %collective-permute-done.39 = bf16[80,2048]{1,0:T(8,128)(2,1)S(1)} collective-permute-done((bf16[80,2048]{1,0:T(8,128)(2,1)S(1)}, bf16[80,2048]{1,0:T(8,128)(2,1)S(1)}, u32[]{:S(2)}, u32[]{:S(2)}) %collective-permute-start.39) | collective-permute-done | bytes 327712 | tf_op jit(solution)/shard_map/ppermute | solution.py:26
  (95 shorter events, 25.9 us)
Async XLA Ops:
  0.0 80.8 %collective-permute-start.18 = (bf16[1,2048,704]{1,2,0:T(8,128)(2,1)}, bf16[1,2048,704]{1,2,0:T(8,128)(2,1)}, u32[]{:S(2)}, u32[]{:S(2)}) collective-permute-start(bf16[1,2048,704]{1,2,0:T(8,128)(2,1)} %param.21), channel_id=1, source_target_pairs={{0,1},{1,0},{2,3},{3,2},{4,5},{5,4},{6,7},{7,6},{8,9},{9,8},{10,11... | collective-permute-start | bytes 8650760 | tf_op jit(solution)/shard_map/ppermute | solution.py:26
  0.5 80.3 %collective-permute-start.19 = (bf16[1,2048,704]{1,2,0:T(8,128)(2,1)}, bf16[1,2048,704]{1,2,0:T(8,128)(2,1)}, u32[]{:S(2)}, u32[]{:S(2)}) collective-permute-start(bf16[1,2048,704]{1,2,0:T(8,128)(2,1)} %param.22), channel_id=1, source_target_pairs={{0,1},{1,0},{2,3},{3,2},{4,5},{5,4},{6,7},{7,6},{8,9},{9,8},{10,11... | collective-permute-start | bytes 8650760 | tf_op jit(solution)/shard_map/ppermute | solution.py:26
  0.5 80.3 %collective-permute-start.20 = (bf16[1,704,2048]{2,1,0:T(8,128)(2,1)}, bf16[1,704,2048]{2,1,0:T(8,128)(2,1)}, u32[]{:S(2)}, u32[]{:S(2)}) collective-permute-start(bf16[1,704,2048]{2,1,0:T(8,128)(2,1)} %param.23), channel_id=1, source_target_pairs={{0,1},{1,0},{2,3},{3,2},{4,5},{5,4},{6,7},{7,6},{8,9},{9,8},{10,11... | collective-permute-start | bytes 8650760 | tf_op jit(solution)/shard_map/ppermute | solution.py:26
  1.0 18.5 %collective-permute-start.1 = (bf16[80,2048]{1,0:T(8,128)(2,1)}, bf16[80,2048]{1,0:T(8,128)(2,1)S(1)}, u32[]{:S(2)}, u32[]{:S(2)}) collective-permute-start(bf16[80,2048]{1,0:T(8,128)(2,1)} %inputs.1), channel_id=1, source_target_pairs={{0,2},{1,3},{2,0},{3,1},{4,6},{5,7},{6,4},{7,5},{8,10},{9,11},{10,... | collective-permute-start | bytes 983048 | tf_op jit(solution)/shard_map/ppermute | solution.py:26
  4.9 5.4 %collective-permute-start.2 = (f32[80,12]{0,1:T(8,128)S(1)}, f32[80,12]{0,1:T(8,128)S(1)}, u32[]{:S(2)}, u32[]{:S(2)}) collective-permute-start(f32[80,12]{0,1:T(8,128)S(1)} %pad_maximum_fusion.2), channel_id=1, source_target_pairs={{0,8},{1,9},{2,10},{3,11},{4,12},{5,13},{6,14},{7,15},{8,16},{9,17... | collective-permute-start | bytes 11528 | tf_op jit(solution)/shard_map/ppermute | solution.py:26
  10.3 3.7 %collective-permute-start.4 = (f32[80,12]{0,1:T(8,128)S(1)}, f32[80,12]{0,1:T(8,128)S(1)}, u32[]{:S(2)}, u32[]{:S(2)}) collective-permute-start(f32[80,12]{0,1:T(8,128)S(1)} %pad_maximum_fusion.2), channel_id=1, source_target_pairs={{0,24},{1,25},{2,26},{3,27},{4,28},{5,29},{6,30},{7,31},{8,0},{9,1... | collective-permute-start | bytes 11528 | tf_op jit(solution)/shard_map/ppermute | solution.py:26
  14.0 5.4 %collective-permute-start.3 = (f32[80,12]{0,1:T(8,128)S(1)}, f32[80,12]{0,1:T(8,128)S(1)}, u32[]{:S(2)}, u32[]{:S(2)}) collective-permute-start(f32[80,12]{0,1:T(8,128)S(1)} %collective-permute-done.2), channel_id=1, source_target_pairs={{0,8},{1,9},{2,10},{3,11},{4,12},{5,13},{6,14},{7,15},{8,16},{9,17... | collective-permute-start | bytes 11528 | tf_op jit(solution)/shard_map/ppermute | solution.py:26
  19.4 2.2 %collective-permute-start = (bf16[80,2048]{1,0:T(8,128)(2,1)}, bf16[80,2048]{1,0:T(8,128)(2,1)S(1)}, u32[]{:S(2)}, u32[]{:S(2)}) collective-permute-start(bf16[80,2048]{1,0:T(8,128)(2,1)} %inputs.1), channel_id=1, source_target_pairs={{0,1},{1,0},{2,3},{3,2},{4,5},{5,4},{6,7},{7,6},{8,9},{9,8},{10,11... | collective-permute-start | bytes 983048 | tf_op jit(solution)/shard_map/ppermute | solution.py:26
  19.4 2.2 %collective-permute-start.5 = (bf16[80,2048]{1,0:T(8,128)(2,1)S(1)}, bf16[80,2048]{1,0:T(8,128)(2,1)S(1)}, u32[]{:S(2)}, u32[]{:S(2)}) collective-permute-start(bf16[80,2048]{1,0:T(8,128)(2,1)S(1)} %collective-permute-done.1.refs_2_), channel_id=1, source_target_pairs={{0,1},{1,0},{2,3},{3,2},{4,5},{5,4},{6,7},{7,6},{8,9},{9,8},{10,11... | collective-permute-start | bytes 983048 | tf_op jit(solution)/shard_map/ppermute | solution.py:26
  31.8 0.8 collective-permute-start.6
  32.5 9.2 %collective-permute-start.7 = (bf16[336,384]{1,0:T(8,128)(2,1)S(1)}, bf16[336,384]{1,0:T(8,128)(2,1)S(1)}, u32[]{:S(2)}, u32[]{:S(2)}) collective-permute-start(bf16[336,384]{1,0:T(8,128)(2,1)S(1)} %get-tuple-element.51), channel_id=1, source_target_pairs={{0,8},{1,12},{2,10},{3,14},{4,9},{5,13},{6,11},{7,15},{8,16},{9,20... | collective-permute-start | bytes 774152 | tf_op jit(solution)/shard_map/ppermute | solution.py:26
  32.6 20.1 %collective-permute-start.8 = (bf16[336,384]{1,0:T(8,128)(2,1)S(1)}, bf16[336,384]{1,0:T(8,128)(2,1)S(1)}, u32[]{:S(2)}, u32[]{:S(2)}) collective-permute-start(bf16[336,384]{1,0:T(8,128)(2,1)S(1)} %get-tuple-element.52), channel_id=1, source_target_pairs={{0,16},{1,20},{2,18},{3,22},{4,17},{5,21},{6,19},{7,23},{8,24},{9,... | collective-permute-start | bytes 774152 | tf_op jit(solution)/shard_map/ppermute | solution.py:26
  41.7 39.1 %copy-start.13 = (bf16[512,2048]{1,0:T(8,128)(2,1)S(1)}, bf16[512,2048]{1,0:T(8,128)(2,1)}, u32[]{:S(2)}) copy-start(bf16[512,2048]{1,0:T(8,128)(2,1)} %refs_4_.1) | copy-start | bytes 6291460
  41.7 12.9 %collective-permute-start.9 = (bf16[336,384]{1,0:T(8,128)(2,1)S(1)}, bf16[336,384]{1,0:T(8,128)(2,1)S(1)}, u32[]{:S(2)}, u32[]{:S(2)}) collective-permute-start(bf16[336,384]{1,0:T(8,128)(2,1)S(1)} %get-tuple-element.53), channel_id=1, source_target_pairs={{0,24},{1,28},{2,26},{3,30},{4,25},{5,29},{6,27},{7,31},{8,0},{9,4... | collective-permute-start | bytes 774152 | tf_op jit(solution)/shard_map/ppermute | solution.py:26
  52.7 5.4 %collective-permute-start.10 = (bf16[336,384]{1,0:T(8,128)(2,1)S(1)}, bf16[336,384]{1,0:T(8,128)(2,1)S(1)}, u32[]{:S(2)}, u32[]{:S(2)}) collective-permute-start(bf16[336,384]{1,0:T(8,128)(2,1)S(1)} %collective-permute-done.6.refs_0_), channel_id=1, source_target_pairs={{0,1},{1,0},{2,3},{3,2},{4,5},{5,4},{6,7},{7,6},{8,9},{9,8},{10,11... | collective-permute-start | bytes 774152 | tf_op jit(solution)/shard_map/ppermute | solution.py:26
  54.6 4.7 %collective-permute-start.11 = (bf16[336,384]{1,0:T(8,128)(2,1)S(1)}, bf16[336,384]{1,0:T(8,128)(2,1)S(1)}, u32[]{:S(2)}, u32[]{:S(2)}) collective-permute-start(bf16[336,384]{1,0:T(8,128)(2,1)S(1)} %collective-permute-done.7.refs_1_), channel_id=1, source_target_pairs={{0,1},{1,0},{2,3},{3,2},{4,5},{5,4},{6,7},{7,6},{8,9},{9,8},{10,11... | collective-permute-start | bytes 774152 | tf_op jit(solution)/shard_map/ppermute | solution.py:26
  58.2 1.5 collective-permute-start.12
  59.3 1.5 collective-permute-start.13
  68.7 30.4 %copy-start.4 = (bf16[80,2048]{1,0:T(8,128)(2,1)S(1)}, bf16[80,2048]{1,0:T(8,128)(2,1)}, u32[]{:S(2)}) copy-start(bf16[80,2048]{1,0:T(8,128)(2,1)} %inputs.1) | copy-start | bytes 983044
  68.8 30.4 %copy-start.6 = (f32[2048]{0:T(1024)S(1)}, f32[2048]{0:T(1024)}, u32[]{:S(2)}) copy-start(f32[2048]{0:T(1024)} %param.20) | copy-start | bytes 24580
  68.8 3.0 %collective-permute-start.14 = (bf16[320,128]{1,0:T(8,128)(2,1)S(1)}, bf16[320,128]{1,0:T(8,128)(2,1)S(1)}, u32[]{:S(2)}, u32[]{:S(2)}) collective-permute-start(bf16[320,128]{1,0:T(8,128)(2,1)S(1)} %get-tuple-element.54), channel_id=1, source_target_pairs={{0,0},{1,4},{2,2},{3,6},{4,1},{5,5},{6,3},{7,7},{8,8},{9,12},{10,1... | collective-permute-start | bytes 245768 | tf_op jit(solution)/shard_map/ppermute | solution.py:26
  69.6 4.5 %collective-permute-start.15 = (bf16[320,128]{1,0:T(8,128)(2,1)S(1)}, bf16[320,128]{1,0:T(8,128)(2,1)S(1)}, u32[]{:S(2)}, u32[]{:S(2)}) collective-permute-start(bf16[320,128]{1,0:T(8,128)(2,1)S(1)} %get-tuple-element.55), channel_id=1, source_target_pairs={{0,24},{1,28},{2,26},{3,30},{4,25},{5,29},{6,27},{7,31},{8,0},{9,4... | collective-permute-start | bytes 245768 | tf_op jit(solution)/shard_map/ppermute | solution.py:26
  71.8 5.8 %collective-permute-start.16 = (bf16[320,128]{1,0:T(8,128)(2,1)S(1)}, bf16[320,128]{1,0:T(8,128)(2,1)S(1)}, u32[]{:S(2)}, u32[]{:S(2)}) collective-permute-start(bf16[320,128]{1,0:T(8,128)(2,1)S(1)} %get-tuple-element.56), channel_id=1, source_target_pairs={{0,16},{1,20},{2,18},{3,22},{4,17},{5,21},{6,19},{7,23},{8,24},{9,... | collective-permute-start | bytes 245768 | tf_op jit(solution)/shard_map/ppermute | solution.py:26
  74.1 6.7 %collective-permute-start.17 = (bf16[320,128]{1,0:T(8,128)(2,1)S(1)}, bf16[320,128]{1,0:T(8,128)(2,1)S(1)}, u32[]{:S(2)}, u32[]{:S(2)}) collective-permute-start(bf16[320,128]{1,0:T(8,128)(2,1)S(1)} %get-tuple-element.57), channel_id=1, source_target_pairs={{0,8},{1,12},{2,10},{3,14},{4,9},{5,13},{6,11},{7,15},{8,16},{9,20... | collective-permute-start | bytes 245768 | tf_op jit(solution)/shard_map/ppermute | solution.py:26
  82.3 6.7 %collective-permute-start.21 = (bf16[2,80,2048]{2,1,0:T(8,128)(2,1)S(1)}, bf16[2,80,2048]{2,1,0:T(8,128)(2,1)S(1)}, u32[]{:S(2)}, u32[]{:S(2)}) collective-permute-start(bf16[2,80,2048]{2,1,0:T(8,128)(2,1)S(1)} %get-tuple-element.63), channel_id=1, source_target_pairs={{0,1},{1,0},{2,3},{3,2},{4,5},{5,4},{6,7},{7,6},{8,9},{9,8},{10,11... | collective-permute-start | bytes 1966088 | tf_op jit(solution)/shard_map/ppermute | solution.py:26
  89.1 10.1 %collective-permute-start.22 = (bf16[80,2048]{1,0:T(8,128)(2,1)S(1)}, bf16[80,2048]{1,0:T(8,128)(2,1)S(1)}, u32[]{:S(2)}, u32[]{:S(2)}) collective-permute-start(bf16[80,2048]{1,0:T(8,128)(2,1)S(1)} %fusion), channel_id=1, source_target_pairs={{0,2},{1,3},{2,0},{3,1},{4,6},{5,7},{6,4},{7,5},{8,10},{9,11},{10,... | collective-permute-start | bytes 983048 | tf_op jit(solution)/shard_map/ppermute | solution.py:26
  99.5 12.5 %collective-permute-start.23 = (bf16[80,2048]{1,0:T(8,128)(2,1)S(1)}, bf16[80,2048]{1,0:T(8,128)(2,1)S(1)}, u32[]{:S(2)}, u32[]{:S(2)}) collective-permute-start(bf16[80,2048]{1,0:T(8,128)(2,1)S(1)} %get-tuple-element.67.refs_0_), channel_id=1, source_target_pairs={{0,8},{1,9},{2,10},{3,11},{4,12},{5,13},{6,14},{7,15},{8,16},{9,17... | collective-permute-start | bytes 983048 | tf_op jit(solution)/shard_map/ppermute | solution.py:26
  99.6 16.2 %collective-permute-start.30 = (bf16[80,2048]{1,0:T(8,128)(2,1)S(1)}, bf16[80,2048]{1,0:T(8,128)(2,1)S(1)}, u32[]{:S(2)}, u32[]{:S(2)}) collective-permute-start(bf16[80,2048]{1,0:T(8,128)(2,1)S(1)} %get-tuple-element.67.refs_0_), channel_id=1, source_target_pairs={{0,24},{1,25},{2,26},{3,27},{4,28},{5,29},{6,30},{7,31},{8,0},{9,1... | collective-permute-start | bytes 983048 | tf_op jit(solution)/shard_map/ppermute | solution.py:26
  112.0 12.6 %collective-permute-start.31 = (bf16[80,2048]{1,0:T(8,128)(2,1)S(1)}, bf16[80,2048]{1,0:T(8,128)(2,1)S(1)}, u32[]{:S(2)}, u32[]{:S(2)}) collective-permute-start(bf16[80,2048]{1,0:T(8,128)(2,1)S(1)} %collective-permute-done.23.refs_1_), channel_id=1, source_target_pairs={{0,8},{1,9},{2,10},{3,11},{4,12},{5,13},{6,14},{7,15},{8,16},{9,17... | collective-permute-start | bytes 983048 | tf_op jit(solution)/shard_map/ppermute | solution.py:26
  127.0 16.2 %collective-permute-start.32 = (bf16[80,2048]{1,0:T(8,128)(2,1)S(1)}, bf16[80,2048]{1,0:T(8,128)(2,1)S(1)}, u32[]{:S(2)}, u32[]{:S(2)}) collective-permute-start(bf16[80,2048]{1,0:T(8,128)(2,1)S(1)} %get-tuple-element.83), channel_id=1, source_target_pairs={{0,2},{1,3},{2,0},{3,1},{4,6},{5,7},{6,4},{7,5},{8,10},{9,11},{10,... | collective-permute-start | bytes 983048 | tf_op jit(solution)/shard_map/ppermute | solution.py:26
  127.7 16.4 %collective-permute-start.33 = (bf16[80,2048]{1,0:T(8,128)(2,1)S(1)}, bf16[80,2048]{1,0:T(8,128)(2,1)S(1)}, u32[]{:S(2)}, u32[]{:S(2)}) collective-permute-start(bf16[80,2048]{1,0:T(8,128)(2,1)S(1)} %get-tuple-element.84), channel_id=1, source_target_pairs={{0,4},{1,5},{2,6},{3,7},{4,0},{5,1},{6,2},{7,3},{8,12},{9,13},{10,... | collective-permute-start | bytes 983048 | tf_op jit(solution)/shard_map/ppermute | solution.py:26
  128.9 17.2 %collective-permute-start.34 = (bf16[80,2048]{1,0:T(8,128)(2,1)S(1)}, bf16[80,2048]{1,0:T(8,128)(2,1)S(1)}, u32[]{:S(2)}, u32[]{:S(2)}) collective-permute-start(bf16[80,2048]{1,0:T(8,128)(2,1)S(1)} %get-tuple-element.85), channel_id=1, source_target_pairs={{0,6},{1,7},{2,4},{3,5},{4,2},{5,3},{6,0},{7,1},{8,14},{9,15},{10,... | collective-permute-start | bytes 983048 | tf_op jit(solution)/shard_map/ppermute | solution.py:26
  132.3 32.3 %collective-permute-start.24 = (bf16[80,2048]{1,0:T(8,128)(2,1)S(1)}, bf16[80,2048]{1,0:T(8,128)(2,1)S(1)}, u32[]{:S(2)}, u32[]{:S(2)}) collective-permute-start(bf16[80,2048]{1,0:T(8,128)(2,1)S(1)} %get-tuple-element.69), channel_id=1, source_target_pairs={{0,2},{1,3},{2,0},{3,1},{4,6},{5,7},{6,4},{7,5},{8,10},{9,11},{10,... | collective-permute-start | bytes 983048 | tf_op jit(solution)/shard_map/ppermute | solution.py:26
  133.1 33.1 %collective-permute-start.25 = (bf16[80,2048]{1,0:T(8,128)(2,1)S(1)}, bf16[80,2048]{1,0:T(8,128)(2,1)S(1)}, u32[]{:S(2)}, u32[]{:S(2)}) collective-permute-start(bf16[80,2048]{1,0:T(8,128)(2,1)S(1)} %get-tuple-element.70), channel_id=1, source_target_pairs={{0,4},{1,5},{2,6},{3,7},{4,0},{5,1},{6,2},{7,3},{8,12},{9,13},{10,... | collective-permute-start | bytes 983048 | tf_op jit(solution)/shard_map/ppermute | solution.py:26
  143.1 23.0 %collective-permute-start.26 = (bf16[80,2048]{1,0:T(8,128)(2,1)S(1)}, bf16[80,2048]{1,0:T(8,128)(2,1)S(1)}, u32[]{:S(2)}, u32[]{:S(2)}) collective-permute-start(bf16[80,2048]{1,0:T(8,128)(2,1)S(1)} %get-tuple-element.71), channel_id=1, source_target_pairs={{0,6},{1,7},{2,4},{3,5},{4,2},{5,3},{6,0},{7,1},{8,14},{9,15},{10,... | collective-permute-start | bytes 983048 | tf_op jit(solution)/shard_map/ppermute | solution.py:26
  152.6 13.6 %copy-start.8 = (bf16[1,2048,704]{1,2,0:T(8,128)(2,1)S(1)}, bf16[1,2048,704]{1,2,0:T(8,128)(2,1)}, u32[]{:S(2)}) copy-start(bf16[1,2048,704]{1,2,0:T(8,128)(2,1)} %param.21) | copy-start | bytes 8650756
  152.6 13.6 %copy-start.10 = (bf16[1,2048,704]{1,2,0:T(8,128)(2,1)S(1)}, bf16[1,2048,704]{1,2,0:T(8,128)(2,1)}, u32[]{:S(2)}) copy-start(bf16[1,2048,704]{1,2,0:T(8,128)(2,1)} %param.22) | copy-start | bytes 8650756
  152.6 13.6 %copy-start.12 = (bf16[1,704,2048]{2,1,0:T(8,128)(2,1)S(1)}, bf16[1,704,2048]{2,1,0:T(8,128)(2,1)}, u32[]{:S(2)}) copy-start(bf16[1,704,2048]{2,1,0:T(8,128)(2,1)} %param.23) | copy-start | bytes 8650756
  162.6 15.7 %collective-permute-start.35 = (bf16[80,2048]{1,0:T(8,128)(2,1)S(1)}, bf16[80,2048]{1,0:T(8,128)(2,1)S(1)}, u32[]{:S(2)}, u32[]{:S(2)}) collective-permute-start(bf16[80,2048]{1,0:T(8,128)(2,1)S(1)} %get-tuple-element.87), channel_id=1, source_target_pairs={{0,2},{1,3},{2,0},{3,1},{4,6},{5,7},{6,4},{7,5},{8,10},{9,11},{10,... | collective-permute-start | bytes 983048 | tf_op jit(solution)/shard_map/ppermute | solution.py:26
  163.3 16.5 %collective-permute-start.36 = (bf16[80,2048]{1,0:T(8,128)(2,1)S(1)}, bf16[80,2048]{1,0:T(8,128)(2,1)S(1)}, u32[]{:S(2)}, u32[]{:S(2)}) collective-permute-start(bf16[80,2048]{1,0:T(8,128)(2,1)S(1)} %get-tuple-element.88), channel_id=1, source_target_pairs={{0,4},{1,5},{2,6},{3,7},{4,0},{5,1},{6,2},{7,3},{8,12},{9,13},{10,... | collective-permute-start | bytes 983048 | tf_op jit(solution)/shard_map/ppermute | solution.py:26
  164.6 15.2 %collective-permute-start.37 = (bf16[80,2048]{1,0:T(8,128)(2,1)S(1)}, bf16[80,2048]{1,0:T(8,128)(2,1)S(1)}, u32[]{:S(2)}, u32[]{:S(2)}) collective-permute-start(bf16[80,2048]{1,0:T(8,128)(2,1)S(1)} %get-tuple-element.89), channel_id=1, source_target_pairs={{0,6},{1,7},{2,4},{3,5},{4,2},{5,3},{6,0},{7,1},{8,14},{9,15},{10,... | collective-permute-start | bytes 983048 | tf_op jit(solution)/shard_map/ppermute | solution.py:26
  176.2 6.6 %copy-start.14 = (bf16[80,2048]{1,0:T(8,128)(2,1)}, bf16[80,2048]{1,0:T(8,128)(2,1)S(1)}, u32[]{:S(2)}) copy-start(bf16[80,2048]{1,0:T(8,128)(2,1)S(1)} %get-tuple-element.75.refs_0_) | copy-start | bytes 983044
  176.2 9.6 %collective-permute-start.27 = (bf16[80,2048]{1,0:T(8,128)(2,1)S(1)}, bf16[80,2048]{1,0:T(8,128)(2,1)S(1)}, u32[]{:S(2)}, u32[]{:S(2)}) collective-permute-start(bf16[80,2048]{1,0:T(8,128)(2,1)S(1)} %get-tuple-element.76), channel_id=1, source_target_pairs={{0,2},{1,3},{2,0},{3,1},{4,6},{5,7},{6,4},{7,5},{8,10},{9,11},{10,... | collective-permute-start | bytes 983048 | tf_op jit(solution)/shard_map/ppermute | solution.py:26
  177.0 8.9 %collective-permute-start.28 = (bf16[80,2048]{1,0:T(8,128)(2,1)S(1)}, bf16[80,2048]{1,0:T(8,128)(2,1)S(1)}, u32[]{:S(2)}, u32[]{:S(2)}) collective-permute-start(bf16[80,2048]{1,0:T(8,128)(2,1)S(1)} %get-tuple-element.77), channel_id=1, source_target_pairs={{0,4},{1,5},{2,6},{3,7},{4,0},{5,1},{6,2},{7,3},{8,12},{9,13},{10,... | collective-permute-start | bytes 983048 | tf_op jit(solution)/shard_map/ppermute | solution.py:26
  178.3 11.1 %collective-permute-start.29 = (bf16[80,2048]{1,0:T(8,128)(2,1)S(1)}, bf16[80,2048]{1,0:T(8,128)(2,1)S(1)}, u32[]{:S(2)}, u32[]{:S(2)}) collective-permute-start(bf16[80,2048]{1,0:T(8,128)(2,1)S(1)} %get-tuple-element.78), channel_id=1, source_target_pairs={{0,6},{1,7},{2,4},{3,5},{4,2},{5,3},{6,0},{7,1},{8,14},{9,15},{10,... | collective-permute-start | bytes 983048 | tf_op jit(solution)/shard_map/ppermute | solution.py:26
  182.8 10.6 %collective-permute-start.38 = (bf16[80,2048]{1,0:T(8,128)(2,1)S(1)}, bf16[80,2048]{1,0:T(8,128)(2,1)}, u32[]{:S(2)}, u32[]{:S(2)}) collective-permute-start(bf16[80,2048]{1,0:T(8,128)(2,1)S(1)} %get-tuple-element.90), channel_id=1, source_target_pairs={{0,24},{1,25},{2,26},{3,27},{4,28},{5,29},{6,30},{7,31},{8,0},{9,1... | collective-permute-start | bytes 983048 | tf_op jit(solution)/shard_map/ppermute | solution.py:26
  193.4 9.1 %collective-permute-start.40 = (bf16[80,2048]{1,0:T(8,128)(2,1)S(1)}, bf16[80,2048]{1,0:T(8,128)(2,1)S(1)}, u32[]{:S(2)}, u32[]{:S(2)}) collective-permute-start(bf16[80,2048]{1,0:T(8,128)(2,1)S(1)} %get-tuple-element.92), channel_id=1, source_target_pairs={{0,8},{1,9},{2,10},{3,11},{4,12},{5,13},{6,14},{7,15},{8,16},{9,17... | collective-permute-start | bytes 983048 | tf_op jit(solution)/shard_map/ppermute | solution.py:26
  194.5 11.3 %collective-permute-start.39 = (bf16[80,2048]{1,0:T(8,128)(2,1)S(1)}, bf16[80,2048]{1,0:T(8,128)(2,1)S(1)}, u32[]{:S(2)}, u32[]{:S(2)}) collective-permute-start(bf16[80,2048]{1,0:T(8,128)(2,1)S(1)} %add_convert_fusion.1), channel_id=1, source_target_pairs={{0,24},{1,25},{2,26},{3,27},{4,28},{5,29},{6,30},{7,31},{8,0},{9,1... | collective-permute-start | bytes 983048 | tf_op jit(solution)/shard_map/ppermute | solution.py:26
  (11 other events, 14.6 us)

commit v3 on v2

--- a/solution.py
+++ b/solution.py
@@ -9,7 +9,7 @@
 from jax.sharding import PartitionSpec as P
 
 AXES = ("ctx", "exp")
-PARAMS = pltpu.CompilerParams(vmem_limit_bytes=24 * 1024 * 1024)
+PARAMS = pltpu.CompilerParams(vmem_limit_bytes=20 * 1024 * 1024)
 VMEM = pl.BlockSpec(memory_space=pltpu.VMEM)
 SMEM = pl.BlockSpec(memory_space=pltpu.SMEM)
 PAD_ROWS = 16
@@ -47,20 +47,6 @@
     for turn in range(depth - 1, depth // 2, -1):
         column[turn] = turn_z(column[(turn + 1) % depth], -1)
     return column
-
-
-def scatter_z(sums):
-    depth = len(sums)
-
-    def added(left, right):
-        return (left.astype(jnp.float32) + right.astype(jnp.float32)).astype(left.dtype)
-
-    below, above = None, None
-    for turn in range(depth // 2, 0, -1):
-        below = turn_z(sums[turn] if below is None else added(below, sums[turn]), -1)
-    for turn in range(depth // 2 + 1, depth):
-        above = turn_z(sums[turn] if above is None else added(above, sums[turn]), 1)
-    return [part for part in (below, above) if part is not None]
 
 
 def head_out(block, turn):
@@ -104,6 +90,36 @@
             transcendentals=0,
         ),
     )(*operands)
+
+
+def after(value, *others):
+    return lax.optimization_barrier((value, *others))[0]
+
+
+def load_kernel(count, *refs):
+    sources, targets, sems = refs[:count], refs[count : 2 * count], refs[2 * count]
+    copies = [
+        pltpu.make_async_copy(sources[i], targets[i], sems.at[i]) for i in range(count)
+    ]
+    for copy in copies:
+        copy.start()
+    for copy in copies:
+        copy.wait()
+
+
+def load(arrays):
+    count = len(arrays)
+    return pl.pallas_call(
+        functools.partial(load_kernel, count),
+        out_shape=[struct(*a.shape) for a in arrays],
+        in_specs=[pl.BlockSpec(memory_space=pltpu.HBM)] * count,
+        out_specs=[VMEM] * count,
+        scratch_shapes=[pltpu.SemaphoreType.DMA((count,))],
+        compiler_params=PARAMS,
+        cost_estimate=pl.CostEstimate(
+            flops=0, bytes_accessed=sum(2 * a.size * 2 for a in arrays), transcendentals=0
+        ),
+    )(*[pltpu.with_memory_space_constraint(a, pltpu.HBM) for a in arrays])
 
 
 def project_kernel(hops, depth, head_dim, place, *refs):
@@ -341,16 +357,15 @@
         [exp_index, z_index, exp_index % 2, z_index if by_head else jnp.zeros_like(z_index), expert]
     ).astype(jnp.int32)
 
-    noted = gather_z(jnp.concatenate([routes.astype(jnp.float32), gate_weights], axis=1))
+    far = move(inputs, lambda z, x, y, c: (z, x, y ^ 1, c))
+    near = swap_core(inputs)
+    near, far, w_query, w_key, w_value, w_out = lax.optimization_barrier(
+        (near, far, *load([w_query, w_key, w_value, w_out]))
+    )
+    far_near = swap_core(far)
     top_count = routes.shape[1]
-
+    noted = jnp.concatenate([routes.astype(jnp.float32), gate_weights], axis=1)
     weights = (w_gate, w_up, w_down)
-    other_weights = tuple(swap_core(weight) for weight in weights)
-
-    near = swap_core(inputs)
-    far = move(inputs, lambda z, x, y, c: (z, x, y ^ 1, c))
-    far, noted = lax.optimization_barrier((far, noted))
-    far_near = swap_core(far)
     if by_head:
         marks = jnp.sum(
             jnp.where(sel_blocks < ctx_index, jnp.left_shift(1, jnp.minimum(sel_blocks, 30)), 0), axis=2
@@ -369,7 +384,11 @@
             flops=6 * block_len * model_width * hidden_cols,
         )
         own = [head_out(sent[turn], turn) for turn in range(depth)]
+        noted = after(noted, sent[0])
+        noted = [noted] + [turn_z(noted, turn) for turn in range(1, depth)]
+        own[-1], noted = lax.optimization_barrier((own[-1], noted))
         beside = [swap_core(block) for block in own]
+        other_weights = [swap_core(after(weight, *beside)) for weight in weights]
         mixed = call(
             functools.partial(attend_kernel, depth, block_len, head_dim),
             [struct(block_len, head_dim)] * depth,
@@ -386,8 +405,8 @@
         block = jnp.stack([inputs, near, far, far_near])[exp_index ^ jnp.arange(exp_count)]
         normed = normalize(block.reshape(block_len, model_width), attn_gain)
         heads = attend_gathered(normed, w_query, w_key, w_value, sel_blocks)
-
-    heads, other_weights = lax.optimization_barrier((heads, other_weights))
+        noted = [noted] + [turn_z(noted, turn) for turn in range(1, depth)]
+        other_weights = [swap_core(weight) for weight in weights]
 
     halves = struct(exp_count // 2, tok_rows, model_width)
     kept, given = call(
@@ -402,7 +421,12 @@
     )
     given = swap_core(given)
     beyond = (kept[1].astype(jnp.float32) + given[1].astype(jnp.float32)).astype(jnp.bfloat16)
+    own_weights, other_weights = (
+        [gate[0].T, up[0].T, down[0]] for gate, up, down in (weights, other_weights)
+    )
+    expert_weights = [*load([after(weight, beyond) for weight in own_weights]), *other_weights]
     beyond = move(beyond, lambda z, x, y, c: (z, x, y ^ 1, c))
+    beyond, expert_weights = lax.optimization_barrier((beyond, expert_weights))
     residual, ffn_in = call(
         residual_kernel,
         [struct(tok_rows, model_width)] * 2,
@@ -418,13 +442,10 @@
     groups = [nearest[first : first + group_size] for first in range(0, depth, group_size)]
     notes = [jnp.concatenate([noted[turn] for turn in group], axis=0) for group in groups]
     slots = group_size * capacity
-    expert_weights = [
-        array
-        for gate, up, down in (weights, other_weights)
-        for array in (gate[0].T, up[0].T, down[0])
-    ]
     arrived = []
     for group, note in zip(groups, notes):
+        if arrived:
+            note = after(note, arrived[-1][0])
         packed = call(
             functools.partial(pack_kernel, group_size, capacity),
             [struct(slots, model_width)] * 4,
@@ -436,6 +457,8 @@
     sums = [None] * depth
     returned = []
     for rows in arrived:
+        if returned:
+            rows = [after(rows[0], returned[-1][0])] + rows[1:]
         results = call(
             functools.partial(expert_kernel, 4),
             [struct(slots, model_width)] * 4,
@@ -454,8 +477,8 @@
         for turn, part in zip(group, parts):
             sums[turn] = part
     layer_out = residual.astype(jnp.float32) + sums[0].astype(jnp.float32)
-    for part in scatter_z(sums):
-        layer_out = layer_out + part.astype(jnp.float32)
+    for turn in range(1, depth):
+        layer_out = layer_out + turn_z(sums[turn], -turn).astype(jnp.float32)
     return layer_out.astype(jnp.bfloat16)
 
 

time: 207 us -> 192 us (0.928)
  waiting for transfers between devices: 92.6 us -> 83.7 us
  local copies, waits for them, and re-layouts: 15.1 us -> 11.2 us
  other arithmetic: 4.25 us -> 1.24 us
    ppermute x41, waiting for transfers between devices: 92.6 us -> 83.7 us  [move(): return lax.ppermute(block, AXES, route)]
    pallas_call x0 -> x2, Pallas kernels: none -> 7.11 us  [load(): pl.pallas_call(functools.partial(load_kernel, count), out_shape=[struct(*...]
    pallas_call x10, Pallas kernels: 42.8 us -> 36.7 us  [call(): pl.pallas_call(kernel, out_shape=outs, in_specs=[SMEM] * smem + [VMEM] *...]
    unnamed x40, local copies, waits for them, and re-layouts: 15 us -> 11.1 us
  transfers between devices with their start and end apart: 41 -> 41, of which waited for: 22 -> 23; matrix products, arithmetic and copies ran while one was open for 2% -> 0% of each run, Pallas kernels for 19% -> 21%
where the time goes in v3:
time: 192 us
  waiting for transfers between devices  83.7 us (44%)
  starting transfers between devices  51.3 us (27%)
  Pallas kernels  43.8 us (23%)
  local copies, waits for them, and re-layouts  11.2 us (6%)
    ppermute x41, waiting for transfers between devices, move(): return lax.ppermute(block, AXES, route)  83.7 us
    ppermute x41, starting transfers between devices, move(): return lax.ppermute(block, AXES, route)  51.3 us
    pallas_call x10, Pallas kernels, call(): pl.pallas_call(kernel, out_shape=outs, in_specs=[SMEM] * smem + [VMEM] *...  36.7 us
    unnamed x40, local copies, waits for them, and re-layouts  11.1 us
    pallas_call x2, Pallas kernels, load(): pl.pallas_call(functools.partial(load_kernel, count), out_shape=[struct(*...  7.11 us
  transfers between devices with their start and end apart: 41, of which 23 were waited for; matrix products, arithmetic and copies ran while one was open for 0% of the time, Pallas kernels for 21%

profile of v3, /device:TPU:0, one launch (start us, length us, event | category | flops | bytes accessed | tf_op | source)
XLA Modules:
  0.0 191.6 jit_solution(2254886902660472652)
XLA Ops:
  0.5 2.5 %collective-permute-start.1 = (bf16[80,2048]{1,0:T(8,128)(2,1)}, bf16[80,2048]{1,0:T(8,128)(2,1)S(1)}, u32[]{:S(2)}, u32[]{:S(2)}) collective-permute-start(bf16[80,2048]{1,0:T(8,128)(2,1)} %inputs.1), channel_id=1, source_target_pairs={{0,2},{1,3},{2,0},{3,1},{4,6},{5,7},{6,4},{7,5},{8,10},{9,11},{10,... | collective-permute-start | bytes 983048 | tf_op jit(solution)/shard_map/ppermute | solution.py:26
  3.0 3.5 %shard_map.127 = (bf16[2048,512]{1,0:T(8,128)(2,1)S(1)}, bf16[2048,512]{1,0:T(8,128)(2,1)S(1)}, bf16[2048,512]{1,0:T(8,128)(2,1)S(1)}, bf16[512,2048]{1,0:T(8,128)(2,1)S(1)}) custom-call(bf16[2048,512]{1,0:T(8,128)(2,1)} %refs_0_.2, bf16[2048,512]{1,0:T(8,128)(2,1)} %refs_1_.1, bf16[2048,512]{1,0:T(8,128)(2,1)} %refs_2_.1, bf16[512,2048]{1,0:T(8,128)(2,1)} %refs_3_.1), custom_call_target="tpu_custom_call" | custom-call | bytes 16777216 | tf_op jit(solution)/shard_map/pallas_call | solution.py:112
  6.5 1.3 copy-done
  7.9 1.3 copy-done.2
  9.2 1.4 copy-done.7
  11.7 1.5 collective-permute-done.2.refs_3_
  13.2 1.6 copy-done.1
  14.8 1.6 copy-done.3
  16.4 3.6 %shard_map.128 = (bf16[336,384]{1,0:T(8,128)(2,1)S(1)}, bf16[336,384]{1,0:T(8,128)(2,1)S(1)}, bf16[336,384]{1,0:T(8,128)(2,1)S(1)}, bf16[336,384]{1,0:T(8,128)(2,1)S(1)}) custom-call(s32[5]{0:T(128)S(1)} %stack.20.place, bf16[80,2048]{1,0:T(8,128)(2,1)S(1)} %copy-done.4, bf16[80,2048]{1,0:T(8,128)(2,1)S(1)} %collective-permute-done.refs_1_, ...), custom_call_target="tpu_custom_call" | custom-call | flops 2013265920 | bytes 7659540 | tf_op jit(solution)/shard_map/pallas_call | solution.py:80
  20.0 3.9 %collective-permute-start.6 = (bf16[336,384]{1,0:T(8,128)(2,1)S(1)}, bf16[336,384]{1,0:T(8,128)(2,1)S(1)}, u32[]{:S(2)}, u32[]{:S(2)}) collective-permute-start(bf16[336,384]{1,0:T(8,128)(2,1)S(1)} %get-tuple-element.83), channel_id=1, source_target_pairs={{0,24},{1,28},{2,26},{3,30},{4,25},{5,29},{6,27},{7,31},{8,0},{9,4... | collective-permute-start | bytes 774152 | tf_op jit(solution)/shard_map/ppermute | solution.py:26
  25.7 3.4 %collective-permute-start.7 = (f32[80,12]{0,1:T(8,128)S(1)}, f32[80,12]{0,1:T(8,128)S(1)}, u32[]{:S(2)}, u32[]{:S(2)}) collective-permute-start(f32[80,12]{0,1:T(8,128)S(1)} %pad_maximum_fusion.2), channel_id=1, source_target_pairs={{0,8},{1,9},{2,10},{3,11},{4,12},{5,13},{6,14},{7,15},{8,16},{9,17... | collective-permute-start | bytes 11528 | tf_op jit(solution)/shard_map/ppermute | solution.py:26
  29.1 12.5 %collective-permute-done.7 = f32[80,12]{0,1:T(8,128)S(1)} collective-permute-done((f32[80,12]{0,1:T(8,128)S(1)}, f32[80,12]{0,1:T(8,128)S(1)}, u32[]{:S(2)}, u32[]{:S(2)}) %collective-permute-start.7) | collective-permute-done | bytes 3872 | tf_op jit(solution)/shard_map/ppermute | solution.py:26
  41.6 7.4 %collective-permute-start.8 = (f32[80,12]{0,1:T(8,128)S(1)}, f32[80,12]{0,1:T(8,128)S(1)}, u32[]{:S(2)}, u32[]{:S(2)}) collective-permute-start(f32[80,12]{0,1:T(8,128)S(1)} %pad_maximum_fusion.2), channel_id=1, source_target_pairs={{0,16},{1,17},{2,18},{3,19},{4,20},{5,21},{6,22},{7,23},{8,24},{9,... | collective-permute-start | bytes 11528 | tf_op jit(solution)/shard_map/ppermute | solution.py:26
  49.0 1.7 collective-permute-done.8
  51.1 3.3 %collective-permute-done.9 = f32[80,12]{0,1:T(8,128)S(1)} collective-permute-done((f32[80,12]{0,1:T(8,128)S(1)}, f32[80,12]{0,1:T(8,128)S(1)}, u32[]{:S(2)}, u32[]{:S(2)}) %collective-permute-start.9) | collective-permute-done | bytes 3872 | tf_op jit(solution)/shard_map/ppermute | solution.py:26
  57.7 7.9 %shard_map.129 = (bf16[320,128]{1,0:T(8,128)(2,1)S(1)}, bf16[320,128]{1,0:T(8,128)(2,1)S(1)}, bf16[320,128]{1,0:T(8,128)(2,1)S(1)}, bf16[320,128]{1,0:T(8,128)(2,1)S(1)}) custom-call(s32[5]{0:T(128)S(1)} %stack.20.place, bf16[336,384]{1,0:T(8,128)(2,1)S(1)} %collective-permute-done.3.refs_0_, bf16[336,384]{1,0:T(8,128)(2,1)S(1)} %collective-permute-done.4.refs_1_, ...), custom_call_target="tpu_custom_call" | custom-call | flops 1677721600 | bytes 2064404 | tf_op jit(solution)/shard_map/pallas_call | solution.py:80
  66.2 2.3 %collective-permute-start.15 = (bf16[320,128]{1,0:T(8,128)(2,1)S(1)}, bf16[320,128]{1,0:T(8,128)(2,1)S(1)}, u32[]{:S(2)}, u32[]{:S(2)}) collective-permute-start(bf16[320,128]{1,0:T(8,128)(2,1)S(1)} %get-tuple-element.87), channel_id=1, source_target_pairs={{0,24},{1,28},{2,26},{3,30},{4,25},{5,29},{6,27},{7,31},{8,0},{9,4... | collective-permute-start | bytes 245768 | tf_op jit(solution)/shard_map/ppermute | solution.py:26
  69.2 1.5 collective-permute-done.15.refs_1_
  70.7 1.4 collective-permute-start.17
  72.1 3.3 %collective-permute-done.16.refs_2_ = bf16[320,128]{1,0:T(8,128)(2,1)S(1)} collective-permute-done((bf16[320,128]{1,0:T(8,128)(2,1)S(1)}, bf16[320,128]{1,0:T(8,128)(2,1)S(1)}, u32[]{:S(2)}, u32[]{:S(2)}) %collective-permute-start.16) | collective-permute-done | bytes 81952 | tf_op jit(solution)/shard_map/ppermute | solution.py:26
  75.4 2.2 %collective-permute-done.17.refs_3_ = bf16[320,128]{1,0:T(8,128)(2,1)S(1)} collective-permute-done((bf16[320,128]{1,0:T(8,128)(2,1)S(1)}, bf16[320,128]{1,0:T(8,128)(2,1)S(1)}, u32[]{:S(2)}, u32[]{:S(2)}) %collective-permute-start.17) | collective-permute-done | bytes 81952 | tf_op jit(solution)/shard_map/ppermute | solution.py:26
  77.6 1.5 shard_map.130
  79.1 4.1 %collective-permute-start.18 = (bf16[2,80,2048]{2,1,0:T(8,128)(2,1)S(1)}, bf16[2,80,2048]{2,1,0:T(8,128)(2,1)S(1)}, u32[]{:S(2)}, u32[]{:S(2)}) collective-permute-start(bf16[2,80,2048]{2,1,0:T(8,128)(2,1)S(1)} %get-tuple-element.92), channel_id=1, source_target_pairs={{0,1},{1,0},{2,3},{3,2},{4,5},{5,4},{6,7},{7,6},{8,9},{9,8},{10,11... | collective-permute-start | bytes 1966088 | tf_op jit(solution)/shard_map/ppermute | solution.py:26
  83.2 1.7 collective-permute-done.18.given
  85.0 1.6 collective-permute-start.19
  86.6 3.6 %shard_map.131 = (bf16[704,2048]{1,0:T(8,128)(2,1)S(1)}, bf16[704,2048]{1,0:T(8,128)(2,1)S(1)}, bf16[704,2048]{1,0:T(8,128)(2,1)S(1)}) custom-call(bf16[704,2048]{1,0:T(8,128)(2,1)} %bitcast.39, bf16[704,2048]{1,0:T(8,128)(2,1)} %bitcast.38, bf16[704,2048]{1,0:T(8,128)(2,1)} %bitcast.37), custom_call_target="tpu_custom_call" | custom-call | bytes 17301504 | tf_op jit(solution)/shard_map/pallas_call | solution.py:112
  90.2 4.9 %collective-permute-done.19.far = bf16[80,2048]{1,0:T(8,128)(2,1)S(1)} collective-permute-done((bf16[80,2048]{1,0:T(8,128)(2,1)S(1)}, bf16[80,2048]{1,0:T(8,128)(2,1)S(1)}, u32[]{:S(2)}, u32[]{:S(2)}) %collective-permute-start.19) | collective-permute-done | bytes 327712 | tf_op jit(solution)/shard_map/ppermute | solution.py:26
  95.6 3.8 %collective-permute-start.31 = (bf16[80,2048]{1,0:T(8,128)(2,1)S(1)}, bf16[80,2048]{1,0:T(8,128)(2,1)S(1)}, u32[]{:S(2)}, u32[]{:S(2)}) collective-permute-start(bf16[80,2048]{1,0:T(8,128)(2,1)S(1)} %get-tuple-element.106.refs_0_), channel_id=1, source_target_pairs={{0,24},{1,25},{2,26},{3,27},{4,28},{5,29},{6,30},{7,31},{8,0},{9,1... | collective-permute-start | bytes 983048 | tf_op jit(solution)/shard_map/ppermute | solution.py:26
  99.4 8.5 %collective-permute-done.23.refs_1_ = bf16[80,2048]{1,0:T(8,128)(2,1)S(1)} collective-permute-done((bf16[80,2048]{1,0:T(8,128)(2,1)S(1)}, bf16[80,2048]{1,0:T(8,128)(2,1)S(1)}, u32[]{:S(2)}, u32[]{:S(2)}) %collective-permute-start.23) | collective-permute-done | bytes 327712 | tf_op jit(solution)/shard_map/ppermute | solution.py:26
  108.0 1.6 shard_map.133
  109.6 1.6 collective-permute-start.24
  113.2 8.8 %collective-permute-done.32.refs_1_ = bf16[80,2048]{1,0:T(8,128)(2,1)S(1)} collective-permute-done((bf16[80,2048]{1,0:T(8,128)(2,1)S(1)}, bf16[80,2048]{1,0:T(8,128)(2,1)S(1)}, u32[]{:S(2)}, u32[]{:S(2)}) %collective-permute-start.32) | collective-permute-done | bytes 327712 | tf_op jit(solution)/shard_map/ppermute | solution.py:26
  122.0 1.6 shard_map.136
  123.6 1.6 collective-permute-start.33
  127.2 6.3 %shard_map.134 = (bf16[80,2048]{1,0:T(8,128)(2,1)S(1)}, bf16[80,2048]{1,0:T(8,128)(2,1)S(1)}, bf16[80,2048]{1,0:T(8,128)(2,1)S(1)}, bf16[80,2048]{1,0:T(8,128)(2,1)S(1)}) custom-call(bf16[80,2048]{1,0:T(8,128)(2,1)S(1)} %get-tuple-element.107.refs_0_, bf16[80,2048]{1,0:T(8,128)(2,1)S(1)} %collective-permute-done.24.refs_1_, ...), custom_call_target="tpu_custom_call" | custom-call | flops 5536481280 | bytes 18612224 | tf_op jit(solution)/shard_map/pallas_call | solution.py:80
  134.3 1.5 collective-permute-start.27
  136.7 2.4 %collective-permute-done.33.refs_1_ = bf16[80,2048]{1,0:T(8,128)(2,1)S(1)} collective-permute-done((bf16[80,2048]{1,0:T(8,128)(2,1)S(1)}, bf16[80,2048]{1,0:T(8,128)(2,1)S(1)}, u32[]{:S(2)}, u32[]{:S(2)}) %collective-permute-start.33) | collective-permute-done | bytes 327712 | tf_op jit(solution)/shard_map/ppermute | solution.py:26
  139.1 1.4 collective-permute-start.29
  140.5 2.4 %collective-permute-done.35.refs_3_ = bf16[80,2048]{1,0:T(8,128)(2,1)S(1)} collective-permute-done((bf16[80,2048]{1,0:T(8,128)(2,1)S(1)}, bf16[80,2048]{1,0:T(8,128)(2,1)S(1)}, u32[]{:S(2)}, u32[]{:S(2)}) %collective-permute-start.35) | collective-permute-done | bytes 327712 | tf_op jit(solution)/shard_map/ppermute | solution.py:26
  142.9 7.0 %shard_map.137 = (bf16[80,2048]{1,0:T(8,128)(2,1)S(1)}, bf16[80,2048]{1,0:T(8,128)(2,1)}, bf16[80,2048]{1,0:T(8,128)(2,1)S(1)}, bf16[80,2048]{1,0:T(8,128)(2,1)S(1)}) custom-call(bf16[80,2048]{1,0:T(8,128)(2,1)S(1)} %get-tuple-element.127.refs_0_, bf16[80,2048]{1,0:T(8,128)(2,1)S(1)} %collective-permute-done.33.refs_1_, ...), custom_call_target="tpu_custom_call" | custom-call | flops 5536481280 | bytes 18612224 | tf_op jit(solution)/shard_map/pallas_call | solution.py:80
  150.6 1.5 collective-permute-start.36
  153.1 1.4 collective-permute-start.38
  155.0 2.0 %collective-permute-done.29.refs_3_ = bf16[80,2048]{1,0:T(8,128)(2,1)S(1)} collective-permute-done((bf16[80,2048]{1,0:T(8,128)(2,1)S(1)}, bf16[80,2048]{1,0:T(8,128)(2,1)S(1)}, u32[]{:S(2)}, u32[]{:S(2)}) %collective-permute-start.29) | collective-permute-done | bytes 327712 | tf_op jit(solution)/shard_map/ppermute | solution.py:26
  158.0 3.3 %shard_map.135 = (bf16[80,2048]{1,0:T(8,128)(2,1)S(1)}, bf16[80,2048]{1,0:T(8,128)(2,1)S(1)}) custom-call(s32[5]{0:T(128)S(1)} %stack.20.place, f32[160,6]{1,0:T(8,128)S(1)} %copy.23.routes, f32[160,6]{1,0:T(8,128)S(1)} %copy.24.gates, bf16[80,2048]{1,0:T(8,128)(2,1)S(1)} %copy-done.10, bf16[80,2048]{1,0:T(8,128)(2,1)S(1)} %collective-permute-done.27.refs_1_, ...), custom_call_target="tpu_custom_call" | custom-call | flops 419430400 | bytes 1318420 | tf_op jit(solution)/shard_map/pallas_call | solution.py:80
  161.3 2.0 %collective-permute-done.36.refs_1_ = bf16[80,2048]{1,0:T(8,128)(2,1)S(1)} collective-permute-done((bf16[80,2048]{1,0:T(8,128)(2,1)}, bf16[80,2048]{1,0:T(8,128)(2,1)S(1)}, u32[]{:S(2)}, u32[]{:S(2)}) %collective-permute-start.36) | collective-permute-done | bytes 327712 | tf_op jit(solution)/shard_map/ppermute | solution.py:26
  163.6 3.5 %collective-permute-done.38.refs_3_ = bf16[80,2048]{1,0:T(8,128)(2,1)} collective-permute-done((bf16[80,2048]{1,0:T(8,128)(2,1)S(1)}, bf16[80,2048]{1,0:T(8,128)(2,1)}, u32[]{:S(2)}, u32[]{:S(2)}) %collective-permute-start.38) | collective-permute-done | bytes 327712 | tf_op jit(solution)/shard_map/ppermute | solution.py:26
  168.0 3.6 %shard_map.138 = (bf16[80,2048]{1,0:T(8,128)(2,1)S(1)}, bf16[80,2048]{1,0:T(8,128)(2,1)S(1)}) custom-call(s32[5]{0:T(128)S(1)} %stack.20.place, f32[160,6]{1,0:T(8,128)S(1)} %copy.25.routes, f32[160,6]{1,0:T(8,128)S(1)} %copy.26.gates, bf16[80,2048]{1,0:T(8,128)(2,1)S(1)} %copy-done.12, bf16[80,2048]{1,0:T(8,128)(2,1)S(1)} %collective-permute-done.36.refs_1_, ...), custom_call_target="tpu_custom_call" | custom-call | flops 419430400 | bytes 1318420 | tf_op jit(solution)/shard_map/pallas_call | solution.py:80
  171.9 18.7 %collective-permute-done.39 = bf16[80,2048]{1,0:T(8,128)(2,1)S(1)} collective-permute-done((bf16[80,2048]{1,0:T(8,128)(2,1)S(1)}, bf16[80,2048]{1,0:T(8,128)(2,1)S(1)}, u32[]{:S(2)}, u32[]{:S(2)}) %collective-permute-start.39) | collective-permute-done | bytes 327712 | tf_op jit(solution)/shard_map/ppermute | solution.py:26
  (98 shorter events, 20.4 us)
Async XLA Ops:
  0.0 10.6 %collective-permute-start = (bf16[80,2048]{1,0:T(8,128)(2,1)}, bf16[80,2048]{1,0:T(8,128)(2,1)S(1)}, u32[]{:S(2)}, u32[]{:S(2)}) collective-permute-start(bf16[80,2048]{1,0:T(8,128)(2,1)} %inputs.1), channel_id=1, source_target_pairs={{0,1},{1,0},{2,3},{3,2},{4,5},{5,4},{6,7},{7,6},{8,9},{9,8},{10,11... | collective-permute-start | bytes 983048 | tf_op jit(solution)/shard_map/ppermute | solution.py:26
  0.5 11.1 %collective-permute-start.1 = (bf16[80,2048]{1,0:T(8,128)(2,1)}, bf16[80,2048]{1,0:T(8,128)(2,1)S(1)}, u32[]{:S(2)}, u32[]{:S(2)}) collective-permute-start(bf16[80,2048]{1,0:T(8,128)(2,1)} %inputs.1), channel_id=1, source_target_pairs={{0,2},{1,3},{2,0},{3,1},{4,6},{5,7},{6,4},{7,5},{8,10},{9,11},{10,... | collective-permute-start | bytes 983048 | tf_op jit(solution)/shard_map/ppermute | solution.py:26
  3.0 10.2 %copy-start.4 = (bf16[80,2048]{1,0:T(8,128)(2,1)S(1)}, bf16[80,2048]{1,0:T(8,128)(2,1)}, u32[]{:S(2)}) copy-start(bf16[80,2048]{1,0:T(8,128)(2,1)} %inputs.1) | copy-start | bytes 983044
  3.0 10.2 %copy-start.5 = (f32[2048]{0:T(1024)S(1)}, f32[2048]{0:T(1024)}, u32[]{:S(2)}) copy-start(f32[2048]{0:T(1024)} %param.14) | copy-start | bytes 24580
  11.6 1.6 collective-permute-start.2
  16.4 9.2 %copy-start.16 = (s32[80,6]{0,1:T(8,128)S(1)}, s32[80,6]{0,1:T(8,128)}, u32[]{:S(2)}) copy-start(s32[80,6]{0,1:T(8,128)} %param.24) | copy-start | bytes 5764
  16.4 9.2 %copy-start.17 = (f32[80,6]{0,1:T(8,128)S(1)}, f32[80,6]{0,1:T(8,128)}, u32[]{:S(2)}) copy-start(f32[80,6]{0,1:T(8,128)} %param.25) | copy-start | bytes 5764
  16.4 40.6 %copy-start.13 = (bf16[1,704,2048]{2,1,0:T(8,128)(2,1)S(1)}, bf16[1,704,2048]{2,1,0:T(8,128)(2,1)}, u32[]{:S(2)}) copy-start(bf16[1,704,2048]{2,1,0:T(8,128)(2,1)} %param.23) | copy-start | bytes 8650756
  16.4 40.7 %copy-start.14 = (bf16[1,2048,704]{1,2,0:T(8,128)(2,1)S(1)}, bf16[1,2048,704]{1,2,0:T(8,128)(2,1)}, u32[]{:S(2)}) copy-start(bf16[1,2048,704]{1,2,0:T(8,128)(2,1)} %param.22) | copy-start | bytes 8650756
  20.0 34.3 %collective-permute-start.6 = (bf16[336,384]{1,0:T(8,128)(2,1)S(1)}, bf16[336,384]{1,0:T(8,128)(2,1)S(1)}, u32[]{:S(2)}, u32[]{:S(2)}) collective-permute-start(bf16[336,384]{1,0:T(8,128)(2,1)S(1)} %get-tuple-element.83), channel_id=1, source_target_pairs={{0,24},{1,28},{2,26},{3,30},{4,25},{5,29},{6,27},{7,31},{8,0},{9,4... | collective-permute-start | bytes 774152 | tf_op jit(solution)/shard_map/ppermute | solution.py:26
  23.9 30.5 %collective-permute-start.3 = (bf16[336,384]{1,0:T(8,128)(2,1)S(1)}, bf16[336,384]{1,0:T(8,128)(2,1)S(1)}, u32[]{:S(2)}, u32[]{:S(2)}) collective-permute-start(bf16[336,384]{1,0:T(8,128)(2,1)S(1)} %get-tuple-element.80), channel_id=1, source_target_pairs={{0,0},{1,4},{2,2},{3,6},{4,1},{5,5},{6,3},{7,7},{8,8},{9,12},{10,1... | collective-permute-start | bytes 774152 | tf_op jit(solution)/shard_map/ppermute | solution.py:26
  24.6 30.3 %collective-permute-start.4 = (bf16[336,384]{1,0:T(8,128)(2,1)S(1)}, bf16[336,384]{1,0:T(8,128)(2,1)S(1)}, u32[]{:S(2)}, u32[]{:S(2)}) collective-permute-start(bf16[336,384]{1,0:T(8,128)(2,1)S(1)} %get-tuple-element.81), channel_id=1, source_target_pairs={{0,8},{1,12},{2,10},{3,14},{4,9},{5,13},{6,11},{7,15},{8,16},{9,20... | collective-permute-start | bytes 774152 | tf_op jit(solution)/shard_map/ppermute | solution.py:26
  24.6 30.3 %collective-permute-start.5 = (bf16[336,384]{1,0:T(8,128)(2,1)S(1)}, bf16[336,384]{1,0:T(8,128)(2,1)S(1)}, u32[]{:S(2)}, u32[]{:S(2)}) collective-permute-start(bf16[336,384]{1,0:T(8,128)(2,1)S(1)} %get-tuple-element.82), channel_id=1, source_target_pairs={{0,16},{1,20},{2,18},{3,22},{4,17},{5,21},{6,19},{7,23},{8,24},{9,... | collective-permute-start | bytes 774152 | tf_op jit(solution)/shard_map/ppermute | solution.py:26
  25.7 51.9 %copy-start.8 = (bf16[512,2048]{1,0:T(8,128)(2,1)S(1)}, bf16[512,2048]{1,0:T(8,128)(2,1)}, u32[]{:S(2)}) copy-start(bf16[512,2048]{1,0:T(8,128)(2,1)} %copy-done.7) | copy-start | bytes 6291460
  25.7 15.9 %collective-permute-start.7 = (f32[80,12]{0,1:T(8,128)S(1)}, f32[80,12]{0,1:T(8,128)S(1)}, u32[]{:S(2)}, u32[]{:S(2)}) collective-permute-start(f32[80,12]{0,1:T(8,128)S(1)} %pad_maximum_fusion.2), channel_id=1, source_target_pairs={{0,8},{1,9},{2,10},{3,11},{4,12},{5,13},{6,14},{7,15},{8,16},{9,17... | collective-permute-start | bytes 11528 | tf_op jit(solution)/shard_map/ppermute | solution.py:26
  41.6 9.1 %collective-permute-start.8 = (f32[80,12]{0,1:T(8,128)S(1)}, f32[80,12]{0,1:T(8,128)S(1)}, u32[]{:S(2)}, u32[]{:S(2)}) collective-permute-start(f32[80,12]{0,1:T(8,128)S(1)} %pad_maximum_fusion.2), channel_id=1, source_target_pairs={{0,16},{1,17},{2,18},{3,19},{4,20},{5,21},{6,22},{7,23},{8,24},{9,... | collective-permute-start | bytes 11528 | tf_op jit(solution)/shard_map/ppermute | solution.py:26
  50.7 3.7 %collective-permute-start.9 = (f32[80,12]{0,1:T(8,128)S(1)}, f32[80,12]{0,1:T(8,128)S(1)}, u32[]{:S(2)}, u32[]{:S(2)}) collective-permute-start(f32[80,12]{0,1:T(8,128)S(1)} %pad_maximum_fusion.2), channel_id=1, source_target_pairs={{0,24},{1,25},{2,26},{3,27},{4,28},{5,29},{6,30},{7,31},{8,0},{9,1... | collective-permute-start | bytes 11528 | tf_op jit(solution)/shard_map/ppermute | solution.py:26
  54.4 1.5 collective-permute-start.13
  54.4 1.9 collective-permute-start.10
  54.9 1.8 collective-permute-start.11
  54.9 2.0 %collective-permute-start.12 = (bf16[336,384]{1,0:T(8,128)(2,1)S(1)}, bf16[336,384]{1,0:T(8,128)(2,1)S(1)}, u32[]{:S(2)}, u32[]{:S(2)}) collective-permute-start(bf16[336,384]{1,0:T(8,128)(2,1)S(1)} %collective-permute-done.5.refs_2_), channel_id=1, source_target_pairs={{0,1},{1,0},{2,3},{3,2},{4,5},{5,4},{6,7},{7,6},{8,9},{9,8},{10,11... | collective-permute-start | bytes 774152 | tf_op jit(solution)/shard_map/ppermute | solution.py:26
  57.0 38.1 %collective-permute-start.22 = (bf16[1,704,2048]{2,1,0:T(8,128)(2,1)S(1)}, bf16[1,704,2048]{2,1,0:T(8,128)(2,1)S(1)}, u32[]{:S(2)}, u32[]{:S(2)}) collective-permute-start(bf16[1,704,2048]{2,1,0:T(8,128)(2,1)S(1)} %copy-done.13), channel_id=1, source_target_pairs={{0,1},{1,0},{2,3},{3,2},{4,5},{5,4},{6,7},{7,6},{8,9},{9,8},{10,11... | collective-permute-start | bytes 8650760 | tf_op jit(solution)/shard_map/ppermute | solution.py:26
  57.1 38.0 %collective-permute-start.21 = (bf16[1,2048,704]{1,2,0:T(8,128)(2,1)S(1)}, bf16[1,2048,704]{1,2,0:T(8,128)(2,1)S(1)}, u32[]{:S(2)}, u32[]{:S(2)}) collective-permute-start(bf16[1,2048,704]{1,2,0:T(8,128)(2,1)S(1)} %copy-done.14), channel_id=1, source_target_pairs={{0,1},{1,0},{2,3},{3,2},{4,5},{5,4},{6,7},{7,6},{8,9},{9,8},{10,11... | collective-permute-start | bytes 8650760 | tf_op jit(solution)/shard_map/ppermute | solution.py:26
  57.5 37.6 %collective-permute-start.20 = (bf16[1,2048,704]{1,2,0:T(8,128)(2,1)}, bf16[1,2048,704]{1,2,0:T(8,128)(2,1)S(1)}, u32[]{:S(2)}, u32[]{:S(2)}) collective-permute-start(bf16[1,2048,704]{1,2,0:T(8,128)(2,1)} %param.21), channel_id=1, source_target_pairs={{0,1},{1,0},{2,3},{3,2},{4,5},{5,4},{6,7},{7,6},{8,9},{9,8},{10,11... | collective-permute-start | bytes 8650760 | tf_op jit(solution)/shard_map/ppermute | solution.py:26
  65.6 2.9 %collective-permute-start.14 = (bf16[320,128]{1,0:T(8,128)(2,1)S(1)}, bf16[320,128]{1,0:T(8,128)(2,1)S(1)}, u32[]{:S(2)}, u32[]{:S(2)}) collective-permute-start(bf16[320,128]{1,0:T(8,128)(2,1)S(1)} %get-tuple-element.86), channel_id=1, source_target_pairs={{0,0},{1,4},{2,2},{3,6},{4,1},{5,5},{6,3},{7,7},{8,8},{9,12},{10,1... | collective-permute-start | bytes 245768 | tf_op jit(solution)/shard_map/ppermute | solution.py:26
  66.2 4.5 %collective-permute-start.15 = (bf16[320,128]{1,0:T(8,128)(2,1)S(1)}, bf16[320,128]{1,0:T(8,128)(2,1)S(1)}, u32[]{:S(2)}, u32[]{:S(2)}) collective-permute-start(bf16[320,128]{1,0:T(8,128)(2,1)S(1)} %get-tuple-element.87), channel_id=1, source_target_pairs={{0,24},{1,28},{2,26},{3,30},{4,25},{5,29},{6,27},{7,31},{8,0},{9,4... | collective-permute-start | bytes 245768 | tf_op jit(solution)/shard_map/ppermute | solution.py:26
  68.5 6.9 %collective-permute-start.16 = (bf16[320,128]{1,0:T(8,128)(2,1)S(1)}, bf16[320,128]{1,0:T(8,128)(2,1)S(1)}, u32[]{:S(2)}, u32[]{:S(2)}) collective-permute-start(bf16[320,128]{1,0:T(8,128)(2,1)S(1)} %get-tuple-element.88), channel_id=1, source_target_pairs={{0,16},{1,20},{2,18},{3,22},{4,17},{5,21},{6,19},{7,23},{8,24},{9,... | collective-permute-start | bytes 245768 | tf_op jit(solution)/shard_map/ppermute | solution.py:26
  70.7 6.9 %collective-permute-start.17 = (bf16[320,128]{1,0:T(8,128)(2,1)S(1)}, bf16[320,128]{1,0:T(8,128)(2,1)S(1)}, u32[]{:S(2)}, u32[]{:S(2)}) collective-permute-start(bf16[320,128]{1,0:T(8,128)(2,1)S(1)} %get-tuple-element.89), channel_id=1, source_target_pairs={{0,8},{1,12},{2,10},{3,14},{4,9},{5,13},{6,11},{7,15},{8,16},{9,20... | collective-permute-start | bytes 245768 | tf_op jit(solution)/shard_map/ppermute | solution.py:26
  79.1 5.9 %collective-permute-start.18 = (bf16[2,80,2048]{2,1,0:T(8,128)(2,1)S(1)}, bf16[2,80,2048]{2,1,0:T(8,128)(2,1)S(1)}, u32[]{:S(2)}, u32[]{:S(2)}) collective-permute-start(bf16[2,80,2048]{2,1,0:T(8,128)(2,1)S(1)} %get-tuple-element.92), channel_id=1, source_target_pairs={{0,1},{1,0},{2,3},{3,2},{4,5},{5,4},{6,7},{7,6},{8,9},{9,8},{10,11... | collective-permute-start | bytes 1966088 | tf_op jit(solution)/shard_map/ppermute | solution.py:26
  85.0 10.1 %collective-permute-start.19 = (bf16[80,2048]{1,0:T(8,128)(2,1)S(1)}, bf16[80,2048]{1,0:T(8,128)(2,1)S(1)}, u32[]{:S(2)}, u32[]{:S(2)}) collective-permute-start(bf16[80,2048]{1,0:T(8,128)(2,1)S(1)} %fusion), channel_id=1, source_target_pairs={{0,2},{1,3},{2,0},{3,1},{4,6},{5,7},{6,4},{7,5},{8,10},{9,11},{10,... | collective-permute-start | bytes 983048 | tf_op jit(solution)/shard_map/ppermute | solution.py:26
  95.5 12.5 %collective-permute-start.23 = (bf16[80,2048]{1,0:T(8,128)(2,1)S(1)}, bf16[80,2048]{1,0:T(8,128)(2,1)S(1)}, u32[]{:S(2)}, u32[]{:S(2)}) collective-permute-start(bf16[80,2048]{1,0:T(8,128)(2,1)S(1)} %get-tuple-element.106.refs_0_), channel_id=1, source_target_pairs={{0,8},{1,9},{2,10},{3,11},{4,12},{5,13},{6,14},{7,15},{8,16},{9,17... | collective-permute-start | bytes 983048 | tf_op jit(solution)/shard_map/ppermute | solution.py:26
  95.6 17.6 %collective-permute-start.31 = (bf16[80,2048]{1,0:T(8,128)(2,1)S(1)}, bf16[80,2048]{1,0:T(8,128)(2,1)S(1)}, u32[]{:S(2)}, u32[]{:S(2)}) collective-permute-start(bf16[80,2048]{1,0:T(8,128)(2,1)S(1)} %get-tuple-element.106.refs_0_), channel_id=1, source_target_pairs={{0,24},{1,25},{2,26},{3,27},{4,28},{5,29},{6,30},{7,31},{8,0},{9,1... | collective-permute-start | bytes 983048 | tf_op jit(solution)/shard_map/ppermute | solution.py:26
  109.6 16.6 %collective-permute-start.24 = (bf16[80,2048]{1,0:T(8,128)(2,1)S(1)}, bf16[80,2048]{1,0:T(8,128)(2,1)S(1)}, u32[]{:S(2)}, u32[]{:S(2)}) collective-permute-start(bf16[80,2048]{1,0:T(8,128)(2,1)S(1)} %get-tuple-element.108), channel_id=1, source_target_pairs={{0,2},{1,3},{2,0},{3,1},{4,6},{5,7},{6,4},{7,5},{8,10},{9,11},{10,... | collective-permute-start | bytes 983048 | tf_op jit(solution)/shard_map/ppermute | solution.py:26
  111.2 16.0 %collective-permute-start.25 = (bf16[80,2048]{1,0:T(8,128)(2,1)S(1)}, bf16[80,2048]{1,0:T(8,128)(2,1)S(1)}, u32[]{:S(2)}, u32[]{:S(2)}) collective-permute-start(bf16[80,2048]{1,0:T(8,128)(2,1)S(1)} %get-tuple-element.109), channel_id=1, source_target_pairs={{0,4},{1,5},{2,6},{3,7},{4,0},{5,1},{6,2},{7,3},{8,12},{9,13},{10,... | collective-permute-start | bytes 983048 | tf_op jit(solution)/shard_map/ppermute | solution.py:26
  112.1 15.1 %collective-permute-start.26 = (bf16[80,2048]{1,0:T(8,128)(2,1)S(1)}, bf16[80,2048]{1,0:T(8,128)(2,1)S(1)}, u32[]{:S(2)}, u32[]{:S(2)}) collective-permute-start(bf16[80,2048]{1,0:T(8,128)(2,1)S(1)} %get-tuple-element.110), channel_id=1, source_target_pairs={{0,6},{1,7},{2,4},{3,5},{4,2},{5,3},{6,0},{7,1},{8,14},{9,15},{10,... | collective-permute-start | bytes 983048 | tf_op jit(solution)/shard_map/ppermute | solution.py:26
  113.1 8.9 %collective-permute-start.32 = (bf16[80,2048]{1,0:T(8,128)(2,1)S(1)}, bf16[80,2048]{1,0:T(8,128)(2,1)S(1)}, u32[]{:S(2)}, u32[]{:S(2)}) collective-permute-start(bf16[80,2048]{1,0:T(8,128)(2,1)S(1)} %collective-permute-done.23.refs_1_), channel_id=1, source_target_pairs={{0,8},{1,9},{2,10},{3,11},{4,12},{5,13},{6,14},{7,15},{8,16},{9,17... | collective-permute-start | bytes 983048 | tf_op jit(solution)/shard_map/ppermute | solution.py:26
  123.6 15.5 %collective-permute-start.33 = (bf16[80,2048]{1,0:T(8,128)(2,1)S(1)}, bf16[80,2048]{1,0:T(8,128)(2,1)S(1)}, u32[]{:S(2)}, u32[]{:S(2)}) collective-permute-start(bf16[80,2048]{1,0:T(8,128)(2,1)S(1)} %get-tuple-element.128), channel_id=1, source_target_pairs={{0,2},{1,3},{2,0},{3,1},{4,6},{5,7},{6,4},{7,5},{8,10},{9,11},{10,... | collective-permute-start | bytes 983048 | tf_op jit(solution)/shard_map/ppermute | solution.py:26
  125.2 15.3 %collective-permute-start.34 = (bf16[80,2048]{1,0:T(8,128)(2,1)S(1)}, bf16[80,2048]{1,0:T(8,128)(2,1)S(1)}, u32[]{:S(2)}, u32[]{:S(2)}) collective-permute-start(bf16[80,2048]{1,0:T(8,128)(2,1)S(1)} %get-tuple-element.129), channel_id=1, source_target_pairs={{0,4},{1,5},{2,6},{3,7},{4,0},{5,1},{6,2},{7,3},{8,12},{9,13},{10,... | collective-permute-start | bytes 983048 | tf_op jit(solution)/shard_map/ppermute | solution.py:26
  126.1 16.8 %collective-permute-start.35 = (bf16[80,2048]{1,0:T(8,128)(2,1)S(1)}, bf16[80,2048]{1,0:T(8,128)(2,1)S(1)}, u32[]{:S(2)}, u32[]{:S(2)}) collective-permute-start(bf16[80,2048]{1,0:T(8,128)(2,1)S(1)} %get-tuple-element.130), channel_id=1, source_target_pairs={{0,6},{1,7},{2,4},{3,5},{4,2},{5,3},{6,0},{7,1},{8,14},{9,15},{10,... | collective-permute-start | bytes 983048 | tf_op jit(solution)/shard_map/ppermute | solution.py:26
  134.3 18.9 %collective-permute-start.27 = (bf16[80,2048]{1,0:T(8,128)(2,1)S(1)}, bf16[80,2048]{1,0:T(8,128)(2,1)S(1)}, u32[]{:S(2)}, u32[]{:S(2)}) collective-permute-start(bf16[80,2048]{1,0:T(8,128)(2,1)S(1)} %get-tuple-element.118), channel_id=1, source_target_pairs={{0,2},{1,3},{2,0},{3,1},{4,6},{5,7},{6,4},{7,5},{8,10},{9,11},{10,... | collective-permute-start | bytes 983048 | tf_op jit(solution)/shard_map/ppermute | solution.py:26
  135.8 19.2 %collective-permute-start.28 = (bf16[80,2048]{1,0:T(8,128)(2,1)S(1)}, bf16[80,2048]{1,0:T(8,128)(2,1)S(1)}, u32[]{:S(2)}, u32[]{:S(2)}) collective-permute-start(bf16[80,2048]{1,0:T(8,128)(2,1)S(1)} %get-tuple-element.119), channel_id=1, source_target_pairs={{0,4},{1,5},{2,6},{3,7},{4,0},{5,1},{6,2},{7,3},{8,12},{9,13},{10,... | collective-permute-start | bytes 983048 | tf_op jit(solution)/shard_map/ppermute | solution.py:26
  139.1 17.9 %collective-permute-start.29 = (bf16[80,2048]{1,0:T(8,128)(2,1)S(1)}, bf16[80,2048]{1,0:T(8,128)(2,1)S(1)}, u32[]{:S(2)}, u32[]{:S(2)}) collective-permute-start(bf16[80,2048]{1,0:T(8,128)(2,1)S(1)} %get-tuple-element.120), channel_id=1, source_target_pairs={{0,6},{1,7},{2,4},{3,5},{4,2},{5,3},{6,0},{7,1},{8,14},{9,15},{10,... | collective-permute-start | bytes 983048 | tf_op jit(solution)/shard_map/ppermute | solution.py:26
  150.6 12.7 %collective-permute-start.36 = (bf16[80,2048]{1,0:T(8,128)(2,1)}, bf16[80,2048]{1,0:T(8,128)(2,1)S(1)}, u32[]{:S(2)}, u32[]{:S(2)}) collective-permute-start(bf16[80,2048]{1,0:T(8,128)(2,1)} %get-tuple-element.132), channel_id=1, source_target_pairs={{0,2},{1,3},{2,0},{3,1},{4,6},{5,7},{6,4},{7,5},{8,10},{9,11},{10,... | collective-permute-start | bytes 983048 | tf_op jit(solution)/shard_map/ppermute | solution.py:26
  152.2 11.4 %collective-permute-start.37 = (bf16[80,2048]{1,0:T(8,128)(2,1)S(1)}, bf16[80,2048]{1,0:T(8,128)(2,1)}, u32[]{:S(2)}, u32[]{:S(2)}) collective-permute-start(bf16[80,2048]{1,0:T(8,128)(2,1)S(1)} %get-tuple-element.133), channel_id=1, source_target_pairs={{0,4},{1,5},{2,6},{3,7},{4,0},{5,1},{6,2},{7,3},{8,12},{9,13},{10,... | collective-permute-start | bytes 983048 | tf_op jit(solution)/shard_map/ppermute | solution.py:26
  153.1 13.9 %collective-permute-start.38 = (bf16[80,2048]{1,0:T(8,128)(2,1)S(1)}, bf16[80,2048]{1,0:T(8,128)(2,1)}, u32[]{:S(2)}, u32[]{:S(2)}) collective-permute-start(bf16[80,2048]{1,0:T(8,128)(2,1)S(1)} %get-tuple-element.134), channel_id=1, source_target_pairs={{0,6},{1,7},{2,4},{3,5},{4,2},{5,3},{6,0},{7,1},{8,14},{9,15},{10,... | collective-permute-start | bytes 983048 | tf_op jit(solution)/shard_map/ppermute | solution.py:26
  161.2 10.6 %collective-permute-start.30 = (bf16[80,2048]{1,0:T(8,128)(2,1)S(1)}, bf16[80,2048]{1,0:T(8,128)(2,1)S(1)}, u32[]{:S(2)}, u32[]{:S(2)}) collective-permute-start(bf16[80,2048]{1,0:T(8,128)(2,1)S(1)} %get-tuple-element.122), channel_id=1, source_target_pairs={{0,24},{1,25},{2,26},{3,27},{4,28},{5,29},{6,30},{7,31},{8,0},{9,1... | collective-permute-start | bytes 983048 | tf_op jit(solution)/shard_map/ppermute | solution.py:26
  171.6 19.0 %collective-permute-start.39 = (bf16[80,2048]{1,0:T(8,128)(2,1)S(1)}, bf16[80,2048]{1,0:T(8,128)(2,1)S(1)}, u32[]{:S(2)}, u32[]{:S(2)}) collective-permute-start(bf16[80,2048]{1,0:T(8,128)(2,1)S(1)} %get-tuple-element.135), channel_id=1, source_target_pairs={{0,16},{1,17},{2,18},{3,19},{4,20},{5,21},{6,22},{7,23},{8,24},{9,... | collective-permute-start | bytes 983048 | tf_op jit(solution)/shard_map/ppermute | solution.py:26
  171.7 18.9 %collective-permute-start.40 = (bf16[80,2048]{1,0:T(8,128)(2,1)S(1)}, bf16[80,2048]{1,0:T(8,128)(2,1)S(1)}, u32[]{:S(2)}, u32[]{:S(2)}) collective-permute-start(bf16[80,2048]{1,0:T(8,128)(2,1)S(1)} %get-tuple-element.136), channel_id=1, source_target_pairs={{0,8},{1,9},{2,10},{3,11},{4,12},{5,13},{6,14},{7,15},{8,16},{9,17... | collective-permute-start | bytes 983048 | tf_op jit(solution)/shard_map/ppermute | solution.py:26
  (11 other events, 27.7 us)

commit v4 on v3

--- a/solution.py
+++ b/solution.py
@@ -9,9 +9,10 @@
 from jax.sharding import PartitionSpec as P
 
 AXES = ("ctx", "exp")
-PARAMS = pltpu.CompilerParams(vmem_limit_bytes=20 * 1024 * 1024)
+MIB = 1024 * 1024
 VMEM = pl.BlockSpec(memory_space=pltpu.VMEM)
 SMEM = pl.BlockSpec(memory_space=pltpu.SMEM)
+HBM = pl.BlockSpec(memory_space=pltpu.HBM)
 PAD_ROWS = 16
 LANES = 128
 
@@ -73,17 +74,19 @@
     return pltpu.VMEM(shape, dtype)
 
 
-def call(kernel, outs, operands, scratch=(), flops=0, smem=1):
-    operands = operands[:smem] + [
-        pltpu.with_memory_space_constraint(a, pltpu.VMEM) for a in operands[smem:]
+def call(kernel, outs, operands, scratch=(), flops=0, smem=1, hbm=0, limit=16 * MIB):
+    last = len(operands) - hbm
+    operands = [
+        a if i < smem else pltpu.with_memory_space_constraint(a, pltpu.VMEM if i < last else pltpu.HBM)
+        for i, a in enumerate(operands)
     ]
     return pl.pallas_call(
         kernel,
         out_shape=outs,
-        in_specs=[SMEM] * smem + [VMEM] * (len(operands) - smem),
+        in_specs=[SMEM] * smem + [VMEM] * (last - smem) + [HBM] * hbm,
         out_specs=jax.tree.map(lambda _: VMEM, outs),
         scratch_shapes=list(scratch),
-        compiler_params=PARAMS,
+        compiler_params=pltpu.CompilerParams(vmem_limit_bytes=limit),
         cost_estimate=pl.CostEstimate(
             flops=flops,
             bytes_accessed=sum(a.size * a.dtype.itemsize for a in operands),
@@ -108,31 +111,32 @@
 
 
 def load(arrays):
-    count = len(arrays)
-    return pl.pallas_call(
-        functools.partial(load_kernel, count),
-        out_shape=[struct(*a.shape) for a in arrays],
-        in_specs=[pl.BlockSpec(memory_space=pltpu.HBM)] * count,
-        out_specs=[VMEM] * count,
-        scratch_shapes=[pltpu.SemaphoreType.DMA((count,))],
-        compiler_params=PARAMS,
-        cost_estimate=pl.CostEstimate(
-            flops=0, bytes_accessed=sum(2 * a.size * 2 for a in arrays), transcendentals=0
-        ),
-    )(*[pltpu.with_memory_space_constraint(a, pltpu.HBM) for a in arrays])
+    return call(
+        functools.partial(load_kernel, len(arrays)),
+        [struct(*a.shape) for a in arrays],
+        arrays,
+        [pltpu.SemaphoreType.DMA((len(arrays),))],
+        smem=0,
+        hbm=len(arrays),
+        limit=MIB,
+    )
 
 
 def project_kernel(hops, depth, head_dim, place, *refs):
-    row_refs, (gain, w_query, w_key, w_value, marks) = refs[:hops], refs[hops : hops + 5]
-    outs, (rows, mixed) = refs[hops + 5 : hops + 5 + depth], refs[hops + 5 + depth :]
+    row_refs, (gain, marks), weights = refs[:hops], refs[hops : hops + 2], refs[hops + 2 : hops + 5]
+    outs, (rows, mixed, held, sems) = refs[hops + 5 : hops + 5 + depth], refs[hops + 5 + depth :]
     exp_index, z_index = place[0], place[1]
     tok_rows = row_refs[0].shape[0]
     block_len = hops * tok_rows
+    copies = [pltpu.make_async_copy(weights[i], held.at[i], sems.at[i]) for i in range(3)]
+    for copy in copies:
+        copy.start()
     for hop, row_ref in enumerate(row_refs):
         start = pl.multiple_of((exp_index ^ hop) * tok_rows, 16)
         rows[pl.ds(start, tok_rows), :] = normalize(row_ref[...], gain[...])
-    for part, weight in enumerate((w_query, w_key, w_value)):
-        mixed[part] = f32_dot(rows[...], weight[...]).astype(jnp.bfloat16)
+    for part, copy in enumerate(copies):
+        copy.wait()
+        mixed[part] = f32_dot(rows[...], held[part]).astype(jnp.bfloat16)
     for turn in range(depth):
         head = lax.rem(z_index + turn, depth)
         columns = pl.ds(pl.multiple_of(head * head_dim, head_dim), head_dim)
@@ -145,7 +149,7 @@
     own_refs, near_refs = refs[:depth], refs[depth : 2 * depth]
     outs, (own, near, mixed) = refs[2 * depth : 3 * depth], refs[3 * depth :]
     z_index, core = place[1], place[2]
-    scaling = 1.0 / math.sqrt(head_dim)
+    scaling = math.log2(math.e) / math.sqrt(head_dim)
     for turn in range(depth):
         source = lax.rem(z_index + depth - turn, depth)
         own[source] = own_refs[turn][...]
@@ -165,18 +169,21 @@
                 value = own[c, 0:block_len, 2 * head_dim : 3 * head_dim]
             else:
                 key, value = near[c, :, 0:head_dim], near[c, :, head_dim : 2 * head_dim]
-            scores = scaling * lax.dot_general(
+            scores = lax.dot_general(
                 key, query, (((1,), (1,)), ((), ())), preferred_element_type=jnp.float32
             )
-            if mine and c == level:
+            if run_max is None:
                 scores = scores + causal
+                shift = run_max = jnp.max(scores, axis=0, keepdims=True)
             else:
                 bit = 2 * c + (core if mine else 1 - core)
                 chosen = lax.shift_right_logical(marks, jnp.broadcast_to(bit, marks.shape)) & 1
-                scores = jnp.where(chosen == 1, scores, -1e30)
-            top = jnp.max(scores, axis=0, keepdims=True)
-            new_max = top if run_max is None else jnp.maximum(run_max, top)
-            weights = jnp.exp(scores - new_max)
+                top = jnp.where(chosen == 1, jnp.max(scores, axis=0, keepdims=True), -1e30)
+                new_max = jnp.maximum(run_max, top)
+                rescale = jnp.exp2((run_max - new_max) * scaling)
+                run_max = new_max
+                shift = jnp.where(chosen == 1, new_max, 1e30)
+            weights = jnp.exp2((scores - shift) * scaling)
             added = jnp.sum(weights, axis=0, keepdims=True)
             product = lax.dot_general(
                 value,
@@ -184,12 +191,10 @@
                 (((0,), (0,)), ((), ())),
                 preferred_element_type=jnp.float32,
             )
-            if run_max is None:
+            if total is None:
                 run_sum, total = added, product
             else:
-                rescale = jnp.exp(run_max - new_max)
                 run_sum, total = run_sum * rescale + added, total * rescale + product
-            run_max = new_max
         mixed[level] = (total / run_sum).T.astype(jnp.bfloat16)
     for turn in range(depth):
         outs[turn][...] = mixed[lax.rem(z_index + depth - turn, depth)]
@@ -259,27 +264,41 @@
         (given if hop & 1 else kept)[hop >> 1] = mixed[pl.ds(start, tok_rows), :]
 
 
-def residual_kernel(inputs, kept, given, far, gain, residual, ffn_in):
+def residual_kernel(top_count, inputs, kept, given, far, gain, noted, residual, ffn_in):
     summed = kept[0].astype(jnp.float32) + given[0].astype(jnp.float32) + far[...].astype(jnp.float32)
     rounded = (inputs[...].astype(jnp.float32) + summed).astype(jnp.bfloat16)
     residual[...] = rounded
-    ffn_in[...] = normalize(rounded, gain[...])
-
-
-def pack_kernel(depth, capacity, place, routes, *refs):
-    sources, outs, (rows,) = refs[:depth], refs[depth : depth + 4], refs[depth + 4 :]
+    model_width = rounded.shape[1]
+    ffn_in[:, 0:model_width] = normalize(rounded, gain[...])
+    lane = lax.broadcasted_iota(jnp.int32, noted.shape, 1)
+    left = noted[...]
+    upper = left.astype(jnp.bfloat16).astype(jnp.float32)
+    left = left - upper
+    middle = left.astype(jnp.bfloat16).astype(jnp.float32)
+    lower = left - middle
+    parts = jnp.where(lane < 2 * top_count, upper, jnp.where(lane < 3 * top_count, middle, lower))
+    ffn_in[:, model_width:] = parts.astype(jnp.bfloat16)
+
+
+def pack_kernel(count, capacity, top_count, place, *refs):
+    sources, outs, (notes, rows) = refs[:count], refs[count : count + 4], refs[count + 4 :]
     expert = place[4]
     tok_rows = sources[0].shape[0]
-    total = depth * tok_rows
-    for turn in range(depth):
-        rows[turn * tok_rows : (turn + 1) * tok_rows, :] = sources[turn][...]
+    total = count * tok_rows
+    model_width = rows.shape[1]
+    for turn in range(count):
+        part = slice(turn * tok_rows, (turn + 1) * tok_rows)
+        rows[part, :] = sources[turn][:, 0:model_width]
+        notes[part, :] = sources[turn][:, model_width:]
+    routes = notes[...].astype(jnp.float32).T[0:8]
+    routes = jnp.where(lax.broadcasted_iota(jnp.int32, routes.shape, 0) < top_count, routes, -1.0)
     earlier = lax.broadcasted_iota(jnp.int32, (total, total), 0)
     later = lax.broadcasted_iota(jnp.int32, (total, total), 1)
     before = ((earlier < later) & (earlier // tok_rows == later // tok_rows)).astype(jnp.bfloat16)
     first_slot = lax.broadcasted_iota(jnp.int32, (1, total), 1) // tok_rows * capacity
-    slot = lax.broadcasted_iota(jnp.int32, (depth * capacity, total), 0)
+    slot = lax.broadcasted_iota(jnp.int32, (count * capacity, total), 0)
     for hop in range(4):
-        hit = jnp.where(routes[...] == (expert ^ hop).astype(jnp.float32), 1.0, 0.0)
+        hit = jnp.where(routes == (expert ^ hop).astype(jnp.float32), 1.0, 0.0)
         member = jnp.sum(hit, axis=0, keepdims=True)
         place_in = f32_dot(jnp.broadcast_to(member, (16, total)).astype(jnp.bfloat16), before)[0:1]
         target = jnp.where(member > 0.5, place_in.astype(jnp.int32) + first_slot, -1)
@@ -287,10 +306,14 @@
         outs[hop][...] = f32_dot(placing, rows[...]).astype(jnp.bfloat16)
 
 
-def expert_kernel(parts, *refs):
-    row_refs, weights, outs = refs[:parts], refs[parts : parts + 6], refs[parts + 6 :]
+def expert_kernel(parts, stride, *refs):
+    row_refs, weights = refs[:parts], refs[parts : parts + 6]
+    outs, (held,) = refs[parts + 6 : 2 * parts + 6], refs[2 * parts + 6 :]
     across = (((1,), (1,)), ((), ()))
-    rows = jnp.concatenate([row_ref[...] for row_ref in row_refs], axis=0)
+    count = row_refs[0].shape[0]
+    for part, row_ref in enumerate(row_refs):
+        held[part * stride : part * stride + count, :] = row_ref[...]
+    rows = held[...]
     result = None
     for w_gate, w_up, w_down in (weights[:3], weights[3:]):
         gate_part = lax.dot_general(rows, w_gate[...], across, preferred_element_type=jnp.float32)
@@ -298,33 +321,38 @@
         hidden = (gate_part / (1.0 + jnp.exp(-gate_part)) * up_part).astype(jnp.bfloat16)
         product = f32_dot(hidden, w_down[...])
         result = product if result is None else result + product
-    count = row_refs[0].shape[0]
     for part, out in enumerate(outs):
-        out[...] = result[part * count : (part + 1) * count].astype(jnp.bfloat16)
-
-
-def combine_kernel(depth, capacity, place, routes, gates, *refs):
-    returned, outs = refs[:4], refs[4 : 4 + depth]
+        out[...] = result[part * stride : part * stride + count].astype(jnp.bfloat16)
+
+
+def combine_kernel(count, capacity, top_count, place, notes, *refs):
+    returned, outs = refs[:4], refs[4 : 4 + count]
     expert = place[4]
-    total = routes.shape[0]
-    tok_rows = total // depth
+    total = notes.shape[0]
+    tok_rows = total // count
+    row = lax.broadcasted_iota(jnp.int32, (LANES, LANES), 0)
+    lane = lax.broadcasted_iota(jnp.int32, (LANES, LANES), 1)
+    added = (lane < top_count) & (row >= top_count) & (row < 4 * top_count) & (row % top_count == lane)
+    gates = f32_dot(notes[...], jnp.where(added, 1.0, 0.0).astype(jnp.bfloat16))
+    routes = notes[...].astype(jnp.float32)
+    routes = jnp.where(lax.broadcasted_iota(jnp.int32, routes.shape, 1) < top_count, routes, -1.0)
     later = lax.broadcasted_iota(jnp.int32, (total, total), 0)
     earlier = lax.broadcasted_iota(jnp.int32, (total, total), 1)
     before = ((earlier < later) & (earlier // tok_rows == later // tok_rows)).astype(jnp.bfloat16)
     first_slot = lax.broadcasted_iota(jnp.int32, (total, 1), 0) // tok_rows * capacity
-    slot = lax.broadcasted_iota(jnp.int32, (total, depth * capacity), 1)
+    slot = lax.broadcasted_iota(jnp.int32, (total, count * capacity), 1)
     mixed = jnp.zeros((total, returned[0].shape[1]), jnp.float32)
     for hop in range(4):
-        hit = routes[...] == (expert ^ hop).astype(jnp.float32)
+        hit = routes == (expert ^ hop).astype(jnp.float32)
         member = jnp.sum(jnp.where(hit, 1.0, 0.0), axis=1, keepdims=True)
-        factor = jnp.sum(jnp.where(hit, gates[...], 0.0), axis=1, keepdims=True)
+        factor = jnp.sum(jnp.where(hit, gates, 0.0), axis=1, keepdims=True)
         place_in = f32_dot(before, jnp.broadcast_to(member, (total, LANES)).astype(jnp.bfloat16))[:, 0:1]
         target = jnp.where(member > 0.5, place_in.astype(jnp.int32) + first_slot, -1)
         placing = jnp.where(slot == target, factor, 0.0)
         upper = placing.astype(jnp.bfloat16)
         lower = (placing - upper.astype(jnp.float32)).astype(jnp.bfloat16)
         mixed = mixed + f32_dot(upper, returned[hop][...]) + f32_dot(lower, returned[hop][...])
-    for turn in range(depth):
+    for turn in range(count):
         outs[turn][...] = mixed[turn * tok_rows : (turn + 1) * tok_rows].astype(jnp.bfloat16)
 
 
@@ -359,13 +387,11 @@
 
     far = move(inputs, lambda z, x, y, c: (z, x, y ^ 1, c))
     near = swap_core(inputs)
-    near, far, w_query, w_key, w_value, w_out = lax.optimization_barrier(
-        (near, far, *load([w_query, w_key, w_value, w_out]))
-    )
     far_near = swap_core(far)
+    weights = (w_gate, w_up, w_down)
     top_count = routes.shape[1]
-    noted = jnp.concatenate([routes.astype(jnp.float32), gate_weights], axis=1)
-    weights = (w_gate, w_up, w_down)
+    noted = jnp.concatenate([routes.astype(jnp.float32)] + [gate_weights] * 3, axis=1)
+    noted = jnp.pad(noted, ((0, 0), (0, LANES - noted.shape[1])))
     if by_head:
         marks = jnp.sum(
             jnp.where(sel_blocks < ctx_index, jnp.left_shift(1, jnp.minimum(sel_blocks, 30)), 0), axis=2
@@ -376,17 +402,17 @@
         sent = call(
             functools.partial(project_kernel, exp_count, depth, head_dim),
             [payload] * depth,
-            [place, inputs, near, far, far_near, attn_gain.reshape(1, -1), w_query, w_key, w_value, marks],
+            [place, inputs, near, far, far_near, attn_gain.reshape(1, -1), marks, w_query, w_key, w_value],
             [
                 pltpu.VMEM((block_len, model_width), jnp.bfloat16),
                 pltpu.VMEM((3, block_len, hidden_cols), jnp.bfloat16),
+                pltpu.VMEM((3, model_width, hidden_cols), jnp.bfloat16),
+                pltpu.SemaphoreType.DMA((3,)),
             ],
             flops=6 * block_len * model_width * hidden_cols,
+            hbm=3,
         )
         own = [head_out(sent[turn], turn) for turn in range(depth)]
-        noted = after(noted, sent[0])
-        noted = [noted] + [turn_z(noted, turn) for turn in range(1, depth)]
-        own[-1], noted = lax.optimization_barrier((own[-1], noted))
         beside = [swap_core(block) for block in own]
         other_weights = [swap_core(after(weight, *beside)) for weight in weights]
         mixed = call(
@@ -405,7 +431,6 @@
         block = jnp.stack([inputs, near, far, far_near])[exp_index ^ jnp.arange(exp_count)]
         normed = normalize(block.reshape(block_len, model_width), attn_gain)
         heads = attend_gathered(normed, w_query, w_key, w_value, sel_blocks)
-        noted = [noted] + [turn_z(noted, turn) for turn in range(1, depth)]
         other_weights = [swap_core(weight) for weight in weights]
 
     halves = struct(exp_count // 2, tok_rows, model_width)
@@ -428,51 +453,63 @@
     beyond = move(beyond, lambda z, x, y, c: (z, x, y ^ 1, c))
     beyond, expert_weights = lax.optimization_barrier((beyond, expert_weights))
     residual, ffn_in = call(
-        residual_kernel,
-        [struct(tok_rows, model_width)] * 2,
-        [inputs, kept, given, beyond, ffn_gain.reshape(1, -1)],
+        functools.partial(residual_kernel, top_count),
+        [struct(tok_rows, model_width), struct(tok_rows, model_width + LANES)],
+        [inputs, kept, given, beyond, ffn_gain.reshape(1, -1), noted],
         smem=0,
     )
 
     experts = ctx_count * exp_count // 2
     capacity = 2 * max(1, (tok_rows * top_count + experts - 1) // experts * 2 // 3)
     column = gather_z(ffn_in)
-    nearest = sorted(range(depth), key=lambda turn: min(turn, depth - turn))
-    group_size = depth // 2
-    groups = [nearest[first : first + group_size] for first in range(0, depth, group_size)]
-    notes = [jnp.concatenate([noted[turn] for turn in group], axis=0) for group in groups]
-    slots = group_size * capacity
-    arrived = []
-    for group, note in zip(groups, notes):
-        if arrived:
-            note = after(note, arrived[-1][0])
-        packed = call(
-            functools.partial(pack_kernel, group_size, capacity),
-            [struct(slots, model_width)] * 4,
-            [place, note[:, :top_count].T, *[column[turn] for turn in group]],
-            [pltpu.VMEM((group_size * tok_rows, model_width), jnp.bfloat16)],
-            flops=8 * slots * group_size * tok_rows * model_width,
+    groups = [[0], [1, depth - 1], list(range(2, depth - 1))]
+    arrived, notes = [], []
+    for group in groups:
+        count = len(group)
+        first = column[group[0]]
+        *packed, note = call(
+            functools.partial(pack_kernel, count, capacity, top_count),
+            [struct(count * capacity, model_width)] * 4 + [struct(count * tok_rows, LANES)],
+            [place, after(first, arrived[-1][0]) if arrived else first, *[column[t] for t in group[1:]]],
+            [pltpu.VMEM((count * tok_rows, model_width), jnp.bfloat16)],
+            flops=8 * count * capacity * count * tok_rows * model_width,
+            limit=8 * MIB + 16 * (count * tok_rows) ** 2 + 8 * count * tok_rows * model_width,
         )
         arrived.append([packed[0]] + [swap_layer(packed[hop], hop) for hop in range(1, 4)])
+        notes.append(note)
+    results = []
+    for group, rows in zip(groups, arrived):
+        slots = len(group) * capacity
+        stride = -(-slots // 16) * 16
+        if results:
+            rows = [after(rows[0], results[-1][0])] + rows[1:]
+        results.append(
+            call(
+                functools.partial(expert_kernel, 4, stride),
+                [struct(slots, model_width)] * 4,
+                [*rows, *expert_weights],
+                [pltpu.VMEM((4 * stride, model_width), jnp.bfloat16)],
+                flops=48 * slots * model_width * w_gate.shape[2],
+                smem=0,
+                limit=8 * MIB + 4 * stride * (12 * model_width + 16 * w_gate.shape[2]),
+            )
+        )
     sums = [None] * depth
-    returned = []
-    for rows in arrived:
-        if returned:
-            rows = [after(rows[0], returned[-1][0])] + rows[1:]
-        results = call(
-            functools.partial(expert_kernel, 4),
-            [struct(slots, model_width)] * 4,
-            [*rows, *expert_weights],
-            flops=48 * slots * model_width * w_gate.shape[2],
-            smem=0,
-        )
-        returned.append([results[0]] + [swap_layer(results[hop], hop) for hop in range(1, 4)])
-    for group, note, rows in zip(groups, notes, returned):
+    sent_last = None
+    for index in (0, 2, 1):
+        group, rows = groups[index], list(results[index])
+        if sent_last is not None:
+            rows[1:] = [after(row, sent_last) for row in rows[1:]]
+        sent_last = rows[3]
+        rows = [rows[0]] + [swap_layer(rows[hop], hop) for hop in range(1, 4)]
+        count = len(group)
+        total = count * tok_rows
         parts = call(
-            functools.partial(combine_kernel, group_size, capacity),
-            [struct(tok_rows, model_width)] * group_size,
-            [place, note[:, :top_count], note[:, top_count:], *rows],
-            flops=16 * slots * group_size * tok_rows * model_width,
+            functools.partial(combine_kernel, count, capacity, top_count),
+            [struct(tok_rows, model_width)] * count,
+            [place, notes[index], *rows],
+            flops=16 * count * capacity * total * model_width,
+            limit=8 * MIB + 16 * total * total + 16 * total * model_width,
         )
         for turn, part in zip(group, parts):
             sums[turn] = part

time: 192 us -> 194 us (1.010)
  waiting for transfers between devices: 83.7 us -> 62.9 us
  starting transfers between devices: 51.3 us -> 66.3 us
  Pallas kernels: 43.8 us -> 56.2 us
  local copies, waits for them, and re-layouts: 11.2 us -> 4.13 us
    ppermute x41 -> x44, waiting for transfers between devices: 83.7 us -> 62.9 us  [move(): return lax.ppermute(block, AXES, route)]
    pallas_call x10 -> x14, Pallas kernels: 36.7 us -> 56.2 us  [call(): pl.pallas_call(kernel, out_shape=outs, in_specs=[SMEM] * smem + [VMEM] *...]
    ppermute x41 -> x44, starting transfers between devices: 51.3 us -> 66.3 us  [move(): return lax.ppermute(block, AXES, route)]
    unnamed x40 -> x18, local copies, waits for them, and re-layouts: 11.1 us -> 2.54 us
    pallas_call x2 -> x0, Pallas kernels: 7.11 us -> none  [load(): pl.pallas_call(functools.partial(load_kernel, count), out_shape=[struct(*...]
  transfers between devices with their start and end apart: 41 -> 44, of which waited for: 23 -> 19; matrix products, arithmetic and copies ran while one was open for 0% -> 2% of each run, Pallas kernels for 21% -> 22%
where the time goes in v4:
time: 194 us; the launch traced here: 192 us
  starting transfers between devices  66.3 us (34%)
  waiting for transfers between devices  62.9 us (32%)
  Pallas kernels  56.2 us (29%)
  local copies, waits for them, and re-layouts  4.13 us (2%)
  other arithmetic  2.55 us (1%)
    ppermute x44, starting transfers between devices, move(): return lax.ppermute(block, AXES, route)  66.3 us
    ppermute x44, waiting for transfers between devices, move(): return lax.ppermute(block, AXES, route)  62.9 us
    pallas_call x14, Pallas kernels, call(): pl.pallas_call(kernel, out_shape=outs, in_specs=[SMEM] * smem + [VMEM] *...  56.2 us
  transfers between devices with their start and end apart: 44, of which 19 were waited for; matrix products, arithmetic and copies ran while one was open for 2% of the time, Pallas kernels for 22%

profile of v4, /device:TPU:0, one launch (start us, length us, event | category | flops | bytes accessed | tf_op | source)
XLA Modules:
  0.0 192.5 jit_solution(2675441822472569759)
XLA Ops:
  0.0 3.0 %collective-permute-start.1 = (bf16[80,2048]{1,0:T(8,128)(2,1)}, bf16[80,2048]{1,0:T(8,128)(2,1)S(1)}, u32[]{:S(2)}, u32[]{:S(2)}) collective-permute-start(bf16[80,2048]{1,0:T(8,128)(2,1)} %inputs.1), channel_id=1, source_target_pairs={{0,2},{1,3},{2,0},{3,1},{4,6},{5,7},{6,4},{7,5},{8,10},{9,11},{10,... | collective-permute-start | bytes 983048 | tf_op jit(solution)/shard_map/ppermute | solution.py:27
  3.0 7.9 %collective-permute-done.1.refs_2_ = bf16[80,2048]{1,0:T(8,128)(2,1)S(1)} collective-permute-done((bf16[80,2048]{1,0:T(8,128)(2,1)}, bf16[80,2048]{1,0:T(8,128)(2,1)S(1)}, u32[]{:S(2)}, u32[]{:S(2)}) %collective-permute-start.1) | collective-permute-done | bytes 327712 | tf_op jit(solution)/shard_map/ppermute | solution.py:27
  14.2 5.1 %shard_map.127 = (bf16[336,384]{1,0:T(8,128)(2,1)S(1)}, bf16[336,384]{1,0:T(8,128)(2,1)S(1)}, bf16[336,384]{1,0:T(8,128)(2,1)S(1)}, bf16[336,384]{1,0:T(8,128)(2,1)S(1)}) custom-call(s32[5]{0:T(128)S(1)} %stack.20.place, bf16[80,2048]{1,0:T(8,128)(2,1)S(1)} %copy-done.2, bf16[80,2048]{1,0:T(8,128)(2,1)S(1)} %collective-permute-done.refs_1_, ...), custom_call_target="tpu_custom_call" | custom-call | flops 2013265920 | bytes 7659540 | tf_op jit(solution)/shard_map/pallas_call | solution.py:83
  20.0 1.9 collective-permute-start.4
  21.9 2.6 %collective-permute-start.5 = (bf16[336,384]{1,0:T(8,128)(2,1)S(1)}, bf16[336,384]{1,0:T(8,128)(2,1)S(1)}, u32[]{:S(2)}, u32[]{:S(2)}) collective-permute-start(bf16[336,384]{1,0:T(8,128)(2,1)S(1)} %get-tuple-element.74), channel_id=1, source_target_pairs={{0,16},{1,20},{2,18},{3,22},{4,17},{5,21},{6,19},{7,23},{8,24},{9,... | collective-permute-start | bytes 774152 | tf_op jit(solution)/shard_map/ppermute | solution.py:27
  25.9 3.2 %collective-permute-start.7 = (bf16[336,384]{1,0:T(8,128)(2,1)S(1)}, bf16[336,384]{1,0:T(8,128)(2,1)S(1)}, u32[]{:S(2)}, u32[]{:S(2)}) collective-permute-start(bf16[336,384]{1,0:T(8,128)(2,1)S(1)} %collective-permute-done.3.refs_0_), channel_id=1, source_target_pairs={{0,1},{1,0},{2,3},{3,2},{4,5},{5,4},{6,7},{7,6},{8,9},{9,8},{10,11... | collective-permute-start | bytes 774152 | tf_op jit(solution)/shard_map/ppermute | solution.py:27
  29.0 5.4 %collective-permute-start.8 = (bf16[336,384]{1,0:T(8,128)(2,1)S(1)}, bf16[336,384]{1,0:T(8,128)(2,1)S(1)}, u32[]{:S(2)}, u32[]{:S(2)}) collective-permute-start(bf16[336,384]{1,0:T(8,128)(2,1)S(1)} %collective-permute-done.4.refs_1_), channel_id=1, source_target_pairs={{0,1},{1,0},{2,3},{3,2},{4,5},{5,4},{6,7},{7,6},{8,9},{9,8},{10,11... | collective-permute-start | bytes 774152 | tf_op jit(solution)/shard_map/ppermute | solution.py:27
  34.4 7.5 %collective-permute-done.5.refs_2_ = bf16[336,384]{1,0:T(8,128)(2,1)S(1)} collective-permute-done((bf16[336,384]{1,0:T(8,128)(2,1)S(1)}, bf16[336,384]{1,0:T(8,128)(2,1)S(1)}, u32[]{:S(2)}, u32[]{:S(2)}) %collective-permute-start.5) | collective-permute-done | bytes 258080 | tf_op jit(solution)/shard_map/ppermute | solution.py:27
  44.8 7.9 %shard_map.128 = (bf16[320,128]{1,0:T(8,128)(2,1)S(1)}, bf16[320,128]{1,0:T(8,128)(2,1)S(1)}, bf16[320,128]{1,0:T(8,128)(2,1)S(1)}, bf16[320,128]{1,0:T(8,128)(2,1)S(1)}) custom-call(s32[5]{0:T(128)S(1)} %stack.20.place, bf16[336,384]{1,0:T(8,128)(2,1)S(1)} %collective-permute-done.3.refs_0_, bf16[336,384]{1,0:T(8,128)(2,1)S(1)} %collective-permute-done.4.refs_1_, ...), custom_call_target="tpu_custom_call" | custom-call | flops 1677721600 | bytes 2064404 | tf_op jit(solution)/shard_map/pallas_call | solution.py:83
  53.4 7.1 %collective-permute-start.12 = (bf16[320,128]{1,0:T(8,128)(2,1)S(1)}, bf16[320,128]{1,0:T(8,128)(2,1)S(1)}, u32[]{:S(2)}, u32[]{:S(2)}) collective-permute-start(bf16[320,128]{1,0:T(8,128)(2,1)S(1)} %get-tuple-element.77), channel_id=1, source_target_pairs={{0,24},{1,28},{2,26},{3,30},{4,25},{5,29},{6,27},{7,31},{8,0},{9,4... | collective-permute-start | bytes 245768 | tf_op jit(solution)/shard_map/ppermute | solution.py:27
  60.5 2.0 %collective-permute-done.12.refs_1_ = bf16[320,128]{1,0:T(8,128)(2,1)S(1)} collective-permute-done((bf16[320,128]{1,0:T(8,128)(2,1)S(1)}, bf16[320,128]{1,0:T(8,128)(2,1)S(1)}, u32[]{:S(2)}, u32[]{:S(2)}) %collective-permute-start.12) | collective-permute-done | bytes 81952 | tf_op jit(solution)/shard_map/ppermute | solution.py:27
  63.5 2.3 %collective-permute-done.13.refs_2_ = bf16[320,128]{1,0:T(8,128)(2,1)S(1)} collective-permute-done((bf16[320,128]{1,0:T(8,128)(2,1)S(1)}, bf16[320,128]{1,0:T(8,128)(2,1)S(1)}, u32[]{:S(2)}, u32[]{:S(2)}) %collective-permute-start.13) | collective-permute-done | bytes 81952 | tf_op jit(solution)/shard_map/ppermute | solution.py:27
  65.9 4.3 %collective-permute-done.14.refs_3_ = bf16[320,128]{1,0:T(8,128)(2,1)S(1)} collective-permute-done((bf16[320,128]{1,0:T(8,128)(2,1)S(1)}, bf16[320,128]{1,0:T(8,128)(2,1)S(1)}, u32[]{:S(2)}, u32[]{:S(2)}) %collective-permute-start.14) | collective-permute-done | bytes 81952 | tf_op jit(solution)/shard_map/ppermute | solution.py:27
  70.1 1.5 shard_map.129
  71.7 1.8 collective-permute-start.15
  73.4 1.7 collective-permute-done.15.given
  76.8 1.5 collective-permute-start.16
  79.9 3.6 %shard_map.130 = (bf16[704,2048]{1,0:T(8,128)(2,1)S(1)}, bf16[704,2048]{1,0:T(8,128)(2,1)S(1)}, bf16[704,2048]{1,0:T(8,128)(2,1)S(1)}) custom-call(bf16[704,2048]{1,0:T(8,128)(2,1)} %bitcast.8.refs_0_, bf16[704,2048]{1,0:T(8,128)(2,1)} %bitcast.10.refs_1_, bf16[704,2048]{1,0:T(8,128)(2,1)} %bitcast.11.refs_2_), custom_call_target="tpu_custom_call" | custom-call | bytes 8650752 | tf_op jit(solution)/shard_map/pallas_call | solution.py:83
  83.5 3.6 %collective-permute-done.16.far = bf16[80,2048]{1,0:T(8,128)(2,1)} collective-permute-done((bf16[80,2048]{1,0:T(8,128)(2,1)}, bf16[80,2048]{1,0:T(8,128)(2,1)}, u32[]{:S(2)}, u32[]{:S(2)}) %collective-permute-start.16) | collective-permute-done | bytes 327712 | tf_op jit(solution)/shard_map/ppermute | solution.py:27
  88.9 3.5 %collective-permute-start.27 = (bf16[80,2176]{1,0:T(8,128)(2,1)S(1)}, bf16[80,2176]{1,0:T(8,128)(2,1)S(1)}, u32[]{:S(2)}, u32[]{:S(2)}) collective-permute-start(bf16[80,2176]{1,0:T(8,128)(2,1)S(1)} %get-tuple-element.93.refs_0_), channel_id=1, source_target_pairs={{0,24},{1,25},{2,26},{3,27},{4,28},{5,29},{6,30},{7,31},{8,0},{9,1... | collective-permute-start | bytes 1044488 | tf_op jit(solution)/shard_map/ppermute | solution.py:27
  92.4 1.5 shard_map.132
  93.9 1.6 collective-permute-start.20
  95.5 1.7 collective-permute-start.21
  97.4 4.0 %collective-permute-done.26.refs_0_ = bf16[80,2176]{1,0:T(8,128)(2,1)S(1)} collective-permute-done((bf16[80,2176]{1,0:T(8,128)(2,1)S(1)}, bf16[80,2176]{1,0:T(8,128)(2,1)S(1)}, u32[]{:S(2)}, u32[]{:S(2)}) %collective-permute-start.26) | collective-permute-done | bytes 348192 | tf_op jit(solution)/shard_map/ppermute | solution.py:27
  101.4 4.3 %collective-permute-done.27.refs_1_ = bf16[80,2176]{1,0:T(8,128)(2,1)S(1)} collective-permute-done((bf16[80,2176]{1,0:T(8,128)(2,1)S(1)}, bf16[80,2176]{1,0:T(8,128)(2,1)S(1)}, u32[]{:S(2)}, u32[]{:S(2)}) %collective-permute-start.27) | collective-permute-done | bytes 348192 | tf_op jit(solution)/shard_map/ppermute | solution.py:27
  105.7 1.7 shard_map.135
  107.4 1.6 collective-permute-start.28
  110.9 7.5 %shard_map.133 = (bf16[40,2048]{1,0:T(8,128)(2,1)S(1)}, bf16[40,2048]{1,0:T(8,128)(2,1)S(1)}, bf16[40,2048]{1,0:T(8,128)(2,1)S(1)}, bf16[40,2048]{1,0:T(8,128)(2,1)S(1)}) custom-call(bf16[40,2048]{1,0:T(8,128)(2,1)S(1)} %get-tuple-element.95.refs_0_, bf16[40,2048]{1,0:T(8,128)(2,1)S(1)} %collective-permute-done.20.refs_1_, ...), custom_call_target="tpu_custom_call" | custom-call | flops 2768240640 | bytes 17956864 | tf_op jit(solution)/shard_map/pallas_call | solution.py:83
  120.0 1.6 collective-permute-start.32
  123.5 2.4 %collective-permute-done.30.refs_3_ = bf16[80,2048]{1,0:T(8,128)(2,1)S(1)} collective-permute-done((bf16[80,2048]{1,0:T(8,128)(2,1)S(1)}, bf16[80,2048]{1,0:T(8,128)(2,1)S(1)}, u32[]{:S(2)}, u32[]{:S(2)}) %collective-permute-start.30) | collective-permute-done | bytes 327712 | tf_op jit(solution)/shard_map/ppermute | solution.py:27
  125.9 9.0 %shard_map.136 = (bf16[80,2048]{1,0:T(8,128)(2,1)S(1)}, bf16[80,2048]{1,0:T(8,128)(2,1)S(1)}, bf16[80,2048]{1,0:T(8,128)(2,1)S(1)}, bf16[80,2048]{1,0:T(8,128)(2,1)S(1)}) custom-call(bf16[80,2048]{1,0:T(8,128)(2,1)S(1)} %get-tuple-element.112.refs_0_, bf16[80,2048]{1,0:T(8,128)(2,1)S(1)} %collective-permute-done.28.refs_1_, ...), custom_call_target="tpu_custom_call" | custom-call | flops 5536481280 | bytes 18612224 | tf_op jit(solution)/shard_map/pallas_call | solution.py:83
  135.0 7.8 %shard_map.138 = (bf16[40,2048]{1,0:T(8,128)(2,1)S(1)}, bf16[40,2048]{1,0:T(8,128)(2,1)S(1)}, bf16[40,2048]{1,0:T(8,128)(2,1)S(1)}, bf16[40,2048]{1,0:T(8,128)(2,1)S(1)}) custom-call(bf16[40,2048]{1,0:T(8,128)(2,1)S(1)} %get-tuple-element.120.refs_0_, bf16[40,2048]{1,0:T(8,128)(2,1)S(1)} %collective-permute-done.32.refs_1_, ...), custom_call_target="tpu_custom_call" | custom-call | flops 2768240640 | bytes 17956864 | tf_op jit(solution)/shard_map/pallas_call | solution.py:83
  142.7 1.6 collective-permute-start.39
  146.3 1.6 collective-permute-start.37
  149.2 2.3 %collective-permute-done.39.refs_1_ = bf16[40,2048]{1,0:T(8,128)(2,1)S(1)} collective-permute-done((bf16[40,2048]{1,0:T(8,128)(2,1)S(1)}, bf16[40,2048]{1,0:T(8,128)(2,1)S(1)}, u32[]{:S(2)}, u32[]{:S(2)}) %collective-permute-start.39) | collective-permute-done | bytes 163872 | tf_op jit(solution)/shard_map/ppermute | solution.py:27
  151.5 1.7 collective-permute-start.41
  153.2 7.9 %collective-permute-done.40.refs_2_ = bf16[40,2048]{1,0:T(8,128)(2,1)S(1)} collective-permute-done((bf16[40,2048]{1,0:T(8,128)(2,1)S(1)}, bf16[40,2048]{1,0:T(8,128)(2,1)S(1)}, u32[]{:S(2)}, u32[]{:S(2)}) %collective-permute-start.40) | collective-permute-done | bytes 163872 | tf_op jit(solution)/shard_map/ppermute | solution.py:27
  161.2 1.5 collective-permute-start.23
  163.9 2.3 %shard_map.140 = bf16[80,2048]{1,0:T(8,128)(2,1)S(1)} custom-call(s32[5]{0:T(128)S(1)} %stack.20.place, bf16[80,128]{1,0:T(8,128)(2,1)S(1)} %get-tuple-element.132.notes, bf16[40,2048]{1,0:T(8,128)(2,1)S(1)} %get-tuple-element.133.refs_0_, bf16[40,2048]{1,0:T(8,128)(2,1)S(1)} %collective-permute-done.39.refs_1_, ...), custom_call_target="tpu_custom_call" | custom-call | flops 104857600 | bytes 675860 | tf_op jit(solution)/shard_map/pallas_call | solution.py:83
  166.2 2.6 %collective-permute-start.42 = (bf16[80,2048]{1,0:T(8,128)(2,1)S(1)}, bf16[80,2048]{1,0:T(8,128)(2,1)S(1)}, u32[]{:S(2)}, u32[]{:S(2)}) collective-permute-start(bf16[80,2048]{1,0:T(8,128)(2,1)S(1)} %shard_map.140), channel_id=1, source_target_pairs={{0,16},{1,17},{2,18},{3,19},{4,20},{5,21},{6,22},{7,23},{8,24},{9,... | collective-permute-start | bytes 983048 | tf_op jit(solution)/shard_map/ppermute | solution.py:27
  168.9 3.1 %shard_map.139 = (bf16[80,2048]{1,0:T(8,128)(2,1)S(1)}, bf16[80,2048]{1,0:T(8,128)(2,1)S(1)}) custom-call(s32[5]{0:T(128)S(1)} %stack.20.place, bf16[160,128]{1,0:T(8,128)(2,1)S(1)} %get-tuple-element.110.notes, bf16[80,2048]{1,0:T(8,128)(2,1)S(1)} %get-tuple-element.116.refs_0_, bf16[80,2048]{1,0:T(8,128)(2,1)S(1)} %collective-permute-done.35.refs_1_, ...), custom_call_target="tpu_custom_call" | custom-call | flops 419430400 | bytes 1351700 | tf_op jit(solution)/shard_map/pallas_call | solution.py:83
  172.0 3.5 %collective-permute-start.43 = (bf16[80,2048]{1,0:T(8,128)(2,1)S(1)}, bf16[80,2048]{1,0:T(8,128)(2,1)S(1)}, u32[]{:S(2)}, u32[]{:S(2)}) collective-permute-start(bf16[80,2048]{1,0:T(8,128)(2,1)S(1)} %get-tuple-element.138), channel_id=1, source_target_pairs={{0,8},{1,9},{2,10},{3,11},{4,12},{5,13},{6,14},{7,15},{8,16},{9,17... | collective-permute-start | bytes 983048 | tf_op jit(solution)/shard_map/ppermute | solution.py:27
  175.4 2.4 %collective-permute-start.38 = (bf16[80,2048]{1,0:T(8,128)(2,1)S(1)}, bf16[80,2048]{1,0:T(8,128)(2,1)S(1)}, u32[]{:S(2)}, u32[]{:S(2)}) collective-permute-start(bf16[80,2048]{1,0:T(8,128)(2,1)S(1)} %get-tuple-element.131), channel_id=1, source_target_pairs={{0,24},{1,25},{2,26},{3,27},{4,28},{5,29},{6,30},{7,31},{8,0},{9,1... | collective-permute-start | bytes 983048 | tf_op jit(solution)/shard_map/ppermute | solution.py:27
  178.4 1.5 collective-permute-start.25
  179.9 3.2 %collective-permute-done.24.refs_2_ = bf16[40,2048]{1,0:T(8,128)(2,1)S(1)} collective-permute-done((bf16[40,2048]{1,0:T(8,128)(2,1)S(1)}, bf16[40,2048]{1,0:T(8,128)(2,1)S(1)}, u32[]{:S(2)}, u32[]{:S(2)}) %collective-permute-start.24) | collective-permute-done | bytes 163872 | tf_op jit(solution)/shard_map/ppermute | solution.py:27
  183.1 1.8 collective-permute-done.25.refs_3_
  185.0 2.3 %shard_map.134 = bf16[80,2048]{1,0:T(8,128)(2,1)S(1)} custom-call(s32[5]{0:T(128)S(1)} %stack.20.place, bf16[80,128]{1,0:T(8,128)(2,1)S(1)} %get-tuple-element.94.notes, bf16[40,2048]{1,0:T(8,128)(2,1)S(1)} %get-tuple-element.105.refs_0_, bf16[40,2048]{1,0:T(8,128)(2,1)S(1)} %collective-permute-done.23.refs_1_, ...), custom_call_target="tpu_custom_call" | custom-call | flops 104857600 | bytes 675860 | tf_op jit(solution)/shard_map/pallas_call | solution.py:83
  187.3 4.2 %collective-permute-done.42 = bf16[80,2048]{1,0:T(8,128)(2,1)S(1)} collective-permute-done((bf16[80,2048]{1,0:T(8,128)(2,1)S(1)}, bf16[80,2048]{1,0:T(8,128)(2,1)S(1)}, u32[]{:S(2)}, u32[]{:S(2)}) %collective-permute-start.42) | collective-permute-done | bytes 327712 | tf_op jit(solution)/shard_map/ppermute | solution.py:27
  (83 shorter events, 26.5 us)
Async XLA Ops:
  0.0 10.9 %collective-permute-start.1 = (bf16[80,2048]{1,0:T(8,128)(2,1)}, bf16[80,2048]{1,0:T(8,128)(2,1)S(1)}, u32[]{:S(2)}, u32[]{:S(2)}) collective-permute-start(bf16[80,2048]{1,0:T(8,128)(2,1)} %inputs.1), channel_id=1, source_target_pairs={{0,2},{1,3},{2,0},{3,1},{4,6},{5,7},{6,4},{7,5},{8,10},{9,11},{10,... | collective-permute-start | bytes 983048 | tf_op jit(solution)/shard_map/ppermute | solution.py:27
  3.0 8.8 %collective-permute-start = (bf16[80,2048]{1,0:T(8,128)(2,1)}, bf16[80,2048]{1,0:T(8,128)(2,1)S(1)}, u32[]{:S(2)}, u32[]{:S(2)}) collective-permute-start(bf16[80,2048]{1,0:T(8,128)(2,1)} %inputs.1), channel_id=1, source_target_pairs={{0,1},{1,0},{2,3},{3,2},{4,5},{5,4},{6,7},{7,6},{8,9},{9,8},{10,11... | collective-permute-start | bytes 983048 | tf_op jit(solution)/shard_map/ppermute | solution.py:27
  10.9 1.6 collective-permute-start.2
  19.4 6.5 %collective-permute-start.3 = (bf16[336,384]{1,0:T(8,128)(2,1)S(1)}, bf16[336,384]{1,0:T(8,128)(2,1)S(1)}, u32[]{:S(2)}, u32[]{:S(2)}) collective-permute-start(bf16[336,384]{1,0:T(8,128)(2,1)S(1)} %get-tuple-element.72), channel_id=1, source_target_pairs={{0,0},{1,4},{2,2},{3,6},{4,1},{5,5},{6,3},{7,7},{8,8},{9,12},{10,1... | collective-permute-start | bytes 774152 | tf_op jit(solution)/shard_map/ppermute | solution.py:27
  20.0 9.0 %collective-permute-start.4 = (bf16[336,384]{1,0:T(8,128)(2,1)S(1)}, bf16[336,384]{1,0:T(8,128)(2,1)S(1)}, u32[]{:S(2)}, u32[]{:S(2)}) collective-permute-start(bf16[336,384]{1,0:T(8,128)(2,1)S(1)} %get-tuple-element.73), channel_id=1, source_target_pairs={{0,8},{1,12},{2,10},{3,14},{4,9},{5,13},{6,11},{7,15},{8,16},{9,20... | collective-permute-start | bytes 774152 | tf_op jit(solution)/shard_map/ppermute | solution.py:27
  21.9 20.1 %collective-permute-start.5 = (bf16[336,384]{1,0:T(8,128)(2,1)S(1)}, bf16[336,384]{1,0:T(8,128)(2,1)S(1)}, u32[]{:S(2)}, u32[]{:S(2)}) collective-permute-start(bf16[336,384]{1,0:T(8,128)(2,1)S(1)} %get-tuple-element.74), channel_id=1, source_target_pairs={{0,16},{1,20},{2,18},{3,22},{4,17},{5,21},{6,19},{7,23},{8,24},{9,... | collective-permute-start | bytes 774152 | tf_op jit(solution)/shard_map/ppermute | solution.py:27
  24.5 45.6 %copy-start.6 = (bf16[512,2048]{1,0:T(8,128)(2,1)S(1)}, bf16[512,2048]{1,0:T(8,128)(2,1)}, u32[]{:S(2)}) copy-start(bf16[512,2048]{1,0:T(8,128)(2,1)} %refs_4_.1) | copy-start | bytes 6291460
  24.5 17.9 %collective-permute-start.6 = (bf16[336,384]{1,0:T(8,128)(2,1)S(1)}, bf16[336,384]{1,0:T(8,128)(2,1)S(1)}, u32[]{:S(2)}, u32[]{:S(2)}) collective-permute-start(bf16[336,384]{1,0:T(8,128)(2,1)S(1)} %get-tuple-element.75), channel_id=1, source_target_pairs={{0,24},{1,28},{2,26},{3,30},{4,25},{5,29},{6,27},{7,31},{8,0},{9,4... | collective-permute-start | bytes 774152 | tf_op jit(solution)/shard_map/ppermute | solution.py:27
  25.9 16.6 %collective-permute-start.7 = (bf16[336,384]{1,0:T(8,128)(2,1)S(1)}, bf16[336,384]{1,0:T(8,128)(2,1)S(1)}, u32[]{:S(2)}, u32[]{:S(2)}) collective-permute-start(bf16[336,384]{1,0:T(8,128)(2,1)S(1)} %collective-permute-done.3.refs_0_), channel_id=1, source_target_pairs={{0,1},{1,0},{2,3},{3,2},{4,5},{5,4},{6,7},{7,6},{8,9},{9,8},{10,11... | collective-permute-start | bytes 774152 | tf_op jit(solution)/shard_map/ppermute | solution.py:27
  29.0 13.5 %collective-permute-start.8 = (bf16[336,384]{1,0:T(8,128)(2,1)S(1)}, bf16[336,384]{1,0:T(8,128)(2,1)S(1)}, u32[]{:S(2)}, u32[]{:S(2)}) collective-permute-start(bf16[336,384]{1,0:T(8,128)(2,1)S(1)} %collective-permute-done.4.refs_1_), channel_id=1, source_target_pairs={{0,1},{1,0},{2,3},{3,2},{4,5},{5,4},{6,7},{7,6},{8,9},{9,8},{10,11... | collective-permute-start | bytes 774152 | tf_op jit(solution)/shard_map/ppermute | solution.py:27
  42.0 1.5 collective-permute-start.9
  42.4 1.5 collective-permute-start.10
  43.9 43.2 %collective-permute-start.17 = (bf16[1,2048,704]{1,2,0:T(8,128)(2,1)}, bf16[1,2048,704]{1,2,0:T(8,128)(2,1)S(1)}, u32[]{:S(2)}, u32[]{:S(2)}) collective-permute-start(bf16[1,2048,704]{1,2,0:T(8,128)(2,1)} %param.21), channel_id=1, source_target_pairs={{0,1},{1,0},{2,3},{3,2},{4,5},{5,4},{6,7},{7,6},{8,9},{9,8},{10,11... | collective-permute-start | bytes 8650760 | tf_op jit(solution)/shard_map/ppermute | solution.py:27
  44.2 42.9 %collective-permute-start.18 = (bf16[1,2048,704]{1,2,0:T(8,128)(2,1)}, bf16[1,2048,704]{1,2,0:T(8,128)(2,1)}, u32[]{:S(2)}, u32[]{:S(2)}) collective-permute-start(bf16[1,2048,704]{1,2,0:T(8,128)(2,1)} %param.22), channel_id=1, source_target_pairs={{0,1},{1,0},{2,3},{3,2},{4,5},{5,4},{6,7},{7,6},{8,9},{9,8},{10,11... | collective-permute-start | bytes 8650760 | tf_op jit(solution)/shard_map/ppermute | solution.py:27
  44.4 42.7 %collective-permute-start.19 = (bf16[1,704,2048]{2,1,0:T(8,128)(2,1)}, bf16[1,704,2048]{2,1,0:T(8,128)(2,1)}, u32[]{:S(2)}, u32[]{:S(2)}) collective-permute-start(bf16[1,704,2048]{2,1,0:T(8,128)(2,1)} %param.23), channel_id=1, source_target_pairs={{0,1},{1,0},{2,3},{3,2},{4,5},{5,4},{6,7},{7,6},{8,9},{9,8},{10,11... | collective-permute-start | bytes 8650760 | tf_op jit(solution)/shard_map/ppermute | solution.py:27
  52.7 25.6 %copy-start.8 = (s32[80,6]{0,1:T(8,128)S(1)}, s32[80,6]{0,1:T(8,128)}, u32[]{:S(2)}) copy-start(s32[80,6]{0,1:T(8,128)} %param.24) | copy-start | bytes 5764
  52.7 25.6 %copy-start.7 = (f32[80,6]{0,1:T(8,128)S(1)}, f32[80,6]{0,1:T(8,128)}, u32[]{:S(2)}) copy-start(f32[80,6]{0,1:T(8,128)} %param.25) | copy-start | bytes 5764
  52.7 7.8 %collective-permute-start.11 = (bf16[320,128]{1,0:T(8,128)(2,1)S(1)}, bf16[320,128]{1,0:T(8,128)(2,1)S(1)}, u32[]{:S(2)}, u32[]{:S(2)}) collective-permute-start(bf16[320,128]{1,0:T(8,128)(2,1)S(1)} %get-tuple-element.76), channel_id=1, source_target_pairs={{0,0},{1,4},{2,2},{3,6},{4,1},{5,5},{6,3},{7,7},{8,8},{9,12},{10,1... | collective-permute-start | bytes 245768 | tf_op jit(solution)/shard_map/ppermute | solution.py:27
  53.4 9.2 %collective-permute-start.12 = (bf16[320,128]{1,0:T(8,128)(2,1)S(1)}, bf16[320,128]{1,0:T(8,128)(2,1)S(1)}, u32[]{:S(2)}, u32[]{:S(2)}) collective-permute-start(bf16[320,128]{1,0:T(8,128)(2,1)S(1)} %get-tuple-element.77), channel_id=1, source_target_pairs={{0,24},{1,28},{2,26},{3,30},{4,25},{5,29},{6,27},{7,31},{8,0},{9,4... | collective-permute-start | bytes 245768 | tf_op jit(solution)/shard_map/ppermute | solution.py:27
  60.5 5.3 %collective-permute-start.13 = (bf16[320,128]{1,0:T(8,128)(2,1)S(1)}, bf16[320,128]{1,0:T(8,128)(2,1)S(1)}, u32[]{:S(2)}, u32[]{:S(2)}) collective-permute-start(bf16[320,128]{1,0:T(8,128)(2,1)S(1)} %get-tuple-element.78), channel_id=1, source_target_pairs={{0,16},{1,20},{2,18},{3,22},{4,17},{5,21},{6,19},{7,23},{8,24},{9,... | collective-permute-start | bytes 245768 | tf_op jit(solution)/shard_map/ppermute | solution.py:27
  62.6 7.6 %collective-permute-start.14 = (bf16[320,128]{1,0:T(8,128)(2,1)S(1)}, bf16[320,128]{1,0:T(8,128)(2,1)S(1)}, u32[]{:S(2)}, u32[]{:S(2)}) collective-permute-start(bf16[320,128]{1,0:T(8,128)(2,1)S(1)} %get-tuple-element.79), channel_id=1, source_target_pairs={{0,8},{1,12},{2,10},{3,14},{4,9},{5,13},{6,11},{7,15},{8,16},{9,20... | collective-permute-start | bytes 245768 | tf_op jit(solution)/shard_map/ppermute | solution.py:27
  71.7 3.5 %collective-permute-start.15 = (bf16[2,80,2048]{2,1,0:T(8,128)(2,1)S(1)}, bf16[2,80,2048]{2,1,0:T(8,128)(2,1)S(1)}, u32[]{:S(2)}, u32[]{:S(2)}) collective-permute-start(bf16[2,80,2048]{2,1,0:T(8,128)(2,1)S(1)} %get-tuple-element.81), channel_id=1, source_target_pairs={{0,1},{1,0},{2,3},{3,2},{4,5},{5,4},{6,7},{7,6},{8,9},{9,8},{10,11... | collective-permute-start | bytes 1966088 | tf_op jit(solution)/shard_map/ppermute | solution.py:27
  76.8 10.3 %collective-permute-start.16 = (bf16[80,2048]{1,0:T(8,128)(2,1)}, bf16[80,2048]{1,0:T(8,128)(2,1)}, u32[]{:S(2)}, u32[]{:S(2)}) collective-permute-start(bf16[80,2048]{1,0:T(8,128)(2,1)} %fusion), channel_id=1, source_target_pairs={{0,2},{1,3},{2,0},{3,1},{4,6},{5,7},{6,4},{7,5},{8,10},{9,11},{10,... | collective-permute-start | bytes 983048 | tf_op jit(solution)/shard_map/ppermute | solution.py:27
  79.9 7.3 %copy-start.5 = (f32[2048]{0:T(1024)S(1)}, f32[2048]{0:T(1024)}, u32[]{:S(2)}) copy-start(f32[2048]{0:T(1024)} %param.20) | copy-start | bytes 24580
  88.5 12.9 %collective-permute-start.26 = (bf16[80,2176]{1,0:T(8,128)(2,1)S(1)}, bf16[80,2176]{1,0:T(8,128)(2,1)S(1)}, u32[]{:S(2)}, u32[]{:S(2)}) collective-permute-start(bf16[80,2176]{1,0:T(8,128)(2,1)S(1)} %get-tuple-element.93.refs_0_), channel_id=1, source_target_pairs={{0,8},{1,9},{2,10},{3,11},{4,12},{5,13},{6,14},{7,15},{8,16},{9,17... | collective-permute-start | bytes 1044488 | tf_op jit(solution)/shard_map/ppermute | solution.py:27
  88.9 16.8 %collective-permute-start.27 = (bf16[80,2176]{1,0:T(8,128)(2,1)S(1)}, bf16[80,2176]{1,0:T(8,128)(2,1)S(1)}, u32[]{:S(2)}, u32[]{:S(2)}) collective-permute-start(bf16[80,2176]{1,0:T(8,128)(2,1)S(1)} %get-tuple-element.93.refs_0_), channel_id=1, source_target_pairs={{0,24},{1,25},{2,26},{3,27},{4,28},{5,29},{6,30},{7,31},{8,0},{9,1... | collective-permute-start | bytes 1044488 | tf_op jit(solution)/shard_map/ppermute | solution.py:27
  93.9 15.1 %collective-permute-start.20 = (bf16[40,2048]{1,0:T(8,128)(2,1)S(1)}, bf16[40,2048]{1,0:T(8,128)(2,1)S(1)}, u32[]{:S(2)}, u32[]{:S(2)}) collective-permute-start(bf16[40,2048]{1,0:T(8,128)(2,1)S(1)} %get-tuple-element.96), channel_id=1, source_target_pairs={{0,2},{1,3},{2,0},{3,1},{4,6},{5,7},{6,4},{7,5},{8,10},{9,11},{10,... | collective-permute-start | bytes 491528 | tf_op jit(solution)/shard_map/ppermute | solution.py:27
  95.5 14.9 %collective-permute-start.21 = (bf16[40,2048]{1,0:T(8,128)(2,1)S(1)}, bf16[40,2048]{1,0:T(8,128)(2,1)S(1)}, u32[]{:S(2)}, u32[]{:S(2)}) collective-permute-start(bf16[40,2048]{1,0:T(8,128)(2,1)S(1)} %get-tuple-element.97), channel_id=1, source_target_pairs={{0,4},{1,5},{2,6},{3,7},{4,0},{5,1},{6,2},{7,3},{8,12},{9,13},{10,... | collective-permute-start | bytes 491528 | tf_op jit(solution)/shard_map/ppermute | solution.py:27
  97.1 13.8 %collective-permute-start.22 = (bf16[40,2048]{1,0:T(8,128)(2,1)S(1)}, bf16[40,2048]{1,0:T(8,128)(2,1)S(1)}, u32[]{:S(2)}, u32[]{:S(2)}) collective-permute-start(bf16[40,2048]{1,0:T(8,128)(2,1)S(1)} %get-tuple-element.98), channel_id=1, source_target_pairs={{0,6},{1,7},{2,4},{3,5},{4,2},{5,3},{6,0},{7,1},{8,14},{9,15},{10,... | collective-permute-start | bytes 491528 | tf_op jit(solution)/shard_map/ppermute | solution.py:27
  101.4 17.0 %collective-permute-start.31 = (bf16[80,2176]{1,0:T(8,128)(2,1)S(1)}, bf16[80,2176]{1,0:T(8,128)(2,1)S(1)}, u32[]{:S(2)}, u32[]{:S(2)}) collective-permute-start(bf16[80,2176]{1,0:T(8,128)(2,1)S(1)} %collective-permute-done.26.refs_0_), channel_id=1, source_target_pairs={{0,8},{1,9},{2,10},{3,11},{4,12},{5,13},{6,14},{7,15},{8,16},{9,17... | collective-permute-start | bytes 1044488 | tf_op jit(solution)/shard_map/ppermute | solution.py:27
  107.4 15.6 %collective-permute-start.28 = (bf16[80,2048]{1,0:T(8,128)(2,1)S(1)}, bf16[80,2048]{1,0:T(8,128)(2,1)S(1)}, u32[]{:S(2)}, u32[]{:S(2)}) collective-permute-start(bf16[80,2048]{1,0:T(8,128)(2,1)S(1)} %get-tuple-element.113), channel_id=1, source_target_pairs={{0,2},{1,3},{2,0},{3,1},{4,6},{5,7},{6,4},{7,5},{8,10},{9,11},{10,... | collective-permute-start | bytes 983048 | tf_op jit(solution)/shard_map/ppermute | solution.py:27
  109.0 14.6 %collective-permute-start.29 = (bf16[80,2048]{1,0:T(8,128)(2,1)S(1)}, bf16[80,2048]{1,0:T(8,128)(2,1)S(1)}, u32[]{:S(2)}, u32[]{:S(2)}) collective-permute-start(bf16[80,2048]{1,0:T(8,128)(2,1)S(1)} %get-tuple-element.114), channel_id=1, source_target_pairs={{0,4},{1,5},{2,6},{3,7},{4,0},{5,1},{6,2},{7,3},{8,12},{9,13},{10,... | collective-permute-start | bytes 983048 | tf_op jit(solution)/shard_map/ppermute | solution.py:27
  110.4 15.5 %collective-permute-start.30 = (bf16[80,2048]{1,0:T(8,128)(2,1)S(1)}, bf16[80,2048]{1,0:T(8,128)(2,1)S(1)}, u32[]{:S(2)}, u32[]{:S(2)}) collective-permute-start(bf16[80,2048]{1,0:T(8,128)(2,1)S(1)} %get-tuple-element.115), channel_id=1, source_target_pairs={{0,6},{1,7},{2,4},{3,5},{4,2},{5,3},{6,0},{7,1},{8,14},{9,15},{10,... | collective-permute-start | bytes 983048 | tf_op jit(solution)/shard_map/ppermute | solution.py:27
  120.0 15.0 %collective-permute-start.32 = (bf16[40,2048]{1,0:T(8,128)(2,1)S(1)}, bf16[40,2048]{1,0:T(8,128)(2,1)S(1)}, u32[]{:S(2)}, u32[]{:S(2)}) collective-permute-start(bf16[40,2048]{1,0:T(8,128)(2,1)S(1)} %get-tuple-element.121), channel_id=1, source_target_pairs={{0,2},{1,3},{2,0},{3,1},{4,6},{5,7},{6,4},{7,5},{8,10},{9,11},{10,... | collective-permute-start | bytes 491528 | tf_op jit(solution)/shard_map/ppermute | solution.py:27
  121.6 13.4 %collective-permute-start.33 = (bf16[40,2048]{1,0:T(8,128)(2,1)S(1)}, bf16[40,2048]{1,0:T(8,128)(2,1)S(1)}, u32[]{:S(2)}, u32[]{:S(2)}) collective-permute-start(bf16[40,2048]{1,0:T(8,128)(2,1)S(1)} %get-tuple-element.122), channel_id=1, source_target_pairs={{0,4},{1,5},{2,6},{3,7},{4,0},{5,1},{6,2},{7,3},{8,12},{9,13},{10,... | collective-permute-start | bytes 491528 | tf_op jit(solution)/shard_map/ppermute | solution.py:27
  123.0 12.0 %collective-permute-start.34 = (bf16[40,2048]{1,0:T(8,128)(2,1)S(1)}, bf16[40,2048]{1,0:T(8,128)(2,1)S(1)}, u32[]{:S(2)}, u32[]{:S(2)}) collective-permute-start(bf16[40,2048]{1,0:T(8,128)(2,1)S(1)} %get-tuple-element.123), channel_id=1, source_target_pairs={{0,6},{1,7},{2,4},{3,5},{4,2},{5,3},{6,0},{7,1},{8,14},{9,15},{10,... | collective-permute-start | bytes 491528 | tf_op jit(solution)/shard_map/ppermute | solution.py:27
  142.7 8.8 %collective-permute-start.39 = (bf16[40,2048]{1,0:T(8,128)(2,1)S(1)}, bf16[40,2048]{1,0:T(8,128)(2,1)S(1)}, u32[]{:S(2)}, u32[]{:S(2)}) collective-permute-start(bf16[40,2048]{1,0:T(8,128)(2,1)S(1)} %get-tuple-element.135), channel_id=1, source_target_pairs={{0,2},{1,3},{2,0},{3,1},{4,6},{5,7},{6,4},{7,5},{8,10},{9,11},{10,... | collective-permute-start | bytes 491528 | tf_op jit(solution)/shard_map/ppermute | solution.py:27
  144.3 24.5 %collective-permute-start.35 = (bf16[80,2048]{1,0:T(8,128)(2,1)S(1)}, bf16[80,2048]{1,0:T(8,128)(2,1)S(1)}, u32[]{:S(2)}, u32[]{:S(2)}) collective-permute-start(bf16[80,2048]{1,0:T(8,128)(2,1)S(1)} %get-tuple-element.126), channel_id=1, source_target_pairs={{0,2},{1,3},{2,0},{3,1},{4,6},{5,7},{6,4},{7,5},{8,10},{9,11},{10,... | collective-permute-start | bytes 983048 | tf_op jit(solution)/shard_map/ppermute | solution.py:27
  144.8 24.0 %collective-permute-start.36 = (bf16[80,2048]{1,0:T(8,128)(2,1)S(1)}, bf16[80,2048]{1,0:T(8,128)(2,1)S(1)}, u32[]{:S(2)}, u32[]{:S(2)}) collective-permute-start(bf16[80,2048]{1,0:T(8,128)(2,1)S(1)} %get-tuple-element.128), channel_id=1, source_target_pairs={{0,4},{1,5},{2,6},{3,7},{4,0},{5,1},{6,2},{7,3},{8,12},{9,13},{10,... | collective-permute-start | bytes 983048 | tf_op jit(solution)/shard_map/ppermute | solution.py:27
  146.3 22.6 %collective-permute-start.37 = (bf16[80,2048]{1,0:T(8,128)(2,1)S(1)}, bf16[80,2048]{1,0:T(8,128)(2,1)S(1)}, u32[]{:S(2)}, u32[]{:S(2)}) collective-permute-start(bf16[80,2048]{1,0:T(8,128)(2,1)S(1)} %get-tuple-element.130), channel_id=1, source_target_pairs={{0,6},{1,7},{2,4},{3,5},{4,2},{5,3},{6,0},{7,1},{8,14},{9,15},{10,... | collective-permute-start | bytes 983048 | tf_op jit(solution)/shard_map/ppermute | solution.py:27
  147.8 13.4 %collective-permute-start.40 = (bf16[40,2048]{1,0:T(8,128)(2,1)S(1)}, bf16[40,2048]{1,0:T(8,128)(2,1)S(1)}, u32[]{:S(2)}, u32[]{:S(2)}) collective-permute-start(bf16[40,2048]{1,0:T(8,128)(2,1)S(1)} %get-tuple-element.137), channel_id=1, source_target_pairs={{0,4},{1,5},{2,6},{3,7},{4,0},{5,1},{6,2},{7,3},{8,12},{9,13},{10,... | collective-permute-start | bytes 491528 | tf_op jit(solution)/shard_map/ppermute | solution.py:27
  151.5 12.4 %collective-permute-start.41 = (bf16[40,2048]{1,0:T(8,128)(2,1)S(1)}, bf16[40,2048]{1,0:T(8,128)(2,1)S(1)}, u32[]{:S(2)}, u32[]{:S(2)}) collective-permute-start(bf16[40,2048]{1,0:T(8,128)(2,1)S(1)} %get-tuple-element.125), channel_id=1, source_target_pairs={{0,6},{1,7},{2,4},{3,5},{4,2},{5,3},{6,0},{7,1},{8,14},{9,15},{10,... | collective-permute-start | bytes 491528 | tf_op jit(solution)/shard_map/ppermute | solution.py:27
  161.2 17.2 %collective-permute-start.23 = (bf16[40,2048]{1,0:T(8,128)(2,1)S(1)}, bf16[40,2048]{1,0:T(8,128)(2,1)S(1)}, u32[]{:S(2)}, u32[]{:S(2)}) collective-permute-start(bf16[40,2048]{1,0:T(8,128)(2,1)S(1)} %get-tuple-element.106), channel_id=1, source_target_pairs={{0,2},{1,3},{2,0},{3,1},{4,6},{5,7},{6,4},{7,5},{8,10},{9,11},{10,... | collective-permute-start | bytes 491528 | tf_op jit(solution)/shard_map/ppermute | solution.py:27
  166.2 25.3 %collective-permute-start.42 = (bf16[80,2048]{1,0:T(8,128)(2,1)S(1)}, bf16[80,2048]{1,0:T(8,128)(2,1)S(1)}, u32[]{:S(2)}, u32[]{:S(2)}) collective-permute-start(bf16[80,2048]{1,0:T(8,128)(2,1)S(1)} %shard_map.140), channel_id=1, source_target_pairs={{0,16},{1,17},{2,18},{3,19},{4,20},{5,21},{6,22},{7,23},{8,24},{9,... | collective-permute-start | bytes 983048 | tf_op jit(solution)/shard_map/ppermute | solution.py:27
  172.0 19.5 %collective-permute-start.43 = (bf16[80,2048]{1,0:T(8,128)(2,1)S(1)}, bf16[80,2048]{1,0:T(8,128)(2,1)S(1)}, u32[]{:S(2)}, u32[]{:S(2)}) collective-permute-start(bf16[80,2048]{1,0:T(8,128)(2,1)S(1)} %get-tuple-element.138), channel_id=1, source_target_pairs={{0,8},{1,9},{2,10},{3,11},{4,12},{5,13},{6,14},{7,15},{8,16},{9,17... | collective-permute-start | bytes 983048 | tf_op jit(solution)/shard_map/ppermute | solution.py:27
  175.4 16.0 %collective-permute-start.38 = (bf16[80,2048]{1,0:T(8,128)(2,1)S(1)}, bf16[80,2048]{1,0:T(8,128)(2,1)S(1)}, u32[]{:S(2)}, u32[]{:S(2)}) collective-permute-start(bf16[80,2048]{1,0:T(8,128)(2,1)S(1)} %get-tuple-element.131), channel_id=1, source_target_pairs={{0,24},{1,25},{2,26},{3,27},{4,28},{5,29},{6,30},{7,31},{8,0},{9,1... | collective-permute-start | bytes 983048 | tf_op jit(solution)/shard_map/ppermute | solution.py:27
  177.8 5.3 %collective-permute-start.24 = (bf16[40,2048]{1,0:T(8,128)(2,1)S(1)}, bf16[40,2048]{1,0:T(8,128)(2,1)S(1)}, u32[]{:S(2)}, u32[]{:S(2)}) collective-permute-start(bf16[40,2048]{1,0:T(8,128)(2,1)S(1)} %get-tuple-element.107), channel_id=1, source_target_pairs={{0,4},{1,5},{2,6},{3,7},{4,0},{5,1},{6,2},{7,3},{8,12},{9,13},{10,... | collective-permute-start | bytes 491528 | tf_op jit(solution)/shard_map/ppermute | solution.py:27
  178.4 6.6 %collective-permute-start.25 = (bf16[40,2048]{1,0:T(8,128)(2,1)S(1)}, bf16[40,2048]{1,0:T(8,128)(2,1)S(1)}, u32[]{:S(2)}, u32[]{:S(2)}) collective-permute-start(bf16[40,2048]{1,0:T(8,128)(2,1)S(1)} %get-tuple-element.108), channel_id=1, source_target_pairs={{0,6},{1,7},{2,4},{3,5},{4,2},{5,3},{6,0},{7,1},{8,14},{9,15},{10,... | collective-permute-start | bytes 491528 | tf_op jit(solution)/shard_map/ppermute | solution.py:27
  (5 other events, 17.1 us)

commit v5 on v4

--- a/solution.py
+++ b/solution.py
@@ -111,30 +111,36 @@
 
 
 def load(arrays):
-    return call(
-        functools.partial(load_kernel, len(arrays)),
-        [struct(*a.shape) for a in arrays],
-        arrays,
-        [pltpu.SemaphoreType.DMA((len(arrays),))],
-        smem=0,
-        hbm=len(arrays),
-        limit=MIB,
-    )
+    count = len(arrays)
+    return pl.pallas_call(
+        functools.partial(load_kernel, count),
+        out_shape=[struct(*a.shape) for a in arrays],
+        in_specs=[pl.BlockSpec(memory_space=pl.ANY)] * count,
+        out_specs=[VMEM] * count,
+        scratch_shapes=[pltpu.SemaphoreType.DMA((count,))],
+        compiler_params=pltpu.CompilerParams(vmem_limit_bytes=MIB),
+        cost_estimate=pl.CostEstimate(
+            flops=0, bytes_accessed=sum(2 * a.size * a.dtype.itemsize for a in arrays), transcendentals=0
+        ),
+    )(*arrays)
 
 
 def project_kernel(hops, depth, head_dim, place, *refs):
-    row_refs, (gain, marks), weights = refs[:hops], refs[hops : hops + 2], refs[hops + 2 : hops + 5]
-    outs, (rows, mixed, held, sems) = refs[hops + 5 : hops + 5 + depth], refs[hops + 5 + depth :]
+    row_refs, marks, sources = refs[: hops - 1], refs[hops - 1], refs[hops : hops + 5]
+    outs, (rows, mixed, own, gain, held, sems) = refs[hops + 5 : hops + 5 + depth], refs[hops + 5 + depth :]
     exp_index, z_index = place[0], place[1]
     tok_rows = row_refs[0].shape[0]
     block_len = hops * tok_rows
-    copies = [pltpu.make_async_copy(weights[i], held.at[i], sems.at[i]) for i in range(3)]
+    targets = [own, gain, *(held.at[i] for i in range(3))]
+    copies = [pltpu.make_async_copy(sources[i], targets[i], sems.at[i]) for i in range(5)]
     for copy in copies:
         copy.start()
-    for hop, row_ref in enumerate(row_refs):
+    copies[0].wait()
+    copies[1].wait()
+    for hop, row_ref in enumerate((own, *row_refs)):
         start = pl.multiple_of((exp_index ^ hop) * tok_rows, 16)
         rows[pl.ds(start, tok_rows), :] = normalize(row_ref[...], gain[...])
-    for part, copy in enumerate(copies):
+    for part, copy in enumerate(copies[2:]):
         copy.wait()
         mixed[part] = f32_dot(rows[...], held[part]).astype(jnp.bfloat16)
     for turn in range(depth):
@@ -264,9 +270,14 @@
         (given if hop & 1 else kept)[hop >> 1] = mixed[pl.ds(start, tok_rows), :]
 
 
-def residual_kernel(top_count, inputs, kept, given, far, gain, noted, residual, ffn_in):
-    summed = kept[0].astype(jnp.float32) + given[0].astype(jnp.float32) + far[...].astype(jnp.float32)
-    rounded = (inputs[...].astype(jnp.float32) + summed).astype(jnp.bfloat16)
+def halves_kernel(inputs, kept, given, here, beyond):
+    summed = kept[0].astype(jnp.float32) + given[0].astype(jnp.float32)
+    here[...] = inputs[...].astype(jnp.float32) + summed
+    beyond[...] = (kept[1].astype(jnp.float32) + given[1].astype(jnp.float32)).astype(jnp.bfloat16)
+
+
+def residual_kernel(top_count, here, far, gain, noted, residual, ffn_in):
+    rounded = (here[...] + far[...].astype(jnp.float32)).astype(jnp.bfloat16)
     residual[...] = rounded
     model_width = rounded.shape[1]
     ffn_in[:, 0:model_width] = normalize(rounded, gain[...])
@@ -306,13 +317,13 @@
         outs[hop][...] = f32_dot(placing, rows[...]).astype(jnp.bfloat16)
 
 
-def expert_kernel(parts, stride, *refs):
+def expert_kernel(starts, *refs):
+    parts = len(starts)
     row_refs, weights = refs[:parts], refs[parts : parts + 6]
     outs, (held,) = refs[parts + 6 : 2 * parts + 6], refs[2 * parts + 6 :]
     across = (((1,), (1,)), ((), ()))
-    count = row_refs[0].shape[0]
-    for part, row_ref in enumerate(row_refs):
-        held[part * stride : part * stride + count, :] = row_ref[...]
+    for start, row_ref in zip(starts, row_refs):
+        held[start : start + row_ref.shape[0], :] = row_ref[...]
     rows = held[...]
     result = None
     for w_gate, w_up, w_down in (weights[:3], weights[3:]):
@@ -321,8 +332,8 @@
         hidden = (gate_part / (1.0 + jnp.exp(-gate_part)) * up_part).astype(jnp.bfloat16)
         product = f32_dot(hidden, w_down[...])
         result = product if result is None else result + product
-    for part, out in enumerate(outs):
-        out[...] = result[part * stride : part * stride + count].astype(jnp.bfloat16)
+    for start, out in zip(starts, outs):
+        out[...] = result[start : start + out.shape[0]].astype(jnp.bfloat16)
 
 
 def combine_kernel(count, capacity, top_count, place, notes, *refs):
@@ -402,19 +413,22 @@
         sent = call(
             functools.partial(project_kernel, exp_count, depth, head_dim),
             [payload] * depth,
-            [place, inputs, near, far, far_near, attn_gain.reshape(1, -1), marks, w_query, w_key, w_value],
+            [place, near, far, far_near, marks, inputs, attn_gain.reshape(1, -1), w_query, w_key, w_value],
             [
                 pltpu.VMEM((block_len, model_width), jnp.bfloat16),
                 pltpu.VMEM((3, block_len, hidden_cols), jnp.bfloat16),
+                pltpu.VMEM((tok_rows, model_width), jnp.bfloat16),
+                pltpu.VMEM((1, model_width), jnp.float32),
                 pltpu.VMEM((3, model_width, hidden_cols), jnp.bfloat16),
-                pltpu.SemaphoreType.DMA((3,)),
+                pltpu.SemaphoreType.DMA((5,)),
             ],
             flops=6 * block_len * model_width * hidden_cols,
-            hbm=3,
+            hbm=5,
         )
         own = [head_out(sent[turn], turn) for turn in range(depth)]
         beside = [swap_core(block) for block in own]
-        other_weights = [swap_core(after(weight, *beside)) for weight in weights]
+        early = [swap_core(after(weight, sent[0])) for weight in weights[:2]]
+        other_weights = [*early, swap_core(after(weights[2], *beside))]
         mixed = call(
             functools.partial(attend_kernel, depth, block_len, head_dim),
             [struct(block_len, head_dim)] * depth,
@@ -445,17 +459,22 @@
         flops=2 * block_len * model_width * hidden_cols,
     )
     given = swap_core(given)
-    beyond = (kept[1].astype(jnp.float32) + given[1].astype(jnp.float32)).astype(jnp.bfloat16)
+    here, beyond = call(
+        halves_kernel,
+        [struct(tok_rows, model_width, dtype=jnp.float32), struct(tok_rows, model_width)],
+        [inputs, kept, given],
+        smem=0,
+    )
     own_weights, other_weights = (
         [gate[0].T, up[0].T, down[0]] for gate, up, down in (weights, other_weights)
     )
-    expert_weights = [*load([after(weight, beyond) for weight in own_weights]), *other_weights]
+    expert_weights = load([after(weight, beyond) for weight in own_weights + other_weights])
     beyond = move(beyond, lambda z, x, y, c: (z, x, y ^ 1, c))
     beyond, expert_weights = lax.optimization_barrier((beyond, expert_weights))
     residual, ffn_in = call(
         functools.partial(residual_kernel, top_count),
         [struct(tok_rows, model_width), struct(tok_rows, model_width + LANES)],
-        [inputs, kept, given, beyond, ffn_gain.reshape(1, -1), noted],
+        [here, beyond, ffn_gain.reshape(1, -1), noted],
         smem=0,
     )
 
@@ -477,30 +496,31 @@
         )
         arrived.append([packed[0]] + [swap_layer(packed[hop], hop) for hop in range(1, 4)])
         notes.append(note)
-    results = []
-    for group, rows in zip(groups, arrived):
-        slots = len(group) * capacity
-        stride = -(-slots // 16) * 16
-        if results:
-            rows = [after(rows[0], results[-1][0])] + rows[1:]
-        results.append(
-            call(
-                functools.partial(expert_kernel, 4, stride),
-                [struct(slots, model_width)] * 4,
-                [*rows, *expert_weights],
-                [pltpu.VMEM((4 * stride, model_width), jnp.bfloat16)],
-                flops=48 * slots * model_width * w_gate.shape[2],
-                smem=0,
-                limit=8 * MIB + 4 * stride * (12 * model_width + 16 * w_gate.shape[2]),
-            )
-        )
+
+    def expert_rows(rows):
+        starts, total = [], 0
+        for row in rows:
+            starts.append(total)
+            total += -(-row.shape[0] // 16) * 16
+        return call(
+            functools.partial(expert_kernel, starts),
+            [struct(*row.shape) for row in rows],
+            [*rows, *expert_weights],
+            [pltpu.VMEM((total, model_width), jnp.bfloat16)],
+            flops=12 * total * model_width * w_gate.shape[2],
+            smem=0,
+            limit=4 * MIB + 32 * 1024 * total,
+        )
+
+    results = [None, expert_rows(arrived[1]), None]
+    far_rows = [after(arrived[2][0], results[1][0])] + arrived[2][1:]
+    both = expert_rows(arrived[0] + far_rows)
+    results[0], results[2] = both[:4], both[4:]
     sums = [None] * depth
-    sent_last = None
-    for index in (0, 2, 1):
+    for index in (1, 2, 0):
         group, rows = groups[index], list(results[index])
-        if sent_last is not None:
-            rows[1:] = [after(row, sent_last) for row in rows[1:]]
-        sent_last = rows[3]
+        if index == 0:
+            rows[1:] = [after(row, sums[1]) for row in rows[1:]]
         rows = [rows[0]] + [swap_layer(rows[hop], hop) for hop in range(1, 4)]
         count = len(group)
         total = count * tok_rows

time: 194 us -> 185 us (0.954)
  Pallas kernels: 56.2 us -> 48.8 us
  waiting for transfers between devices: 62.9 us -> 65.4 us
    pallas_call x14 -> x13, Pallas kernels: 56.2 us -> 43.4 us  [call(): pl.pallas_call(kernel, out_shape=outs, in_specs=[SMEM] * smem + [VMEM] *...]
    pallas_call x0 -> x1, Pallas kernels: none -> 5.43 us  [load(): pl.pallas_call(functools.partial(load_kernel, count), out_shape=[struct(*...]
    ppermute x44, waiting for transfers between devices: 62.9 us -> 65.4 us  [move(): return lax.ppermute(block, AXES, route)]
  transfers between devices with their start and end apart: 44 -> 44, of which waited for: 19 -> 17; matrix products, arithmetic and copies ran while one was open for 2% -> 1% of each run, Pallas kernels for 22% -> 23%
where the time goes in v5:
time: 185 us; the launch traced here: 184 us
  waiting for transfers between devices  65.4 us (35%)
  starting transfers between devices  64.9 us (35%)
  Pallas kernels  48.8 us (26%)
  local copies, waits for them, and re-layouts  3.3 us (2%)
    ppermute x44, waiting for transfers between devices, move(): return lax.ppermute(block, AXES, route)  65.4 us
    ppermute x44, starting transfers between devices, move(): return lax.ppermute(block, AXES, route)  64.9 us
    pallas_call x13, Pallas kernels, call(): pl.pallas_call(kernel, out_shape=outs, in_specs=[SMEM] * smem + [VMEM] *...  43.4 us
    pallas_call x1, Pallas kernels, load(): pl.pallas_call(functools.partial(load_kernel, count), out_shape=[struct(*...  5.43 us
  transfers between devices with their start and end apart: 44, of which 17 were waited for; matrix products, arithmetic and copies ran while one was open for 1% of the time, Pallas kernels for 23%

profile of v5, /device:TPU:0, one launch (start us, length us, event | category | flops | bytes accessed | tf_op | source)
XLA Modules:
  0.0 184.3 jit_solution(8435300759220492173)
XLA Ops:
  0.0 3.0 %collective-permute-start.1 = (bf16[80,2048]{1,0:T(8,128)(2,1)}, bf16[80,2048]{1,0:T(8,128)(2,1)S(1)}, u32[]{:S(2)}, u32[]{:S(2)}) collective-permute-start(bf16[80,2048]{1,0:T(8,128)(2,1)} %inputs.1), channel_id=1, source_target_pairs={{0,2},{1,3},{2,0},{3,1},{4,6},{5,7},{6,4},{7,5},{8,10},{9,11},{10,... | collective-permute-start | bytes 983048 | tf_op jit(solution)/shard_map/ppermute | solution.py:27
  3.0 7.9 %collective-permute-done.1.refs_1_ = bf16[80,2048]{1,0:T(8,128)(2,1)S(1)} collective-permute-done((bf16[80,2048]{1,0:T(8,128)(2,1)}, bf16[80,2048]{1,0:T(8,128)(2,1)S(1)}, u32[]{:S(2)}, u32[]{:S(2)}) %collective-permute-start.1) | collective-permute-done | bytes 327712 | tf_op jit(solution)/shard_map/ppermute | solution.py:27
  14.2 5.3 %shard_map.127 = (bf16[336,384]{1,0:T(8,128)(2,1)S(1)}, bf16[336,384]{1,0:T(8,128)(2,1)S(1)}, bf16[336,384]{1,0:T(8,128)(2,1)S(1)}, bf16[336,384]{1,0:T(8,128)(2,1)S(1)}) custom-call(s32[5]{0:T(128)S(1)} %stack.20.place, bf16[80,2048]{1,0:T(8,128)(2,1)S(1)} %collective-permute-done.refs_0_, bf16[80,2048]{1,0:T(8,128)(2,1)S(1)} %collective-permute-done.1.refs_1_, ...), custom_call_target="tpu_custom_call" | custom-call | flops 2013265920 | bytes 7659540 | tf_op jit(solution)/shard_map/pallas_call | solution.py:83
  20.2 1.9 %collective-permute-start.4 = (bf16[336,384]{1,0:T(8,128)(2,1)S(1)}, bf16[336,384]{1,0:T(8,128)(2,1)S(1)}, u32[]{:S(2)}, u32[]{:S(2)}) collective-permute-start(bf16[336,384]{1,0:T(8,128)(2,1)S(1)} %get-tuple-element.77), channel_id=1, source_target_pairs={{0,8},{1,12},{2,10},{3,14},{4,9},{5,13},{6,11},{7,15},{8,16},{9,20... | collective-permute-start | bytes 774152 | tf_op jit(solution)/shard_map/ppermute | solution.py:27
  22.1 2.6 %collective-permute-start.5 = (bf16[336,384]{1,0:T(8,128)(2,1)S(1)}, bf16[336,384]{1,0:T(8,128)(2,1)S(1)}, u32[]{:S(2)}, u32[]{:S(2)}) collective-permute-start(bf16[336,384]{1,0:T(8,128)(2,1)S(1)} %get-tuple-element.78), channel_id=1, source_target_pairs={{0,16},{1,20},{2,18},{3,22},{4,17},{5,21},{6,19},{7,23},{8,24},{9,... | collective-permute-start | bytes 774152 | tf_op jit(solution)/shard_map/ppermute | solution.py:27
  24.7 1.3 collective-permute-start.6
  26.0 3.2 %collective-permute-start.7 = (bf16[336,384]{1,0:T(8,128)(2,1)S(1)}, bf16[336,384]{1,0:T(8,128)(2,1)S(1)}, u32[]{:S(2)}, u32[]{:S(2)}) collective-permute-start(bf16[336,384]{1,0:T(8,128)(2,1)S(1)} %collective-permute-done.3.refs_0_), channel_id=1, source_target_pairs={{0,1},{1,0},{2,3},{3,2},{4,5},{5,4},{6,7},{7,6},{8,9},{9,8},{10,11... | collective-permute-start | bytes 774152 | tf_op jit(solution)/shard_map/ppermute | solution.py:27
  29.2 5.4 %collective-permute-start.8 = (bf16[336,384]{1,0:T(8,128)(2,1)S(1)}, bf16[336,384]{1,0:T(8,128)(2,1)S(1)}, u32[]{:S(2)}, u32[]{:S(2)}) collective-permute-start(bf16[336,384]{1,0:T(8,128)(2,1)S(1)} %collective-permute-done.4.refs_1_), channel_id=1, source_target_pairs={{0,1},{1,0},{2,3},{3,2},{4,5},{5,4},{6,7},{7,6},{8,9},{9,8},{10,11... | collective-permute-start | bytes 774152 | tf_op jit(solution)/shard_map/ppermute | solution.py:27
  34.6 7.5 %collective-permute-done.5.refs_2_ = bf16[336,384]{1,0:T(8,128)(2,1)S(1)} collective-permute-done((bf16[336,384]{1,0:T(8,128)(2,1)S(1)}, bf16[336,384]{1,0:T(8,128)(2,1)S(1)}, u32[]{:S(2)}, u32[]{:S(2)}) %collective-permute-start.5) | collective-permute-done | bytes 258080 | tf_op jit(solution)/shard_map/ppermute | solution.py:27
  44.4 7.9 %shard_map.128 = (bf16[320,128]{1,0:T(8,128)(2,1)S(1)}, bf16[320,128]{1,0:T(8,128)(2,1)S(1)}, bf16[320,128]{1,0:T(8,128)(2,1)S(1)}, bf16[320,128]{1,0:T(8,128)(2,1)S(1)}) custom-call(s32[5]{0:T(128)S(1)} %stack.20.place, bf16[336,384]{1,0:T(8,128)(2,1)S(1)} %collective-permute-done.3.refs_0_, bf16[336,384]{1,0:T(8,128)(2,1)S(1)} %collective-permute-done.4.refs_1_, ...), custom_call_target="tpu_custom_call" | custom-call | flops 1677721600 | bytes 2064404 | tf_op jit(solution)/shard_map/pallas_call | solution.py:83
  53.0 7.1 %collective-permute-start.12 = (bf16[320,128]{1,0:T(8,128)(2,1)S(1)}, bf16[320,128]{1,0:T(8,128)(2,1)S(1)}, u32[]{:S(2)}, u32[]{:S(2)}) collective-permute-start(bf16[320,128]{1,0:T(8,128)(2,1)S(1)} %get-tuple-element.81), channel_id=1, source_target_pairs={{0,24},{1,28},{2,26},{3,30},{4,25},{5,29},{6,27},{7,31},{8,0},{9,4... | collective-permute-start | bytes 245768 | tf_op jit(solution)/shard_map/ppermute | solution.py:27
  60.2 2.0 %collective-permute-done.12.refs_1_ = bf16[320,128]{1,0:T(8,128)(2,1)S(1)} collective-permute-done((bf16[320,128]{1,0:T(8,128)(2,1)S(1)}, bf16[320,128]{1,0:T(8,128)(2,1)S(1)}, u32[]{:S(2)}, u32[]{:S(2)}) %collective-permute-start.12) | collective-permute-done | bytes 81952 | tf_op jit(solution)/shard_map/ppermute | solution.py:27
  63.2 2.3 %collective-permute-done.13.refs_2_ = bf16[320,128]{1,0:T(8,128)(2,1)S(1)} collective-permute-done((bf16[320,128]{1,0:T(8,128)(2,1)S(1)}, bf16[320,128]{1,0:T(8,128)(2,1)S(1)}, u32[]{:S(2)}, u32[]{:S(2)}) %collective-permute-start.13) | collective-permute-done | bytes 81952 | tf_op jit(solution)/shard_map/ppermute | solution.py:27
  65.5 4.2 %collective-permute-done.14.refs_3_ = bf16[320,128]{1,0:T(8,128)(2,1)S(1)} collective-permute-done((bf16[320,128]{1,0:T(8,128)(2,1)S(1)}, bf16[320,128]{1,0:T(8,128)(2,1)S(1)}, u32[]{:S(2)}, u32[]{:S(2)}) %collective-permute-start.14) | collective-permute-done | bytes 81952 | tf_op jit(solution)/shard_map/ppermute | solution.py:27
  69.7 1.5 shard_map.129
  71.2 1.9 %collective-permute-start.15 = (bf16[2,80,2048]{2,1,0:T(8,128)(2,1)S(1)}, bf16[2,80,2048]{2,1,0:T(8,128)(2,1)S(1)}, u32[]{:S(2)}, u32[]{:S(2)}) collective-permute-start(bf16[2,80,2048]{2,1,0:T(8,128)(2,1)S(1)} %get-tuple-element.85), channel_id=1, source_target_pairs={{0,1},{1,0},{2,3},{3,2},{4,5},{5,4},{6,7},{7,6},{8,9},{9,8},{10,11... | collective-permute-start | bytes 1966088 | tf_op jit(solution)/shard_map/ppermute | solution.py:27
  73.1 1.7 collective-permute-done.15.given
  75.6 1.5 collective-permute-start.16
  78.7 5.4 %shard_map.131 = (bf16[704,2048]{1,0:T(8,128)(2,1)S(1)}, bf16[704,2048]{1,0:T(8,128)(2,1)S(1)}, bf16[704,2048]{1,0:T(8,128)(2,1)S(1)}, bf16[704,2048]{1,0:T(8,12...) custom-call(bf16[704,2048]{1,0:T(8,128)(2,1)S(1)} %bitcast.22, ...), custom_call_target="tpu_custom_call" | custom-call | bytes 34603008 | tf_op jit(solution)/shard_map/pallas_call | solution.py:115
  84.1 1.8 collective-permute-done.16.far
  87.5 3.5 %collective-permute-start.25 = (bf16[80,2176]{1,0:T(8,128)(2,1)S(1)}, bf16[80,2176]{1,0:T(8,128)(2,1)S(1)}, u32[]{:S(2)}, u32[]{:S(2)}) collective-permute-start(bf16[80,2176]{1,0:T(8,128)(2,1)S(1)} %get-tuple-element.105.refs_0_), channel_id=1, source_target_pairs={{0,24},{1,25},{2,26},{3,27},{4,28},{5,29},{6,30},{7,31},{8,0},{9,1... | collective-permute-start | bytes 1044488 | tf_op jit(solution)/shard_map/ppermute | solution.py:27
  91.1 9.0 %collective-permute-done.23.refs_0_ = bf16[80,2176]{1,0:T(8,128)(2,1)S(1)} collective-permute-done((bf16[80,2176]{1,0:T(8,128)(2,1)S(1)}, bf16[80,2176]{1,0:T(8,128)(2,1)S(1)}, u32[]{:S(2)}, u32[]{:S(2)}) %collective-permute-start.23) | collective-permute-done | bytes 348192 | tf_op jit(solution)/shard_map/ppermute | solution.py:27
  100.1 1.5 shard_map.133
  101.6 2.8 %collective-permute-done.25.refs_1_ = bf16[80,2176]{1,0:T(8,128)(2,1)S(1)} collective-permute-done((bf16[80,2176]{1,0:T(8,128)(2,1)S(1)}, bf16[80,2176]{1,0:T(8,128)(2,1)S(1)}, u32[]{:S(2)}, u32[]{:S(2)}) %collective-permute-start.25) | collective-permute-done | bytes 348192 | tf_op jit(solution)/shard_map/ppermute | solution.py:27
  104.4 1.7 shard_map.134
  106.0 1.6 collective-permute-start.26
  107.6 1.4 collective-permute-start.27
  109.6 1.5 collective-permute-start.20
  111.1 2.5 %collective-permute-done.24.refs_0_ = bf16[80,2176]{1,0:T(8,128)(2,1)S(1)} collective-permute-done((bf16[80,2176]{1,0:T(8,128)(2,1)S(1)}, bf16[80,2176]{1,0:T(8,128)(2,1)S(1)}, u32[]{:S(2)}, u32[]{:S(2)}) %collective-permute-start.24) | collective-permute-done | bytes 348192 | tf_op jit(solution)/shard_map/ppermute | solution.py:27
  113.6 1.4 collective-permute-start.21
  115.0 1.5 shard_map.135
  116.5 10.6 %collective-permute-done.20.refs_1_ = bf16[40,2048]{1,0:T(8,128)(2,1)S(1)} collective-permute-done((bf16[40,2048]{1,0:T(8,128)(2,1)S(1)}, bf16[40,2048]{1,0:T(8,128)(2,1)S(1)}, u32[]{:S(2)}, u32[]{:S(2)}) %collective-permute-start.20) | collective-permute-done | bytes 163872 | tf_op jit(solution)/shard_map/ppermute | solution.py:27
  127.1 3.3 %collective-permute-start.22 = (bf16[40,2048]{1,0:T(8,128)(2,1)S(1)}, bf16[40,2048]{1,0:T(8,128)(2,1)S(1)}, u32[]{:S(2)}, u32[]{:S(2)}) collective-permute-start(bf16[40,2048]{1,0:T(8,128)(2,1)S(1)} %get-tuple-element.110), channel_id=1, source_target_pairs={{0,6},{1,7},{2,4},{3,5},{4,2},{5,3},{6,0},{7,1},{8,14},{9,15},{10,... | collective-permute-start | bytes 491528 | tf_op jit(solution)/shard_map/ppermute | solution.py:27
  131.0 2.9 %collective-permute-start.31 = (bf16[40,2048]{1,0:T(8,128)(2,1)S(1)}, bf16[40,2048]{1,0:T(8,128)(2,1)S(1)}, u32[]{:S(2)}, u32[]{:S(2)}) collective-permute-start(bf16[40,2048]{1,0:T(8,128)(2,1)S(1)} %get-tuple-element.128), channel_id=1, source_target_pairs={{0,6},{1,7},{2,4},{3,5},{4,2},{5,3},{6,0},{7,1},{8,14},{9,15},{10,... | collective-permute-start | bytes 491528 | tf_op jit(solution)/shard_map/ppermute | solution.py:27
  133.9 6.4 %shard_map.136 = (bf16[80,2048]{1,0:T(8,128)(2,1)S(1)}, bf16[80,2048]{1,0:T(8,128)(2,1)S(1)}, bf16[80,2048]{1,0:T(8,128)(2,1)S(1)}, bf16[80,2048]{1,0:T(8,128)(2,1)S(1)}) custom-call(bf16[80,2048]{1,0:T(8,128)(2,1)S(1)} %get-tuple-element.112.refs_0_, bf16[80,2048]{1,0:T(8,128)(2,1)S(1)} %collective-permute-done.26.refs_1_, ...), custom_call_target="tpu_custom_call" | custom-call | flops 5536481280 | bytes 18612224 | tf_op jit(solution)/shard_map/pallas_call | solution.py:83
  141.0 2.9 %collective-permute-start.34 = (bf16[80,2048]{1,0:T(8,128)(2,1)S(1)}, bf16[80,2048]{1,0:T(8,128)(2,1)S(1)}, u32[]{:S(2)}, u32[]{:S(2)}) collective-permute-start(bf16[80,2048]{1,0:T(8,128)(2,1)S(1)} %get-tuple-element.134), channel_id=1, source_target_pairs={{0,6},{1,7},{2,4},{3,5},{4,2},{5,3},{6,0},{7,1},{8,14},{9,15},{10,... | collective-permute-start | bytes 983048 | tf_op jit(solution)/shard_map/ppermute | solution.py:27
  143.9 7.9 %shard_map.137 = (bf16[40,2048]{1,0:T(8,128)(2,1)S(1)}, bf16[40,2048]{1,0:T(8,128)(2,1)S(1)}, bf16[40,2048]{1,0:T(8,128)(2,1)S(1)}, bf16[40,2048]{1,0:T(8,128)(2...) custom-call(bf16[40,2048]{1,0:T(8,128)(2,1)S(1)} %get-tuple-element., ...), custom_call_target="tpu_custom_call" | custom-call | flops 6643777536 | bytes 18612224 | tf_op jit(solution)/shard_map/pallas_call | solution.py:83
  152.1 2.0 %collective-permute-start.40 = (bf16[40,2048]{1,0:T(8,128)(2,1)S(1)}, bf16[40,2048]{1,0:T(8,128)(2,1)S(1)}, u32[]{:S(2)}, u32[]{:S(2)}) collective-permute-start(bf16[40,2048]{1,0:T(8,128)(2,1)S(1)} %get-tuple-element.144), channel_id=1, source_target_pairs={{0,4},{1,5},{2,6},{3,7},{4,0},{5,1},{6,2},{7,3},{8,12},{9,13},{10,... | collective-permute-start | bytes 491528 | tf_op jit(solution)/shard_map/ppermute | solution.py:27
  155.3 3.1 %shard_map.138 = (bf16[80,2048]{1,0:T(8,128)(2,1)S(1)}, bf16[80,2048]{1,0:T(8,128)(2,1)S(1)}) custom-call(s32[5]{0:T(128)S(1)} %stack.20.place, bf16[160,128]{1,0:T(8,128)(2,1)S(1)} %get-tuple-element.131.notes, bf16[80,2048]{1,0:T(8,128)(2,1)S(1)} %get-tuple-element.124.refs_0_, bf16[80,2048]{1,0:T(8,128)(2,1)S(1)} %collective-permute-done.32.refs_1_, ...), custom_call_target="tpu_custom_call" | custom-call | flops 419430400 | bytes 1351700 | tf_op jit(solution)/shard_map/pallas_call | solution.py:83
  158.4 2.3 %collective-permute-start.38 = (bf16[80,2048]{1,0:T(8,128)(2,1)S(1)}, bf16[80,2048]{1,0:T(8,128)(2,1)S(1)}, u32[]{:S(2)}, u32[]{:S(2)}) collective-permute-start(bf16[80,2048]{1,0:T(8,128)(2,1)S(1)} %get-tuple-element.135), channel_id=1, source_target_pairs={{0,24},{1,25},{2,26},{3,27},{4,28},{5,29},{6,30},{7,31},{8,0},{9,1... | collective-permute-start | bytes 983048 | tf_op jit(solution)/shard_map/ppermute | solution.py:27
  161.2 2.8 %collective-permute-start.43 = (bf16[80,2048]{1,0:T(8,128)(2,1)S(1)}, bf16[80,2048]{1,0:T(8,128)(2,1)S(1)}, u32[]{:S(2)}, u32[]{:S(2)}) collective-permute-start(bf16[80,2048]{1,0:T(8,128)(2,1)S(1)} %get-tuple-element.146), channel_id=1, source_target_pairs={{0,8},{1,9},{2,10},{3,11},{4,12},{5,13},{6,14},{7,15},{8,16},{9,17... | collective-permute-start | bytes 983048 | tf_op jit(solution)/shard_map/ppermute | solution.py:27
  163.9 2.3 %shard_map.140 = bf16[80,2048]{1,0:T(8,128)(2,1)S(1)} custom-call(s32[5]{0:T(128)S(1)} %stack.20.place, bf16[80,128]{1,0:T(8,128)(2,1)S(1)} %get-tuple-element.141.notes, bf16[40,2048]{1,0:T(8,128)(2,1)S(1)} %get-tuple-element.142.refs_0_, bf16[40,2048]{1,0:T(8,128)(2,1)S(1)} %collective-permute-done.39.refs_1_, ...), custom_call_target="tpu_custom_call" | custom-call | flops 104857600 | bytes 675860 | tf_op jit(solution)/shard_map/pallas_call | solution.py:83
  166.2 1.4 collective-permute-start.42
  167.6 1.7 collective-permute-start.36
  169.8 3.2 %collective-permute-done.36.refs_2_ = bf16[40,2048]{1,0:T(8,128)(2,1)S(1)} collective-permute-done((bf16[40,2048]{1,0:T(8,128)(2,1)S(1)}, bf16[40,2048]{1,0:T(8,128)(2,1)S(1)}, u32[]{:S(2)}, u32[]{:S(2)}) %collective-permute-start.36) | collective-permute-done | bytes 163872 | tf_op jit(solution)/shard_map/ppermute | solution.py:27
  173.0 2.6 %collective-permute-done.37.refs_3_ = bf16[40,2048]{1,0:T(8,128)(2,1)S(1)} collective-permute-done((bf16[40,2048]{1,0:T(8,128)(2,1)S(1)}, bf16[40,2048]{1,0:T(8,128)(2,1)S(1)}, u32[]{:S(2)}, u32[]{:S(2)}) %collective-permute-start.37) | collective-permute-done | bytes 163872 | tf_op jit(solution)/shard_map/ppermute | solution.py:27
  175.5 2.3 %shard_map.139 = bf16[80,2048]{1,0:T(8,128)(2,1)S(1)} custom-call(s32[5]{0:T(128)S(1)} %stack.20.place, bf16[80,128]{1,0:T(8,128)(2,1)S(1)} %get-tuple-element.106.notes, bf16[40,2048]{1,0:T(8,128)(2,1)S(1)} %get-tuple-element.129.refs_0_, bf16[40,2048]{1,0:T(8,128)(2,1)S(1)} %collective-permute-done.35.refs_1_, ...), custom_call_target="tpu_custom_call" | custom-call | flops 104857600 | bytes 675860 | tf_op jit(solution)/shard_map/pallas_call | solution.py:83
  177.9 5.5 %collective-permute-done.42 = bf16[80,2048]{1,0:T(8,128)(2,1)S(1)} collective-permute-done((bf16[80,2048]{1,0:T(8,128)(2,1)S(1)}, bf16[80,2048]{1,0:T(8,128)(2,1)S(1)}, u32[]{:S(2)}, u32[]{:S(2)}) %collective-permute-start.42) | collective-permute-done | bytes 327712 | tf_op jit(solution)/shard_map/ppermute | solution.py:27
  (80 shorter events, 17.1 us)
Async XLA Ops:
  0.0 10.9 %collective-permute-start.1 = (bf16[80,2048]{1,0:T(8,128)(2,1)}, bf16[80,2048]{1,0:T(8,128)(2,1)S(1)}, u32[]{:S(2)}, u32[]{:S(2)}) collective-permute-start(bf16[80,2048]{1,0:T(8,128)(2,1)} %inputs.1), channel_id=1, source_target_pairs={{0,2},{1,3},{2,0},{3,1},{4,6},{5,7},{6,4},{7,5},{8,10},{9,11},{10,... | collective-permute-start | bytes 983048 | tf_op jit(solution)/shard_map/ppermute | solution.py:27
  3.0 8.8 %collective-permute-start = (bf16[80,2048]{1,0:T(8,128)(2,1)}, bf16[80,2048]{1,0:T(8,128)(2,1)S(1)}, u32[]{:S(2)}, u32[]{:S(2)}) collective-permute-start(bf16[80,2048]{1,0:T(8,128)(2,1)} %inputs.1), channel_id=1, source_target_pairs={{0,1},{1,0},{2,3},{3,2},{4,5},{5,4},{6,7},{7,6},{8,9},{9,8},{10,11... | collective-permute-start | bytes 983048 | tf_op jit(solution)/shard_map/ppermute | solution.py:27
  10.9 1.6 collective-permute-start.2
  14.2 28.4 %copy-start = (bf16[1,2048,704]{1,2,0:T(8,128)(2,1)S(1)}, bf16[1,2048,704]{1,2,0:T(8,128)(2,1)}, u32[]{:S(2)}) copy-start(bf16[1,2048,704]{1,2,0:T(8,128)(2,1)} %param.21) | copy-start | bytes 8650756
  19.5 6.5 %collective-permute-start.3 = (bf16[336,384]{1,0:T(8,128)(2,1)S(1)}, bf16[336,384]{1,0:T(8,128)(2,1)S(1)}, u32[]{:S(2)}, u32[]{:S(2)}) collective-permute-start(bf16[336,384]{1,0:T(8,128)(2,1)S(1)} %get-tuple-element.76), channel_id=1, source_target_pairs={{0,0},{1,4},{2,2},{3,6},{4,1},{5,5},{6,3},{7,7},{8,8},{9,12},{10,1... | collective-permute-start | bytes 774152 | tf_op jit(solution)/shard_map/ppermute | solution.py:27
  20.2 9.0 %collective-permute-start.4 = (bf16[336,384]{1,0:T(8,128)(2,1)S(1)}, bf16[336,384]{1,0:T(8,128)(2,1)S(1)}, u32[]{:S(2)}, u32[]{:S(2)}) collective-permute-start(bf16[336,384]{1,0:T(8,128)(2,1)S(1)} %get-tuple-element.77), channel_id=1, source_target_pairs={{0,8},{1,12},{2,10},{3,14},{4,9},{5,13},{6,11},{7,15},{8,16},{9,20... | collective-permute-start | bytes 774152 | tf_op jit(solution)/shard_map/ppermute | solution.py:27
  22.1 20.1 %collective-permute-start.5 = (bf16[336,384]{1,0:T(8,128)(2,1)S(1)}, bf16[336,384]{1,0:T(8,128)(2,1)S(1)}, u32[]{:S(2)}, u32[]{:S(2)}) collective-permute-start(bf16[336,384]{1,0:T(8,128)(2,1)S(1)} %get-tuple-element.78), channel_id=1, source_target_pairs={{0,16},{1,20},{2,18},{3,22},{4,17},{5,21},{6,19},{7,23},{8,24},{9,... | collective-permute-start | bytes 774152 | tf_op jit(solution)/shard_map/ppermute | solution.py:27
  24.7 45.0 %copy-start.5 = (bf16[512,2048]{1,0:T(8,128)(2,1)S(1)}, bf16[512,2048]{1,0:T(8,128)(2,1)}, u32[]{:S(2)}) copy-start(bf16[512,2048]{1,0:T(8,128)(2,1)} %refs_4_.3) | copy-start | bytes 6291460
  24.7 50.1 %copy-start.1 = (bf16[80,2048]{1,0:T(8,128)(2,1)S(1)}, bf16[80,2048]{1,0:T(8,128)(2,1)}, u32[]{:S(2)}) copy-start(bf16[80,2048]{1,0:T(8,128)(2,1)} %inputs.1) | copy-start | bytes 983044
  24.7 17.9 %collective-permute-start.6 = (bf16[336,384]{1,0:T(8,128)(2,1)S(1)}, bf16[336,384]{1,0:T(8,128)(2,1)S(1)}, u32[]{:S(2)}, u32[]{:S(2)}) collective-permute-start(bf16[336,384]{1,0:T(8,128)(2,1)S(1)} %get-tuple-element.79), channel_id=1, source_target_pairs={{0,24},{1,28},{2,26},{3,30},{4,25},{5,29},{6,27},{7,31},{8,0},{9,4... | collective-permute-start | bytes 774152 | tf_op jit(solution)/shard_map/ppermute | solution.py:27
  26.0 17.0 %collective-permute-start.7 = (bf16[336,384]{1,0:T(8,128)(2,1)S(1)}, bf16[336,384]{1,0:T(8,128)(2,1)S(1)}, u32[]{:S(2)}, u32[]{:S(2)}) collective-permute-start(bf16[336,384]{1,0:T(8,128)(2,1)S(1)} %collective-permute-done.3.refs_0_), channel_id=1, source_target_pairs={{0,1},{1,0},{2,3},{3,2},{4,5},{5,4},{6,7},{7,6},{8,9},{9,8},{10,11... | collective-permute-start | bytes 774152 | tf_op jit(solution)/shard_map/ppermute | solution.py:27
  29.2 14.0 %collective-permute-start.8 = (bf16[336,384]{1,0:T(8,128)(2,1)S(1)}, bf16[336,384]{1,0:T(8,128)(2,1)S(1)}, u32[]{:S(2)}, u32[]{:S(2)}) collective-permute-start(bf16[336,384]{1,0:T(8,128)(2,1)S(1)} %collective-permute-done.4.refs_1_), channel_id=1, source_target_pairs={{0,1},{1,0},{2,3},{3,2},{4,5},{5,4},{6,7},{7,6},{8,9},{9,8},{10,11... | collective-permute-start | bytes 774152 | tf_op jit(solution)/shard_map/ppermute | solution.py:27
  42.1 1.5 collective-permute-start.9
  42.5 1.5 collective-permute-start.10
  42.6 36.0 %collective-permute-start.17 = (bf16[1,2048,704]{1,2,0:T(8,128)(2,1)S(1)}, bf16[1,2048,704]{1,2,0:T(8,128)(2,1)}, u32[]{:S(2)}, u32[]{:S(2)}) collective-permute-start(bf16[1,2048,704]{1,2,0:T(8,128)(2,1)S(1)} %copy-done), channel_id=1, source_target_pairs={{0,1},{1,0},{2,3},{3,2},{4,5},{5,4},{6,7},{7,6},{8,9},{9,8},{10,11... | collective-permute-start | bytes 8650760 | tf_op jit(solution)/shard_map/ppermute | solution.py:27
  43.0 35.6 %collective-permute-start.18 = (bf16[1,2048,704]{1,2,0:T(8,128)(2,1)}, bf16[1,2048,704]{1,2,0:T(8,128)(2,1)}, u32[]{:S(2)}, u32[]{:S(2)}) collective-permute-start(bf16[1,2048,704]{1,2,0:T(8,128)(2,1)} %param.22), channel_id=1, source_target_pairs={{0,1},{1,0},{2,3},{3,2},{4,5},{5,4},{6,7},{7,6},{8,9},{9,8},{10,11... | collective-permute-start | bytes 8650760 | tf_op jit(solution)/shard_map/ppermute | solution.py:27
  44.1 34.6 %collective-permute-start.19 = (bf16[1,704,2048]{2,1,0:T(8,128)(2,1)}, bf16[1,704,2048]{2,1,0:T(8,128)(2,1)}, u32[]{:S(2)}, u32[]{:S(2)}) collective-permute-start(bf16[1,704,2048]{2,1,0:T(8,128)(2,1)} %param.23), channel_id=1, source_target_pairs={{0,1},{1,0},{2,3},{3,2},{4,5},{5,4},{6,7},{7,6},{8,9},{9,8},{10,11... | collective-permute-start | bytes 8650760 | tf_op jit(solution)/shard_map/ppermute | solution.py:27
  52.3 24.8 %copy-start.7 = (s32[80,6]{0,1:T(8,128)S(1)}, s32[80,6]{0,1:T(8,128)}, u32[]{:S(2)}) copy-start(s32[80,6]{0,1:T(8,128)} %param.24) | copy-start | bytes 5764
  52.4 7.8 %collective-permute-start.11 = (bf16[320,128]{1,0:T(8,128)(2,1)S(1)}, bf16[320,128]{1,0:T(8,128)(2,1)S(1)}, u32[]{:S(2)}, u32[]{:S(2)}) collective-permute-start(bf16[320,128]{1,0:T(8,128)(2,1)S(1)} %get-tuple-element.80), channel_id=1, source_target_pairs={{0,0},{1,4},{2,2},{3,6},{4,1},{5,5},{6,3},{7,7},{8,8},{9,12},{10,1... | collective-permute-start | bytes 245768 | tf_op jit(solution)/shard_map/ppermute | solution.py:27
  53.0 9.2 %collective-permute-start.12 = (bf16[320,128]{1,0:T(8,128)(2,1)S(1)}, bf16[320,128]{1,0:T(8,128)(2,1)S(1)}, u32[]{:S(2)}, u32[]{:S(2)}) collective-permute-start(bf16[320,128]{1,0:T(8,128)(2,1)S(1)} %get-tuple-element.81), channel_id=1, source_target_pairs={{0,24},{1,28},{2,26},{3,30},{4,25},{5,29},{6,27},{7,31},{8,0},{9,4... | collective-permute-start | bytes 245768 | tf_op jit(solution)/shard_map/ppermute | solution.py:27
  60.2 5.3 %collective-permute-start.13 = (bf16[320,128]{1,0:T(8,128)(2,1)S(1)}, bf16[320,128]{1,0:T(8,128)(2,1)S(1)}, u32[]{:S(2)}, u32[]{:S(2)}) collective-permute-start(bf16[320,128]{1,0:T(8,128)(2,1)S(1)} %get-tuple-element.82), channel_id=1, source_target_pairs={{0,16},{1,20},{2,18},{3,22},{4,17},{5,21},{6,19},{7,23},{8,24},{9,... | collective-permute-start | bytes 245768 | tf_op jit(solution)/shard_map/ppermute | solution.py:27
  62.2 7.4 %collective-permute-start.14 = (bf16[320,128]{1,0:T(8,128)(2,1)S(1)}, bf16[320,128]{1,0:T(8,128)(2,1)S(1)}, u32[]{:S(2)}, u32[]{:S(2)}) collective-permute-start(bf16[320,128]{1,0:T(8,128)(2,1)S(1)} %get-tuple-element.83), channel_id=1, source_target_pairs={{0,8},{1,12},{2,10},{3,14},{4,9},{5,13},{6,11},{7,15},{8,16},{9,20... | collective-permute-start | bytes 245768 | tf_op jit(solution)/shard_map/ppermute | solution.py:27
  71.2 3.6 %collective-permute-start.15 = (bf16[2,80,2048]{2,1,0:T(8,128)(2,1)S(1)}, bf16[2,80,2048]{2,1,0:T(8,128)(2,1)S(1)}, u32[]{:S(2)}, u32[]{:S(2)}) collective-permute-start(bf16[2,80,2048]{2,1,0:T(8,128)(2,1)S(1)} %get-tuple-element.85), channel_id=1, source_target_pairs={{0,1},{1,0},{2,3},{3,2},{4,5},{5,4},{6,7},{7,6},{8,9},{9,8},{10,11... | collective-permute-start | bytes 1966088 | tf_op jit(solution)/shard_map/ppermute | solution.py:27
  75.6 10.3 %collective-permute-start.16 = (bf16[80,2048]{1,0:T(8,128)(2,1)}, bf16[80,2048]{1,0:T(8,128)(2,1)}, u32[]{:S(2)}, u32[]{:S(2)}) collective-permute-start(bf16[80,2048]{1,0:T(8,128)(2,1)} %get-tuple-element.87), channel_id=1, source_target_pairs={{0,2},{1,3},{2,0},{3,1},{4,6},{5,7},{6,4},{7,5},{8,10},{9,11},{10,... | collective-permute-start | bytes 983048 | tf_op jit(solution)/shard_map/ppermute | solution.py:27
  87.2 12.9 %collective-permute-start.23 = (bf16[80,2176]{1,0:T(8,128)(2,1)S(1)}, bf16[80,2176]{1,0:T(8,128)(2,1)S(1)}, u32[]{:S(2)}, u32[]{:S(2)}) collective-permute-start(bf16[80,2176]{1,0:T(8,128)(2,1)S(1)} %get-tuple-element.105.refs_0_), channel_id=1, source_target_pairs={{0,8},{1,9},{2,10},{3,11},{4,12},{5,13},{6,14},{7,15},{8,16},{9,17... | collective-permute-start | bytes 1044488 | tf_op jit(solution)/shard_map/ppermute | solution.py:27
  87.5 16.8 %collective-permute-start.25 = (bf16[80,2176]{1,0:T(8,128)(2,1)S(1)}, bf16[80,2176]{1,0:T(8,128)(2,1)S(1)}, u32[]{:S(2)}, u32[]{:S(2)}) collective-permute-start(bf16[80,2176]{1,0:T(8,128)(2,1)S(1)} %get-tuple-element.105.refs_0_), channel_id=1, source_target_pairs={{0,24},{1,25},{2,26},{3,27},{4,28},{5,29},{6,30},{7,31},{8,0},{9,1... | collective-permute-start | bytes 1044488 | tf_op jit(solution)/shard_map/ppermute | solution.py:27
  100.1 13.5 %collective-permute-start.24 = (bf16[80,2176]{1,0:T(8,128)(2,1)S(1)}, bf16[80,2176]{1,0:T(8,128)(2,1)S(1)}, u32[]{:S(2)}, u32[]{:S(2)}) collective-permute-start(bf16[80,2176]{1,0:T(8,128)(2,1)S(1)} %collective-permute-done.23.refs_0_), channel_id=1, source_target_pairs={{0,8},{1,9},{2,10},{3,11},{4,12},{5,13},{6,14},{7,15},{8,16},{9,17... | collective-permute-start | bytes 1044488 | tf_op jit(solution)/shard_map/ppermute | solution.py:27
  106.0 24.4 %collective-permute-start.26 = (bf16[80,2048]{1,0:T(8,128)(2,1)S(1)}, bf16[80,2048]{1,0:T(8,128)(2,1)S(1)}, u32[]{:S(2)}, u32[]{:S(2)}) collective-permute-start(bf16[80,2048]{1,0:T(8,128)(2,1)S(1)} %get-tuple-element.115), channel_id=1, source_target_pairs={{0,2},{1,3},{2,0},{3,1},{4,6},{5,7},{6,4},{7,5},{8,10},{9,11},{10,... | collective-permute-start | bytes 983048 | tf_op jit(solution)/shard_map/ppermute | solution.py:27
  107.6 22.8 %collective-permute-start.27 = (bf16[80,2048]{1,0:T(8,128)(2,1)S(1)}, bf16[80,2048]{1,0:T(8,128)(2,1)S(1)}, u32[]{:S(2)}, u32[]{:S(2)}) collective-permute-start(bf16[80,2048]{1,0:T(8,128)(2,1)S(1)} %get-tuple-element.116), channel_id=1, source_target_pairs={{0,4},{1,5},{2,6},{3,7},{4,0},{5,1},{6,2},{7,3},{8,12},{9,13},{10,... | collective-permute-start | bytes 983048 | tf_op jit(solution)/shard_map/ppermute | solution.py:27
  109.1 22.0 %collective-permute-start.28 = (bf16[80,2048]{1,0:T(8,128)(2,1)S(1)}, bf16[80,2048]{1,0:T(8,128)(2,1)S(1)}, u32[]{:S(2)}, u32[]{:S(2)}) collective-permute-start(bf16[80,2048]{1,0:T(8,128)(2,1)S(1)} %get-tuple-element.117), channel_id=1, source_target_pairs={{0,6},{1,7},{2,4},{3,5},{4,2},{5,3},{6,0},{7,1},{8,14},{9,15},{10,... | collective-permute-start | bytes 983048 | tf_op jit(solution)/shard_map/ppermute | solution.py:27
  109.6 17.5 %collective-permute-start.20 = (bf16[40,2048]{1,0:T(8,128)(2,1)S(1)}, bf16[40,2048]{1,0:T(8,128)(2,1)S(1)}, u32[]{:S(2)}, u32[]{:S(2)}) collective-permute-start(bf16[40,2048]{1,0:T(8,128)(2,1)S(1)} %get-tuple-element.108), channel_id=1, source_target_pairs={{0,2},{1,3},{2,0},{3,1},{4,6},{5,7},{6,4},{7,5},{8,10},{9,11},{10,... | collective-permute-start | bytes 491528 | tf_op jit(solution)/shard_map/ppermute | solution.py:27
  113.6 26.7 %collective-permute-start.21 = (bf16[40,2048]{1,0:T(8,128)(2,1)S(1)}, bf16[40,2048]{1,0:T(8,128)(2,1)S(1)}, u32[]{:S(2)}, u32[]{:S(2)}) collective-permute-start(bf16[40,2048]{1,0:T(8,128)(2,1)S(1)} %get-tuple-element.109), channel_id=1, source_target_pairs={{0,4},{1,5},{2,6},{3,7},{4,0},{5,1},{6,2},{7,3},{8,12},{9,13},{10,... | collective-permute-start | bytes 491528 | tf_op jit(solution)/shard_map/ppermute | solution.py:27
  127.1 13.3 %collective-permute-start.22 = (bf16[40,2048]{1,0:T(8,128)(2,1)S(1)}, bf16[40,2048]{1,0:T(8,128)(2,1)S(1)}, u32[]{:S(2)}, u32[]{:S(2)}) collective-permute-start(bf16[40,2048]{1,0:T(8,128)(2,1)S(1)} %get-tuple-element.110), channel_id=1, source_target_pairs={{0,6},{1,7},{2,4},{3,5},{4,2},{5,3},{6,0},{7,1},{8,14},{9,15},{10,... | collective-permute-start | bytes 491528 | tf_op jit(solution)/shard_map/ppermute | solution.py:27
  130.4 10.5 %collective-permute-start.29 = (bf16[40,2048]{1,0:T(8,128)(2,1)S(1)}, bf16[40,2048]{1,0:T(8,128)(2,1)S(1)}, u32[]{:S(2)}, u32[]{:S(2)}) collective-permute-start(bf16[40,2048]{1,0:T(8,128)(2,1)S(1)} %get-tuple-element.126), channel_id=1, source_target_pairs={{0,2},{1,3},{2,0},{3,1},{4,6},{5,7},{6,4},{7,5},{8,10},{9,11},{10,... | collective-permute-start | bytes 491528 | tf_op jit(solution)/shard_map/ppermute | solution.py:27
  130.5 13.5 %collective-permute-start.30 = (bf16[40,2048]{1,0:T(8,128)(2,1)S(1)}, bf16[40,2048]{1,0:T(8,128)(2,1)S(1)}, u32[]{:S(2)}, u32[]{:S(2)}) collective-permute-start(bf16[40,2048]{1,0:T(8,128)(2,1)S(1)} %get-tuple-element.127), channel_id=1, source_target_pairs={{0,4},{1,5},{2,6},{3,7},{4,0},{5,1},{6,2},{7,3},{8,12},{9,13},{10,... | collective-permute-start | bytes 491528 | tf_op jit(solution)/shard_map/ppermute | solution.py:27
  131.0 12.9 %collective-permute-start.31 = (bf16[40,2048]{1,0:T(8,128)(2,1)S(1)}, bf16[40,2048]{1,0:T(8,128)(2,1)S(1)}, u32[]{:S(2)}, u32[]{:S(2)}) collective-permute-start(bf16[40,2048]{1,0:T(8,128)(2,1)S(1)} %get-tuple-element.128), channel_id=1, source_target_pairs={{0,6},{1,7},{2,4},{3,5},{4,2},{5,3},{6,0},{7,1},{8,14},{9,15},{10,... | collective-permute-start | bytes 491528 | tf_op jit(solution)/shard_map/ppermute | solution.py:27
  140.3 13.8 %collective-permute-start.32 = (bf16[80,2048]{1,0:T(8,128)(2,1)S(1)}, bf16[80,2048]{1,0:T(8,128)(2,1)S(1)}, u32[]{:S(2)}, u32[]{:S(2)}) collective-permute-start(bf16[80,2048]{1,0:T(8,128)(2,1)S(1)} %get-tuple-element.132), channel_id=1, source_target_pairs={{0,2},{1,3},{2,0},{3,1},{4,6},{5,7},{6,4},{7,5},{8,10},{9,11},{10,... | collective-permute-start | bytes 983048 | tf_op jit(solution)/shard_map/ppermute | solution.py:27
  140.5 14.9 %collective-permute-start.33 = (bf16[80,2048]{1,0:T(8,128)(2,1)S(1)}, bf16[80,2048]{1,0:T(8,128)(2,1)S(1)}, u32[]{:S(2)}, u32[]{:S(2)}) collective-permute-start(bf16[80,2048]{1,0:T(8,128)(2,1)S(1)} %get-tuple-element.133), channel_id=1, source_target_pairs={{0,4},{1,5},{2,6},{3,7},{4,0},{5,1},{6,2},{7,3},{8,12},{9,13},{10,... | collective-permute-start | bytes 983048 | tf_op jit(solution)/shard_map/ppermute | solution.py:27
  141.0 14.4 %collective-permute-start.34 = (bf16[80,2048]{1,0:T(8,128)(2,1)S(1)}, bf16[80,2048]{1,0:T(8,128)(2,1)S(1)}, u32[]{:S(2)}, u32[]{:S(2)}) collective-permute-start(bf16[80,2048]{1,0:T(8,128)(2,1)S(1)} %get-tuple-element.134), channel_id=1, source_target_pairs={{0,6},{1,7},{2,4},{3,5},{4,2},{5,3},{6,0},{7,1},{8,14},{9,15},{10,... | collective-permute-start | bytes 983048 | tf_op jit(solution)/shard_map/ppermute | solution.py:27
  151.8 9.4 %collective-permute-start.39 = (bf16[40,2048]{1,0:T(8,128)(2,1)S(1)}, bf16[40,2048]{1,0:T(8,128)(2,1)S(1)}, u32[]{:S(2)}, u32[]{:S(2)}) collective-permute-start(bf16[40,2048]{1,0:T(8,128)(2,1)S(1)} %get-tuple-element.143), channel_id=1, source_target_pairs={{0,2},{1,3},{2,0},{3,1},{4,6},{5,7},{6,4},{7,5},{8,10},{9,11},{10,... | collective-permute-start | bytes 491528 | tf_op jit(solution)/shard_map/ppermute | solution.py:27
  152.1 11.8 %collective-permute-start.40 = (bf16[40,2048]{1,0:T(8,128)(2,1)S(1)}, bf16[40,2048]{1,0:T(8,128)(2,1)S(1)}, u32[]{:S(2)}, u32[]{:S(2)}) collective-permute-start(bf16[40,2048]{1,0:T(8,128)(2,1)S(1)} %get-tuple-element.144), channel_id=1, source_target_pairs={{0,4},{1,5},{2,6},{3,7},{4,0},{5,1},{6,2},{7,3},{8,12},{9,13},{10,... | collective-permute-start | bytes 491528 | tf_op jit(solution)/shard_map/ppermute | solution.py:27
  154.1 9.8 %collective-permute-start.41 = (bf16[40,2048]{1,0:T(8,128)(2,1)S(1)}, bf16[40,2048]{1,0:T(8,128)(2,1)S(1)}, u32[]{:S(2)}, u32[]{:S(2)}) collective-permute-start(bf16[40,2048]{1,0:T(8,128)(2,1)S(1)} %get-tuple-element.145), channel_id=1, source_target_pairs={{0,6},{1,7},{2,4},{3,5},{4,2},{5,3},{6,0},{7,1},{8,14},{9,15},{10,... | collective-permute-start | bytes 491528 | tf_op jit(solution)/shard_map/ppermute | solution.py:27
  158.4 19.4 %collective-permute-start.38 = (bf16[80,2048]{1,0:T(8,128)(2,1)S(1)}, bf16[80,2048]{1,0:T(8,128)(2,1)S(1)}, u32[]{:S(2)}, u32[]{:S(2)}) collective-permute-start(bf16[80,2048]{1,0:T(8,128)(2,1)S(1)} %get-tuple-element.135), channel_id=1, source_target_pairs={{0,24},{1,25},{2,26},{3,27},{4,28},{5,29},{6,30},{7,31},{8,0},{9,1... | collective-permute-start | bytes 983048 | tf_op jit(solution)/shard_map/ppermute | solution.py:27
  160.7 8.6 %collective-permute-start.35 = (bf16[40,2048]{1,0:T(8,128)(2,1)S(1)}, bf16[40,2048]{1,0:T(8,128)(2,1)S(1)}, u32[]{:S(2)}, u32[]{:S(2)}) collective-permute-start(bf16[40,2048]{1,0:T(8,128)(2,1)S(1)} %get-tuple-element.136), channel_id=1, source_target_pairs={{0,2},{1,3},{2,0},{3,1},{4,6},{5,7},{6,4},{7,5},{8,10},{9,11},{10,... | collective-permute-start | bytes 491528 | tf_op jit(solution)/shard_map/ppermute | solution.py:27
  161.2 16.7 %collective-permute-start.43 = (bf16[80,2048]{1,0:T(8,128)(2,1)S(1)}, bf16[80,2048]{1,0:T(8,128)(2,1)S(1)}, u32[]{:S(2)}, u32[]{:S(2)}) collective-permute-start(bf16[80,2048]{1,0:T(8,128)(2,1)S(1)} %get-tuple-element.146), channel_id=1, source_target_pairs={{0,8},{1,9},{2,10},{3,11},{4,12},{5,13},{6,14},{7,15},{8,16},{9,17... | collective-permute-start | bytes 983048 | tf_op jit(solution)/shard_map/ppermute | solution.py:27
  166.2 17.1 %collective-permute-start.42 = (bf16[80,2048]{1,0:T(8,128)(2,1)S(1)}, bf16[80,2048]{1,0:T(8,128)(2,1)S(1)}, u32[]{:S(2)}, u32[]{:S(2)}) collective-permute-start(bf16[80,2048]{1,0:T(8,128)(2,1)S(1)} %shard_map.140), channel_id=1, source_target_pairs={{0,16},{1,17},{2,18},{3,19},{4,20},{5,21},{6,22},{7,23},{8,24},{9,... | collective-permute-start | bytes 983048 | tf_op jit(solution)/shard_map/ppermute | solution.py:27
  167.6 5.3 %collective-permute-start.36 = (bf16[40,2048]{1,0:T(8,128)(2,1)S(1)}, bf16[40,2048]{1,0:T(8,128)(2,1)S(1)}, u32[]{:S(2)}, u32[]{:S(2)}) collective-permute-start(bf16[40,2048]{1,0:T(8,128)(2,1)S(1)} %get-tuple-element.138), channel_id=1, source_target_pairs={{0,4},{1,5},{2,6},{3,7},{4,0},{5,1},{6,2},{7,3},{8,12},{9,13},{10,... | collective-permute-start | bytes 491528 | tf_op jit(solution)/shard_map/ppermute | solution.py:27
  169.3 6.2 %collective-permute-start.37 = (bf16[40,2048]{1,0:T(8,128)(2,1)S(1)}, bf16[40,2048]{1,0:T(8,128)(2,1)S(1)}, u32[]{:S(2)}, u32[]{:S(2)}) collective-permute-start(bf16[40,2048]{1,0:T(8,128)(2,1)S(1)} %get-tuple-element.140), channel_id=1, source_target_pairs={{0,6},{1,7},{2,4},{3,5},{4,2},{5,3},{6,0},{7,1},{8,14},{9,15},{10,... | collective-permute-start | bytes 491528 | tf_op jit(solution)/shard_map/ppermute | solution.py:27
  (4 other events, 33.8 us)

commit v6 on v5

--- a/solution.py
+++ b/solution.py
@@ -12,6 +12,7 @@
 MIB = 1024 * 1024
 VMEM = pl.BlockSpec(memory_space=pltpu.VMEM)
 SMEM = pl.BlockSpec(memory_space=pltpu.SMEM)
+ANY = pl.BlockSpec(memory_space=pl.ANY)
 HBM = pl.BlockSpec(memory_space=pltpu.HBM)
 PAD_ROWS = 16
 LANES = 128
@@ -74,16 +75,19 @@
     return pltpu.VMEM(shape, dtype)
 
 
-def call(kernel, outs, operands, scratch=(), flops=0, smem=1, hbm=0, limit=16 * MIB):
-    last = len(operands) - hbm
+def call(kernel, outs, operands, scratch=(), flops=0, smem=1, anywhere=0, hbm=0, limit=16 * MIB):
+    far = len(operands) - hbm
+    last = far - anywhere
     operands = [
-        a if i < smem else pltpu.with_memory_space_constraint(a, pltpu.VMEM if i < last else pltpu.HBM)
+        pltpu.with_memory_space_constraint(a, pltpu.VMEM if i < last else pltpu.HBM)
+        if smem <= i < last or i >= far
+        else a
         for i, a in enumerate(operands)
     ]
     return pl.pallas_call(
         kernel,
         out_shape=outs,
-        in_specs=[SMEM] * smem + [VMEM] * (last - smem) + [HBM] * hbm,
+        in_specs=[SMEM] * smem + [VMEM] * (last - smem) + [ANY] * anywhere + [HBM] * hbm,
         out_specs=jax.tree.map(lambda _: VMEM, outs),
         scratch_shapes=list(scratch),
         compiler_params=pltpu.CompilerParams(vmem_limit_bytes=limit),
@@ -110,37 +114,36 @@
         copy.wait()
 
 
-def load(arrays):
-    count = len(arrays)
-    return pl.pallas_call(
-        functools.partial(load_kernel, count),
-        out_shape=[struct(*a.shape) for a in arrays],
-        in_specs=[pl.BlockSpec(memory_space=pl.ANY)] * count,
-        out_specs=[VMEM] * count,
-        scratch_shapes=[pltpu.SemaphoreType.DMA((count,))],
-        compiler_params=pltpu.CompilerParams(vmem_limit_bytes=MIB),
-        cost_estimate=pl.CostEstimate(
-            flops=0, bytes_accessed=sum(2 * a.size * a.dtype.itemsize for a in arrays), transcendentals=0
-        ),
-    )(*arrays)
-
-
-def project_kernel(hops, depth, head_dim, place, *refs):
-    row_refs, marks, sources = refs[: hops - 1], refs[hops - 1], refs[hops : hops + 5]
-    outs, (rows, mixed, own, gain, held, sems) = refs[hops + 5 : hops + 5 + depth], refs[hops + 5 + depth :]
+def load(received, held):
+    arrays = [*received, *held]
+    return call(
+        functools.partial(load_kernel, len(arrays)),
+        [struct(*a.shape) for a in arrays],
+        arrays,
+        [pltpu.SemaphoreType.DMA((len(arrays),))],
+        smem=0,
+        anywhere=len(received),
+        hbm=len(held),
+        limit=MIB,
+    )
+
+
+def project_kernel(hops, depth, head_dim, place, marks, *refs):
+    sources, outs = refs[: hops + 4], refs[hops + 4 : hops + 4 + depth]
+    given, rows, mixed, gain, held, sems = refs[hops + 4 + depth :]
     exp_index, z_index = place[0], place[1]
-    tok_rows = row_refs[0].shape[0]
+    tok_rows = given.shape[1]
     block_len = hops * tok_rows
-    targets = [own, gain, *(held.at[i] for i in range(3))]
-    copies = [pltpu.make_async_copy(sources[i], targets[i], sems.at[i]) for i in range(5)]
+    targets = [*(given.at[i] for i in range(1, hops)), gain, given.at[0], *(held.at[i] for i in range(3))]
+    copies = [pltpu.make_async_copy(sources[i], targets[i], sems.at[i]) for i in range(hops + 4)]
     for copy in copies:
         copy.start()
-    copies[0].wait()
-    copies[1].wait()
-    for hop, row_ref in enumerate((own, *row_refs)):
+    for copy in copies[: hops + 1]:
+        copy.wait()
+    for hop in range(hops):
         start = pl.multiple_of((exp_index ^ hop) * tok_rows, 16)
-        rows[pl.ds(start, tok_rows), :] = normalize(row_ref[...], gain[...])
-    for part, copy in enumerate(copies[2:]):
+        rows[pl.ds(start, tok_rows), :] = normalize(given[hop], gain[...])
+    for part, copy in enumerate(copies[hops + 1 :]):
         copy.wait()
         mixed[part] = f32_dot(rows[...], held[part]).astype(jnp.bfloat16)
     for turn in range(depth):
@@ -400,6 +403,8 @@
     near = swap_core(inputs)
     far_near = swap_core(far)
     weights = (w_gate, w_up, w_down)
+    other_gate, other_up, other_down = swap_core(w_gate), None, None
+    far_near, other_gate = lax.optimization_barrier((far_near, other_gate))
     top_count = routes.shape[1]
     noted = jnp.concatenate([routes.astype(jnp.float32)] + [gate_weights] * 3, axis=1)
     noted = jnp.pad(noted, ((0, 0), (0, LANES - noted.shape[1])))
@@ -413,22 +418,29 @@
         sent = call(
             functools.partial(project_kernel, exp_count, depth, head_dim),
             [payload] * depth,
-            [place, near, far, far_near, marks, inputs, attn_gain.reshape(1, -1), w_query, w_key, w_value],
             [
+                place,
+                marks,
+                *(near, far, far_near),
+                *(attn_gain.reshape(1, -1), inputs, w_query, w_key, w_value),
+            ],
+            [
+                pltpu.VMEM((exp_count, tok_rows, model_width), jnp.bfloat16),
                 pltpu.VMEM((block_len, model_width), jnp.bfloat16),
                 pltpu.VMEM((3, block_len, hidden_cols), jnp.bfloat16),
-                pltpu.VMEM((tok_rows, model_width), jnp.bfloat16),
                 pltpu.VMEM((1, model_width), jnp.float32),
                 pltpu.VMEM((3, model_width, hidden_cols), jnp.bfloat16),
-                pltpu.SemaphoreType.DMA((5,)),
+                pltpu.SemaphoreType.DMA((exp_count + 4,)),
             ],
             flops=6 * block_len * model_width * hidden_cols,
+            anywhere=exp_count - 1,
             hbm=5,
         )
         own = [head_out(sent[turn], turn) for turn in range(depth)]
         beside = [swap_core(block) for block in own]
-        early = [swap_core(after(weight, sent[0])) for weight in weights[:2]]
-        other_weights = [*early, swap_core(after(weights[2], *beside))]
+        other_down = swap_core(after(w_down, sent[0]))
+        beside[-1], other_down = lax.optimization_barrier((beside[-1], other_down))
+        other_up = swap_core(after(w_up, *beside))
         mixed = call(
             functools.partial(attend_kernel, depth, block_len, head_dim),
             [struct(block_len, head_dim)] * depth,
@@ -440,12 +452,13 @@
             ],
             flops=4 * depth * ctx_count * block_len * block_len * head_dim,
         )
+        *mixed, other_up = lax.optimization_barrier((*mixed, other_up))
         heads = [head_back(mixed[turn], turn) for turn in range(depth)]
     else:
         block = jnp.stack([inputs, near, far, far_near])[exp_index ^ jnp.arange(exp_count)]
         normed = normalize(block.reshape(block_len, model_width), attn_gain)
         heads = attend_gathered(normed, w_query, w_key, w_value, sel_blocks)
-        other_weights = [swap_core(weight) for weight in weights]
+        other_up, other_down = swap_core(w_up), swap_core(w_down)
 
     halves = struct(exp_count // 2, tok_rows, model_width)
     kept, given = call(
@@ -466,9 +479,9 @@
         smem=0,
     )
     own_weights, other_weights = (
-        [gate[0].T, up[0].T, down[0]] for gate, up, down in (weights, other_weights)
-    )
-    expert_weights = load([after(weight, beyond) for weight in own_weights + other_weights])
+        [gate[0].T, up[0].T, down[0]] for gate, up, down in (weights, (other_gate, other_up, other_down))
+    )
+    expert_weights = load(other_weights, [after(weight, beyond) for weight in own_weights])
     beyond = move(beyond, lambda z, x, y, c: (z, x, y ^ 1, c))
     beyond, expert_weights = lax.optimization_barrier((beyond, expert_weights))
     residual, ffn_in = call(
@@ -486,10 +499,14 @@
     for group in groups:
         count = len(group)
         first = column[group[0]]
+        if len(arrived) == 1:
+            first = after(first, *arrived[0])
+        elif arrived:
+            first = after(first, arrived[-1][0])
         *packed, note = call(
             functools.partial(pack_kernel, count, capacity, top_count),
             [struct(count * capacity, model_width)] * 4 + [struct(count * tok_rows, LANES)],
-            [place, after(first, arrived[-1][0]) if arrived else first, *[column[t] for t in group[1:]]],
+            [place, first, *[column[t] for t in group[1:]]],
             [pltpu.VMEM((count * tok_rows, model_width), jnp.bfloat16)],
             flops=8 * count * capacity * count * tok_rows * model_width,
             limit=8 * MIB + 16 * (count * tok_rows) ** 2 + 8 * count * tok_rows * model_width,

time: 185 us -> 180 us (0.973)
  local copies, waits for them, and re-layouts: 3.3 us -> 8.41 us
  starting transfers between devices: 64.9 us -> 60.5 us
  waiting for transfers between devices: 65.4 us -> 61.2 us
    pallas_call x1 -> x0, Pallas kernels: 5.43 us -> none  [load(): pl.pallas_call(functools.partial(load_kernel, count), out_shape=[struct(*...]
    unnamed x16 -> x22, local copies, waits for them, and re-layouts: 1.72 us -> 6.82 us
    pallas_call x13 -> x14, Pallas kernels: 43.4 us -> 48 us  [call(): pl.pallas_call(kernel, out_shape=outs, in_specs=[SMEM] * smem + [VMEM] *...]
    ppermute x44, starting transfers between devices: 64.9 us -> 60.5 us  [move(): return lax.ppermute(block, AXES, route)]
    ppermute x44, waiting for transfers between devices: 65.4 us -> 61.2 us  [move(): return lax.ppermute(block, AXES, route)]
  transfers between devices with their start and end apart: 44 -> 44, of which waited for: 17 -> 17; matrix products, arithmetic and copies ran while one was open for 1% -> 1% of each run, Pallas kernels for 23% -> 21%
where the time goes in v6:
time: 180 us
  waiting for transfers between devices  61.2 us (34%)
  starting transfers between devices  60.5 us (34%)
  Pallas kernels  48 us (27%)
  local copies, waits for them, and re-layouts  8.41 us (5%)
    ppermute x44, waiting for transfers between devices, move(): return lax.ppermute(block, AXES, route)  61.2 us
    ppermute x44, starting transfers between devices, move(): return lax.ppermute(block, AXES, route)  60.5 us
    pallas_call x14, Pallas kernels, call(): pl.pallas_call(kernel, out_shape=outs, in_specs=[SMEM] * smem + [VMEM] *...  48 us
    unnamed x22, local copies, waits for them, and re-layouts  6.82 us
  transfers between devices with their start and end apart: 44, of which 17 were waited for; matrix products, arithmetic and copies ran while one was open for 1% of the time, Pallas kernels for 21%

profile of v6, /device:TPU:0, one launch (start us, length us, event | category | flops | bytes accessed | tf_op | source)
XLA Modules:
  0.0 180.1 jit_solution(10752168036787019256)
XLA Ops:
  0.5 2.5 %collective-permute-start.1 = (bf16[80,2048]{1,0:T(8,128)(2,1)}, bf16[80,2048]{1,0:T(8,128)(2,1)S(1)}, u32[]{:S(2)}, u32[]{:S(2)}) collective-permute-start(bf16[80,2048]{1,0:T(8,128)(2,1)} %inputs.1), channel_id=1, source_target_pairs={{0,2},{1,3},{2,0},{3,1},{4,6},{5,7},{6,4},{7,5},{8,10},{9,11},{10,... | collective-permute-start | bytes 983048 | tf_op jit(solution)/shard_map/ppermute | solution.py:28
  3.2 8.4 %collective-permute-done.1.refs_1_ = bf16[80,2048]{1,0:T(8,128)(2,1)S(1)} collective-permute-done((bf16[80,2048]{1,0:T(8,128)(2,1)}, bf16[80,2048]{1,0:T(8,128)(2,1)S(1)}, u32[]{:S(2)}, u32[]{:S(2)}) %collective-permute-start.1) | collective-permute-done | bytes 327712 | tf_op jit(solution)/shard_map/ppermute | solution.py:28
  13.4 5.7 %shard_map.127 = (bf16[336,384]{1,0:T(8,128)(2,1)S(1)}, bf16[336,384]{1,0:T(8,128)(2,1)S(1)}, bf16[336,384]{1,0:T(8,128)(2,1)S(1)}, bf16[336,384]{1,0:T(8,128)(2,1)S(1)}) custom-call(s32[5]{0:T(128)S(1)} %stack.20.place, bf16[4,16,384]{2,1,0:T(8,128)(2,1)S(1)} %broadcast_in_dim.11.marks, bf16[80,2048]{1,0:T(8,128)(2,1)S(1)} %collective-permute-done.refs_0_, ...), custom_call_target="tpu_custom_call" | custom-call | flops 2013265920 | bytes 7659540 | tf_op jit(solution)/shard_map/pallas_call | solution.py:87
  19.3 3.8 %collective-permute-start.7 = (bf16[336,384]{1,0:T(8,128)(2,1)S(1)}, bf16[336,384]{1,0:T(8,128)(2,1)S(1)}, u32[]{:S(2)}, u32[]{:S(2)}) collective-permute-start(bf16[336,384]{1,0:T(8,128)(2,1)S(1)} %get-tuple-element.85), channel_id=1, source_target_pairs={{0,24},{1,28},{2,26},{3,30},{4,25},{5,29},{6,27},{7,31},{8,0},{9,4... | collective-permute-start | bytes 774152 | tf_op jit(solution)/shard_map/ppermute | solution.py:28
  24.9 4.6 %collective-permute-done.7.refs_3_ = bf16[336,384]{1,0:T(8,128)(2,1)S(1)} collective-permute-done((bf16[336,384]{1,0:T(8,128)(2,1)S(1)}, bf16[336,384]{1,0:T(8,128)(2,1)S(1)}, u32[]{:S(2)}, u32[]{:S(2)}) %collective-permute-start.7) | collective-permute-done | bytes 258080 | tf_op jit(solution)/shard_map/ppermute | solution.py:28
  30.2 1.9 %collective-permute-start.8 = (bf16[336,384]{1,0:T(8,128)(2,1)S(1)}, bf16[336,384]{1,0:T(8,128)(2,1)S(1)}, u32[]{:S(2)}, u32[]{:S(2)}) collective-permute-start(bf16[336,384]{1,0:T(8,128)(2,1)S(1)} %collective-permute-done.4.refs_0_), channel_id=1, source_target_pairs={{0,1},{1,0},{2,3},{3,2},{4,5},{5,4},{6,7},{7,6},{8,9},{9,8},{10,11... | collective-permute-start | bytes 774152 | tf_op jit(solution)/shard_map/ppermute | solution.py:28
  32.1 2.9 %collective-permute-done.5.refs_1_ = bf16[336,384]{1,0:T(8,128)(2,1)S(1)} collective-permute-done((bf16[336,384]{1,0:T(8,128)(2,1)S(1)}, bf16[336,384]{1,0:T(8,128)(2,1)S(1)}, u32[]{:S(2)}, u32[]{:S(2)}) %collective-permute-start.5) | collective-permute-done | bytes 258080 | tf_op jit(solution)/shard_map/ppermute | solution.py:28
  35.1 2.9 %collective-permute-start.9 = (bf16[336,384]{1,0:T(8,128)(2,1)S(1)}, bf16[336,384]{1,0:T(8,128)(2,1)S(1)}, u32[]{:S(2)}, u32[]{:S(2)}) collective-permute-start(bf16[336,384]{1,0:T(8,128)(2,1)S(1)} %collective-permute-done.5.refs_1_), channel_id=1, source_target_pairs={{0,1},{1,0},{2,3},{3,2},{4,5},{5,4},{6,7},{7,6},{8,9},{9,8},{10,11... | collective-permute-start | bytes 774152 | tf_op jit(solution)/shard_map/ppermute | solution.py:28
  38.0 7.0 %collective-permute-done.6.refs_2_ = bf16[336,384]{1,0:T(8,128)(2,1)S(1)} collective-permute-done((bf16[336,384]{1,0:T(8,128)(2,1)S(1)}, bf16[336,384]{1,0:T(8,128)(2,1)S(1)}, u32[]{:S(2)}, u32[]{:S(2)}) %collective-permute-start.6) | collective-permute-done | bytes 258080 | tf_op jit(solution)/shard_map/ppermute | solution.py:28
  45.0 1.3 collective-permute-start.10
  46.4 1.6 copy-done
  48.1 7.9 %shard_map.128 = (bf16[320,128]{1,0:T(8,128)(2,1)S(1)}, bf16[320,128]{1,0:T(8,128)(2,1)S(1)}, bf16[320,128]{1,0:T(8,128)(2,1)S(1)}, bf16[320,128]{1,0:T(8,128)(2,1)S(1)}) custom-call(s32[5]{0:T(128)S(1)} %stack.20.place, bf16[336,384]{1,0:T(8,128)(2,1)S(1)} %collective-permute-done.4.refs_0_, bf16[336,384]{1,0:T(8,128)(2,1)S(1)} %collective-permute-done.5.refs_1_, ...), custom_call_target="tpu_custom_call" | custom-call | flops 1677721600 | bytes 2064404 | tf_op jit(solution)/shard_map/pallas_call | solution.py:87
  56.1 1.5 copy-done.2
  58.3 3.4 %collective-permute-start.15 = (bf16[320,128]{1,0:T(8,128)(2,1)S(1)}, bf16[320,128]{1,0:T(8,128)(2,1)S(1)}, u32[]{:S(2)}, u32[]{:S(2)}) collective-permute-start(bf16[320,128]{1,0:T(8,128)(2,1)S(1)} %get-tuple-element.94), channel_id=1, source_target_pairs={{0,24},{1,28},{2,26},{3,30},{4,25},{5,29},{6,27},{7,31},{8,0},{9,4... | collective-permute-start | bytes 245768 | tf_op jit(solution)/shard_map/ppermute | solution.py:28
  62.4 1.4 collective-permute-done.15.refs_1_
  63.8 3.3 %collective-permute-done.16.refs_2_ = bf16[320,128]{1,0:T(8,128)(2,1)S(1)} collective-permute-done((bf16[320,128]{1,0:T(8,128)(2,1)S(1)}, bf16[320,128]{1,0:T(8,128)(2,1)S(1)}, u32[]{:S(2)}, u32[]{:S(2)}) %collective-permute-start.16) | collective-permute-done | bytes 81952 | tf_op jit(solution)/shard_map/ppermute | solution.py:28
  67.1 1.5 collective-permute-done.17.refs_3_
  68.6 1.5 shard_map.129
  70.1 2.7 %collective-permute-start.18 = (bf16[2,80,2048]{2,1,0:T(8,128)(2,1)S(1)}, bf16[2,80,2048]{2,1,0:T(8,128)(2,1)S(1)}, u32[]{:S(2)}, u32[]{:S(2)}) collective-permute-start(bf16[2,80,2048]{2,1,0:T(8,128)(2,1)S(1)} %get-tuple-element.98), channel_id=1, source_target_pairs={{0,1},{1,0},{2,3},{3,2},{4,5},{5,4},{6,7},{7,6},{8,9},{9,8},{10,11... | collective-permute-start | bytes 1966088 | tf_op jit(solution)/shard_map/ppermute | solution.py:28
  72.8 1.7 collective-permute-done.18.given
  75.4 1.5 collective-permute-start.19
  78.4 1.8 %copy-done.1 = bf16[1,704,2048]{2,1,0:T(8,128)(2,1)S(1)} copy-done((bf16[1,704,2048]{2,1,0:T(8,128)(2,1)S(1)}, bf16[1,704,2048]{2,1,0:T(8,128)(2,1)}, u32[]{:S(2)}) %copy-start.1) | copy-done | bytes 2883608
  80.2 1.8 %copy-done.3 = bf16[1,2048,704]{1,2,0:T(8,128)(2,1)S(1)} copy-done((bf16[1,2048,704]{1,2,0:T(8,128)(2,1)S(1)}, bf16[1,2048,704]{1,2,0:T(8,128)(2,1)}, u32[]{:S(2)}) %copy-start.3) | copy-done | bytes 2883608
  82.0 4.2 %shard_map.131 = (bf16[704,2048]{1,0:T(8,128)(2,1)S(1)}, bf16[704,2048]{1,0:T(8,128)(2,1)S(1)}, bf16[704,2048]{1,0:T(8,128)(2,1)S(1)}, bf16[704,2048]{1,0:T(8,12...) custom-call(bf16[704,2048]{1,0:T(8,128)(2,1)S(1)} %bitcast.22, bf16[704,2048]{1,0:T(8,128)(2,1)S(1)} %bitcast.24, ...), custom_call_target="tpu_custom_call" | custom-call | bytes 17301504 | tf_op jit(solution)/shard_map/pallas_call | solution.py:87
  88.0 3.3 %collective-permute-start.25 = (bf16[80,2176]{1,0:T(8,128)(2,1)S(1)}, bf16[80,2176]{1,0:T(8,128)(2,1)S(1)}, u32[]{:S(2)}, u32[]{:S(2)}) collective-permute-start(bf16[80,2176]{1,0:T(8,128)(2,1)S(1)} %get-tuple-element.115.refs_0_), channel_id=1, source_target_pairs={{0,24},{1,25},{2,26},{3,27},{4,28},{5,29},{6,30},{7,31},{8,0},{9,1... | collective-permute-start | bytes 1044488 | tf_op jit(solution)/shard_map/ppermute | solution.py:28
  91.3 1.5 shard_map.133
  93.9 1.7 collective-permute-start.21
  96.4 4.0 %collective-permute-done.23.refs_0_ = bf16[80,2176]{1,0:T(8,128)(2,1)S(1)} collective-permute-done((bf16[80,2176]{1,0:T(8,128)(2,1)S(1)}, bf16[80,2176]{1,0:T(8,128)(2,1)S(1)}, u32[]{:S(2)}, u32[]{:S(2)}) %collective-permute-start.23) | collective-permute-done | bytes 348192 | tf_op jit(solution)/shard_map/ppermute | solution.py:28
  100.4 5.6 %collective-permute-start.24 = (bf16[80,2176]{1,0:T(8,128)(2,1)S(1)}, bf16[80,2176]{1,0:T(8,128)(2,1)S(1)}, u32[]{:S(2)}, u32[]{:S(2)}) collective-permute-start(bf16[80,2176]{1,0:T(8,128)(2,1)S(1)} %collective-permute-done.23.refs_0_), channel_id=1, source_target_pairs={{0,8},{1,9},{2,10},{3,11},{4,12},{5,13},{6,14},{7,15},{8,16},{9,17... | collective-permute-start | bytes 1044488 | tf_op jit(solution)/shard_map/ppermute | solution.py:28
  106.0 1.7 shard_map.134
  109.1 2.1 %collective-permute-start.28 = (bf16[80,2048]{1,0:T(8,128)(2,1)S(1)}, bf16[80,2048]{1,0:T(8,128)(2,1)S(1)}, u32[]{:S(2)}, u32[]{:S(2)}) collective-permute-start(bf16[80,2048]{1,0:T(8,128)(2,1)S(1)} %get-tuple-element.127), channel_id=1, source_target_pairs={{0,6},{1,7},{2,4},{3,5},{4,2},{5,3},{6,0},{7,1},{8,14},{9,15},{10,... | collective-permute-start | bytes 983048 | tf_op jit(solution)/shard_map/ppermute | solution.py:28
  111.2 3.2 %collective-permute-done.24.refs_0_ = bf16[80,2176]{1,0:T(8,128)(2,1)S(1)} collective-permute-done((bf16[80,2176]{1,0:T(8,128)(2,1)S(1)}, bf16[80,2176]{1,0:T(8,128)(2,1)S(1)}, u32[]{:S(2)}, u32[]{:S(2)}) %collective-permute-start.24) | collective-permute-done | bytes 348192 | tf_op jit(solution)/shard_map/ppermute | solution.py:28
  114.4 1.5 shard_map.135
  116.5 1.7 collective-permute-start.30
  119.5 7.5 %collective-permute-done.28.refs_3_ = bf16[80,2048]{1,0:T(8,128)(2,1)S(1)} collective-permute-done((bf16[80,2048]{1,0:T(8,128)(2,1)S(1)}, bf16[80,2048]{1,0:T(8,128)(2,1)S(1)}, u32[]{:S(2)}, u32[]{:S(2)}) %collective-permute-start.28) | collective-permute-done | bytes 327712 | tf_op jit(solution)/shard_map/ppermute | solution.py:28
  127.0 6.4 %shard_map.136 = (bf16[80,2048]{1,0:T(8,128)(2,1)S(1)}, bf16[80,2048]{1,0:T(8,128)(2,1)S(1)}, bf16[80,2048]{1,0:T(8,128)(2,1)S(1)}, bf16[80,2048]{1,0:T(8,128)(2,1)S(1)}) custom-call(bf16[80,2048]{1,0:T(8,128)(2,1)S(1)} %get-tuple-element.122.refs_0_, bf16[80,2048]{1,0:T(8,128)(2,1)S(1)} %collective-permute-done.26.refs_1_, ...), custom_call_target="tpu_custom_call" | custom-call | flops 5536481280 | bytes 18612224 | tf_op jit(solution)/shard_map/pallas_call | solution.py:87
  134.8 2.1 %collective-permute-start.34 = (bf16[80,2048]{1,0:T(8,128)(2,1)S(1)}, bf16[80,2048]{1,0:T(8,128)(2,1)S(1)}, u32[]{:S(2)}, u32[]{:S(2)}) collective-permute-start(bf16[80,2048]{1,0:T(8,128)(2,1)S(1)} %get-tuple-element.144), channel_id=1, source_target_pairs={{0,6},{1,7},{2,4},{3,5},{4,2},{5,3},{6,0},{7,1},{8,14},{9,15},{10,... | collective-permute-start | bytes 983048 | tf_op jit(solution)/shard_map/ppermute | solution.py:28
  136.9 7.9 %shard_map.137 = (bf16[40,2048]{1,0:T(8,128)(2,1)S(1)}, bf16[40,2048]{1,0:T(8,128)(2,1)S(1)}, bf16[40,2048]{1,0:T(8,128)(2,1)S(1)}, bf16[40,2048]{1,0:T(8,128)(2...) custom-call(bf16[40,2048]{1,0:T(8,128)(2,1)S(1)} %get-tuple-element., ...), custom_call_target="tpu_custom_call" | custom-call | flops 6643777536 | bytes 18612224 | tf_op jit(solution)/shard_map/pallas_call | solution.py:87
  146.3 2.1 %collective-permute-start.41 = (bf16[40,2048]{1,0:T(8,128)(2,1)S(1)}, bf16[40,2048]{1,0:T(8,128)(2,1)S(1)}, u32[]{:S(2)}, u32[]{:S(2)}) collective-permute-start(bf16[40,2048]{1,0:T(8,128)(2,1)S(1)} %get-tuple-element.155), channel_id=1, source_target_pairs={{0,6},{1,7},{2,4},{3,5},{4,2},{5,3},{6,0},{7,1},{8,14},{9,15},{10,... | collective-permute-start | bytes 491528 | tf_op jit(solution)/shard_map/ppermute | solution.py:28
  148.4 2.0 %collective-permute-done.34.refs_3_ = bf16[80,2048]{1,0:T(8,128)(2,1)S(1)} collective-permute-done((bf16[80,2048]{1,0:T(8,128)(2,1)S(1)}, bf16[80,2048]{1,0:T(8,128)(2,1)S(1)}, u32[]{:S(2)}, u32[]{:S(2)}) %collective-permute-start.34) | collective-permute-done | bytes 327712 | tf_op jit(solution)/shard_map/ppermute | solution.py:28
  150.4 3.1 %shard_map.138 = (bf16[80,2048]{1,0:T(8,128)(2,1)S(1)}, bf16[80,2048]{1,0:T(8,128)(2,1)S(1)}) custom-call(s32[5]{0:T(128)S(1)} %stack.20.place, bf16[160,128]{1,0:T(8,128)(2,1)S(1)} %get-tuple-element.141.notes, bf16[80,2048]{1,0:T(8,128)(2,1)S(1)} %get-tuple-element.134.refs_0_, bf16[80,2048]{1,0:T(8,128)(2,1)S(1)} %collective-permute-done.32.refs_1_, ...), custom_call_target="tpu_custom_call" | custom-call | flops 419430400 | bytes 1351700 | tf_op jit(solution)/shard_map/pallas_call | solution.py:87
  155.7 3.5 %collective-permute-start.43 = (bf16[80,2048]{1,0:T(8,128)(2,1)S(1)}, bf16[80,2048]{1,0:T(8,128)(2,1)S(1)}, u32[]{:S(2)}, u32[]{:S(2)}) collective-permute-start(bf16[80,2048]{1,0:T(8,128)(2,1)S(1)} %get-tuple-element.156), channel_id=1, source_target_pairs={{0,8},{1,9},{2,10},{3,11},{4,12},{5,13},{6,14},{7,15},{8,16},{9,17... | collective-permute-start | bytes 983048 | tf_op jit(solution)/shard_map/ppermute | solution.py:28
  159.2 2.3 %shard_map.140 = bf16[80,2048]{1,0:T(8,128)(2,1)S(1)} custom-call(s32[5]{0:T(128)S(1)} %stack.20.place, bf16[80,128]{1,0:T(8,128)(2,1)S(1)} %get-tuple-element.151.notes, bf16[40,2048]{1,0:T(8,128)(2,1)S(1)} %get-tuple-element.152.refs_0_, bf16[40,2048]{1,0:T(8,128)(2,1)S(1)} %collective-permute-done.39.refs_1_, ...), custom_call_target="tpu_custom_call" | custom-call | flops 104857600 | bytes 675860 | tf_op jit(solution)/shard_map/pallas_call | solution.py:87
  162.9 1.6 collective-permute-start.37
  164.5 3.1 %collective-permute-done.36.refs_2_ = bf16[40,2048]{1,0:T(8,128)(2,1)S(1)} collective-permute-done((bf16[40,2048]{1,0:T(8,128)(2,1)S(1)}, bf16[40,2048]{1,0:T(8,128)(2,1)S(1)}, u32[]{:S(2)}, u32[]{:S(2)}) %collective-permute-start.36) | collective-permute-done | bytes 163872 | tf_op jit(solution)/shard_map/ppermute | solution.py:28
  167.6 1.9 %collective-permute-done.37.refs_3_ = bf16[40,2048]{1,0:T(8,128)(2,1)S(1)} collective-permute-done((bf16[40,2048]{1,0:T(8,128)(2,1)S(1)}, bf16[40,2048]{1,0:T(8,128)(2,1)S(1)}, u32[]{:S(2)}, u32[]{:S(2)}) %collective-permute-start.37) | collective-permute-done | bytes 163872 | tf_op jit(solution)/shard_map/ppermute | solution.py:28
  169.5 2.3 %shard_map.139 = bf16[80,2048]{1,0:T(8,128)(2,1)S(1)} custom-call(s32[5]{0:T(128)S(1)} %stack.20.place, bf16[80,128]{1,0:T(8,128)(2,1)S(1)} %get-tuple-element.116.notes, bf16[40,2048]{1,0:T(8,128)(2,1)S(1)} %get-tuple-element.139.refs_0_, bf16[40,2048]{1,0:T(8,128)(2,1)S(1)} %collective-permute-done.35.refs_1_, ...), custom_call_target="tpu_custom_call" | custom-call | flops 104857600 | bytes 675860 | tf_op jit(solution)/shard_map/pallas_call | solution.py:87
  171.9 7.3 %collective-permute-done.42 = bf16[80,2048]{1,0:T(8,128)(2,1)S(1)} collective-permute-done((bf16[80,2048]{1,0:T(8,128)(2,1)S(1)}, bf16[80,2048]{1,0:T(8,128)(2,1)S(1)}, u32[]{:S(2)}, u32[]{:S(2)}) %collective-permute-start.42) | collective-permute-done | bytes 327712 | tf_op jit(solution)/shard_map/ppermute | solution.py:28
  (86 shorter events, 23.1 us)
Async XLA Ops:
  0.0 13.3 %collective-permute-start.3 = (bf16[1,2048,704]{1,2,0:T(8,128)(2,1)}, bf16[1,2048,704]{1,2,0:T(8,128)(2,1)S(1)}, u32[]{:S(2)}, u32[]{:S(2)}) collective-permute-start(bf16[1,2048,704]{1,2,0:T(8,128)(2,1)} %param.21), channel_id=1, source_target_pairs={{0,1},{1,0},{2,3},{3,2},{4,5},{5,4},{6,7},{7,6},{8,9},{9,8},{10,11... | collective-permute-start | bytes 8650760 | tf_op jit(solution)/shard_map/ppermute | solution.py:28
  0.5 11.1 %collective-permute-start.1 = (bf16[80,2048]{1,0:T(8,128)(2,1)}, bf16[80,2048]{1,0:T(8,128)(2,1)S(1)}, u32[]{:S(2)}, u32[]{:S(2)}) collective-permute-start(bf16[80,2048]{1,0:T(8,128)(2,1)} %inputs.1), channel_id=1, source_target_pairs={{0,2},{1,3},{2,0},{3,1},{4,6},{5,7},{6,4},{7,5},{8,10},{9,11},{10,... | collective-permute-start | bytes 983048 | tf_op jit(solution)/shard_map/ppermute | solution.py:28
  3.0 10.4 %collective-permute-start = (bf16[80,2048]{1,0:T(8,128)(2,1)}, bf16[80,2048]{1,0:T(8,128)(2,1)S(1)}, u32[]{:S(2)}, u32[]{:S(2)}) collective-permute-start(bf16[80,2048]{1,0:T(8,128)(2,1)} %inputs.1), channel_id=1, source_target_pairs={{0,1},{1,0},{2,3},{3,2},{4,5},{5,4},{6,7},{7,6},{8,9},{9,8},{10,11... | collective-permute-start | bytes 983048 | tf_op jit(solution)/shard_map/ppermute | solution.py:28
  11.6 1.8 collective-permute-start.2
  13.4 34.7 %copy-start.7 = (bf16[1,2048,704]{1,2,0:T(8,128)(2,1)S(1)}, bf16[1,2048,704]{1,2,0:T(8,128)(2,1)}, u32[]{:S(2)}) copy-start(bf16[1,2048,704]{1,2,0:T(8,128)(2,1)} %param.22) | copy-start | bytes 8650756
  19.1 27.3 %collective-permute-start.12 = (bf16[1,704,2048]{2,1,0:T(8,128)(2,1)S(1)}, bf16[1,704,2048]{2,1,0:T(8,128)(2,1)S(1)}, u32[]{:S(2)}, u32[]{:S(2)}) collective-permute-start(bf16[1,704,2048]{2,1,0:T(8,128)(2,1)S(1)} %copy-done.8), channel_id=1, source_target_pairs={{0,1},{1,0},{2,3},{3,2},{4,5},{5,4},{6,7},{7,6},{8,9},{9,8},{10,11... | collective-permute-start | bytes 8650760 | tf_op jit(solution)/shard_map/ppermute | solution.py:28
  19.3 10.2 %collective-permute-start.7 = (bf16[336,384]{1,0:T(8,128)(2,1)S(1)}, bf16[336,384]{1,0:T(8,128)(2,1)S(1)}, u32[]{:S(2)}, u32[]{:S(2)}) collective-permute-start(bf16[336,384]{1,0:T(8,128)(2,1)S(1)} %get-tuple-element.85), channel_id=1, source_target_pairs={{0,24},{1,28},{2,26},{3,30},{4,25},{5,29},{6,27},{7,31},{8,0},{9,4... | collective-permute-start | bytes 774152 | tf_op jit(solution)/shard_map/ppermute | solution.py:28
  23.1 7.0 %collective-permute-start.4 = (bf16[336,384]{1,0:T(8,128)(2,1)S(1)}, bf16[336,384]{1,0:T(8,128)(2,1)S(1)}, u32[]{:S(2)}, u32[]{:S(2)}) collective-permute-start(bf16[336,384]{1,0:T(8,128)(2,1)S(1)} %get-tuple-element.82), channel_id=1, source_target_pairs={{0,0},{1,4},{2,2},{3,6},{4,1},{5,5},{6,3},{7,7},{8,8},{9,12},{10,1... | collective-permute-start | bytes 774152 | tf_op jit(solution)/shard_map/ppermute | solution.py:28
  23.8 11.2 %collective-permute-start.5 = (bf16[336,384]{1,0:T(8,128)(2,1)S(1)}, bf16[336,384]{1,0:T(8,128)(2,1)S(1)}, u32[]{:S(2)}, u32[]{:S(2)}) collective-permute-start(bf16[336,384]{1,0:T(8,128)(2,1)S(1)} %get-tuple-element.83), channel_id=1, source_target_pairs={{0,8},{1,12},{2,10},{3,14},{4,9},{5,13},{6,11},{7,15},{8,16},{9,20... | collective-permute-start | bytes 774152 | tf_op jit(solution)/shard_map/ppermute | solution.py:28
  23.9 44.7 %copy-start.6 = (bf16[512,2048]{1,0:T(8,128)(2,1)S(1)}, bf16[512,2048]{1,0:T(8,128)(2,1)}, u32[]{:S(2)}) copy-start(bf16[512,2048]{1,0:T(8,128)(2,1)} %refs_4_.3) | copy-start | bytes 6291460
  23.9 50.6 %copy-start.4 = (bf16[80,2048]{1,0:T(8,128)(2,1)S(1)}, bf16[80,2048]{1,0:T(8,128)(2,1)}, u32[]{:S(2)}) copy-start(bf16[80,2048]{1,0:T(8,128)(2,1)} %inputs.1) | copy-start | bytes 983044
  23.9 21.1 %collective-permute-start.6 = (bf16[336,384]{1,0:T(8,128)(2,1)S(1)}, bf16[336,384]{1,0:T(8,128)(2,1)S(1)}, u32[]{:S(2)}, u32[]{:S(2)}) collective-permute-start(bf16[336,384]{1,0:T(8,128)(2,1)S(1)} %get-tuple-element.84), channel_id=1, source_target_pairs={{0,16},{1,20},{2,18},{3,22},{4,17},{5,21},{6,19},{7,23},{8,24},{9,... | collective-permute-start | bytes 774152 | tf_op jit(solution)/shard_map/ppermute | solution.py:28
  29.5 16.8 %collective-permute-start.11 = (bf16[336,384]{1,0:T(8,128)(2,1)S(1)}, bf16[336,384]{1,0:T(8,128)(2,1)S(1)}, u32[]{:S(2)}, u32[]{:S(2)}) collective-permute-start(bf16[336,384]{1,0:T(8,128)(2,1)S(1)} %collective-permute-done.7.refs_3_), channel_id=1, source_target_pairs={{0,1},{1,0},{2,3},{3,2},{4,5},{5,4},{6,7},{7,6},{8,9},{9,8},{10,11... | collective-permute-start | bytes 774152 | tf_op jit(solution)/shard_map/ppermute | solution.py:28
  30.2 17.8 %collective-permute-start.8 = (bf16[336,384]{1,0:T(8,128)(2,1)S(1)}, bf16[336,384]{1,0:T(8,128)(2,1)S(1)}, u32[]{:S(2)}, u32[]{:S(2)}) collective-permute-start(bf16[336,384]{1,0:T(8,128)(2,1)S(1)} %collective-permute-done.4.refs_0_), channel_id=1, source_target_pairs={{0,1},{1,0},{2,3},{3,2},{4,5},{5,4},{6,7},{7,6},{8,9},{9,8},{10,11... | collective-permute-start | bytes 774152 | tf_op jit(solution)/shard_map/ppermute | solution.py:28
  35.1 12.9 %collective-permute-start.9 = (bf16[336,384]{1,0:T(8,128)(2,1)S(1)}, bf16[336,384]{1,0:T(8,128)(2,1)S(1)}, u32[]{:S(2)}, u32[]{:S(2)}) collective-permute-start(bf16[336,384]{1,0:T(8,128)(2,1)S(1)} %collective-permute-done.5.refs_1_), channel_id=1, source_target_pairs={{0,1},{1,0},{2,3},{3,2},{4,5},{5,4},{6,7},{7,6},{8,9},{9,8},{10,11... | collective-permute-start | bytes 774152 | tf_op jit(solution)/shard_map/ppermute | solution.py:28
  45.0 3.0 %collective-permute-start.10 = (bf16[336,384]{1,0:T(8,128)(2,1)S(1)}, bf16[336,384]{1,0:T(8,128)(2,1)S(1)}, u32[]{:S(2)}, u32[]{:S(2)}) collective-permute-start(bf16[336,384]{1,0:T(8,128)(2,1)S(1)} %collective-permute-done.6.refs_2_), channel_id=1, source_target_pairs={{0,1},{1,0},{2,3},{3,2},{4,5},{5,4},{6,7},{7,6},{8,9},{9,8},{10,11... | collective-permute-start | bytes 774152 | tf_op jit(solution)/shard_map/ppermute | solution.py:28
  48.0 8.0 %collective-permute-start.13 = (bf16[1,2048,704]{1,2,0:T(8,128)(2,1)S(1)}, bf16[1,2048,704]{1,2,0:T(8,128)(2,1)S(1)}, u32[]{:S(2)}, u32[]{:S(2)}) collective-permute-start(bf16[1,2048,704]{1,2,0:T(8,128)(2,1)S(1)} %copy-done.7), channel_id=1, source_target_pairs={{0,1},{1,0},{2,3},{3,2},{4,5},{5,4},{6,7},{7,6},{8,9},{9,8},{10,11... | collective-permute-start | bytes 8650760 | tf_op jit(solution)/shard_map/ppermute | solution.py:28
  56.0 20.9 %copy-start.10 = (s32[80,6]{0,1:T(8,128)S(1)}, s32[80,6]{0,1:T(8,128)}, u32[]{:S(2)}) copy-start(s32[80,6]{0,1:T(8,128)} %param.24) | copy-start | bytes 5764
  57.6 4.7 %collective-permute-start.14 = (bf16[320,128]{1,0:T(8,128)(2,1)S(1)}, bf16[320,128]{1,0:T(8,128)(2,1)S(1)}, u32[]{:S(2)}, u32[]{:S(2)}) collective-permute-start(bf16[320,128]{1,0:T(8,128)(2,1)S(1)} %get-tuple-element.93), channel_id=1, source_target_pairs={{0,0},{1,4},{2,2},{3,6},{4,1},{5,5},{6,3},{7,7},{8,8},{9,12},{10,1... | collective-permute-start | bytes 245768 | tf_op jit(solution)/shard_map/ppermute | solution.py:28
  58.3 5.5 %collective-permute-start.15 = (bf16[320,128]{1,0:T(8,128)(2,1)S(1)}, bf16[320,128]{1,0:T(8,128)(2,1)S(1)}, u32[]{:S(2)}, u32[]{:S(2)}) collective-permute-start(bf16[320,128]{1,0:T(8,128)(2,1)S(1)} %get-tuple-element.94), channel_id=1, source_target_pairs={{0,24},{1,28},{2,26},{3,30},{4,25},{5,29},{6,27},{7,31},{8,0},{9,4... | collective-permute-start | bytes 245768 | tf_op jit(solution)/shard_map/ppermute | solution.py:28
  61.7 5.3 %collective-permute-start.16 = (bf16[320,128]{1,0:T(8,128)(2,1)S(1)}, bf16[320,128]{1,0:T(8,128)(2,1)S(1)}, u32[]{:S(2)}, u32[]{:S(2)}) collective-permute-start(bf16[320,128]{1,0:T(8,128)(2,1)S(1)} %get-tuple-element.95), channel_id=1, source_target_pairs={{0,16},{1,20},{2,18},{3,22},{4,17},{5,21},{6,19},{7,23},{8,24},{9,... | collective-permute-start | bytes 245768 | tf_op jit(solution)/shard_map/ppermute | solution.py:28
  61.7 6.8 %collective-permute-start.17 = (bf16[320,128]{1,0:T(8,128)(2,1)S(1)}, bf16[320,128]{1,0:T(8,128)(2,1)S(1)}, u32[]{:S(2)}, u32[]{:S(2)}) collective-permute-start(bf16[320,128]{1,0:T(8,128)(2,1)S(1)} %get-tuple-element.96), channel_id=1, source_target_pairs={{0,8},{1,12},{2,10},{3,14},{4,9},{5,13},{6,11},{7,15},{8,16},{9,20... | collective-permute-start | bytes 245768 | tf_op jit(solution)/shard_map/ppermute | solution.py:28
  70.1 4.4 %collective-permute-start.18 = (bf16[2,80,2048]{2,1,0:T(8,128)(2,1)S(1)}, bf16[2,80,2048]{2,1,0:T(8,128)(2,1)S(1)}, u32[]{:S(2)}, u32[]{:S(2)}) collective-permute-start(bf16[2,80,2048]{2,1,0:T(8,128)(2,1)S(1)} %get-tuple-element.98), channel_id=1, source_target_pairs={{0,1},{1,0},{2,3},{3,2},{4,5},{5,4},{6,7},{7,6},{8,9},{9,8},{10,11... | collective-permute-start | bytes 1966088 | tf_op jit(solution)/shard_map/ppermute | solution.py:28
  75.4 10.9 %collective-permute-start.19 = (bf16[80,2048]{1,0:T(8,128)(2,1)}, bf16[80,2048]{1,0:T(8,128)(2,1)}, u32[]{:S(2)}, u32[]{:S(2)}) collective-permute-start(bf16[80,2048]{1,0:T(8,128)(2,1)} %get-tuple-element.100), channel_id=1, source_target_pairs={{0,2},{1,3},{2,0},{3,1},{4,6},{5,7},{6,4},{7,5},{8,10},{9,11},{10,... | collective-permute-start | bytes 983048 | tf_op jit(solution)/shard_map/ppermute | solution.py:28
  87.5 12.9 %collective-permute-start.23 = (bf16[80,2176]{1,0:T(8,128)(2,1)S(1)}, bf16[80,2176]{1,0:T(8,128)(2,1)S(1)}, u32[]{:S(2)}, u32[]{:S(2)}) collective-permute-start(bf16[80,2176]{1,0:T(8,128)(2,1)S(1)} %get-tuple-element.115.refs_0_), channel_id=1, source_target_pairs={{0,8},{1,9},{2,10},{3,11},{4,12},{5,13},{6,14},{7,15},{8,16},{9,17... | collective-permute-start | bytes 1044488 | tf_op jit(solution)/shard_map/ppermute | solution.py:28
  88.0 18.0 %collective-permute-start.25 = (bf16[80,2176]{1,0:T(8,128)(2,1)S(1)}, bf16[80,2176]{1,0:T(8,128)(2,1)S(1)}, u32[]{:S(2)}, u32[]{:S(2)}) collective-permute-start(bf16[80,2176]{1,0:T(8,128)(2,1)S(1)} %get-tuple-element.115.refs_0_), channel_id=1, source_target_pairs={{0,24},{1,25},{2,26},{3,27},{4,28},{5,29},{6,30},{7,31},{8,0},{9,1... | collective-permute-start | bytes 1044488 | tf_op jit(solution)/shard_map/ppermute | solution.py:28
  92.8 13.2 %collective-permute-start.20 = (bf16[40,2048]{1,0:T(8,128)(2,1)S(1)}, bf16[40,2048]{1,0:T(8,128)(2,1)S(1)}, u32[]{:S(2)}, u32[]{:S(2)}) collective-permute-start(bf16[40,2048]{1,0:T(8,128)(2,1)S(1)} %get-tuple-element.118), channel_id=1, source_target_pairs={{0,2},{1,3},{2,0},{3,1},{4,6},{5,7},{6,4},{7,5},{8,10},{9,11},{10,... | collective-permute-start | bytes 491528 | tf_op jit(solution)/shard_map/ppermute | solution.py:28
  93.9 12.2 %collective-permute-start.21 = (bf16[40,2048]{1,0:T(8,128)(2,1)S(1)}, bf16[40,2048]{1,0:T(8,128)(2,1)S(1)}, u32[]{:S(2)}, u32[]{:S(2)}) collective-permute-start(bf16[40,2048]{1,0:T(8,128)(2,1)S(1)} %get-tuple-element.119), channel_id=1, source_target_pairs={{0,4},{1,5},{2,6},{3,7},{4,0},{5,1},{6,2},{7,3},{8,12},{9,13},{10,... | collective-permute-start | bytes 491528 | tf_op jit(solution)/shard_map/ppermute | solution.py:28
  95.6 10.4 %collective-permute-start.22 = (bf16[40,2048]{1,0:T(8,128)(2,1)S(1)}, bf16[40,2048]{1,0:T(8,128)(2,1)S(1)}, u32[]{:S(2)}, u32[]{:S(2)}) collective-permute-start(bf16[40,2048]{1,0:T(8,128)(2,1)S(1)} %get-tuple-element.120), channel_id=1, source_target_pairs={{0,6},{1,7},{2,4},{3,5},{4,2},{5,3},{6,0},{7,1},{8,14},{9,15},{10,... | collective-permute-start | bytes 491528 | tf_op jit(solution)/shard_map/ppermute | solution.py:28
  100.4 14.0 %collective-permute-start.24 = (bf16[80,2176]{1,0:T(8,128)(2,1)S(1)}, bf16[80,2176]{1,0:T(8,128)(2,1)S(1)}, u32[]{:S(2)}, u32[]{:S(2)}) collective-permute-start(bf16[80,2176]{1,0:T(8,128)(2,1)S(1)} %collective-permute-done.23.refs_0_), channel_id=1, source_target_pairs={{0,8},{1,9},{2,10},{3,11},{4,12},{5,13},{6,14},{7,15},{8,16},{9,17... | collective-permute-start | bytes 1044488 | tf_op jit(solution)/shard_map/ppermute | solution.py:28
  107.7 10.5 %collective-permute-start.26 = (bf16[80,2048]{1,0:T(8,128)(2,1)S(1)}, bf16[80,2048]{1,0:T(8,128)(2,1)S(1)}, u32[]{:S(2)}, u32[]{:S(2)}) collective-permute-start(bf16[80,2048]{1,0:T(8,128)(2,1)S(1)} %get-tuple-element.125), channel_id=1, source_target_pairs={{0,2},{1,3},{2,0},{3,1},{4,6},{5,7},{6,4},{7,5},{8,10},{9,11},{10,... | collective-permute-start | bytes 983048 | tf_op jit(solution)/shard_map/ppermute | solution.py:28
  108.5 11.0 %collective-permute-start.27 = (bf16[80,2048]{1,0:T(8,128)(2,1)S(1)}, bf16[80,2048]{1,0:T(8,128)(2,1)S(1)}, u32[]{:S(2)}, u32[]{:S(2)}) collective-permute-start(bf16[80,2048]{1,0:T(8,128)(2,1)S(1)} %get-tuple-element.126), channel_id=1, source_target_pairs={{0,4},{1,5},{2,6},{3,7},{4,0},{5,1},{6,2},{7,3},{8,12},{9,13},{10,... | collective-permute-start | bytes 983048 | tf_op jit(solution)/shard_map/ppermute | solution.py:28
  109.1 17.8 %collective-permute-start.28 = (bf16[80,2048]{1,0:T(8,128)(2,1)S(1)}, bf16[80,2048]{1,0:T(8,128)(2,1)S(1)}, u32[]{:S(2)}, u32[]{:S(2)}) collective-permute-start(bf16[80,2048]{1,0:T(8,128)(2,1)S(1)} %get-tuple-element.127), channel_id=1, source_target_pairs={{0,6},{1,7},{2,4},{3,5},{4,2},{5,3},{6,0},{7,1},{8,14},{9,15},{10,... | collective-permute-start | bytes 983048 | tf_op jit(solution)/shard_map/ppermute | solution.py:28
  115.9 18.9 %collective-permute-start.29 = (bf16[40,2048]{1,0:T(8,128)(2,1)S(1)}, bf16[40,2048]{1,0:T(8,128)(2,1)S(1)}, u32[]{:S(2)}, u32[]{:S(2)}) collective-permute-start(bf16[40,2048]{1,0:T(8,128)(2,1)S(1)} %get-tuple-element.136), channel_id=1, source_target_pairs={{0,2},{1,3},{2,0},{3,1},{4,6},{5,7},{6,4},{7,5},{8,10},{9,11},{10,... | collective-permute-start | bytes 491528 | tf_op jit(solution)/shard_map/ppermute | solution.py:28
  116.5 20.5 %collective-permute-start.30 = (bf16[40,2048]{1,0:T(8,128)(2,1)S(1)}, bf16[40,2048]{1,0:T(8,128)(2,1)S(1)}, u32[]{:S(2)}, u32[]{:S(2)}) collective-permute-start(bf16[40,2048]{1,0:T(8,128)(2,1)S(1)} %get-tuple-element.137), channel_id=1, source_target_pairs={{0,4},{1,5},{2,6},{3,7},{4,0},{5,1},{6,2},{7,3},{8,12},{9,13},{10,... | collective-permute-start | bytes 491528 | tf_op jit(solution)/shard_map/ppermute | solution.py:28
  118.2 18.7 %collective-permute-start.31 = (bf16[40,2048]{1,0:T(8,128)(2,1)S(1)}, bf16[40,2048]{1,0:T(8,128)(2,1)S(1)}, u32[]{:S(2)}, u32[]{:S(2)}) collective-permute-start(bf16[40,2048]{1,0:T(8,128)(2,1)S(1)} %get-tuple-element.138), channel_id=1, source_target_pairs={{0,6},{1,7},{2,4},{3,5},{4,2},{5,3},{6,0},{7,1},{8,14},{9,15},{10,... | collective-permute-start | bytes 491528 | tf_op jit(solution)/shard_map/ppermute | solution.py:28
  133.4 12.9 %collective-permute-start.32 = (bf16[80,2048]{1,0:T(8,128)(2,1)S(1)}, bf16[80,2048]{1,0:T(8,128)(2,1)S(1)}, u32[]{:S(2)}, u32[]{:S(2)}) collective-permute-start(bf16[80,2048]{1,0:T(8,128)(2,1)S(1)} %get-tuple-element.142), channel_id=1, source_target_pairs={{0,2},{1,3},{2,0},{3,1},{4,6},{5,7},{6,4},{7,5},{8,10},{9,11},{10,... | collective-permute-start | bytes 983048 | tf_op jit(solution)/shard_map/ppermute | solution.py:28
  134.2 14.2 %collective-permute-start.33 = (bf16[80,2048]{1,0:T(8,128)(2,1)S(1)}, bf16[80,2048]{1,0:T(8,128)(2,1)S(1)}, u32[]{:S(2)}, u32[]{:S(2)}) collective-permute-start(bf16[80,2048]{1,0:T(8,128)(2,1)S(1)} %get-tuple-element.143), channel_id=1, source_target_pairs={{0,4},{1,5},{2,6},{3,7},{4,0},{5,1},{6,2},{7,3},{8,12},{9,13},{10,... | collective-permute-start | bytes 983048 | tf_op jit(solution)/shard_map/ppermute | solution.py:28
  134.8 15.6 %collective-permute-start.34 = (bf16[80,2048]{1,0:T(8,128)(2,1)S(1)}, bf16[80,2048]{1,0:T(8,128)(2,1)S(1)}, u32[]{:S(2)}, u32[]{:S(2)}) collective-permute-start(bf16[80,2048]{1,0:T(8,128)(2,1)S(1)} %get-tuple-element.144), channel_id=1, source_target_pairs={{0,6},{1,7},{2,4},{3,5},{4,2},{5,3},{6,0},{7,1},{8,14},{9,15},{10,... | collective-permute-start | bytes 983048 | tf_op jit(solution)/shard_map/ppermute | solution.py:28
  144.8 10.9 %collective-permute-start.39 = (bf16[40,2048]{1,0:T(8,128)(2,1)S(1)}, bf16[40,2048]{1,0:T(8,128)(2,1)S(1)}, u32[]{:S(2)}, u32[]{:S(2)}) collective-permute-start(bf16[40,2048]{1,0:T(8,128)(2,1)S(1)} %get-tuple-element.153), channel_id=1, source_target_pairs={{0,2},{1,3},{2,0},{3,1},{4,6},{5,7},{6,4},{7,5},{8,10},{9,11},{10,... | collective-permute-start | bytes 491528 | tf_op jit(solution)/shard_map/ppermute | solution.py:28
  145.6 13.6 %collective-permute-start.40 = (bf16[40,2048]{1,0:T(8,128)(2,1)S(1)}, bf16[40,2048]{1,0:T(8,128)(2,1)S(1)}, u32[]{:S(2)}, u32[]{:S(2)}) collective-permute-start(bf16[40,2048]{1,0:T(8,128)(2,1)S(1)} %get-tuple-element.154), channel_id=1, source_target_pairs={{0,4},{1,5},{2,6},{3,7},{4,0},{5,1},{6,2},{7,3},{8,12},{9,13},{10,... | collective-permute-start | bytes 491528 | tf_op jit(solution)/shard_map/ppermute | solution.py:28
  146.3 13.0 %collective-permute-start.41 = (bf16[40,2048]{1,0:T(8,128)(2,1)S(1)}, bf16[40,2048]{1,0:T(8,128)(2,1)S(1)}, u32[]{:S(2)}, u32[]{:S(2)}) collective-permute-start(bf16[40,2048]{1,0:T(8,128)(2,1)S(1)} %get-tuple-element.155), channel_id=1, source_target_pairs={{0,6},{1,7},{2,4},{3,5},{4,2},{5,3},{6,0},{7,1},{8,14},{9,15},{10,... | collective-permute-start | bytes 491528 | tf_op jit(solution)/shard_map/ppermute | solution.py:28
  153.5 18.3 %collective-permute-start.38 = (bf16[80,2048]{1,0:T(8,128)(2,1)S(1)}, bf16[80,2048]{1,0:T(8,128)(2,1)S(1)}, u32[]{:S(2)}, u32[]{:S(2)}) collective-permute-start(bf16[80,2048]{1,0:T(8,128)(2,1)S(1)} %get-tuple-element.145), channel_id=1, source_target_pairs={{0,24},{1,25},{2,26},{3,27},{4,28},{5,29},{6,30},{7,31},{8,0},{9,1... | collective-permute-start | bytes 983048 | tf_op jit(solution)/shard_map/ppermute | solution.py:28
  154.5 8.3 %collective-permute-start.35 = (bf16[40,2048]{1,0:T(8,128)(2,1)S(1)}, bf16[40,2048]{1,0:T(8,128)(2,1)S(1)}, u32[]{:S(2)}, u32[]{:S(2)}) collective-permute-start(bf16[40,2048]{1,0:T(8,128)(2,1)S(1)} %get-tuple-element.146), channel_id=1, source_target_pairs={{0,2},{1,3},{2,0},{3,1},{4,6},{5,7},{6,4},{7,5},{8,10},{9,11},{10,... | collective-permute-start | bytes 491528 | tf_op jit(solution)/shard_map/ppermute | solution.py:28
  155.7 16.1 %collective-permute-start.43 = (bf16[80,2048]{1,0:T(8,128)(2,1)S(1)}, bf16[80,2048]{1,0:T(8,128)(2,1)S(1)}, u32[]{:S(2)}, u32[]{:S(2)}) collective-permute-start(bf16[80,2048]{1,0:T(8,128)(2,1)S(1)} %get-tuple-element.156), channel_id=1, source_target_pairs={{0,8},{1,9},{2,10},{3,11},{4,12},{5,13},{6,14},{7,15},{8,16},{9,17... | collective-permute-start | bytes 983048 | tf_op jit(solution)/shard_map/ppermute | solution.py:28
  161.5 17.6 %collective-permute-start.42 = (bf16[80,2048]{1,0:T(8,128)(2,1)S(1)}, bf16[80,2048]{1,0:T(8,128)(2,1)S(1)}, u32[]{:S(2)}, u32[]{:S(2)}) collective-permute-start(bf16[80,2048]{1,0:T(8,128)(2,1)S(1)} %shard_map.140), channel_id=1, source_target_pairs={{0,16},{1,17},{2,18},{3,19},{4,20},{5,21},{6,22},{7,23},{8,24},{9,... | collective-permute-start | bytes 983048 | tf_op jit(solution)/shard_map/ppermute | solution.py:28
  162.3 5.3 %collective-permute-start.36 = (bf16[40,2048]{1,0:T(8,128)(2,1)S(1)}, bf16[40,2048]{1,0:T(8,128)(2,1)S(1)}, u32[]{:S(2)}, u32[]{:S(2)}) collective-permute-start(bf16[40,2048]{1,0:T(8,128)(2,1)S(1)} %get-tuple-element.148), channel_id=1, source_target_pairs={{0,4},{1,5},{2,6},{3,7},{4,0},{5,1},{6,2},{7,3},{8,12},{9,13},{10,... | collective-permute-start | bytes 491528 | tf_op jit(solution)/shard_map/ppermute | solution.py:28
  162.9 6.7 %collective-permute-start.37 = (bf16[40,2048]{1,0:T(8,128)(2,1)S(1)}, bf16[40,2048]{1,0:T(8,128)(2,1)S(1)}, u32[]{:S(2)}, u32[]{:S(2)}) collective-permute-start(bf16[40,2048]{1,0:T(8,128)(2,1)S(1)} %get-tuple-element.150), channel_id=1, source_target_pairs={{0,6},{1,7},{2,4},{3,5},{4,2},{5,3},{6,0},{7,1},{8,14},{9,15},{10,... | collective-permute-start | bytes 491528 | tf_op jit(solution)/shard_map/ppermute | solution.py:28
  (7 other events, 37.6 us)

commit v7 on v6

--- a/solution.py
+++ b/solution.py
@@ -403,8 +403,8 @@
     near = swap_core(inputs)
     far_near = swap_core(far)
     weights = (w_gate, w_up, w_down)
-    other_gate, other_up, other_down = swap_core(w_gate), None, None
-    far_near, other_gate = lax.optimization_barrier((far_near, other_gate))
+    other_gate, other_up, other_down = swap_core(w_gate), None, swap_core(w_down)
+    far_near, other_gate, other_down = lax.optimization_barrier((far_near, other_gate, other_down))
     top_count = routes.shape[1]
     noted = jnp.concatenate([routes.astype(jnp.float32)] + [gate_weights] * 3, axis=1)
     noted = jnp.pad(noted, ((0, 0), (0, LANES - noted.shape[1])))
@@ -438,9 +438,6 @@
         )
         own = [head_out(sent[turn], turn) for turn in range(depth)]
         beside = [swap_core(block) for block in own]
-        other_down = swap_core(after(w_down, sent[0]))
-        beside[-1], other_down = lax.optimization_barrier((beside[-1], other_down))
-        other_up = swap_core(after(w_up, *beside))
         mixed = call(
             functools.partial(attend_kernel, depth, block_len, head_dim),
             [struct(block_len, head_dim)] * depth,
@@ -452,13 +449,11 @@
             ],
             flops=4 * depth * ctx_count * block_len * block_len * head_dim,
         )
-        *mixed, other_up = lax.optimization_barrier((*mixed, other_up))
         heads = [head_back(mixed[turn], turn) for turn in range(depth)]
     else:
         block = jnp.stack([inputs, near, far, far_near])[exp_index ^ jnp.arange(exp_count)]
         normed = normalize(block.reshape(block_len, model_width), attn_gain)
         heads = attend_gathered(normed, w_query, w_key, w_value, sel_blocks)
-        other_up, other_down = swap_core(w_up), swap_core(w_down)
 
     halves = struct(exp_count // 2, tok_rows, model_width)
     kept, given = call(
@@ -478,10 +473,13 @@
         [inputs, kept, given],
         smem=0,
     )
+    other_up = swap_core(after(w_up, beyond))
     own_weights, other_weights = (
         [gate[0].T, up[0].T, down[0]] for gate, up, down in (weights, (other_gate, other_up, other_down))
     )
-    expert_weights = load(other_weights, [after(weight, beyond) for weight in own_weights])
+    g, u, d = other_weights
+    *own, g, d = load([], [after(weight, beyond) for weight in [*own_weights, g, d]])
+    expert_weights = [*own, g, u, d]
     beyond = move(beyond, lambda z, x, y, c: (z, x, y ^ 1, c))
     beyond, expert_weights = lax.optimization_barrier((beyond, expert_weights))
     residual, ffn_in = call(

time: 180 us -> 176 us (0.978)
  local copies, waits for them, and re-layouts: 8.41 us -> 0.23 us
  starting transfers between devices: 60.5 us -> 66 us
  waiting for transfers between devices: 61.2 us -> 56.4 us
  Pallas kernels: 48 us -> 50.7 us
    unnamed x22 -> x10, local copies, waits for them, and re-layouts: 6.82 us -> 0.03 us
    ppermute x44, starting transfers between devices: 60.5 us -> 66 us  [move(): return lax.ppermute(block, AXES, route)]
    ppermute x44, waiting for transfers between devices: 61.2 us -> 56.4 us  [move(): return lax.ppermute(block, AXES, route)]
    pallas_call x14, Pallas kernels: 48 us -> 50.7 us  [call(): pl.pallas_call(kernel, out_shape=outs, in_specs=[SMEM] * smem + [VMEM] *...]
  transfers between devices with their start and end apart: 44 -> 44, of which waited for: 17 -> 17; matrix products, arithmetic and copies ran while one was open for 1% -> 1% of each run, Pallas kernels for 21% -> 20%
where the time goes in v7:
time: 176 us; the launch traced here: 175 us
  starting transfers between devices  66 us (38%)
  waiting for transfers between devices  56.4 us (32%)
  Pallas kernels  50.7 us (29%)
    ppermute x44, starting transfers between devices, move(): return lax.ppermute(block, AXES, route)  66 us
    ppermute x44, waiting for transfers between devices, move(): return lax.ppermute(block, AXES, route)  56.4 us
    pallas_call x14, Pallas kernels, call(): pl.pallas_call(kernel, out_shape=outs, in_specs=[SMEM] * smem + [VMEM] *...  50.7 us
  transfers between devices with their start and end apart: 44, of which 17 were waited for; matrix products, arithmetic and copies ran while one was open for 1% of the time, Pallas kernels for 20%

profile of v7, /device:TPU:0, one launch (start us, length us, event | category | flops | bytes accessed | tf_op | source)
XLA Modules:
  0.0 175.3 jit_solution(5960055255090675729)
XLA Ops:
  0.5 3.0 %collective-permute-start.1 = (bf16[80,2048]{1,0:T(8,128)(2,1)}, bf16[80,2048]{1,0:T(8,128)(2,1)S(1)}, u32[]{:S(2)}, u32[]{:S(2)}) collective-permute-start(bf16[80,2048]{1,0:T(8,128)(2,1)} %inputs.1), channel_id=1, source_target_pairs={{0,2},{1,3},{2,0},{3,1},{4,6},{5,7},{6,4},{7,5},{8,10},{9,11},{10,... | collective-permute-start | bytes 983048 | tf_op jit(solution)/shard_map/ppermute | solution.py:28
  3.5 8.1 %collective-permute-done.1.refs_1_ = bf16[80,2048]{1,0:T(8,128)(2,1)S(1)} collective-permute-done((bf16[80,2048]{1,0:T(8,128)(2,1)}, bf16[80,2048]{1,0:T(8,128)(2,1)S(1)}, u32[]{:S(2)}, u32[]{:S(2)}) %collective-permute-start.1) | collective-permute-done | bytes 327712 | tf_op jit(solution)/shard_map/ppermute | solution.py:28
  13.2 5.4 %shard_map.127 = (bf16[336,384]{1,0:T(8,128)(2,1)S(1)}, bf16[336,384]{1,0:T(8,128)(2,1)S(1)}, bf16[336,384]{1,0:T(8,128)(2,1)S(1)}, bf16[336,384]{1,0:T(8,128)(2,1)S(1)}) custom-call(s32[5]{0:T(128)S(1)} %stack.20.place, bf16[4,16,384]{2,1,0:T(8,128)(2,1)S(1)} %broadcast_in_dim.11.marks, bf16[80,2048]{1,0:T(8,128)(2,1)S(1)} %collective-permute-done.refs_0_, ...), custom_call_target="tpu_custom_call" | custom-call | flops 2013265920 | bytes 7659540 | tf_op jit(solution)/shard_map/pallas_call | solution.py:87
  19.3 1.9 %collective-permute-start.6 = (bf16[336,384]{1,0:T(8,128)(2,1)S(1)}, bf16[336,384]{1,0:T(8,128)(2,1)S(1)}, u32[]{:S(2)}, u32[]{:S(2)}) collective-permute-start(bf16[336,384]{1,0:T(8,128)(2,1)S(1)} %get-tuple-element.77), channel_id=1, source_target_pairs={{0,8},{1,12},{2,10},{3,14},{4,9},{5,13},{6,11},{7,15},{8,16},{9,20... | collective-permute-start | bytes 774152 | tf_op jit(solution)/shard_map/ppermute | solution.py:28
  21.1 2.6 %collective-permute-start.7 = (bf16[336,384]{1,0:T(8,128)(2,1)S(1)}, bf16[336,384]{1,0:T(8,128)(2,1)S(1)}, u32[]{:S(2)}, u32[]{:S(2)}) collective-permute-start(bf16[336,384]{1,0:T(8,128)(2,1)S(1)} %get-tuple-element.78), channel_id=1, source_target_pairs={{0,16},{1,20},{2,18},{3,22},{4,17},{5,21},{6,19},{7,23},{8,24},{9,... | collective-permute-start | bytes 774152 | tf_op jit(solution)/shard_map/ppermute | solution.py:28
  23.8 1.3 collective-permute-start.8
  25.1 3.2 %collective-permute-start.9 = (bf16[336,384]{1,0:T(8,128)(2,1)S(1)}, bf16[336,384]{1,0:T(8,128)(2,1)S(1)}, u32[]{:S(2)}, u32[]{:S(2)}) collective-permute-start(bf16[336,384]{1,0:T(8,128)(2,1)S(1)} %collective-permute-done.5.refs_0_), channel_id=1, source_target_pairs={{0,1},{1,0},{2,3},{3,2},{4,5},{5,4},{6,7},{7,6},{8,9},{9,8},{10,11... | collective-permute-start | bytes 774152 | tf_op jit(solution)/shard_map/ppermute | solution.py:28
  28.3 5.4 %collective-permute-start.10 = (bf16[336,384]{1,0:T(8,128)(2,1)S(1)}, bf16[336,384]{1,0:T(8,128)(2,1)S(1)}, u32[]{:S(2)}, u32[]{:S(2)}) collective-permute-start(bf16[336,384]{1,0:T(8,128)(2,1)S(1)} %collective-permute-done.6.refs_1_), channel_id=1, source_target_pairs={{0,1},{1,0},{2,3},{3,2},{4,5},{5,4},{6,7},{7,6},{8,9},{9,8},{10,11... | collective-permute-start | bytes 774152 | tf_op jit(solution)/shard_map/ppermute | solution.py:28
  33.7 7.5 %collective-permute-done.7.refs_2_ = bf16[336,384]{1,0:T(8,128)(2,1)S(1)} collective-permute-done((bf16[336,384]{1,0:T(8,128)(2,1)S(1)}, bf16[336,384]{1,0:T(8,128)(2,1)S(1)}, u32[]{:S(2)}, u32[]{:S(2)}) %collective-permute-start.7) | collective-permute-done | bytes 258080 | tf_op jit(solution)/shard_map/ppermute | solution.py:28
  43.1 7.9 %shard_map.128 = (bf16[320,128]{1,0:T(8,128)(2,1)S(1)}, bf16[320,128]{1,0:T(8,128)(2,1)S(1)}, bf16[320,128]{1,0:T(8,128)(2,1)S(1)}, bf16[320,128]{1,0:T(8,128)(2,1)S(1)}) custom-call(s32[5]{0:T(128)S(1)} %stack.20.place, bf16[336,384]{1,0:T(8,128)(2,1)S(1)} %collective-permute-done.5.refs_0_, bf16[336,384]{1,0:T(8,128)(2,1)S(1)} %collective-permute-done.6.refs_1_, ...), custom_call_target="tpu_custom_call" | custom-call | flops 1677721600 | bytes 2064404 | tf_op jit(solution)/shard_map/pallas_call | solution.py:87
  51.8 7.1 %collective-permute-start.14 = (bf16[320,128]{1,0:T(8,128)(2,1)S(1)}, bf16[320,128]{1,0:T(8,128)(2,1)S(1)}, u32[]{:S(2)}, u32[]{:S(2)}) collective-permute-start(bf16[320,128]{1,0:T(8,128)(2,1)S(1)} %get-tuple-element.81), channel_id=1, source_target_pairs={{0,24},{1,28},{2,26},{3,30},{4,25},{5,29},{6,27},{7,31},{8,0},{9,4... | collective-permute-start | bytes 245768 | tf_op jit(solution)/shard_map/ppermute | solution.py:28
  59.5 1.4 collective-permute-done.14.refs_1_
  61.0 5.1 %collective-permute-done.15.refs_2_ = bf16[320,128]{1,0:T(8,128)(2,1)S(1)} collective-permute-done((bf16[320,128]{1,0:T(8,128)(2,1)S(1)}, bf16[320,128]{1,0:T(8,128)(2,1)S(1)}, u32[]{:S(2)}, u32[]{:S(2)}) %collective-permute-start.15) | collective-permute-done | bytes 81952 | tf_op jit(solution)/shard_map/ppermute | solution.py:28
  66.1 1.5 shard_map.129
  67.6 3.1 %collective-permute-start.17 = (bf16[2,80,2048]{2,1,0:T(8,128)(2,1)S(1)}, bf16[2,80,2048]{2,1,0:T(8,128)(2,1)S(1)}, u32[]{:S(2)}, u32[]{:S(2)}) collective-permute-start(bf16[2,80,2048]{2,1,0:T(8,128)(2,1)S(1)} %get-tuple-element.85), channel_id=1, source_target_pairs={{0,1},{1,0},{2,3},{3,2},{4,5},{5,4},{6,7},{7,6},{8,9},{9,8},{10,11... | collective-permute-start | bytes 1966088 | tf_op jit(solution)/shard_map/ppermute | solution.py:28
  70.7 1.7 collective-permute-done.17.given
  73.0 1.7 collective-permute-start.18
  74.9 5.2 %shard_map.131 = (bf16[704,2048]{1,0:T(8,128)(2,1)S(1)}, bf16[704,2048]{1,0:T(8,128)(2,1)S(1)}, bf16[704,2048]{1,0:T(8,128)(2,1)S(1)}, bf16[704,2048]{1,0:T(8,128)(2,1)S(1)}, bf16[704,2048]{1,0:T(8,128)(2,1)S(1)}) custom-call(bf16[704,2048]{1,0:T(8,128)(2,1)} %bitcast.23, bf16[704,2048]{1,0:T(8,128)(2,1)} %bitcast.9.refs_1_, bf16[704,2048]{1,0:T(8,128)(2,1)} %bitcast.24, ...), custom_call_target="tpu_custom_call" | custom-call | bytes 14417920 | tf_op jit(solution)/shard_map/pallas_call | solution.py:87
  80.1 2.7 %collective-permute-done.18.far = bf16[80,2048]{1,0:T(8,128)(2,1)S(1)} collective-permute-done((bf16[80,2048]{1,0:T(8,128)(2,1)S(1)}, bf16[80,2048]{1,0:T(8,128)(2,1)S(1)}, u32[]{:S(2)}, u32[]{:S(2)}) %collective-permute-start.18) | collective-permute-done | bytes 327712 | tf_op jit(solution)/shard_map/ppermute | solution.py:28
  83.1 3.8 %collective-permute-start.25 = (bf16[80,2176]{1,0:T(8,128)(2,1)S(1)}, bf16[80,2176]{1,0:T(8,128)(2,1)S(1)}, u32[]{:S(2)}, u32[]{:S(2)}) collective-permute-start(bf16[80,2176]{1,0:T(8,128)(2,1)S(1)} %get-tuple-element.103.refs_0_), channel_id=1, source_target_pairs={{0,24},{1,25},{2,26},{3,27},{4,28},{5,29},{6,30},{7,31},{8,0},{9,1... | collective-permute-start | bytes 1044488 | tf_op jit(solution)/shard_map/ppermute | solution.py:28
  86.9 1.5 shard_map.133
  88.4 1.8 %collective-permute-start.20 = (bf16[40,2048]{1,0:T(8,128)(2,1)S(1)}, bf16[40,2048]{1,0:T(8,128)(2,1)S(1)}, u32[]{:S(2)}, u32[]{:S(2)}) collective-permute-start(bf16[40,2048]{1,0:T(8,128)(2,1)S(1)} %get-tuple-element.106), channel_id=1, source_target_pairs={{0,2},{1,3},{2,0},{3,1},{4,6},{5,7},{6,4},{7,5},{8,10},{9,11},{10,... | collective-permute-start | bytes 491528 | tf_op jit(solution)/shard_map/ppermute | solution.py:28
  92.0 4.0 %collective-permute-done.23.refs_0_ = bf16[80,2176]{1,0:T(8,128)(2,1)S(1)} collective-permute-done((bf16[80,2176]{1,0:T(8,128)(2,1)S(1)}, bf16[80,2176]{1,0:T(8,128)(2,1)S(1)}, u32[]{:S(2)}, u32[]{:S(2)}) %collective-permute-start.23) | collective-permute-done | bytes 348192 | tf_op jit(solution)/shard_map/ppermute | solution.py:28
  96.0 2.1 %collective-permute-start.24 = (bf16[80,2176]{1,0:T(8,128)(2,1)S(1)}, bf16[80,2176]{1,0:T(8,128)(2,1)S(1)}, u32[]{:S(2)}, u32[]{:S(2)}) collective-permute-start(bf16[80,2176]{1,0:T(8,128)(2,1)S(1)} %collective-permute-done.23.refs_0_), channel_id=1, source_target_pairs={{0,8},{1,9},{2,10},{3,11},{4,12},{5,13},{6,14},{7,15},{8,16},{9,17... | collective-permute-start | bytes 1044488 | tf_op jit(solution)/shard_map/ppermute | solution.py:28
  98.3 1.7 collective-permute-done.25.refs_1_
  100.0 1.7 shard_map.134
  101.7 1.8 %collective-permute-start.26 = (bf16[80,2048]{1,0:T(8,128)(2,1)S(1)}, bf16[80,2048]{1,0:T(8,128)(2,1)S(1)}, u32[]{:S(2)}, u32[]{:S(2)}) collective-permute-start(bf16[80,2048]{1,0:T(8,128)(2,1)S(1)} %get-tuple-element.113), channel_id=1, source_target_pairs={{0,2},{1,3},{2,0},{3,1},{4,6},{5,7},{6,4},{7,5},{8,10},{9,11},{10,... | collective-permute-start | bytes 983048 | tf_op jit(solution)/shard_map/ppermute | solution.py:28
  105.2 4.0 %collective-permute-done.24.refs_0_ = bf16[80,2176]{1,0:T(8,128)(2,1)S(1)} collective-permute-done((bf16[80,2176]{1,0:T(8,128)(2,1)S(1)}, bf16[80,2176]{1,0:T(8,128)(2,1)S(1)}, u32[]{:S(2)}, u32[]{:S(2)}) %collective-permute-start.24) | collective-permute-done | bytes 348192 | tf_op jit(solution)/shard_map/ppermute | solution.py:28
  109.2 1.5 shard_map.135
  110.7 1.8 %collective-permute-start.29 = (bf16[40,2048]{1,0:T(8,128)(2,1)S(1)}, bf16[40,2048]{1,0:T(8,128)(2,1)S(1)}, u32[]{:S(2)}, u32[]{:S(2)}) collective-permute-start(bf16[40,2048]{1,0:T(8,128)(2,1)S(1)} %get-tuple-element.124), channel_id=1, source_target_pairs={{0,2},{1,3},{2,0},{3,1},{4,6},{5,7},{6,4},{7,5},{8,10},{9,11},{10,... | collective-permute-start | bytes 491528 | tf_op jit(solution)/shard_map/ppermute | solution.py:28
  114.3 6.7 %collective-permute-done.28.refs_3_ = bf16[80,2048]{1,0:T(8,128)(2,1)S(1)} collective-permute-done((bf16[80,2048]{1,0:T(8,128)(2,1)S(1)}, bf16[80,2048]{1,0:T(8,128)(2,1)S(1)}, u32[]{:S(2)}, u32[]{:S(2)}) %collective-permute-start.28) | collective-permute-done | bytes 327712 | tf_op jit(solution)/shard_map/ppermute | solution.py:28
  121.0 8.2 %shard_map.136 = (bf16[80,2048]{1,0:T(8,128)(2,1)S(1)}, bf16[80,2048]{1,0:T(8,128)(2,1)S(1)}, bf16[80,2048]{1,0:T(8,128)(2,1)S(1)}, bf16[80,2048]{1,0:T(8,128)(2,1)S(1)}) custom-call(bf16[80,2048]{1,0:T(8,128)(2,1)S(1)} %get-tuple-element.110.refs_0_, bf16[80,2048]{1,0:T(8,128)(2,1)S(1)} %collective-permute-done.26.refs_1_, ...), custom_call_target="tpu_custom_call" | custom-call | flops 5536481280 | bytes 18612224 | tf_op jit(solution)/shard_map/pallas_call | solution.py:87
  129.2 1.8 %collective-permute-start.32 = (bf16[80,2048]{1,0:T(8,128)(2,1)S(1)}, bf16[80,2048]{1,0:T(8,128)(2,1)S(1)}, u32[]{:S(2)}, u32[]{:S(2)}) collective-permute-start(bf16[80,2048]{1,0:T(8,128)(2,1)S(1)} %get-tuple-element.130), channel_id=1, source_target_pairs={{0,2},{1,3},{2,0},{3,1},{4,6},{5,7},{6,4},{7,5},{8,10},{9,11},{10,... | collective-permute-start | bytes 983048 | tf_op jit(solution)/shard_map/ppermute | solution.py:28
  130.9 1.1 collective-permute-start.33
  132.7 9.7 %shard_map.137 = (bf16[40,2048]{1,0:T(8,128)(2,1)S(1)}, bf16[40,2048]{1,0:T(8,128)(2,1)S(1)}, bf16[40,2048]{1,0:T(8,128)(2,1)S(1)}, bf16[40,2048]{1,0:T(8,128)(2...) custom-call(bf16[40,2048]{1,0:T(8,128)(2,1)S(1)} %get-tuple-element., ...), custom_call_target="tpu_custom_call" | custom-call | flops 6643777536 | bytes 18612224 | tf_op jit(solution)/shard_map/pallas_call | solution.py:87
  142.4 1.8 %collective-permute-start.39 = (bf16[40,2048]{1,0:T(8,128)(2,1)S(1)}, bf16[40,2048]{1,0:T(8,128)(2,1)S(1)}, u32[]{:S(2)}, u32[]{:S(2)}) collective-permute-start(bf16[40,2048]{1,0:T(8,128)(2,1)S(1)} %get-tuple-element.141), channel_id=1, source_target_pairs={{0,2},{1,3},{2,0},{3,1},{4,6},{5,7},{6,4},{7,5},{8,10},{9,11},{10,... | collective-permute-start | bytes 491528 | tf_op jit(solution)/shard_map/ppermute | solution.py:28
  144.2 1.1 collective-permute-start.40
  146.0 3.1 %shard_map.138 = (bf16[80,2048]{1,0:T(8,128)(2,1)S(1)}, bf16[80,2048]{1,0:T(8,128)(2,1)S(1)}) custom-call(s32[5]{0:T(128)S(1)} %stack.20.place, bf16[160,128]{1,0:T(8,128)(2,1)S(1)} %get-tuple-element.129.notes, bf16[80,2048]{1,0:T(8,128)(2,1)S(1)} %get-tuple-element.122.refs_0_, bf16[80,2048]{1,0:T(8,128)(2,1)S(1)} %collective-permute-done.32.refs_1_, ...), custom_call_target="tpu_custom_call" | custom-call | flops 419430400 | bytes 1351700 | tf_op jit(solution)/shard_map/pallas_call | solution.py:87
  149.1 3.1 %collective-permute-start.38 = (bf16[80,2048]{1,0:T(8,128)(2,1)S(1)}, bf16[80,2048]{1,0:T(8,128)(2,1)S(1)}, u32[]{:S(2)}, u32[]{:S(2)}) collective-permute-start(bf16[80,2048]{1,0:T(8,128)(2,1)S(1)} %get-tuple-element.133), channel_id=1, source_target_pairs={{0,24},{1,25},{2,26},{3,27},{4,28},{5,29},{6,30},{7,31},{8,0},{9,1... | collective-permute-start | bytes 983048 | tf_op jit(solution)/shard_map/ppermute | solution.py:28
  152.2 1.7 collective-permute-start.35
  153.8 2.3 %shard_map.140 = bf16[80,2048]{1,0:T(8,128)(2,1)S(1)} custom-call(s32[5]{0:T(128)S(1)} %stack.20.place, bf16[80,128]{1,0:T(8,128)(2,1)S(1)} %get-tuple-element.139.notes, bf16[40,2048]{1,0:T(8,128)(2,1)S(1)} %get-tuple-element.140.refs_0_, bf16[40,2048]{1,0:T(8,128)(2,1)S(1)} %collective-permute-done.39.refs_1_, ...), custom_call_target="tpu_custom_call" | custom-call | flops 104857600 | bytes 675860 | tf_op jit(solution)/shard_map/pallas_call | solution.py:87
  156.2 2.1 %collective-permute-start.42 = (bf16[80,2048]{1,0:T(8,128)(2,1)S(1)}, bf16[80,2048]{1,0:T(8,128)(2,1)S(1)}, u32[]{:S(2)}, u32[]{:S(2)}) collective-permute-start(bf16[80,2048]{1,0:T(8,128)(2,1)S(1)} %shard_map.140), channel_id=1, source_target_pairs={{0,16},{1,17},{2,18},{3,19},{4,20},{5,21},{6,22},{7,23},{8,24},{9,... | collective-permute-start | bytes 983048 | tf_op jit(solution)/shard_map/ppermute | solution.py:28
  158.3 1.4 collective-permute-start.36
  159.7 1.3 collective-permute-start.37
  161.0 2.7 %collective-permute-done.36.refs_2_ = bf16[40,2048]{1,0:T(8,128)(2,1)S(1)} collective-permute-done((bf16[40,2048]{1,0:T(8,128)(2,1)S(1)}, bf16[40,2048]{1,0:T(8,128)(2,1)S(1)}, u32[]{:S(2)}, u32[]{:S(2)}) %collective-permute-start.36) | collective-permute-done | bytes 163872 | tf_op jit(solution)/shard_map/ppermute | solution.py:28
  163.6 2.4 %collective-permute-done.37.refs_3_ = bf16[40,2048]{1,0:T(8,128)(2,1)S(1)} collective-permute-done((bf16[40,2048]{1,0:T(8,128)(2,1)S(1)}, bf16[40,2048]{1,0:T(8,128)(2,1)S(1)}, u32[]{:S(2)}, u32[]{:S(2)}) %collective-permute-start.37) | collective-permute-done | bytes 163872 | tf_op jit(solution)/shard_map/ppermute | solution.py:28
  166.0 2.3 %shard_map.139 = bf16[80,2048]{1,0:T(8,128)(2,1)S(1)} custom-call(s32[5]{0:T(128)S(1)} %stack.20.place, bf16[80,128]{1,0:T(8,128)(2,1)S(1)} %get-tuple-element.104.notes, bf16[40,2048]{1,0:T(8,128)(2,1)S(1)} %get-tuple-element.127.refs_0_, bf16[40,2048]{1,0:T(8,128)(2,1)S(1)} %collective-permute-done.35.refs_1_, ...), custom_call_target="tpu_custom_call" | custom-call | flops 104857600 | bytes 675860 | tf_op jit(solution)/shard_map/pallas_call | solution.py:87
  168.3 6.0 %collective-permute-done.42 = bf16[80,2048]{1,0:T(8,128)(2,1)S(1)} collective-permute-done((bf16[80,2048]{1,0:T(8,128)(2,1)S(1)}, bf16[80,2048]{1,0:T(8,128)(2,1)S(1)}, u32[]{:S(2)}, u32[]{:S(2)}) %collective-permute-start.42) | collective-permute-done | bytes 327712 | tf_op jit(solution)/shard_map/ppermute | solution.py:28
  (74 shorter events, 14.8 us)
Async XLA Ops:
  0.0 13.2 %collective-permute-start.3 = (bf16[1,2048,704]{1,2,0:T(8,128)(2,1)}, bf16[1,2048,704]{1,2,0:T(8,128)(2,1)}, u32[]{:S(2)}, u32[]{:S(2)}) collective-permute-start(bf16[1,2048,704]{1,2,0:T(8,128)(2,1)} %param.21), channel_id=1, source_target_pairs={{0,1},{1,0},{2,3},{3,2},{4,5},{5,4},{6,7},{7,6},{8,9},{9,8},{10,11... | collective-permute-start | bytes 8650760 | tf_op jit(solution)/shard_map/ppermute | solution.py:28
  0.5 12.7 %collective-permute-start.4 = (bf16[1,704,2048]{2,1,0:T(8,128)(2,1)}, bf16[1,704,2048]{2,1,0:T(8,128)(2,1)}, u32[]{:S(2)}, u32[]{:S(2)}) collective-permute-start(bf16[1,704,2048]{2,1,0:T(8,128)(2,1)} %param.23), channel_id=1, source_target_pairs={{0,1},{1,0},{2,3},{3,2},{4,5},{5,4},{6,7},{7,6},{8,9},{9,8},{10,11... | collective-permute-start | bytes 8650760 | tf_op jit(solution)/shard_map/ppermute | solution.py:28
  0.5 11.1 %collective-permute-start.1 = (bf16[80,2048]{1,0:T(8,128)(2,1)}, bf16[80,2048]{1,0:T(8,128)(2,1)S(1)}, u32[]{:S(2)}, u32[]{:S(2)}) collective-permute-start(bf16[80,2048]{1,0:T(8,128)(2,1)} %inputs.1), channel_id=1, source_target_pairs={{0,2},{1,3},{2,0},{3,1},{4,6},{5,7},{6,4},{7,5},{8,10},{9,11},{10,... | collective-permute-start | bytes 983048 | tf_op jit(solution)/shard_map/ppermute | solution.py:28
  3.5 9.7 %collective-permute-start = (bf16[80,2048]{1,0:T(8,128)(2,1)}, bf16[80,2048]{1,0:T(8,128)(2,1)S(1)}, u32[]{:S(2)}, u32[]{:S(2)}) collective-permute-start(bf16[80,2048]{1,0:T(8,128)(2,1)} %inputs.1), channel_id=1, source_target_pairs={{0,1},{1,0},{2,3},{3,2},{4,5},{5,4},{6,7},{7,6},{8,9},{9,8},{10,11... | collective-permute-start | bytes 983048 | tf_op jit(solution)/shard_map/ppermute | solution.py:28
  11.6 1.6 collective-permute-start.2
  18.6 6.5 %collective-permute-start.5 = (bf16[336,384]{1,0:T(8,128)(2,1)S(1)}, bf16[336,384]{1,0:T(8,128)(2,1)S(1)}, u32[]{:S(2)}, u32[]{:S(2)}) collective-permute-start(bf16[336,384]{1,0:T(8,128)(2,1)S(1)} %get-tuple-element.76), channel_id=1, source_target_pairs={{0,0},{1,4},{2,2},{3,6},{4,1},{5,5},{6,3},{7,7},{8,8},{9,12},{10,1... | collective-permute-start | bytes 774152 | tf_op jit(solution)/shard_map/ppermute | solution.py:28
  19.3 9.0 %collective-permute-start.6 = (bf16[336,384]{1,0:T(8,128)(2,1)S(1)}, bf16[336,384]{1,0:T(8,128)(2,1)S(1)}, u32[]{:S(2)}, u32[]{:S(2)}) collective-permute-start(bf16[336,384]{1,0:T(8,128)(2,1)S(1)} %get-tuple-element.77), channel_id=1, source_target_pairs={{0,8},{1,12},{2,10},{3,14},{4,9},{5,13},{6,11},{7,15},{8,16},{9,20... | collective-permute-start | bytes 774152 | tf_op jit(solution)/shard_map/ppermute | solution.py:28
  21.1 20.1 %collective-permute-start.7 = (bf16[336,384]{1,0:T(8,128)(2,1)S(1)}, bf16[336,384]{1,0:T(8,128)(2,1)S(1)}, u32[]{:S(2)}, u32[]{:S(2)}) collective-permute-start(bf16[336,384]{1,0:T(8,128)(2,1)S(1)} %get-tuple-element.78), channel_id=1, source_target_pairs={{0,16},{1,20},{2,18},{3,22},{4,17},{5,21},{6,19},{7,23},{8,24},{9,... | collective-permute-start | bytes 774152 | tf_op jit(solution)/shard_map/ppermute | solution.py:28
  23.7 42.3 %copy-start.2 = (bf16[512,2048]{1,0:T(8,128)(2,1)S(1)}, bf16[512,2048]{1,0:T(8,128)(2,1)}, u32[]{:S(2)}) copy-start(bf16[512,2048]{1,0:T(8,128)(2,1)} %refs_4_.3) | copy-start | bytes 6291460
  23.7 48.7 %copy-start = (bf16[80,2048]{1,0:T(8,128)(2,1)S(1)}, bf16[80,2048]{1,0:T(8,128)(2,1)}, u32[]{:S(2)}) copy-start(bf16[80,2048]{1,0:T(8,128)(2,1)} %inputs.1) | copy-start | bytes 983044
  23.8 17.9 %collective-permute-start.8 = (bf16[336,384]{1,0:T(8,128)(2,1)S(1)}, bf16[336,384]{1,0:T(8,128)(2,1)S(1)}, u32[]{:S(2)}, u32[]{:S(2)}) collective-permute-start(bf16[336,384]{1,0:T(8,128)(2,1)S(1)} %get-tuple-element.79), channel_id=1, source_target_pairs={{0,24},{1,28},{2,26},{3,30},{4,25},{5,29},{6,27},{7,31},{8,0},{9,4... | collective-permute-start | bytes 774152 | tf_op jit(solution)/shard_map/ppermute | solution.py:28
  25.1 16.6 %collective-permute-start.9 = (bf16[336,384]{1,0:T(8,128)(2,1)S(1)}, bf16[336,384]{1,0:T(8,128)(2,1)S(1)}, u32[]{:S(2)}, u32[]{:S(2)}) collective-permute-start(bf16[336,384]{1,0:T(8,128)(2,1)S(1)} %collective-permute-done.5.refs_0_), channel_id=1, source_target_pairs={{0,1},{1,0},{2,3},{3,2},{4,5},{5,4},{6,7},{7,6},{8,9},{9,8},{10,11... | collective-permute-start | bytes 774152 | tf_op jit(solution)/shard_map/ppermute | solution.py:28
  28.3 13.5 %collective-permute-start.10 = (bf16[336,384]{1,0:T(8,128)(2,1)S(1)}, bf16[336,384]{1,0:T(8,128)(2,1)S(1)}, u32[]{:S(2)}, u32[]{:S(2)}) collective-permute-start(bf16[336,384]{1,0:T(8,128)(2,1)S(1)} %collective-permute-done.6.refs_1_), channel_id=1, source_target_pairs={{0,1},{1,0},{2,3},{3,2},{4,5},{5,4},{6,7},{7,6},{8,9},{9,8},{10,11... | collective-permute-start | bytes 774152 | tf_op jit(solution)/shard_map/ppermute | solution.py:28
  41.2 1.5 collective-permute-start.11
  41.6 1.5 collective-permute-start.12
  51.1 23.7 %copy-start.4 = (s32[80,6]{0,1:T(8,128)S(1)}, s32[80,6]{0,1:T(8,128)}, u32[]{:S(2)}) copy-start(s32[80,6]{0,1:T(8,128)} %param.24) | copy-start | bytes 5764
  51.1 23.7 %copy-start.3 = (f32[80,6]{0,1:T(8,128)S(1)}, f32[80,6]{0,1:T(8,128)}, u32[]{:S(2)}) copy-start(f32[80,6]{0,1:T(8,128)} %param.25) | copy-start | bytes 5764
  51.1 8.4 %collective-permute-start.13 = (bf16[320,128]{1,0:T(8,128)(2,1)S(1)}, bf16[320,128]{1,0:T(8,128)(2,1)S(1)}, u32[]{:S(2)}, u32[]{:S(2)}) collective-permute-start(bf16[320,128]{1,0:T(8,128)(2,1)S(1)} %get-tuple-element.80), channel_id=1, source_target_pairs={{0,0},{1,4},{2,2},{3,6},{4,1},{5,5},{6,3},{7,7},{8,8},{9,12},{10,1... | collective-permute-start | bytes 245768 | tf_op jit(solution)/shard_map/ppermute | solution.py:28
  51.8 9.2 %collective-permute-start.14 = (bf16[320,128]{1,0:T(8,128)(2,1)S(1)}, bf16[320,128]{1,0:T(8,128)(2,1)S(1)}, u32[]{:S(2)}, u32[]{:S(2)}) collective-permute-start(bf16[320,128]{1,0:T(8,128)(2,1)S(1)} %get-tuple-element.81), channel_id=1, source_target_pairs={{0,24},{1,28},{2,26},{3,30},{4,25},{5,29},{6,27},{7,31},{8,0},{9,4... | collective-permute-start | bytes 245768 | tf_op jit(solution)/shard_map/ppermute | solution.py:28
  58.9 7.2 %collective-permute-start.15 = (bf16[320,128]{1,0:T(8,128)(2,1)S(1)}, bf16[320,128]{1,0:T(8,128)(2,1)S(1)}, u32[]{:S(2)}, u32[]{:S(2)}) collective-permute-start(bf16[320,128]{1,0:T(8,128)(2,1)S(1)} %get-tuple-element.82), channel_id=1, source_target_pairs={{0,16},{1,20},{2,18},{3,22},{4,17},{5,21},{6,19},{7,23},{8,24},{9,... | collective-permute-start | bytes 245768 | tf_op jit(solution)/shard_map/ppermute | solution.py:28
  59.0 7.1 %collective-permute-start.16 = (bf16[320,128]{1,0:T(8,128)(2,1)S(1)}, bf16[320,128]{1,0:T(8,128)(2,1)S(1)}, u32[]{:S(2)}, u32[]{:S(2)}) collective-permute-start(bf16[320,128]{1,0:T(8,128)(2,1)S(1)} %get-tuple-element.83), channel_id=1, source_target_pairs={{0,8},{1,12},{2,10},{3,14},{4,9},{5,13},{6,11},{7,15},{8,16},{9,20... | collective-permute-start | bytes 245768 | tf_op jit(solution)/shard_map/ppermute | solution.py:28
  67.6 4.8 %collective-permute-start.17 = (bf16[2,80,2048]{2,1,0:T(8,128)(2,1)S(1)}, bf16[2,80,2048]{2,1,0:T(8,128)(2,1)S(1)}, u32[]{:S(2)}, u32[]{:S(2)}) collective-permute-start(bf16[2,80,2048]{2,1,0:T(8,128)(2,1)S(1)} %get-tuple-element.85), channel_id=1, source_target_pairs={{0,1},{1,0},{2,3},{3,2},{4,5},{5,4},{6,7},{7,6},{8,9},{9,8},{10,11... | collective-permute-start | bytes 1966088 | tf_op jit(solution)/shard_map/ppermute | solution.py:28
  72.6 10.2 %collective-permute-start.19 = (bf16[1,2048,704]{1,2,0:T(8,128)(2,1)}, bf16[1,2048,704]{1,2,0:T(8,128)(2,1)}, u32[]{:S(2)}, u32[]{:S(2)}) collective-permute-start(bf16[1,2048,704]{1,2,0:T(8,128)(2,1)} %param.22), channel_id=1, source_target_pairs={{0,1},{1,0},{2,3},{3,2},{4,5},{5,4},{6,7},{7,6},{8,9},{9,8},{10,11... | collective-permute-start | bytes 8650760 | tf_op jit(solution)/shard_map/ppermute | solution.py:28
  73.0 9.8 %collective-permute-start.18 = (bf16[80,2048]{1,0:T(8,128)(2,1)S(1)}, bf16[80,2048]{1,0:T(8,128)(2,1)S(1)}, u32[]{:S(2)}, u32[]{:S(2)}) collective-permute-start(bf16[80,2048]{1,0:T(8,128)(2,1)S(1)} %get-tuple-element.87), channel_id=1, source_target_pairs={{0,2},{1,3},{2,0},{3,1},{4,6},{5,7},{6,4},{7,5},{8,10},{9,11},{10,... | collective-permute-start | bytes 983048 | tf_op jit(solution)/shard_map/ppermute | solution.py:28
  83.1 12.9 %collective-permute-start.23 = (bf16[80,2176]{1,0:T(8,128)(2,1)S(1)}, bf16[80,2176]{1,0:T(8,128)(2,1)S(1)}, u32[]{:S(2)}, u32[]{:S(2)}) collective-permute-start(bf16[80,2176]{1,0:T(8,128)(2,1)S(1)} %get-tuple-element.103.refs_0_), channel_id=1, source_target_pairs={{0,8},{1,9},{2,10},{3,11},{4,12},{5,13},{6,14},{7,15},{8,16},{9,17... | collective-permute-start | bytes 1044488 | tf_op jit(solution)/shard_map/ppermute | solution.py:28
  83.1 16.9 %collective-permute-start.25 = (bf16[80,2176]{1,0:T(8,128)(2,1)S(1)}, bf16[80,2176]{1,0:T(8,128)(2,1)S(1)}, u32[]{:S(2)}, u32[]{:S(2)}) collective-permute-start(bf16[80,2176]{1,0:T(8,128)(2,1)S(1)} %get-tuple-element.103.refs_0_), channel_id=1, source_target_pairs={{0,24},{1,25},{2,26},{3,27},{4,28},{5,29},{6,30},{7,31},{8,0},{9,1... | collective-permute-start | bytes 1044488 | tf_op jit(solution)/shard_map/ppermute | solution.py:28
  88.4 9.7 %collective-permute-start.20 = (bf16[40,2048]{1,0:T(8,128)(2,1)S(1)}, bf16[40,2048]{1,0:T(8,128)(2,1)S(1)}, u32[]{:S(2)}, u32[]{:S(2)}) collective-permute-start(bf16[40,2048]{1,0:T(8,128)(2,1)S(1)} %get-tuple-element.106), channel_id=1, source_target_pairs={{0,2},{1,3},{2,0},{3,1},{4,6},{5,7},{6,4},{7,5},{8,10},{9,11},{10,... | collective-permute-start | bytes 491528 | tf_op jit(solution)/shard_map/ppermute | solution.py:28
  90.2 7.9 %collective-permute-start.21 = (bf16[40,2048]{1,0:T(8,128)(2,1)S(1)}, bf16[40,2048]{1,0:T(8,128)(2,1)S(1)}, u32[]{:S(2)}, u32[]{:S(2)}) collective-permute-start(bf16[40,2048]{1,0:T(8,128)(2,1)S(1)} %get-tuple-element.107), channel_id=1, source_target_pairs={{0,4},{1,5},{2,6},{3,7},{4,0},{5,1},{6,2},{7,3},{8,12},{9,13},{10,... | collective-permute-start | bytes 491528 | tf_op jit(solution)/shard_map/ppermute | solution.py:28
  91.1 7.2 %collective-permute-start.22 = (bf16[40,2048]{1,0:T(8,128)(2,1)S(1)}, bf16[40,2048]{1,0:T(8,128)(2,1)S(1)}, u32[]{:S(2)}, u32[]{:S(2)}) collective-permute-start(bf16[40,2048]{1,0:T(8,128)(2,1)S(1)} %get-tuple-element.108), channel_id=1, source_target_pairs={{0,6},{1,7},{2,4},{3,5},{4,2},{5,3},{6,0},{7,1},{8,14},{9,15},{10,... | collective-permute-start | bytes 491528 | tf_op jit(solution)/shard_map/ppermute | solution.py:28
  96.0 13.2 %collective-permute-start.24 = (bf16[80,2176]{1,0:T(8,128)(2,1)S(1)}, bf16[80,2176]{1,0:T(8,128)(2,1)S(1)}, u32[]{:S(2)}, u32[]{:S(2)}) collective-permute-start(bf16[80,2176]{1,0:T(8,128)(2,1)S(1)} %collective-permute-done.23.refs_0_), channel_id=1, source_target_pairs={{0,8},{1,9},{2,10},{3,11},{4,12},{5,13},{6,14},{7,15},{8,16},{9,17... | collective-permute-start | bytes 1044488 | tf_op jit(solution)/shard_map/ppermute | solution.py:28
  101.7 12.0 %collective-permute-start.26 = (bf16[80,2048]{1,0:T(8,128)(2,1)S(1)}, bf16[80,2048]{1,0:T(8,128)(2,1)S(1)}, u32[]{:S(2)}, u32[]{:S(2)}) collective-permute-start(bf16[80,2048]{1,0:T(8,128)(2,1)S(1)} %get-tuple-element.113), channel_id=1, source_target_pairs={{0,2},{1,3},{2,0},{3,1},{4,6},{5,7},{6,4},{7,5},{8,10},{9,11},{10,... | collective-permute-start | bytes 983048 | tf_op jit(solution)/shard_map/ppermute | solution.py:28
  103.5 10.8 %collective-permute-start.27 = (bf16[80,2048]{1,0:T(8,128)(2,1)S(1)}, bf16[80,2048]{1,0:T(8,128)(2,1)S(1)}, u32[]{:S(2)}, u32[]{:S(2)}) collective-permute-start(bf16[80,2048]{1,0:T(8,128)(2,1)S(1)} %get-tuple-element.114), channel_id=1, source_target_pairs={{0,4},{1,5},{2,6},{3,7},{4,0},{5,1},{6,2},{7,3},{8,12},{9,13},{10,... | collective-permute-start | bytes 983048 | tf_op jit(solution)/shard_map/ppermute | solution.py:28
  104.6 16.4 %collective-permute-start.28 = (bf16[80,2048]{1,0:T(8,128)(2,1)S(1)}, bf16[80,2048]{1,0:T(8,128)(2,1)S(1)}, u32[]{:S(2)}, u32[]{:S(2)}) collective-permute-start(bf16[80,2048]{1,0:T(8,128)(2,1)S(1)} %get-tuple-element.115), channel_id=1, source_target_pairs={{0,6},{1,7},{2,4},{3,5},{4,2},{5,3},{6,0},{7,1},{8,14},{9,15},{10,... | collective-permute-start | bytes 983048 | tf_op jit(solution)/shard_map/ppermute | solution.py:28
  110.7 21.4 %collective-permute-start.29 = (bf16[40,2048]{1,0:T(8,128)(2,1)S(1)}, bf16[40,2048]{1,0:T(8,128)(2,1)S(1)}, u32[]{:S(2)}, u32[]{:S(2)}) collective-permute-start(bf16[40,2048]{1,0:T(8,128)(2,1)S(1)} %get-tuple-element.124), channel_id=1, source_target_pairs={{0,2},{1,3},{2,0},{3,1},{4,6},{5,7},{6,4},{7,5},{8,10},{9,11},{10,... | collective-permute-start | bytes 491528 | tf_op jit(solution)/shard_map/ppermute | solution.py:28
  112.5 20.2 %collective-permute-start.30 = (bf16[40,2048]{1,0:T(8,128)(2,1)S(1)}, bf16[40,2048]{1,0:T(8,128)(2,1)S(1)}, u32[]{:S(2)}, u32[]{:S(2)}) collective-permute-start(bf16[40,2048]{1,0:T(8,128)(2,1)S(1)} %get-tuple-element.125), channel_id=1, source_target_pairs={{0,4},{1,5},{2,6},{3,7},{4,0},{5,1},{6,2},{7,3},{8,12},{9,13},{10,... | collective-permute-start | bytes 491528 | tf_op jit(solution)/shard_map/ppermute | solution.py:28
  113.7 19.1 %collective-permute-start.31 = (bf16[40,2048]{1,0:T(8,128)(2,1)S(1)}, bf16[40,2048]{1,0:T(8,128)(2,1)S(1)}, u32[]{:S(2)}, u32[]{:S(2)}) collective-permute-start(bf16[40,2048]{1,0:T(8,128)(2,1)S(1)} %get-tuple-element.126), channel_id=1, source_target_pairs={{0,6},{1,7},{2,4},{3,5},{4,2},{5,3},{6,0},{7,1},{8,14},{9,15},{10,... | collective-permute-start | bytes 491528 | tf_op jit(solution)/shard_map/ppermute | solution.py:28
  129.2 16.2 %collective-permute-start.32 = (bf16[80,2048]{1,0:T(8,128)(2,1)S(1)}, bf16[80,2048]{1,0:T(8,128)(2,1)S(1)}, u32[]{:S(2)}, u32[]{:S(2)}) collective-permute-start(bf16[80,2048]{1,0:T(8,128)(2,1)S(1)} %get-tuple-element.130), channel_id=1, source_target_pairs={{0,2},{1,3},{2,0},{3,1},{4,6},{5,7},{6,4},{7,5},{8,10},{9,11},{10,... | collective-permute-start | bytes 983048 | tf_op jit(solution)/shard_map/ppermute | solution.py:28
  130.9 15.0 %collective-permute-start.33 = (bf16[80,2048]{1,0:T(8,128)(2,1)S(1)}, bf16[80,2048]{1,0:T(8,128)(2,1)S(1)}, u32[]{:S(2)}, u32[]{:S(2)}) collective-permute-start(bf16[80,2048]{1,0:T(8,128)(2,1)S(1)} %get-tuple-element.131), channel_id=1, source_target_pairs={{0,4},{1,5},{2,6},{3,7},{4,0},{5,1},{6,2},{7,3},{8,12},{9,13},{10,... | collective-permute-start | bytes 983048 | tf_op jit(solution)/shard_map/ppermute | solution.py:28
  132.1 13.9 %collective-permute-start.34 = (bf16[80,2048]{1,0:T(8,128)(2,1)S(1)}, bf16[80,2048]{1,0:T(8,128)(2,1)S(1)}, u32[]{:S(2)}, u32[]{:S(2)}) collective-permute-start(bf16[80,2048]{1,0:T(8,128)(2,1)S(1)} %get-tuple-element.132), channel_id=1, source_target_pairs={{0,6},{1,7},{2,4},{3,5},{4,2},{5,3},{6,0},{7,1},{8,14},{9,15},{10,... | collective-permute-start | bytes 983048 | tf_op jit(solution)/shard_map/ppermute | solution.py:28
  142.4 11.4 %collective-permute-start.39 = (bf16[40,2048]{1,0:T(8,128)(2,1)S(1)}, bf16[40,2048]{1,0:T(8,128)(2,1)S(1)}, u32[]{:S(2)}, u32[]{:S(2)}) collective-permute-start(bf16[40,2048]{1,0:T(8,128)(2,1)S(1)} %get-tuple-element.141), channel_id=1, source_target_pairs={{0,2},{1,3},{2,0},{3,1},{4,6},{5,7},{6,4},{7,5},{8,10},{9,11},{10,... | collective-permute-start | bytes 491528 | tf_op jit(solution)/shard_map/ppermute | solution.py:28
  144.2 9.6 %collective-permute-start.40 = (bf16[40,2048]{1,0:T(8,128)(2,1)S(1)}, bf16[40,2048]{1,0:T(8,128)(2,1)S(1)}, u32[]{:S(2)}, u32[]{:S(2)}) collective-permute-start(bf16[40,2048]{1,0:T(8,128)(2,1)S(1)} %get-tuple-element.142), channel_id=1, source_target_pairs={{0,4},{1,5},{2,6},{3,7},{4,0},{5,1},{6,2},{7,3},{8,12},{9,13},{10,... | collective-permute-start | bytes 491528 | tf_op jit(solution)/shard_map/ppermute | solution.py:28
  145.3 8.5 %collective-permute-start.41 = (bf16[40,2048]{1,0:T(8,128)(2,1)S(1)}, bf16[40,2048]{1,0:T(8,128)(2,1)S(1)}, u32[]{:S(2)}, u32[]{:S(2)}) collective-permute-start(bf16[40,2048]{1,0:T(8,128)(2,1)S(1)} %get-tuple-element.143), channel_id=1, source_target_pairs={{0,6},{1,7},{2,4},{3,5},{4,2},{5,3},{6,0},{7,1},{8,14},{9,15},{10,... | collective-permute-start | bytes 491528 | tf_op jit(solution)/shard_map/ppermute | solution.py:28
  149.1 19.2 %collective-permute-start.38 = (bf16[80,2048]{1,0:T(8,128)(2,1)S(1)}, bf16[80,2048]{1,0:T(8,128)(2,1)S(1)}, u32[]{:S(2)}, u32[]{:S(2)}) collective-permute-start(bf16[80,2048]{1,0:T(8,128)(2,1)S(1)} %get-tuple-element.133), channel_id=1, source_target_pairs={{0,24},{1,25},{2,26},{3,27},{4,28},{5,29},{6,30},{7,31},{8,0},{9,1... | collective-permute-start | bytes 983048 | tf_op jit(solution)/shard_map/ppermute | solution.py:28
  152.2 7.5 %collective-permute-start.35 = (bf16[40,2048]{1,0:T(8,128)(2,1)S(1)}, bf16[40,2048]{1,0:T(8,128)(2,1)S(1)}, u32[]{:S(2)}, u32[]{:S(2)}) collective-permute-start(bf16[40,2048]{1,0:T(8,128)(2,1)S(1)} %get-tuple-element.134), channel_id=1, source_target_pairs={{0,2},{1,3},{2,0},{3,1},{4,6},{5,7},{6,4},{7,5},{8,10},{9,11},{10,... | collective-permute-start | bytes 491528 | tf_op jit(solution)/shard_map/ppermute | solution.py:28
  153.8 14.5 %collective-permute-start.43 = (bf16[80,2048]{1,0:T(8,128)(2,1)S(1)}, bf16[80,2048]{1,0:T(8,128)(2,1)S(1)}, u32[]{:S(2)}, u32[]{:S(2)}) collective-permute-start(bf16[80,2048]{1,0:T(8,128)(2,1)S(1)} %get-tuple-element.144), channel_id=1, source_target_pairs={{0,8},{1,9},{2,10},{3,11},{4,12},{5,13},{6,14},{7,15},{8,16},{9,17... | collective-permute-start | bytes 983048 | tf_op jit(solution)/shard_map/ppermute | solution.py:28
  156.2 18.2 %collective-permute-start.42 = (bf16[80,2048]{1,0:T(8,128)(2,1)S(1)}, bf16[80,2048]{1,0:T(8,128)(2,1)S(1)}, u32[]{:S(2)}, u32[]{:S(2)}) collective-permute-start(bf16[80,2048]{1,0:T(8,128)(2,1)S(1)} %shard_map.140), channel_id=1, source_target_pairs={{0,16},{1,17},{2,18},{3,19},{4,20},{5,21},{6,22},{7,23},{8,24},{9,... | collective-permute-start | bytes 983048 | tf_op jit(solution)/shard_map/ppermute | solution.py:28
  158.3 5.3 %collective-permute-start.36 = (bf16[40,2048]{1,0:T(8,128)(2,1)S(1)}, bf16[40,2048]{1,0:T(8,128)(2,1)S(1)}, u32[]{:S(2)}, u32[]{:S(2)}) collective-permute-start(bf16[40,2048]{1,0:T(8,128)(2,1)S(1)} %get-tuple-element.136), channel_id=1, source_target_pairs={{0,4},{1,5},{2,6},{3,7},{4,0},{5,1},{6,2},{7,3},{8,12},{9,13},{10,... | collective-permute-start | bytes 491528 | tf_op jit(solution)/shard_map/ppermute | solution.py:28
  159.7 6.3 %collective-permute-start.37 = (bf16[40,2048]{1,0:T(8,128)(2,1)S(1)}, bf16[40,2048]{1,0:T(8,128)(2,1)S(1)}, u32[]{:S(2)}, u32[]{:S(2)}) collective-permute-start(bf16[40,2048]{1,0:T(8,128)(2,1)S(1)} %get-tuple-element.138), channel_id=1, source_target_pairs={{0,6},{1,7},{2,4},{3,5},{4,2},{5,3},{6,0},{7,1},{8,14},{9,15},{10,... | collective-permute-start | bytes 491528 | tf_op jit(solution)/shard_map/ppermute | solution.py:28
  (1 other events, 7.9 us)

commit v8 on v7

--- a/solution.py
+++ b/solution.py
@@ -155,55 +155,56 @@
 
 
 def attend_kernel(depth, block_len, head_dim, place, *refs):
-    own_refs, near_refs = refs[:depth], refs[depth : 2 * depth]
-    outs, (own, near, mixed) = refs[2 * depth : 3 * depth], refs[3 * depth :]
+    own_refs, near_refs, outs = refs[:depth], refs[depth : 2 * depth], refs[2 * depth : 3 * depth]
+    queries, keys, values, chosen_rows, scores, mixed = refs[3 * depth :]
     z_index, core = place[1], place[2]
     scaling = math.log2(math.e) / math.sqrt(head_dim)
+    width = values.shape[2] // 2
     for turn in range(depth):
         source = lax.rem(z_index + depth - turn, depth)
-        own[source] = own_refs[turn][...]
-        near[source] = near_refs[turn][0:block_len, head_dim : 3 * head_dim]
+        queries[source] = own_refs[turn][0:block_len, 0:head_dim]
+        chosen_rows[source] = own_refs[turn][block_len : block_len + PAD_ROWS, :]
+        for side, ref in enumerate((own_refs[turn], near_refs[turn])):
+            keys[source, side * block_len : (side + 1) * block_len] = ref[0:block_len, head_dim : 2 * head_dim]
+            values[source, :, side * width : side * width + block_len] = ref[
+                0:block_len, 2 * head_dim : 3 * head_dim
+            ].T
     key_pos = lax.broadcasted_iota(jnp.int32, (block_len, block_len), 0)
     query_pos = lax.broadcasted_iota(jnp.int32, (block_len, block_len), 1)
     causal = jnp.where(key_pos <= query_pos, 0.0, -1e30)
     for level in range(depth):
-        query = own[level, 0:block_len, 0:head_dim]
-        marks = own[level, block_len : block_len + PAD_ROWS, 0:block_len].astype(jnp.float32)
-        marks = marks[0:1].astype(jnp.int32)
-        run_max = run_sum = total = None
-        order = [(level, True)] + [(c, True) for c in range(level)] + [(c, False) for c in range(level + 1)]
-        for c, mine in order:
-            if mine:
-                key = own[c, 0:block_len, head_dim : 2 * head_dim]
-                value = own[c, 0:block_len, 2 * head_dim : 3 * head_dim]
-            else:
-                key, value = near[c, :, 0:head_dim], near[c, :, head_dim : 2 * head_dim]
-            scores = lax.dot_general(
-                key, query, (((1,), (1,)), ((), ())), preferred_element_type=jnp.float32
-            )
-            if run_max is None:
-                scores = scores + causal
-                shift = run_max = jnp.max(scores, axis=0, keepdims=True)
-            else:
-                bit = 2 * c + (core if mine else 1 - core)
-                chosen = lax.shift_right_logical(marks, jnp.broadcast_to(bit, marks.shape)) & 1
-                top = jnp.where(chosen == 1, jnp.max(scores, axis=0, keepdims=True), -1e30)
-                new_max = jnp.maximum(run_max, top)
-                rescale = jnp.exp2((run_max - new_max) * scaling)
-                run_max = new_max
-                shift = jnp.where(chosen == 1, new_max, 1e30)
-            weights = jnp.exp2((scores - shift) * scaling)
-            added = jnp.sum(weights, axis=0, keepdims=True)
-            product = lax.dot_general(
-                value,
-                weights.astype(jnp.bfloat16),
-                (((0,), (0,)), ((), ())),
+        query = queries[level]
+        marks = chosen_rows[level, :, 0:block_len].astype(jnp.float32)[0:1].astype(jnp.int32)
+        pairs = [(c, side) for c in range(level + 1) for side in range(2)]
+        run_max, chosen = None, []
+        for index, (c, side) in enumerate(pairs):
+            score = lax.dot_general(
+                keys[c, side * block_len : (side + 1) * block_len],
+                query,
+                (((1,), (1,)), ((), ())),
                 preferred_element_type=jnp.float32,
             )
-            if total is None:
-                run_sum, total = added, product
+            if c == level and side == 0:
+                score = score + causal
+                chosen.append(None)
+                top = jnp.max(score, axis=0, keepdims=True)
             else:
-                run_sum, total = run_sum * rescale + added, total * rescale + product
+                bit = 2 * c + (core if side == 0 else 1 - core)
+                picked = lax.shift_right_logical(marks, jnp.broadcast_to(bit, marks.shape)) & 1
+                chosen.append(picked == 1)
+                top = jnp.where(chosen[-1], jnp.max(score, axis=0, keepdims=True), -1e30)
+            scores[index] = score
+            run_max = top if run_max is None else jnp.maximum(run_max, top)
+        run_sum = total = None
+        for index, (c, side) in enumerate(pairs):
+            shift = run_max if chosen[index] is None else jnp.where(chosen[index], run_max, 1e30)
+            weights = jnp.exp2((scores[index] - shift) * scaling)
+            added = jnp.sum(weights, axis=0, keepdims=True)
+            product = f32_dot(
+                values[c, :, side * width : side * width + block_len], weights.astype(jnp.bfloat16)
+            )
+            run_sum = added if run_sum is None else run_sum + added
+            total = product if total is None else total + product
         mixed[level] = (total / run_sum).T.astype(jnp.bfloat16)
     for turn in range(depth):
         outs[turn][...] = mixed[lax.rem(z_index + depth - turn, depth)]
@@ -259,28 +260,29 @@
     return [attended[head] for head in range(heads_here)]
 
 
-def mix_kernel(hops, heads, head_dim, place, *refs):
+def mix_kernel(heads, head_dim, hop, place, *refs):
     head_refs, w_out = refs[:heads], refs[heads]
-    kept, given, attended, mixed = refs[heads + 1 :]
+    kept, given, attended = refs[heads + 1 :]
     exp_index, turned = place[0], place[3]
-    tok_rows = kept.shape[1]
+    tok_rows = kept.shape[0]
+    starts = [pl.multiple_of((exp_index ^ (hop + side)) * tok_rows, 16) for side in range(2)]
     for turn, head_ref in enumerate(head_refs):
         head = lax.rem(turned + turn, heads)
-        attended[:, pl.ds(pl.multiple_of(head * head_dim, head_dim), head_dim)] = head_ref[...]
-    mixed[...] = f32_dot(attended[...], w_out[...]).astype(jnp.bfloat16)
-    for hop in range(hops):
-        start = pl.multiple_of((exp_index ^ hop) * tok_rows, 16)
-        (given if hop & 1 else kept)[hop >> 1] = mixed[pl.ds(start, tok_rows), :]
-
-
-def halves_kernel(inputs, kept, given, here, beyond):
-    summed = kept[0].astype(jnp.float32) + given[0].astype(jnp.float32)
-    here[...] = inputs[...].astype(jnp.float32) + summed
-    beyond[...] = (kept[1].astype(jnp.float32) + given[1].astype(jnp.float32)).astype(jnp.bfloat16)
-
-
-def residual_kernel(top_count, here, far, gain, noted, residual, ffn_in):
-    rounded = (here[...] + far[...].astype(jnp.float32)).astype(jnp.bfloat16)
+        columns = pl.ds(pl.multiple_of(head * head_dim, head_dim), head_dim)
+        for side in range(2):
+            attended[side * tok_rows : (side + 1) * tok_rows, columns] = head_ref[pl.ds(starts[side], tok_rows), :]
+    mixed = f32_dot(attended[...], w_out[...]).astype(jnp.bfloat16)
+    kept[...] = mixed[:tok_rows]
+    given[...] = mixed[tok_rows:]
+
+
+def sum_kernel(kept, given, summed):
+    summed[...] = (kept[...].astype(jnp.float32) + given[...].astype(jnp.float32)).astype(summed.dtype)
+
+
+def residual_kernel(top_count, inputs, kept, given, far, gain, noted, residual, ffn_in):
+    summed = kept[...].astype(jnp.float32) + given[...].astype(jnp.float32) + far[...].astype(jnp.float32)
+    rounded = (inputs[...].astype(jnp.float32) + summed).astype(jnp.bfloat16)
     residual[...] = rounded
     model_width = rounded.shape[1]
     ffn_in[:, 0:model_width] = normalize(rounded, gain[...])
@@ -320,13 +322,16 @@
         outs[hop][...] = f32_dot(placing, rows[...]).astype(jnp.bfloat16)
 
 
-def expert_kernel(starts, *refs):
-    parts = len(starts)
+def expert_kernel(slabs, *refs):
+    parts = sum(len(members) for _, members in slabs)
     row_refs, weights = refs[:parts], refs[parts : parts + 6]
     outs, (held,) = refs[parts + 6 : 2 * parts + 6], refs[2 * parts + 6 :]
     across = (((1,), (1,)), ((), ()))
-    for start, row_ref in zip(starts, row_refs):
-        held[start : start + row_ref.shape[0], :] = row_ref[...]
+    for start, members in slabs:
+        joined = [row_refs[part][...] for part in members]
+        if len(joined) > 1:
+            joined = [jnp.concatenate([row.astype(jnp.float32) for row in joined]).astype(jnp.bfloat16)]
+        held[start : start + joined[0].shape[0], :] = joined[0]
     rows = held[...]
     result = None
     for w_gate, w_up, w_down in (weights[:3], weights[3:]):
@@ -335,8 +340,11 @@
         hidden = (gate_part / (1.0 + jnp.exp(-gate_part)) * up_part).astype(jnp.bfloat16)
         product = f32_dot(hidden, w_down[...])
         result = product if result is None else result + product
-    for start, out in zip(starts, outs):
-        out[...] = result[start : start + out.shape[0]].astype(jnp.bfloat16)
+    for start, members in slabs:
+        for part in members:
+            count = outs[part].shape[0]
+            outs[part][...] = result[start : start + count].astype(jnp.bfloat16)
+            start += count
 
 
 def combine_kernel(count, capacity, top_count, place, notes, *refs):
@@ -443,8 +451,11 @@
             [struct(block_len, head_dim)] * depth,
             [place, *own, *beside],
             [
-                pltpu.VMEM((depth, block_len + PAD_ROWS, 3 * head_dim), jnp.bfloat16),
-                pltpu.VMEM((depth, block_len, 2 * head_dim), jnp.bfloat16),
+                pltpu.VMEM((depth, block_len, head_dim), jnp.bfloat16),
+                pltpu.VMEM((depth, 2 * block_len, head_dim), jnp.bfloat16),
+                pltpu.VMEM((depth, head_dim, 2 * 3 * head_dim), jnp.bfloat16),
+                pltpu.VMEM((depth, PAD_ROWS, 3 * head_dim), jnp.bfloat16),
+                pltpu.VMEM((2 * depth, block_len, block_len), jnp.float32),
                 pltpu.VMEM((depth, block_len, head_dim), jnp.bfloat16),
             ],
             flops=4 * depth * ctx_count * block_len * block_len * head_dim,
@@ -455,24 +466,20 @@
         normed = normalize(block.reshape(block_len, model_width), attn_gain)
         heads = attend_gathered(normed, w_query, w_key, w_value, sel_blocks)
 
-    halves = struct(exp_count // 2, tok_rows, model_width)
-    kept, given = call(
-        functools.partial(mix_kernel, exp_count, heads_here, head_dim),
-        [halves, halves],
-        [place, *heads, w_out],
-        [
-            pltpu.VMEM((block_len, hidden_cols), jnp.bfloat16),
-            pltpu.VMEM((block_len, model_width), jnp.bfloat16),
-        ],
-        flops=2 * block_len * model_width * hidden_cols,
-    )
-    given = swap_core(given)
-    here, beyond = call(
-        halves_kernel,
-        [struct(tok_rows, model_width, dtype=jnp.float32), struct(tok_rows, model_width)],
-        [inputs, kept, given],
-        smem=0,
-    )
+    def mixed_rows(hop, heads):
+        return call(
+            functools.partial(mix_kernel, heads_here, head_dim, hop),
+            [struct(tok_rows, model_width)] * 2,
+            [place, *heads, w_out],
+            [pltpu.VMEM((2 * tok_rows, hidden_cols), jnp.bfloat16)],
+            flops=4 * tok_rows * model_width * hidden_cols,
+        )
+
+    far_kept, far_given = mixed_rows(2, heads)
+    kept, given = mixed_rows(0, [after(heads[0], far_given)] + heads[1:])
+    far_given = swap_core(far_given)
+    beyond = call(sum_kernel, struct(tok_rows, model_width), [after(far_kept, kept), far_given], smem=0)
+    given = swap_core(after(given, beyond))
     other_up = swap_core(after(w_up, beyond))
     own_weights, other_weights = (
         [gate[0].T, up[0].T, down[0]] for gate, up, down in (weights, (other_gate, other_up, other_down))
@@ -485,7 +492,7 @@
     residual, ffn_in = call(
         functools.partial(residual_kernel, top_count),
         [struct(tok_rows, model_width), struct(tok_rows, model_width + LANES)],
-        [here, beyond, ffn_gain.reshape(1, -1), noted],
+        [inputs, kept, given, beyond, ffn_gain.reshape(1, -1), noted],
         smem=0,
     )
 
@@ -498,7 +505,9 @@
         count = len(group)
         first = column[group[0]]
         if len(arrived) == 1:
-            first = after(first, *arrived[0])
+            (up,) = load([], [after(expert_weights[4], arrived[0][0])])
+            expert_weights[4] = up
+            first = after(first, up, *arrived[0])
         elif arrived:
             first = after(first, arrived[-1][0])
         *packed, note = call(
@@ -513,12 +522,16 @@
         notes.append(note)
 
     def expert_rows(rows):
-        starts, total = [], 0
-        for row in rows:
-            starts.append(total)
-            total += -(-row.shape[0] // 16) * 16
+        slabs, total, part = [], 0, 0
+        while part < len(rows):
+            count = rows[part].shape[0]
+            pair = count % 16 == 8 and part + 1 < len(rows) and rows[part + 1].shape[0] == count
+            members = [part, part + 1] if pair else [part]
+            slabs.append((total, members))
+            total += -(-len(members) * count // 16) * 16
+            part += len(members)
         return call(
-            functools.partial(expert_kernel, starts),
+            functools.partial(expert_kernel, slabs),
             [struct(*row.shape) for row in rows],
             [*rows, *expert_weights],
             [pltpu.VMEM((total, model_width), jnp.bfloat16)],

time: 176 us -> 166 us (0.943)
  starting transfers between devices: 66 us -> 56.3 us
  waiting for transfers between devices: 56.4 us -> 62.5 us
  Pallas kernels: 50.7 us -> 45 us
    ppermute x44 -> x45, starting transfers between devices: 66 us -> 56.3 us  [move(): return lax.ppermute(block, AXES, route)]
    ppermute x44 -> x45, waiting for transfers between devices: 56.4 us -> 62.5 us  [move(): return lax.ppermute(block, AXES, route)]
    pallas_call x14 -> x16, Pallas kernels: 50.7 us -> 45 us  [call(): pl.pallas_call(kernel, out_shape=outs, in_specs=[SMEM] * smem + [VMEM] *...]
  transfers between devices with their start and end apart: 44 -> 45, of which waited for: 17 -> 20; matrix products, arithmetic and copies ran while one was open for 1% -> 1% of each run, Pallas kernels for 20% -> 20%
where the time goes in v8:
time: 166 us
  waiting for transfers between devices  62.5 us (38%)
  starting transfers between devices  56.3 us (34%)
  Pallas kernels  45 us (27%)
  other arithmetic  1.73 us (1%)
    ppermute x45, waiting for transfers between devices, move(): return lax.ppermute(block, AXES, route)  62.5 us
    ppermute x45, starting transfers between devices, move(): return lax.ppermute(block, AXES, route)  56.3 us
    pallas_call x16, Pallas kernels, call(): pl.pallas_call(kernel, out_shape=outs, in_specs=[SMEM] * smem + [VMEM] *...  45 us
  transfers between devices with their start and end apart: 45, of which 20 were waited for; matrix products, arithmetic and copies ran while one was open for 1% of the time, Pallas kernels for 20%

profile of v8, /device:TPU:0, one launch (start us, length us, event | category | flops | bytes accessed | tf_op | source)
XLA Modules:
  0.0 166.1 jit_solution(1701165734208650501)
XLA Ops:
  0.5 3.0 %collective-permute-start.1 = (bf16[80,2048]{1,0:T(8,128)(2,1)}, bf16[80,2048]{1,0:T(8,128)(2,1)S(1)}, u32[]{:S(2)}, u32[]{:S(2)}) collective-permute-start(bf16[80,2048]{1,0:T(8,128)(2,1)} %inputs.1), channel_id=1, source_target_pairs={{0,2},{1,3},{2,0},{3,1},{4,6},{5,7},{6,4},{7,5},{8,10},{9,11},{10,... | collective-permute-start | bytes 983048 | tf_op jit(solution)/shard_map/ppermute | solution.py:28
  3.5 8.1 %collective-permute-done.1.refs_1_ = bf16[80,2048]{1,0:T(8,128)(2,1)S(1)} collective-permute-done((bf16[80,2048]{1,0:T(8,128)(2,1)}, bf16[80,2048]{1,0:T(8,128)(2,1)S(1)}, u32[]{:S(2)}, u32[]{:S(2)}) %collective-permute-start.1) | collective-permute-done | bytes 327712 | tf_op jit(solution)/shard_map/ppermute | solution.py:28
  13.2 5.4 %shard_map.127 = (bf16[336,384]{1,0:T(8,128)(2,1)S(1)}, bf16[336,384]{1,0:T(8,128)(2,1)S(1)}, bf16[336,384]{1,0:T(8,128)(2,1)S(1)}, bf16[336,384]{1,0:T(8,128)(2,1)S(1)}) custom-call(s32[5]{0:T(128)S(1)} %stack.20.place, bf16[4,16,384]{2,1,0:T(8,128)(2,1)S(1)} %broadcast_in_dim.11.marks, bf16[80,2048]{1,0:T(8,128)(2,1)S(1)} %collective-permute-done.refs_0_, ...), custom_call_target="tpu_custom_call" | custom-call | flops 2013265920 | bytes 7659540 | tf_op jit(solution)/shard_map/pallas_call | solution.py:87
  18.6 1.9 %collective-permute-start.6 = (bf16[336,384]{1,0:T(8,128)(2,1)S(1)}, bf16[336,384]{1,0:T(8,128)(2,1)S(1)}, u32[]{:S(2)}, u32[]{:S(2)}) collective-permute-start(bf16[336,384]{1,0:T(8,128)(2,1)S(1)} %get-tuple-element.81), channel_id=1, source_target_pairs={{0,8},{1,12},{2,10},{3,14},{4,9},{5,13},{6,11},{7,15},{8,16},{9,20... | collective-permute-start | bytes 774152 | tf_op jit(solution)/shard_map/ppermute | solution.py:28
  20.5 2.6 %collective-permute-start.7 = (bf16[336,384]{1,0:T(8,128)(2,1)S(1)}, bf16[336,384]{1,0:T(8,128)(2,1)S(1)}, u32[]{:S(2)}, u32[]{:S(2)}) collective-permute-start(bf16[336,384]{1,0:T(8,128)(2,1)S(1)} %get-tuple-element.82), channel_id=1, source_target_pairs={{0,16},{1,20},{2,18},{3,22},{4,17},{5,21},{6,19},{7,23},{8,24},{9,... | collective-permute-start | bytes 774152 | tf_op jit(solution)/shard_map/ppermute | solution.py:28
  23.1 1.3 collective-permute-start.8
  25.2 4.1 %collective-permute-done.6.refs_1_ = bf16[336,384]{1,0:T(8,128)(2,1)S(1)} collective-permute-done((bf16[336,384]{1,0:T(8,128)(2,1)S(1)}, bf16[336,384]{1,0:T(8,128)(2,1)S(1)}, u32[]{:S(2)}, u32[]{:S(2)}) %collective-permute-start.6) | collective-permute-done | bytes 258080 | tf_op jit(solution)/shard_map/ppermute | solution.py:28
  29.3 1.1 collective-permute-start.10
  30.4 10.3 %collective-permute-done.7.refs_2_ = bf16[336,384]{1,0:T(8,128)(2,1)S(1)} collective-permute-done((bf16[336,384]{1,0:T(8,128)(2,1)S(1)}, bf16[336,384]{1,0:T(8,128)(2,1)S(1)}, u32[]{:S(2)}, u32[]{:S(2)}) %collective-permute-start.7) | collective-permute-done | bytes 258080 | tf_op jit(solution)/shard_map/ppermute | solution.py:28
  42.9 4.7 %shard_map.128 = (bf16[320,128]{1,0:T(8,128)(2,1)S(1)}, bf16[320,128]{1,0:T(8,128)(2,1)S(1)}, bf16[320,128]{1,0:T(8,128)(2,1)S(1)}, bf16[320,128]{1,0:T(8,128)(2,1)S(1)}) custom-call(s32[5]{0:T(128)S(1)} %stack.20.place, bf16[336,384]{1,0:T(8,128)(2,1)S(1)} %collective-permute-done.5.refs_0_, bf16[336,384]{1,0:T(8,128)(2,1)S(1)} %collective-permute-done.6.refs_1_, ...), custom_call_target="tpu_custom_call" | custom-call | flops 1677721600 | bytes 2064404 | tf_op jit(solution)/shard_map/pallas_call | solution.py:87
  48.3 7.2 %collective-permute-start.14 = (bf16[320,128]{1,0:T(8,128)(2,1)S(1)}, bf16[320,128]{1,0:T(8,128)(2,1)S(1)}, u32[]{:S(2)}, u32[]{:S(2)}) collective-permute-start(bf16[320,128]{1,0:T(8,128)(2,1)S(1)} %get-tuple-element.85), channel_id=1, source_target_pairs={{0,24},{1,28},{2,26},{3,30},{4,25},{5,29},{6,27},{7,31},{8,0},{9,4... | collective-permute-start | bytes 245768 | tf_op jit(solution)/shard_map/ppermute | solution.py:28
  56.2 1.4 collective-permute-done.14.refs_1_
  57.6 5.0 %collective-permute-done.15.refs_2_ = bf16[320,128]{1,0:T(8,128)(2,1)S(1)} collective-permute-done((bf16[320,128]{1,0:T(8,128)(2,1)S(1)}, bf16[320,128]{1,0:T(8,128)(2,1)S(1)}, u32[]{:S(2)}, u32[]{:S(2)}) %collective-permute-start.15) | collective-permute-done | bytes 81952 | tf_op jit(solution)/shard_map/ppermute | solution.py:28
  62.7 1.1 shard_map.129
  63.7 3.0 %collective-permute-start.17 = (bf16[80,2048]{1,0:T(8,128)(2,1)S(1)}, bf16[80,2048]{1,0:T(8,128)(2,1)S(1)}, u32[]{:S(2)}, u32[]{:S(2)}) collective-permute-start(bf16[80,2048]{1,0:T(8,128)(2,1)S(1)} %get-tuple-element.88), channel_id=1, source_target_pairs={{0,1},{1,0},{2,3},{3,2},{4,5},{5,4},{6,7},{7,6},{8,9},{9,8},{10,11... | collective-permute-start | bytes 983048 | tf_op jit(solution)/shard_map/ppermute | solution.py:28
  66.8 1.1 shard_map.130
  68.5 1.7 %collective-permute-start.19 = (bf16[80,2048]{1,0:T(8,128)(2,1)S(1)}, bf16[80,2048]{1,0:T(8,128)(2,1)S(1)}, u32[]{:S(2)}, u32[]{:S(2)}) collective-permute-start(bf16[80,2048]{1,0:T(8,128)(2,1)S(1)} %shard_map.131), channel_id=1, source_target_pairs={{0,2},{1,3},{2,0},{3,1},{4,6},{5,7},{6,4},{7,5},{8,10},{9,11},{10,... | collective-permute-start | bytes 983048 | tf_op jit(solution)/shard_map/ppermute | solution.py:28
  70.4 5.3 %shard_map.132 = (bf16[704,2048]{1,0:T(8,128)(2,1)S(1)}, bf16[704,2048]{1,0:T(8,128)(2,1)S(1)}, bf16[704,2048]{1,0:T(8,128)(2,1)S(1)}, bf16[704,2048]{1,0:T(8,128)(2,1)S(1)}, bf16[704,2048]{1,0:T(8,128)(2,1)S(1)}) custom-call(bf16[704,2048]{1,0:T(8,128)(2,1)} %bitcast.23, bf16[704,2048]{1,0:T(8,128)(2,1)} %bitcast.9.refs_1_, bf16[704,2048]{1,0:T(8,128)(2,1)} %bitcast.24, ...), custom_call_target="tpu_custom_call" | custom-call | bytes 14417920 | tf_op jit(solution)/shard_map/pallas_call | solution.py:87
  75.7 2.6 %collective-permute-done.19.far = bf16[80,2048]{1,0:T(8,128)(2,1)S(1)} collective-permute-done((bf16[80,2048]{1,0:T(8,128)(2,1)S(1)}, bf16[80,2048]{1,0:T(8,128)(2,1)S(1)}, u32[]{:S(2)}, u32[]{:S(2)}) %collective-permute-start.19) | collective-permute-done | bytes 327712 | tf_op jit(solution)/shard_map/ppermute | solution.py:28
  78.7 3.8 %collective-permute-start.26 = (bf16[80,2176]{1,0:T(8,128)(2,1)S(1)}, bf16[80,2176]{1,0:T(8,128)(2,1)S(1)}, u32[]{:S(2)}, u32[]{:S(2)}) collective-permute-start(bf16[80,2176]{1,0:T(8,128)(2,1)S(1)} %get-tuple-element.110.refs_0_), channel_id=1, source_target_pairs={{0,24},{1,25},{2,26},{3,27},{4,28},{5,29},{6,30},{7,31},{8,0},{9,1... | collective-permute-start | bytes 1044488 | tf_op jit(solution)/shard_map/ppermute | solution.py:28
  82.5 1.5 shard_map.134
  84.0 1.8 %collective-permute-start.21 = (bf16[40,2048]{1,0:T(8,128)(2,1)S(1)}, bf16[40,2048]{1,0:T(8,128)(2,1)S(1)}, u32[]{:S(2)}, u32[]{:S(2)}) collective-permute-start(bf16[40,2048]{1,0:T(8,128)(2,1)S(1)} %get-tuple-element.113), channel_id=1, source_target_pairs={{0,2},{1,3},{2,0},{3,1},{4,6},{5,7},{6,4},{7,5},{8,10},{9,11},{10,... | collective-permute-start | bytes 491528 | tf_op jit(solution)/shard_map/ppermute | solution.py:28
  87.6 4.0 %collective-permute-done.24.refs_0_ = bf16[80,2176]{1,0:T(8,128)(2,1)S(1)} collective-permute-done((bf16[80,2176]{1,0:T(8,128)(2,1)S(1)}, bf16[80,2176]{1,0:T(8,128)(2,1)S(1)}, u32[]{:S(2)}, u32[]{:S(2)}) %collective-permute-start.24) | collective-permute-done | bytes 348192 | tf_op jit(solution)/shard_map/ppermute | solution.py:28
  91.6 1.8 %shard_map.135.refs_8_.refs_12_ = bf16[704,2048]{1,0:T(8,128)(2,1)S(1)} custom-call(bf16[704,2048]{1,0:T(8,128)(2,1)} %bitcast.15.refs_0_), custom_call_target="tpu_custom_call" | custom-call | bytes 2883584 | tf_op jit(solution)/shard_map/pallas_call | solution.py:87
  93.9 1.7 %collective-permute-done.26.refs_1_ = bf16[80,2176]{1,0:T(8,128)(2,1)S(1)} collective-permute-done((bf16[80,2176]{1,0:T(8,128)(2,1)S(1)}, bf16[80,2176]{1,0:T(8,128)(2,1)S(1)}, u32[]{:S(2)}, u32[]{:S(2)}) %collective-permute-start.26) | collective-permute-done | bytes 348192 | tf_op jit(solution)/shard_map/ppermute | solution.py:28
  95.6 1.7 shard_map.136
  97.3 1.8 %collective-permute-start.27 = (bf16[80,2048]{1,0:T(8,128)(2,1)S(1)}, bf16[80,2048]{1,0:T(8,128)(2,1)S(1)}, u32[]{:S(2)}, u32[]{:S(2)}) collective-permute-start(bf16[80,2048]{1,0:T(8,128)(2,1)S(1)} %get-tuple-element.122), channel_id=1, source_target_pairs={{0,2},{1,3},{2,0},{3,1},{4,6},{5,7},{6,4},{7,5},{8,10},{9,11},{10,... | collective-permute-start | bytes 983048 | tf_op jit(solution)/shard_map/ppermute | solution.py:28
  99.0 1.1 collective-permute-start.28
  100.8 4.0 %collective-permute-done.25.refs_0_ = bf16[80,2176]{1,0:T(8,128)(2,1)S(1)} collective-permute-done((bf16[80,2176]{1,0:T(8,128)(2,1)S(1)}, bf16[80,2176]{1,0:T(8,128)(2,1)S(1)}, u32[]{:S(2)}, u32[]{:S(2)}) %collective-permute-start.25) | collective-permute-done | bytes 348192 | tf_op jit(solution)/shard_map/ppermute | solution.py:28
  104.8 1.5 shard_map.137
  106.3 1.8 %collective-permute-start.30 = (bf16[40,2048]{1,0:T(8,128)(2,1)S(1)}, bf16[40,2048]{1,0:T(8,128)(2,1)S(1)}, u32[]{:S(2)}, u32[]{:S(2)}) collective-permute-start(bf16[40,2048]{1,0:T(8,128)(2,1)S(1)} %get-tuple-element.132), channel_id=1, source_target_pairs={{0,2},{1,3},{2,0},{3,1},{4,6},{5,7},{6,4},{7,5},{8,10},{9,11},{10,... | collective-permute-start | bytes 491528 | tf_op jit(solution)/shard_map/ppermute | solution.py:28
  108.1 1.1 collective-permute-start.31
  109.9 6.7 %collective-permute-done.29.refs_3_ = bf16[80,2048]{1,0:T(8,128)(2,1)S(1)} collective-permute-done((bf16[80,2048]{1,0:T(8,128)(2,1)S(1)}, bf16[80,2048]{1,0:T(8,128)(2,1)S(1)}, u32[]{:S(2)}, u32[]{:S(2)}) %collective-permute-start.29) | collective-permute-done | bytes 327712 | tf_op jit(solution)/shard_map/ppermute | solution.py:28
  116.6 6.4 %shard_map.138 = (bf16[80,2048]{1,0:T(8,128)(2,1)S(1)}, bf16[80,2048]{1,0:T(8,128)(2,1)S(1)}, bf16[80,2048]{1,0:T(8,128)(2,1)S(1)}, bf16[80,2048]{1,0:T(8,128)(2,1)S(1)}) custom-call(bf16[80,2048]{1,0:T(8,128)(2,1)S(1)} %get-tuple-element.119.refs_0_, bf16[80,2048]{1,0:T(8,128)(2,1)S(1)} %collective-permute-done.27.refs_1_, ...), custom_call_target="tpu_custom_call" | custom-call | flops 5536481280 | bytes 18612224 | tf_op jit(solution)/shard_map/pallas_call | solution.py:87
  122.9 1.8 %collective-permute-start.33 = (bf16[80,2048]{1,0:T(8,128)(2,1)S(1)}, bf16[80,2048]{1,0:T(8,128)(2,1)S(1)}, u32[]{:S(2)}, u32[]{:S(2)}) collective-permute-start(bf16[80,2048]{1,0:T(8,128)(2,1)S(1)} %get-tuple-element.138), channel_id=1, source_target_pairs={{0,2},{1,3},{2,0},{3,1},{4,6},{5,7},{6,4},{7,5},{8,10},{9,11},{10,... | collective-permute-start | bytes 983048 | tf_op jit(solution)/shard_map/ppermute | solution.py:28
  124.7 1.1 collective-permute-start.34
  126.5 6.4 %shard_map.139 = (bf16[40,2048]{1,0:T(8,128)(2,1)S(1)}, bf16[40,2048]{1,0:T(8,128)(2,1)S(1)}, bf16[40,2048]{1,0:T(8,128)(2,1)S(1)}, bf16[40,2048]{1,0:T(8,128)(2...) custom-call(bf16[40,2048]{1,0:T(8,128)(2,1)S(1)} %get-tuple-element., ...), custom_call_target="tpu_custom_call" | custom-call | flops 5536481280 | bytes 18612224 | tf_op jit(solution)/shard_map/pallas_call | solution.py:87
  132.9 1.8 %collective-permute-start.40 = (bf16[40,2048]{1,0:T(8,128)(2,1)S(1)}, bf16[40,2048]{1,0:T(8,128)(2,1)S(1)}, u32[]{:S(2)}, u32[]{:S(2)}) collective-permute-start(bf16[40,2048]{1,0:T(8,128)(2,1)S(1)} %get-tuple-element.149), channel_id=1, source_target_pairs={{0,2},{1,3},{2,0},{3,1},{4,6},{5,7},{6,4},{7,5},{8,10},{9,11},{10,... | collective-permute-start | bytes 491528 | tf_op jit(solution)/shard_map/ppermute | solution.py:28
  134.6 1.1 collective-permute-start.41
  136.4 3.6 %collective-permute-done.35.refs_3_ = bf16[80,2048]{1,0:T(8,128)(2,1)S(1)} collective-permute-done((bf16[80,2048]{1,0:T(8,128)(2,1)S(1)}, bf16[80,2048]{1,0:T(8,128)(2,1)S(1)}, u32[]{:S(2)}, u32[]{:S(2)}) %collective-permute-start.35) | collective-permute-done | bytes 327712 | tf_op jit(solution)/shard_map/ppermute | solution.py:28
  140.1 3.3 %shard_map.140 = (bf16[80,2048]{1,0:T(8,128)(2,1)S(1)}, bf16[80,2048]{1,0:T(8,128)(2,1)S(1)}) custom-call(s32[5]{0:T(128)S(1)} %stack.20.place, bf16[160,128]{1,0:T(8,128)(2,1)S(1)} %get-tuple-element.137.notes, bf16[80,2048]{1,0:T(8,128)(2,1)S(1)} %get-tuple-element.130.refs_0_, bf16[80,2048]{1,0:T(8,128)(2,1)S(1)} %collective-permute-done.33.refs_1_, ...), custom_call_target="tpu_custom_call" | custom-call | flops 419430400 | bytes 1351700 | tf_op jit(solution)/shard_map/pallas_call | solution.py:87
  143.4 3.4 %collective-permute-start.39 = (bf16[80,2048]{1,0:T(8,128)(2,1)S(1)}, bf16[80,2048]{1,0:T(8,128)(2,1)S(1)}, u32[]{:S(2)}, u32[]{:S(2)}) collective-permute-start(bf16[80,2048]{1,0:T(8,128)(2,1)S(1)} %get-tuple-element.141), channel_id=1, source_target_pairs={{0,24},{1,25},{2,26},{3,27},{4,28},{5,29},{6,30},{7,31},{8,0},{9,1... | collective-permute-start | bytes 983048 | tf_op jit(solution)/shard_map/ppermute | solution.py:28
  146.8 2.4 %collective-permute-start.38 = (bf16[40,2048]{1,0:T(8,128)(2,1)S(1)}, bf16[40,2048]{1,0:T(8,128)(2,1)S(1)}, u32[]{:S(2)}, u32[]{:S(2)}) collective-permute-start(bf16[40,2048]{1,0:T(8,128)(2,1)S(1)} %get-tuple-element.146), channel_id=1, source_target_pairs={{0,6},{1,7},{2,4},{3,5},{4,2},{5,3},{6,0},{7,1},{8,14},{9,15},{10,... | collective-permute-start | bytes 491528 | tf_op jit(solution)/shard_map/ppermute | solution.py:28
  149.2 2.3 %shard_map.142 = bf16[80,2048]{1,0:T(8,128)(2,1)S(1)} custom-call(s32[5]{0:T(128)S(1)} %stack.20.place, bf16[80,128]{1,0:T(8,128)(2,1)S(1)} %get-tuple-element.147.notes, bf16[40,2048]{1,0:T(8,128)(2,1)S(1)} %get-tuple-element.148.refs_0_, bf16[40,2048]{1,0:T(8,128)(2,1)S(1)} %collective-permute-done.40.refs_1_, ...), custom_call_target="tpu_custom_call" | custom-call | flops 104857600 | bytes 675860 | tf_op jit(solution)/shard_map/pallas_call | solution.py:87
  151.5 2.1 %collective-permute-start.43 = (bf16[80,2048]{1,0:T(8,128)(2,1)S(1)}, bf16[80,2048]{1,0:T(8,128)(2,1)S(1)}, u32[]{:S(2)}, u32[]{:S(2)}) collective-permute-start(bf16[80,2048]{1,0:T(8,128)(2,1)S(1)} %shard_map.142), channel_id=1, source_target_pairs={{0,16},{1,17},{2,18},{3,19},{4,20},{5,21},{6,22},{7,23},{8,24},{9,... | collective-permute-start | bytes 983048 | tf_op jit(solution)/shard_map/ppermute | solution.py:28
  154.7 4.3 %collective-permute-done.37.refs_2_ = bf16[40,2048]{1,0:T(8,128)(2,1)S(1)} collective-permute-done((bf16[40,2048]{1,0:T(8,128)(2,1)S(1)}, bf16[40,2048]{1,0:T(8,128)(2,1)S(1)}, u32[]{:S(2)}, u32[]{:S(2)}) %collective-permute-start.37) | collective-permute-done | bytes 163872 | tf_op jit(solution)/shard_map/ppermute | solution.py:28
  159.3 2.3 %shard_map.141 = bf16[80,2048]{1,0:T(8,128)(2,1)S(1)} custom-call(s32[5]{0:T(128)S(1)} %stack.20.place, bf16[80,128]{1,0:T(8,128)(2,1)S(1)} %get-tuple-element.111.notes, bf16[40,2048]{1,0:T(8,128)(2,1)S(1)} %get-tuple-element.135.refs_0_, bf16[40,2048]{1,0:T(8,128)(2,1)S(1)} %collective-permute-done.36.refs_1_, ...), custom_call_target="tpu_custom_call" | custom-call | flops 104857600 | bytes 675860 | tf_op jit(solution)/shard_map/pallas_call | solution.py:87
  161.6 3.5 %collective-permute-done.43 = bf16[80,2048]{1,0:T(8,128)(2,1)S(1)} collective-permute-done((bf16[80,2048]{1,0:T(8,128)(2,1)S(1)}, bf16[80,2048]{1,0:T(8,128)(2,1)S(1)}, u32[]{:S(2)}, u32[]{:S(2)}) %collective-permute-start.43) | collective-permute-done | bytes 327712 | tf_op jit(solution)/shard_map/ppermute | solution.py:28
  (78 shorter events, 14.9 us)
Async XLA Ops:
  0.0 13.2 %collective-permute-start.3 = (bf16[1,2048,704]{1,2,0:T(8,128)(2,1)}, bf16[1,2048,704]{1,2,0:T(8,128)(2,1)}, u32[]{:S(2)}, u32[]{:S(2)}) collective-permute-start(bf16[1,2048,704]{1,2,0:T(8,128)(2,1)} %param.21), channel_id=1, source_target_pairs={{0,1},{1,0},{2,3},{3,2},{4,5},{5,4},{6,7},{7,6},{8,9},{9,8},{10,11... | collective-permute-start | bytes 8650760 | tf_op jit(solution)/shard_map/ppermute | solution.py:28
  0.5 12.7 %collective-permute-start.4 = (bf16[1,704,2048]{2,1,0:T(8,128)(2,1)}, bf16[1,704,2048]{2,1,0:T(8,128)(2,1)}, u32[]{:S(2)}, u32[]{:S(2)}) collective-permute-start(bf16[1,704,2048]{2,1,0:T(8,128)(2,1)} %param.23), channel_id=1, source_target_pairs={{0,1},{1,0},{2,3},{3,2},{4,5},{5,4},{6,7},{7,6},{8,9},{9,8},{10,11... | collective-permute-start | bytes 8650760 | tf_op jit(solution)/shard_map/ppermute | solution.py:28
  0.5 11.1 %collective-permute-start.1 = (bf16[80,2048]{1,0:T(8,128)(2,1)}, bf16[80,2048]{1,0:T(8,128)(2,1)S(1)}, u32[]{:S(2)}, u32[]{:S(2)}) collective-permute-start(bf16[80,2048]{1,0:T(8,128)(2,1)} %inputs.1), channel_id=1, source_target_pairs={{0,2},{1,3},{2,0},{3,1},{4,6},{5,7},{6,4},{7,5},{8,10},{9,11},{10,... | collective-permute-start | bytes 983048 | tf_op jit(solution)/shard_map/ppermute | solution.py:28
  3.5 9.7 %collective-permute-start = (bf16[80,2048]{1,0:T(8,128)(2,1)}, bf16[80,2048]{1,0:T(8,128)(2,1)S(1)}, u32[]{:S(2)}, u32[]{:S(2)}) collective-permute-start(bf16[80,2048]{1,0:T(8,128)(2,1)} %inputs.1), channel_id=1, source_target_pairs={{0,1},{1,0},{2,3},{3,2},{4,5},{5,4},{6,7},{7,6},{8,9},{9,8},{10,11... | collective-permute-start | bytes 983048 | tf_op jit(solution)/shard_map/ppermute | solution.py:28
  11.6 1.6 collective-permute-start.2
  18.6 10.7 %collective-permute-start.6 = (bf16[336,384]{1,0:T(8,128)(2,1)S(1)}, bf16[336,384]{1,0:T(8,128)(2,1)S(1)}, u32[]{:S(2)}, u32[]{:S(2)}) collective-permute-start(bf16[336,384]{1,0:T(8,128)(2,1)S(1)} %get-tuple-element.81), channel_id=1, source_target_pairs={{0,8},{1,12},{2,10},{3,14},{4,9},{5,13},{6,11},{7,15},{8,16},{9,20... | collective-permute-start | bytes 774152 | tf_op jit(solution)/shard_map/ppermute | solution.py:28
  20.5 20.2 %collective-permute-start.7 = (bf16[336,384]{1,0:T(8,128)(2,1)S(1)}, bf16[336,384]{1,0:T(8,128)(2,1)S(1)}, u32[]{:S(2)}, u32[]{:S(2)}) collective-permute-start(bf16[336,384]{1,0:T(8,128)(2,1)S(1)} %get-tuple-element.82), channel_id=1, source_target_pairs={{0,16},{1,20},{2,18},{3,22},{4,17},{5,21},{6,19},{7,23},{8,24},{9,... | collective-permute-start | bytes 774152 | tf_op jit(solution)/shard_map/ppermute | solution.py:28
  23.1 17.9 %collective-permute-start.8 = (bf16[336,384]{1,0:T(8,128)(2,1)S(1)}, bf16[336,384]{1,0:T(8,128)(2,1)S(1)}, u32[]{:S(2)}, u32[]{:S(2)}) collective-permute-start(bf16[336,384]{1,0:T(8,128)(2,1)S(1)} %get-tuple-element.83), channel_id=1, source_target_pairs={{0,24},{1,28},{2,26},{3,30},{4,25},{5,29},{6,27},{7,31},{8,0},{9,4... | collective-permute-start | bytes 774152 | tf_op jit(solution)/shard_map/ppermute | solution.py:28
  24.4 38.3 %copy-start = (bf16[512,2048]{1,0:T(8,128)(2,1)S(1)}, bf16[512,2048]{1,0:T(8,128)(2,1)}, u32[]{:S(2)}) copy-start(bf16[512,2048]{1,0:T(8,128)(2,1)} %refs_4_.5) | copy-start | bytes 6291460
  24.4 16.8 %collective-permute-start.5 = (bf16[336,384]{1,0:T(8,128)(2,1)S(1)}, bf16[336,384]{1,0:T(8,128)(2,1)S(1)}, u32[]{:S(2)}, u32[]{:S(2)}) collective-permute-start(bf16[336,384]{1,0:T(8,128)(2,1)S(1)} %get-tuple-element.80), channel_id=1, source_target_pairs={{0,0},{1,4},{2,2},{3,6},{4,1},{5,5},{6,3},{7,7},{8,8},{9,12},{10,1... | collective-permute-start | bytes 774152 | tf_op jit(solution)/shard_map/ppermute | solution.py:28
  29.3 12.2 %collective-permute-start.10 = (bf16[336,384]{1,0:T(8,128)(2,1)S(1)}, bf16[336,384]{1,0:T(8,128)(2,1)S(1)}, u32[]{:S(2)}, u32[]{:S(2)}) collective-permute-start(bf16[336,384]{1,0:T(8,128)(2,1)S(1)} %collective-permute-done.6.refs_1_), channel_id=1, source_target_pairs={{0,1},{1,0},{2,3},{3,2},{4,5},{5,4},{6,7},{7,6},{8,9},{9,8},{10,11... | collective-permute-start | bytes 774152 | tf_op jit(solution)/shard_map/ppermute | solution.py:28
  40.7 1.5 collective-permute-start.11
  41.0 1.6 collective-permute-start.12
  41.2 1.8 %collective-permute-start.9 = (bf16[336,384]{1,0:T(8,128)(2,1)S(1)}, bf16[336,384]{1,0:T(8,128)(2,1)S(1)}, u32[]{:S(2)}, u32[]{:S(2)}) collective-permute-start(bf16[336,384]{1,0:T(8,128)(2,1)S(1)} %collective-permute-done.5.refs_0_), channel_id=1, source_target_pairs={{0,1},{1,0},{2,3},{3,2},{4,5},{5,4},{6,7},{7,6},{8,9},{9,8},{10,11... | collective-permute-start | bytes 774152 | tf_op jit(solution)/shard_map/ppermute | solution.py:28
  47.7 8.5 %collective-permute-start.13 = (bf16[320,128]{1,0:T(8,128)(2,1)S(1)}, bf16[320,128]{1,0:T(8,128)(2,1)S(1)}, u32[]{:S(2)}, u32[]{:S(2)}) collective-permute-start(bf16[320,128]{1,0:T(8,128)(2,1)S(1)} %get-tuple-element.84), channel_id=1, source_target_pairs={{0,0},{1,4},{2,2},{3,6},{4,1},{5,5},{6,3},{7,7},{8,8},{9,12},{10,1... | collective-permute-start | bytes 245768 | tf_op jit(solution)/shard_map/ppermute | solution.py:28
  48.3 9.3 %collective-permute-start.14 = (bf16[320,128]{1,0:T(8,128)(2,1)S(1)}, bf16[320,128]{1,0:T(8,128)(2,1)S(1)}, u32[]{:S(2)}, u32[]{:S(2)}) collective-permute-start(bf16[320,128]{1,0:T(8,128)(2,1)S(1)} %get-tuple-element.85), channel_id=1, source_target_pairs={{0,24},{1,28},{2,26},{3,30},{4,25},{5,29},{6,27},{7,31},{8,0},{9,4... | collective-permute-start | bytes 245768 | tf_op jit(solution)/shard_map/ppermute | solution.py:28
  55.6 7.1 %collective-permute-start.15 = (bf16[320,128]{1,0:T(8,128)(2,1)S(1)}, bf16[320,128]{1,0:T(8,128)(2,1)S(1)}, u32[]{:S(2)}, u32[]{:S(2)}) collective-permute-start(bf16[320,128]{1,0:T(8,128)(2,1)S(1)} %get-tuple-element.86), channel_id=1, source_target_pairs={{0,16},{1,20},{2,18},{3,22},{4,17},{5,21},{6,19},{7,23},{8,24},{9,... | collective-permute-start | bytes 245768 | tf_op jit(solution)/shard_map/ppermute | solution.py:28
  55.6 14.7 %copy-start.4 = (s32[80,6]{0,1:T(8,128)S(1)}, s32[80,6]{0,1:T(8,128)}, u32[]{:S(2)}) copy-start(s32[80,6]{0,1:T(8,128)} %param.24) | copy-start | bytes 5764
  55.6 14.7 %copy-start.3 = (f32[80,6]{0,1:T(8,128)S(1)}, f32[80,6]{0,1:T(8,128)}, u32[]{:S(2)}) copy-start(f32[80,6]{0,1:T(8,128)} %param.25) | copy-start | bytes 5764
  55.6 7.1 %collective-permute-start.16 = (bf16[320,128]{1,0:T(8,128)(2,1)S(1)}, bf16[320,128]{1,0:T(8,128)(2,1)S(1)}, u32[]{:S(2)}, u32[]{:S(2)}) collective-permute-start(bf16[320,128]{1,0:T(8,128)(2,1)S(1)} %get-tuple-element.87), channel_id=1, source_target_pairs={{0,8},{1,12},{2,10},{3,14},{4,9},{5,13},{6,11},{7,15},{8,16},{9,20... | collective-permute-start | bytes 245768 | tf_op jit(solution)/shard_map/ppermute | solution.py:28
  63.7 4.3 %collective-permute-start.17 = (bf16[80,2048]{1,0:T(8,128)(2,1)S(1)}, bf16[80,2048]{1,0:T(8,128)(2,1)S(1)}, u32[]{:S(2)}, u32[]{:S(2)}) collective-permute-start(bf16[80,2048]{1,0:T(8,128)(2,1)S(1)} %get-tuple-element.88), channel_id=1, source_target_pairs={{0,1},{1,0},{2,3},{3,2},{4,5},{5,4},{6,7},{7,6},{8,9},{9,8},{10,11... | collective-permute-start | bytes 983048 | tf_op jit(solution)/shard_map/ppermute | solution.py:28
  68.1 10.2 %collective-permute-start.20 = (bf16[1,2048,704]{1,2,0:T(8,128)(2,1)}, bf16[1,2048,704]{1,2,0:T(8,128)(2,1)}, u32[]{:S(2)}, u32[]{:S(2)}) collective-permute-start(bf16[1,2048,704]{1,2,0:T(8,128)(2,1)} %param.22), channel_id=1, source_target_pairs={{0,1},{1,0},{2,3},{3,2},{4,5},{5,4},{6,7},{7,6},{8,9},{9,8},{10,11... | collective-permute-start | bytes 8650760 | tf_op jit(solution)/shard_map/ppermute | solution.py:28
  68.5 9.8 %collective-permute-start.19 = (bf16[80,2048]{1,0:T(8,128)(2,1)S(1)}, bf16[80,2048]{1,0:T(8,128)(2,1)S(1)}, u32[]{:S(2)}, u32[]{:S(2)}) collective-permute-start(bf16[80,2048]{1,0:T(8,128)(2,1)S(1)} %shard_map.131), channel_id=1, source_target_pairs={{0,2},{1,3},{2,0},{3,1},{4,6},{5,7},{6,4},{7,5},{8,10},{9,11},{10,... | collective-permute-start | bytes 983048 | tf_op jit(solution)/shard_map/ppermute | solution.py:28
  70.2 8.0 %collective-permute-start.18 = (bf16[80,2048]{1,0:T(8,128)(2,1)S(1)}, bf16[80,2048]{1,0:T(8,128)(2,1)S(1)}, u32[]{:S(2)}, u32[]{:S(2)}) collective-permute-start(bf16[80,2048]{1,0:T(8,128)(2,1)S(1)} %get-tuple-element.94), channel_id=1, source_target_pairs={{0,1},{1,0},{2,3},{3,2},{4,5},{5,4},{6,7},{7,6},{8,9},{9,8},{10,11... | collective-permute-start | bytes 983048 | tf_op jit(solution)/shard_map/ppermute | solution.py:28
  78.7 12.9 %collective-permute-start.24 = (bf16[80,2176]{1,0:T(8,128)(2,1)S(1)}, bf16[80,2176]{1,0:T(8,128)(2,1)S(1)}, u32[]{:S(2)}, u32[]{:S(2)}) collective-permute-start(bf16[80,2176]{1,0:T(8,128)(2,1)S(1)} %get-tuple-element.110.refs_0_), channel_id=1, source_target_pairs={{0,8},{1,9},{2,10},{3,11},{4,12},{5,13},{6,14},{7,15},{8,16},{9,17... | collective-permute-start | bytes 1044488 | tf_op jit(solution)/shard_map/ppermute | solution.py:28
  78.7 16.9 %collective-permute-start.26 = (bf16[80,2176]{1,0:T(8,128)(2,1)S(1)}, bf16[80,2176]{1,0:T(8,128)(2,1)S(1)}, u32[]{:S(2)}, u32[]{:S(2)}) collective-permute-start(bf16[80,2176]{1,0:T(8,128)(2,1)S(1)} %get-tuple-element.110.refs_0_), channel_id=1, source_target_pairs={{0,24},{1,25},{2,26},{3,27},{4,28},{5,29},{6,30},{7,31},{8,0},{9,1... | collective-permute-start | bytes 1044488 | tf_op jit(solution)/shard_map/ppermute | solution.py:28
  84.0 9.4 %collective-permute-start.21 = (bf16[40,2048]{1,0:T(8,128)(2,1)S(1)}, bf16[40,2048]{1,0:T(8,128)(2,1)S(1)}, u32[]{:S(2)}, u32[]{:S(2)}) collective-permute-start(bf16[40,2048]{1,0:T(8,128)(2,1)S(1)} %get-tuple-element.113), channel_id=1, source_target_pairs={{0,2},{1,3},{2,0},{3,1},{4,6},{5,7},{6,4},{7,5},{8,10},{9,11},{10,... | collective-permute-start | bytes 491528 | tf_op jit(solution)/shard_map/ppermute | solution.py:28
  85.8 7.6 %collective-permute-start.22 = (bf16[40,2048]{1,0:T(8,128)(2,1)S(1)}, bf16[40,2048]{1,0:T(8,128)(2,1)S(1)}, u32[]{:S(2)}, u32[]{:S(2)}) collective-permute-start(bf16[40,2048]{1,0:T(8,128)(2,1)S(1)} %get-tuple-element.114), channel_id=1, source_target_pairs={{0,4},{1,5},{2,6},{3,7},{4,0},{5,1},{6,2},{7,3},{8,12},{9,13},{10,... | collective-permute-start | bytes 491528 | tf_op jit(solution)/shard_map/ppermute | solution.py:28
  86.7 7.2 %collective-permute-start.23 = (bf16[40,2048]{1,0:T(8,128)(2,1)S(1)}, bf16[40,2048]{1,0:T(8,128)(2,1)S(1)}, u32[]{:S(2)}, u32[]{:S(2)}) collective-permute-start(bf16[40,2048]{1,0:T(8,128)(2,1)S(1)} %get-tuple-element.115), channel_id=1, source_target_pairs={{0,6},{1,7},{2,4},{3,5},{4,2},{5,3},{6,0},{7,1},{8,14},{9,15},{10,... | collective-permute-start | bytes 491528 | tf_op jit(solution)/shard_map/ppermute | solution.py:28
  91.6 13.2 %collective-permute-start.25 = (bf16[80,2176]{1,0:T(8,128)(2,1)S(1)}, bf16[80,2176]{1,0:T(8,128)(2,1)S(1)}, u32[]{:S(2)}, u32[]{:S(2)}) collective-permute-start(bf16[80,2176]{1,0:T(8,128)(2,1)S(1)} %collective-permute-done.24.refs_0_), channel_id=1, source_target_pairs={{0,8},{1,9},{2,10},{3,11},{4,12},{5,13},{6,14},{7,15},{8,16},{9,17... | collective-permute-start | bytes 1044488 | tf_op jit(solution)/shard_map/ppermute | solution.py:28
  97.3 12.0 %collective-permute-start.27 = (bf16[80,2048]{1,0:T(8,128)(2,1)S(1)}, bf16[80,2048]{1,0:T(8,128)(2,1)S(1)}, u32[]{:S(2)}, u32[]{:S(2)}) collective-permute-start(bf16[80,2048]{1,0:T(8,128)(2,1)S(1)} %get-tuple-element.122), channel_id=1, source_target_pairs={{0,2},{1,3},{2,0},{3,1},{4,6},{5,7},{6,4},{7,5},{8,10},{9,11},{10,... | collective-permute-start | bytes 983048 | tf_op jit(solution)/shard_map/ppermute | solution.py:28
  99.0 10.8 %collective-permute-start.28 = (bf16[80,2048]{1,0:T(8,128)(2,1)S(1)}, bf16[80,2048]{1,0:T(8,128)(2,1)S(1)}, u32[]{:S(2)}, u32[]{:S(2)}) collective-permute-start(bf16[80,2048]{1,0:T(8,128)(2,1)S(1)} %get-tuple-element.123), channel_id=1, source_target_pairs={{0,4},{1,5},{2,6},{3,7},{4,0},{5,1},{6,2},{7,3},{8,12},{9,13},{10,... | collective-permute-start | bytes 983048 | tf_op jit(solution)/shard_map/ppermute | solution.py:28
  100.1 16.4 %collective-permute-start.29 = (bf16[80,2048]{1,0:T(8,128)(2,1)S(1)}, bf16[80,2048]{1,0:T(8,128)(2,1)S(1)}, u32[]{:S(2)}, u32[]{:S(2)}) collective-permute-start(bf16[80,2048]{1,0:T(8,128)(2,1)S(1)} %get-tuple-element.124), channel_id=1, source_target_pairs={{0,6},{1,7},{2,4},{3,5},{4,2},{5,3},{6,0},{7,1},{8,14},{9,15},{10,... | collective-permute-start | bytes 983048 | tf_op jit(solution)/shard_map/ppermute | solution.py:28
  106.3 19.5 %collective-permute-start.30 = (bf16[40,2048]{1,0:T(8,128)(2,1)S(1)}, bf16[40,2048]{1,0:T(8,128)(2,1)S(1)}, u32[]{:S(2)}, u32[]{:S(2)}) collective-permute-start(bf16[40,2048]{1,0:T(8,128)(2,1)S(1)} %get-tuple-element.132), channel_id=1, source_target_pairs={{0,2},{1,3},{2,0},{3,1},{4,6},{5,7},{6,4},{7,5},{8,10},{9,11},{10,... | collective-permute-start | bytes 491528 | tf_op jit(solution)/shard_map/ppermute | solution.py:28
  108.1 18.4 %collective-permute-start.31 = (bf16[40,2048]{1,0:T(8,128)(2,1)S(1)}, bf16[40,2048]{1,0:T(8,128)(2,1)S(1)}, u32[]{:S(2)}, u32[]{:S(2)}) collective-permute-start(bf16[40,2048]{1,0:T(8,128)(2,1)S(1)} %get-tuple-element.133), channel_id=1, source_target_pairs={{0,4},{1,5},{2,6},{3,7},{4,0},{5,1},{6,2},{7,3},{8,12},{9,13},{10,... | collective-permute-start | bytes 491528 | tf_op jit(solution)/shard_map/ppermute | solution.py:28
  109.2 17.3 %collective-permute-start.32 = (bf16[40,2048]{1,0:T(8,128)(2,1)S(1)}, bf16[40,2048]{1,0:T(8,128)(2,1)S(1)}, u32[]{:S(2)}, u32[]{:S(2)}) collective-permute-start(bf16[40,2048]{1,0:T(8,128)(2,1)S(1)} %get-tuple-element.134), channel_id=1, source_target_pairs={{0,6},{1,7},{2,4},{3,5},{4,2},{5,3},{6,0},{7,1},{8,14},{9,15},{10,... | collective-permute-start | bytes 491528 | tf_op jit(solution)/shard_map/ppermute | solution.py:28
  122.9 12.8 %collective-permute-start.33 = (bf16[80,2048]{1,0:T(8,128)(2,1)S(1)}, bf16[80,2048]{1,0:T(8,128)(2,1)S(1)}, u32[]{:S(2)}, u32[]{:S(2)}) collective-permute-start(bf16[80,2048]{1,0:T(8,128)(2,1)S(1)} %get-tuple-element.138), channel_id=1, source_target_pairs={{0,2},{1,3},{2,0},{3,1},{4,6},{5,7},{6,4},{7,5},{8,10},{9,11},{10,... | collective-permute-start | bytes 983048 | tf_op jit(solution)/shard_map/ppermute | solution.py:28
  124.7 11.7 %collective-permute-start.34 = (bf16[80,2048]{1,0:T(8,128)(2,1)S(1)}, bf16[80,2048]{1,0:T(8,128)(2,1)S(1)}, u32[]{:S(2)}, u32[]{:S(2)}) collective-permute-start(bf16[80,2048]{1,0:T(8,128)(2,1)S(1)} %get-tuple-element.139), channel_id=1, source_target_pairs={{0,4},{1,5},{2,6},{3,7},{4,0},{5,1},{6,2},{7,3},{8,12},{9,13},{10,... | collective-permute-start | bytes 983048 | tf_op jit(solution)/shard_map/ppermute | solution.py:28
  125.8 14.3 %collective-permute-start.35 = (bf16[80,2048]{1,0:T(8,128)(2,1)S(1)}, bf16[80,2048]{1,0:T(8,128)(2,1)S(1)}, u32[]{:S(2)}, u32[]{:S(2)}) collective-permute-start(bf16[80,2048]{1,0:T(8,128)(2,1)S(1)} %get-tuple-element.140), channel_id=1, source_target_pairs={{0,6},{1,7},{2,4},{3,5},{4,2},{5,3},{6,0},{7,1},{8,14},{9,15},{10,... | collective-permute-start | bytes 983048 | tf_op jit(solution)/shard_map/ppermute | solution.py:28
  132.9 16.3 %collective-permute-start.40 = (bf16[40,2048]{1,0:T(8,128)(2,1)S(1)}, bf16[40,2048]{1,0:T(8,128)(2,1)S(1)}, u32[]{:S(2)}, u32[]{:S(2)}) collective-permute-start(bf16[40,2048]{1,0:T(8,128)(2,1)S(1)} %get-tuple-element.149), channel_id=1, source_target_pairs={{0,2},{1,3},{2,0},{3,1},{4,6},{5,7},{6,4},{7,5},{8,10},{9,11},{10,... | collective-permute-start | bytes 491528 | tf_op jit(solution)/shard_map/ppermute | solution.py:28
  134.6 14.6 %collective-permute-start.41 = (bf16[40,2048]{1,0:T(8,128)(2,1)S(1)}, bf16[40,2048]{1,0:T(8,128)(2,1)S(1)}, u32[]{:S(2)}, u32[]{:S(2)}) collective-permute-start(bf16[40,2048]{1,0:T(8,128)(2,1)S(1)} %get-tuple-element.150), channel_id=1, source_target_pairs={{0,4},{1,5},{2,6},{3,7},{4,0},{5,1},{6,2},{7,3},{8,12},{9,13},{10,... | collective-permute-start | bytes 491528 | tf_op jit(solution)/shard_map/ppermute | solution.py:28
  135.7 13.5 %collective-permute-start.42 = (bf16[40,2048]{1,0:T(8,128)(2,1)S(1)}, bf16[40,2048]{1,0:T(8,128)(2,1)S(1)}, u32[]{:S(2)}, u32[]{:S(2)}) collective-permute-start(bf16[40,2048]{1,0:T(8,128)(2,1)S(1)} %get-tuple-element.151), channel_id=1, source_target_pairs={{0,6},{1,7},{2,4},{3,5},{4,2},{5,3},{6,0},{7,1},{8,14},{9,15},{10,... | collective-permute-start | bytes 491528 | tf_op jit(solution)/shard_map/ppermute | solution.py:28
  143.4 18.2 %collective-permute-start.39 = (bf16[80,2048]{1,0:T(8,128)(2,1)S(1)}, bf16[80,2048]{1,0:T(8,128)(2,1)S(1)}, u32[]{:S(2)}, u32[]{:S(2)}) collective-permute-start(bf16[80,2048]{1,0:T(8,128)(2,1)S(1)} %get-tuple-element.141), channel_id=1, source_target_pairs={{0,24},{1,25},{2,26},{3,27},{4,28},{5,29},{6,30},{7,31},{8,0},{9,1... | collective-permute-start | bytes 983048 | tf_op jit(solution)/shard_map/ppermute | solution.py:28
  146.8 7.2 %collective-permute-start.38 = (bf16[40,2048]{1,0:T(8,128)(2,1)S(1)}, bf16[40,2048]{1,0:T(8,128)(2,1)S(1)}, u32[]{:S(2)}, u32[]{:S(2)}) collective-permute-start(bf16[40,2048]{1,0:T(8,128)(2,1)S(1)} %get-tuple-element.146), channel_id=1, source_target_pairs={{0,6},{1,7},{2,4},{3,5},{4,2},{5,3},{6,0},{7,1},{8,14},{9,15},{10,... | collective-permute-start | bytes 491528 | tf_op jit(solution)/shard_map/ppermute | solution.py:28
  149.2 12.4 %collective-permute-start.44 = (bf16[80,2048]{1,0:T(8,128)(2,1)S(1)}, bf16[80,2048]{1,0:T(8,128)(2,1)S(1)}, u32[]{:S(2)}, u32[]{:S(2)}) collective-permute-start(bf16[80,2048]{1,0:T(8,128)(2,1)S(1)} %get-tuple-element.152), channel_id=1, source_target_pairs={{0,8},{1,9},{2,10},{3,11},{4,12},{5,13},{6,14},{7,15},{8,16},{9,17... | collective-permute-start | bytes 983048 | tf_op jit(solution)/shard_map/ppermute | solution.py:28
  151.5 13.6 %collective-permute-start.43 = (bf16[80,2048]{1,0:T(8,128)(2,1)S(1)}, bf16[80,2048]{1,0:T(8,128)(2,1)S(1)}, u32[]{:S(2)}, u32[]{:S(2)}) collective-permute-start(bf16[80,2048]{1,0:T(8,128)(2,1)S(1)} %shard_map.142), channel_id=1, source_target_pairs={{0,16},{1,17},{2,18},{3,19},{4,20},{5,21},{6,22},{7,23},{8,24},{9,... | collective-permute-start | bytes 983048 | tf_op jit(solution)/shard_map/ppermute | solution.py:28
  153.7 5.3 %collective-permute-start.37 = (bf16[40,2048]{1,0:T(8,128)(2,1)S(1)}, bf16[40,2048]{1,0:T(8,128)(2,1)S(1)}, u32[]{:S(2)}, u32[]{:S(2)}) collective-permute-start(bf16[40,2048]{1,0:T(8,128)(2,1)S(1)} %get-tuple-element.144), channel_id=1, source_target_pairs={{0,4},{1,5},{2,6},{3,7},{4,0},{5,1},{6,2},{7,3},{8,12},{9,13},{10,... | collective-permute-start | bytes 491528 | tf_op jit(solution)/shard_map/ppermute | solution.py:28
  154.0 5.3 %collective-permute-start.36 = (bf16[40,2048]{1,0:T(8,128)(2,1)S(1)}, bf16[40,2048]{1,0:T(8,128)(2,1)S(1)}, u32[]{:S(2)}, u32[]{:S(2)}) collective-permute-start(bf16[40,2048]{1,0:T(8,128)(2,1)S(1)} %get-tuple-element.142), channel_id=1, source_target_pairs={{0,2},{1,3},{2,0},{3,1},{4,6},{5,7},{6,4},{7,5},{8,10},{9,11},{10,... | collective-permute-start | bytes 491528 | tf_op jit(solution)/shard_map/ppermute | solution.py:28
  (2 other events, 15.8 us)

commit v9 on v8

--- a/solution.py
+++ b/solution.py
@@ -128,24 +128,41 @@
     )
 
 
-def project_kernel(hops, depth, head_dim, place, marks, *refs):
-    sources, outs = refs[: hops + 4], refs[hops + 4 : hops + 4 + depth]
-    given, rows, mixed, gain, held, sems = refs[hops + 4 + depth :]
+def near_kernel(place, *refs):
+    sources, (mixed, *held), (given, gain, rows, sems) = refs[:6], refs[6:10], refs[10:]
+    tok_rows = given.shape[1]
+    targets = [given.at[1], gain, given.at[0], *held]
+    copies = [pltpu.make_async_copy(sources[i], targets[i], sems.at[i]) for i in range(6)]
+    for copy in copies:
+        copy.start()
+    for copy in copies[:3]:
+        copy.wait()
+    for side in range(2):
+        rows[side * tok_rows : (side + 1) * tok_rows, :] = normalize(given[side], gain[...])
+    for part, copy in enumerate(copies[3:]):
+        copy.wait()
+        mixed[part] = f32_dot(rows[...], held[part][...]).astype(jnp.bfloat16)
+
+
+def project_kernel(depth, head_dim, place, marks, near_mixed, gain, *refs):
+    held, sources, outs = refs[:3], refs[3:5], refs[5 : 5 + depth]
+    given, rows, mixed, sems = refs[5 + depth :]
     exp_index, z_index = place[0], place[1]
     tok_rows = given.shape[1]
-    block_len = hops * tok_rows
-    targets = [*(given.at[i] for i in range(1, hops)), gain, given.at[0], *(held.at[i] for i in range(3))]
-    copies = [pltpu.make_async_copy(sources[i], targets[i], sems.at[i]) for i in range(hops + 4)]
+    block_len = 4 * tok_rows
+    copies = [pltpu.make_async_copy(sources[i], given.at[i], sems.at[i]) for i in range(2)]
     for copy in copies:
         copy.start()
-    for copy in copies[: hops + 1]:
+    starts = [pl.multiple_of((exp_index ^ hop) * tok_rows, 16) for hop in range(4)]
+    for side, copy in enumerate(copies):
         copy.wait()
-    for hop in range(hops):
-        start = pl.multiple_of((exp_index ^ hop) * tok_rows, 16)
-        rows[pl.ds(start, tok_rows), :] = normalize(given[hop], gain[...])
-    for part, copy in enumerate(copies[hops + 1 :]):
-        copy.wait()
-        mixed[part] = f32_dot(rows[...], held[part]).astype(jnp.bfloat16)
+        rows[side * tok_rows : (side + 1) * tok_rows, :] = normalize(given[side], gain[...])
+    for part in range(3):
+        far_mixed = f32_dot(rows[...], held[part][...]).astype(jnp.bfloat16)
+        for side in range(2):
+            pick = slice(side * tok_rows, (side + 1) * tok_rows)
+            mixed[part, pl.ds(starts[side], tok_rows), :] = near_mixed[part, pick, :]
+            mixed[part, pl.ds(starts[2 + side], tok_rows), :] = far_mixed[pick]
     for turn in range(depth):
         head = lax.rem(z_index + turn, depth)
         columns = pl.ds(pl.multiple_of(head * head_dim, head_dim), head_dim)
@@ -347,8 +364,7 @@
             start += count
 
 
-def combine_kernel(count, capacity, top_count, place, notes, *refs):
-    returned, outs = refs[:4], refs[4 : 4 + count]
+def weigh_kernel(count, capacity, top_count, place, notes, upper, lower):
     expert = place[4]
     total = notes.shape[0]
     tok_rows = total // count
@@ -363,7 +379,6 @@
     before = ((earlier < later) & (earlier // tok_rows == later // tok_rows)).astype(jnp.bfloat16)
     first_slot = lax.broadcasted_iota(jnp.int32, (total, 1), 0) // tok_rows * capacity
     slot = lax.broadcasted_iota(jnp.int32, (total, count * capacity), 1)
-    mixed = jnp.zeros((total, returned[0].shape[1]), jnp.float32)
     for hop in range(4):
         hit = routes == (expert ^ hop).astype(jnp.float32)
         member = jnp.sum(jnp.where(hit, 1.0, 0.0), axis=1, keepdims=True)
@@ -371,11 +386,33 @@
         place_in = f32_dot(before, jnp.broadcast_to(member, (total, LANES)).astype(jnp.bfloat16))[:, 0:1]
         target = jnp.where(member > 0.5, place_in.astype(jnp.int32) + first_slot, -1)
         placing = jnp.where(slot == target, factor, 0.0)
-        upper = placing.astype(jnp.bfloat16)
-        lower = (placing - upper.astype(jnp.float32)).astype(jnp.bfloat16)
-        mixed = mixed + f32_dot(upper, returned[hop][...]) + f32_dot(lower, returned[hop][...])
+        upper[hop] = placing.astype(jnp.bfloat16)
+        lower[hop] = (placing - upper[hop].astype(jnp.float32)).astype(jnp.bfloat16)
+
+
+def mix_slots(upper, lower, returned):
+    mixed = None
+    for hop in range(4):
+        rows = returned[hop][...]
+        term = f32_dot(upper[hop], rows) + f32_dot(lower[hop], rows)
+        mixed = term if mixed is None else mixed + term
+    return mixed
+
+
+def combine_kernel(count, upper, lower, *refs):
+    returned, outs = refs[:4], refs[4 : 4 + count]
+    tok_rows = upper.shape[1] // count
+    mixed = mix_slots(upper, lower, returned)
     for turn in range(count):
         outs[turn][...] = mixed[turn * tok_rows : (turn + 1) * tok_rows].astype(jnp.bfloat16)
+
+
+def finish_kernel(upper, lower, *refs):
+    returned, (residual, *others), out = refs[:4], refs[4:-1], refs[-1]
+    total = residual[...].astype(jnp.float32) + mix_slots(upper, lower, returned)
+    for other in others:
+        total = total + other[...].astype(jnp.float32)
+    out[...] = total
 
 
 def shards(
@@ -409,10 +446,8 @@
 
     far = move(inputs, lambda z, x, y, c: (z, x, y ^ 1, c))
     near = swap_core(inputs)
-    far_near = swap_core(far)
     weights = (w_gate, w_up, w_down)
     other_gate, other_up, other_down = swap_core(w_gate), None, swap_core(w_down)
-    far_near, other_gate, other_down = lax.optimization_barrier((far_near, other_gate, other_down))
     top_count = routes.shape[1]
     noted = jnp.concatenate([routes.astype(jnp.float32)] + [gate_weights] * 3, axis=1)
     noted = jnp.pad(noted, ((0, 0), (0, LANES - noted.shape[1])))
@@ -423,26 +458,35 @@
         marks = jnp.pad(marks.T.astype(jnp.bfloat16), ((0, 0), (0, 3 * head_dim - block_len)))
         marks = jnp.broadcast_to(marks[:, None], (heads_here, PAD_ROWS, 3 * head_dim))
         payload = struct(block_len + PAD_ROWS, 3 * head_dim)
+        gain_row = attn_gain.reshape(1, -1)
+        near_mixed, *held = call(
+            near_kernel,
+            [struct(3, 2 * tok_rows, hidden_cols)] + [struct(model_width, hidden_cols)] * 3,
+            [place, near, gain_row, inputs, w_query, w_key, w_value],
+            [
+                pltpu.VMEM((2, tok_rows, model_width), jnp.bfloat16),
+                pltpu.VMEM((1, model_width), jnp.float32),
+                pltpu.VMEM((2 * tok_rows, model_width), jnp.bfloat16),
+                pltpu.SemaphoreType.DMA((6,)),
+            ],
+            flops=12 * tok_rows * model_width * hidden_cols,
+            anywhere=1,
+            hbm=5,
+        )
+        far_near = swap_core(after(far, near_mixed))
+        far_near, other_gate, other_down = lax.optimization_barrier((far_near, other_gate, other_down))
         sent = call(
-            functools.partial(project_kernel, exp_count, depth, head_dim),
+            functools.partial(project_kernel, depth, head_dim),
             [payload] * depth,
+            [place, marks, near_mixed, gain_row, *held, far, far_near],
             [
-                place,
-                marks,
-                *(near, far, far_near),
-                *(attn_gain.reshape(1, -1), inputs, w_query, w_key, w_value),
+                pltpu.VMEM((2, tok_rows, model_width), jnp.bfloat16),
+                pltpu.VMEM((2 * tok_rows, model_width), jnp.bfloat16),
+                pltpu.VMEM((3, block_len, hidden_cols), jnp.bfloat16),
+                pltpu.SemaphoreType.DMA((2,)),
             ],
-            [
-                pltpu.VMEM((exp_count, tok_rows, model_width), jnp.bfloat16),
-                pltpu.VMEM((block_len, model_width), jnp.bfloat16),
-                pltpu.VMEM((3, block_len, hidden_cols), jnp.bfloat16),
-                pltpu.VMEM((1, model_width), jnp.float32),
-                pltpu.VMEM((3, model_width, hidden_cols), jnp.bfloat16),
-                pltpu.SemaphoreType.DMA((exp_count + 4,)),
-            ],
-            flops=6 * block_len * model_width * hidden_cols,
-            anywhere=exp_count - 1,
-            hbm=5,
+            flops=12 * tok_rows * model_width * hidden_cols,
+            anywhere=2,
         )
         own = [head_out(sent[turn], turn) for turn in range(depth)]
         beside = [swap_core(block) for block in own]
@@ -462,7 +506,7 @@
         )
         heads = [head_back(mixed[turn], turn) for turn in range(depth)]
     else:
-        block = jnp.stack([inputs, near, far, far_near])[exp_index ^ jnp.arange(exp_count)]
+        block = jnp.stack([inputs, near, far, swap_core(far)])[exp_index ^ jnp.arange(exp_count)]
         normed = normalize(block.reshape(block_len, model_width), attn_gain)
         heads = attend_gathered(normed, w_query, w_key, w_value, sel_blocks)
 
@@ -540,30 +584,52 @@
             limit=4 * MIB + 32 * 1024 * total,
         )
 
+    shares = []
+    for group, note in zip(groups, notes):
+        count = len(group)
+        total = count * tok_rows
+        shares.append(
+            call(
+                functools.partial(weigh_kernel, count, capacity, top_count),
+                [struct(4, total, count * capacity)] * 2,
+                [place, note],
+                flops=8 * total * total * LANES,
+                limit=8 * MIB + 16 * total * total,
+            )
+        )
+    arrived[1][1] = after(arrived[1][1], *(part for share in shares for part in share))
     results = [None, expert_rows(arrived[1]), None]
     far_rows = [after(arrived[2][0], results[1][0])] + arrived[2][1:]
     both = expert_rows(arrived[0] + far_rows)
     results[0], results[2] = both[:4], both[4:]
     sums = [None] * depth
-    for index in (1, 2, 0):
+    home = [None] * depth
+    for index in (1, 2):
         group, rows = groups[index], list(results[index])
-        if index == 0:
-            rows[1:] = [after(row, sums[1]) for row in rows[1:]]
         rows = [rows[0]] + [swap_layer(rows[hop], hop) for hop in range(1, 4)]
         count = len(group)
         total = count * tok_rows
         parts = call(
-            functools.partial(combine_kernel, count, capacity, top_count),
+            functools.partial(combine_kernel, count),
             [struct(tok_rows, model_width)] * count,
-            [place, notes[index], *rows],
+            [*shares[index], *rows],
             flops=16 * count * capacity * total * model_width,
-            limit=8 * MIB + 16 * total * total + 16 * total * model_width,
+            smem=0,
+            limit=8 * MIB + 16 * total * model_width,
         )
         for turn, part in zip(group, parts):
             sums[turn] = part
-    layer_out = residual.astype(jnp.float32) + sums[0].astype(jnp.float32)
-    for turn in range(1, depth):
-        layer_out = layer_out + turn_z(sums[turn], -turn).astype(jnp.float32)
+            home[turn] = turn_z(part, -turn)
+    rows = [results[0][0]] + [swap_layer(after(results[0][hop], sums[1]), hop) for hop in range(1, 4)]
+    layer_out = call(
+        finish_kernel,
+        struct(tok_rows, model_width, dtype=jnp.float32),
+        [*shares[0], *rows, residual, *(home[turn] for turn in groups[1])],
+        flops=16 * capacity * tok_rows * model_width,
+        smem=0,
+    )
+    for turn in groups[2]:
+        layer_out = layer_out + home[turn].astype(jnp.float32)
     return layer_out.astype(jnp.bfloat16)
 
 

time: 166 us -> 162 us (0.976)
  waiting for transfers between devices: 62.5 us -> 57.8 us
  starting transfers between devices: 56.3 us -> 58 us
    ppermute x45, waiting for transfers between devices: 62.5 us -> 57.8 us  [move(): return lax.ppermute(block, AXES, route)]
    ppermute x45, starting transfers between devices: 56.3 us -> 58 us  [move(): return lax.ppermute(block, AXES, route)]
    pallas_call x16 -> x20, Pallas kernels: 45 us -> 44.7 us  [call(): pl.pallas_call(kernel, out_shape=outs, in_specs=[SMEM] * smem + [VMEM] *...]
  transfers between devices with their start and end apart: 45 -> 45, of which waited for: 20 -> 22; matrix products, arithmetic and copies ran while one was open for 1% -> 0% of each run, Pallas kernels for 20% -> 22%
where the time goes in v9:
time: 162 us
  starting transfers between devices  58 us (36%)
  waiting for transfers between devices  57.8 us (36%)
  Pallas kernels  44.7 us (28%)
    ppermute x45, starting transfers between devices, move(): return lax.ppermute(block, AXES, route)  58 us
    ppermute x45, waiting for transfers between devices, move(): return lax.ppermute(block, AXES, route)  57.8 us
    pallas_call x20, Pallas kernels, call(): pl.pallas_call(kernel, out_shape=outs, in_specs=[SMEM] * smem + [VMEM] *...  44.7 us
  transfers between devices with their start and end apart: 45, of which 22 were waited for; matrix products, arithmetic and copies ran while one was open for 0% of the time, Pallas kernels for 22%

profile of v9, /device:TPU:0, one launch (start us, length us, event | category | flops | bytes accessed | tf_op | source)
XLA Modules:
  0.0 161.8 jit_solution(4443594081567971405)
XLA Ops:
  1.0 2.5 %collective-permute-start.1 = (bf16[80,2048]{1,0:T(8,128)(2,1)}, bf16[80,2048]{1,0:T(8,128)(2,1)S(1)}, u32[]{:S(2)}, u32[]{:S(2)}) collective-permute-start(bf16[80,2048]{1,0:T(8,128)(2,1)} %inputs.1), channel_id=1, source_target_pairs={{0,2},{1,3},{2,0},{3,1},{4,6},{5,7},{6,4},{7,5},{8,10},{9,11},{10,... | collective-permute-start | bytes 983048 | tf_op jit(solution)/shard_map/ppermute | solution.py:28
  3.6 2.9 %collective-permute-done.refs_0_ = bf16[80,2048]{1,0:T(8,128)(2,1)S(1)} collective-permute-done((bf16[80,2048]{1,0:T(8,128)(2,1)}, bf16[80,2048]{1,0:T(8,128)(2,1)S(1)}, u32[]{:S(2)}, u32[]{:S(2)}) %collective-permute-start) | collective-permute-done | bytes 327712 | tf_op jit(solution)/shard_map/ppermute | solution.py:28
  6.5 4.2 %shard_map.127 = (bf16[3,160,512]{2,1,0:T(8,128)(2,1)S(1)}, bf16[2048,512]{1,0:T(8,128)(2,1)S(1)}, bf16[2048,512]{1,0:T(8,128)(2,1)S(1)}, bf16[2048,512]{1,0:T(8,128)(2,1)S(1)}) custom-call(s32[5]{0:T(128)S(1)} %stack.20.place, bf16[80,2048]{1,0:T(8,128)(2,1)S(1)} %collective-permute-done.refs_0_, f32[1,2048]{1,0:T(1,128)} %bitcast.22, ...), custom_call_target="tpu_custom_call" | custom-call | flops 1006632960 | bytes 6955028 | tf_op jit(solution)/shard_map/pallas_call | solution.py:87
  10.7 1.3 collective-permute-done.1.refs_3_
  12.1 1.6 collective-permute-done.2.refs_4_
  13.7 2.5 %shard_map.128 = (bf16[336,384]{1,0:T(8,128)(2,1)S(1)}, bf16[336,384]{1,0:T(8,128)(2,1)S(1)}, bf16[336,384]{1,0:T(8,128)(2,1)S(1)}, bf16[336,384]{1,0:T(8,128)(2,1)S(1)}) custom-call(s32[5]{0:T(128)S(1)} %stack.20.place, bf16[4,16,384]{2,1,0:T(8,128)(2,1)S(1)} %broadcast_in_dim.11.marks, bf16[3,160,512]{2,1,0:T(8,128)(2,1)S(1)} %get-tuple-element.91.near_mixed, ...), custom_call_target="tpu_custom_call" | custom-call | flops 1006632960 | bytes 7495700 | tf_op jit(solution)/shard_map/pallas_call | solution.py:87
  16.2 1.9 %collective-permute-start.6 = (bf16[336,384]{1,0:T(8,128)(2,1)S(1)}, bf16[336,384]{1,0:T(8,128)(2,1)S(1)}, u32[]{:S(2)}, u32[]{:S(2)}) collective-permute-start(bf16[336,384]{1,0:T(8,128)(2,1)S(1)} %get-tuple-element.98), channel_id=1, source_target_pairs={{0,8},{1,12},{2,10},{3,14},{4,9},{5,13},{6,11},{7,15},{8,16},{9,20... | collective-permute-start | bytes 774152 | tf_op jit(solution)/shard_map/ppermute | solution.py:28
  18.1 2.6 %collective-permute-start.7 = (bf16[336,384]{1,0:T(8,128)(2,1)S(1)}, bf16[336,384]{1,0:T(8,128)(2,1)S(1)}, u32[]{:S(2)}, u32[]{:S(2)}) collective-permute-start(bf16[336,384]{1,0:T(8,128)(2,1)S(1)} %get-tuple-element.99), channel_id=1, source_target_pairs={{0,16},{1,20},{2,18},{3,22},{4,17},{5,21},{6,19},{7,23},{8,24},{9,... | collective-permute-start | bytes 774152 | tf_op jit(solution)/shard_map/ppermute | solution.py:28
  20.7 1.4 collective-permute-start.8
  22.8 4.0 %collective-permute-done.6.refs_1_ = bf16[336,384]{1,0:T(8,128)(2,1)S(1)} collective-permute-done((bf16[336,384]{1,0:T(8,128)(2,1)S(1)}, bf16[336,384]{1,0:T(8,128)(2,1)S(1)}, u32[]{:S(2)}, u32[]{:S(2)}) %collective-permute-start.6) | collective-permute-done | bytes 258080 | tf_op jit(solution)/shard_map/ppermute | solution.py:28
  26.9 1.2 collective-permute-start.10
  28.0 10.3 %collective-permute-done.7.refs_2_ = bf16[336,384]{1,0:T(8,128)(2,1)S(1)} collective-permute-done((bf16[336,384]{1,0:T(8,128)(2,1)S(1)}, bf16[336,384]{1,0:T(8,128)(2,1)S(1)}, u32[]{:S(2)}, u32[]{:S(2)}) %collective-permute-start.7) | collective-permute-done | bytes 258080 | tf_op jit(solution)/shard_map/ppermute | solution.py:28
  40.5 4.7 %shard_map.129 = (bf16[320,128]{1,0:T(8,128)(2,1)S(1)}, bf16[320,128]{1,0:T(8,128)(2,1)S(1)}, bf16[320,128]{1,0:T(8,128)(2,1)S(1)}, bf16[320,128]{1,0:T(8,128)(2,1)S(1)}) custom-call(s32[5]{0:T(128)S(1)} %stack.20.place, bf16[336,384]{1,0:T(8,128)(2,1)S(1)} %collective-permute-done.5.refs_0_, bf16[336,384]{1,0:T(8,128)(2,1)S(1)} %collective-permute-done.6.refs_1_, ...), custom_call_target="tpu_custom_call" | custom-call | flops 1677721600 | bytes 2064404 | tf_op jit(solution)/shard_map/pallas_call | solution.py:87
  45.9 7.2 %collective-permute-start.14 = (bf16[320,128]{1,0:T(8,128)(2,1)S(1)}, bf16[320,128]{1,0:T(8,128)(2,1)S(1)}, u32[]{:S(2)}, u32[]{:S(2)}) collective-permute-start(bf16[320,128]{1,0:T(8,128)(2,1)S(1)} %get-tuple-element.102), channel_id=1, source_target_pairs={{0,24},{1,28},{2,26},{3,30},{4,25},{5,29},{6,27},{7,31},{8,0},{9,4... | collective-permute-start | bytes 245768 | tf_op jit(solution)/shard_map/ppermute | solution.py:28
  53.8 1.4 collective-permute-done.14.refs_1_
  55.2 5.0 %collective-permute-done.15.refs_2_ = bf16[320,128]{1,0:T(8,128)(2,1)S(1)} collective-permute-done((bf16[320,128]{1,0:T(8,128)(2,1)S(1)}, bf16[320,128]{1,0:T(8,128)(2,1)S(1)}, u32[]{:S(2)}, u32[]{:S(2)}) %collective-permute-start.15) | collective-permute-done | bytes 81952 | tf_op jit(solution)/shard_map/ppermute | solution.py:28
  61.3 3.0 %collective-permute-start.17 = (bf16[80,2048]{1,0:T(8,128)(2,1)S(1)}, bf16[80,2048]{1,0:T(8,128)(2,1)S(1)}, u32[]{:S(2)}, u32[]{:S(2)}) collective-permute-start(bf16[80,2048]{1,0:T(8,128)(2,1)S(1)} %get-tuple-element.105), channel_id=1, source_target_pairs={{0,1},{1,0},{2,3},{3,2},{4,5},{5,4},{6,7},{7,6},{8,9},{9,8},{10,11... | collective-permute-start | bytes 983048 | tf_op jit(solution)/shard_map/ppermute | solution.py:28
  66.1 1.7 %collective-permute-start.19 = (bf16[80,2048]{1,0:T(8,128)(2,1)S(1)}, bf16[80,2048]{1,0:T(8,128)(2,1)S(1)}, u32[]{:S(2)}, u32[]{:S(2)}) collective-permute-start(bf16[80,2048]{1,0:T(8,128)(2,1)S(1)} %shard_map.132), channel_id=1, source_target_pairs={{0,2},{1,3},{2,0},{3,1},{4,6},{5,7},{6,4},{7,5},{8,10},{9,11},{10,... | collective-permute-start | bytes 983048 | tf_op jit(solution)/shard_map/ppermute | solution.py:28
  68.0 5.3 %shard_map.133 = (bf16[704,2048]{1,0:T(8,128)(2,1)S(1)}, bf16[704,2048]{1,0:T(8,128)(2,1)S(1)}, bf16[704,2048]{1,0:T(8,128)(2,1)S(1)}, bf16[704,2048]{1,0:T(8,128)(2,1)S(1)}, bf16[704,2048]{1,0:T(8,128)(2,1)S(1)}) custom-call(bf16[704,2048]{1,0:T(8,128)(2,1)} %bitcast.25, bf16[704,2048]{1,0:T(8,128)(2,1)} %bitcast.9.refs_1_, bf16[704,2048]{1,0:T(8,128)(2,1)} %bitcast.26, ...), custom_call_target="tpu_custom_call" | custom-call | bytes 14417920 | tf_op jit(solution)/shard_map/pallas_call | solution.py:87
  73.3 2.6 %collective-permute-done.19.far = bf16[80,2048]{1,0:T(8,128)(2,1)S(1)} collective-permute-done((bf16[80,2048]{1,0:T(8,128)(2,1)S(1)}, bf16[80,2048]{1,0:T(8,128)(2,1)S(1)}, u32[]{:S(2)}, u32[]{:S(2)}) %collective-permute-start.19) | collective-permute-done | bytes 327712 | tf_op jit(solution)/shard_map/ppermute | solution.py:28
  76.3 3.8 %collective-permute-start.26 = (bf16[80,2176]{1,0:T(8,128)(2,1)S(1)}, bf16[80,2176]{1,0:T(8,128)(2,1)S(1)}, u32[]{:S(2)}, u32[]{:S(2)}) collective-permute-start(bf16[80,2176]{1,0:T(8,128)(2,1)S(1)} %get-tuple-element.126.refs_0_), channel_id=1, source_target_pairs={{0,24},{1,25},{2,26},{3,27},{4,28},{5,29},{6,30},{7,31},{8,0},{9,1... | collective-permute-start | bytes 1044488 | tf_op jit(solution)/shard_map/ppermute | solution.py:28
  80.1 1.5 shard_map.135
  81.6 1.8 %collective-permute-start.21 = (bf16[40,2048]{1,0:T(8,128)(2,1)S(1)}, bf16[40,2048]{1,0:T(8,128)(2,1)S(1)}, u32[]{:S(2)}, u32[]{:S(2)}) collective-permute-start(bf16[40,2048]{1,0:T(8,128)(2,1)S(1)} %get-tuple-element.131), channel_id=1, source_target_pairs={{0,2},{1,3},{2,0},{3,1},{4,6},{5,7},{6,4},{7,5},{8,10},{9,11},{10,... | collective-permute-start | bytes 491528 | tf_op jit(solution)/shard_map/ppermute | solution.py:28
  85.2 4.0 %collective-permute-done.24.refs_0_ = bf16[80,2176]{1,0:T(8,128)(2,1)S(1)} collective-permute-done((bf16[80,2176]{1,0:T(8,128)(2,1)S(1)}, bf16[80,2176]{1,0:T(8,128)(2,1)S(1)}, u32[]{:S(2)}, u32[]{:S(2)}) %collective-permute-start.24) | collective-permute-done | bytes 348192 | tf_op jit(solution)/shard_map/ppermute | solution.py:28
  89.2 1.8 %shard_map.137.refs_8_.refs_12_ = bf16[704,2048]{1,0:T(8,128)(2,1)S(1)} custom-call(bf16[704,2048]{1,0:T(8,128)(2,1)} %bitcast.15.refs_0_), custom_call_target="tpu_custom_call" | custom-call | bytes 2883584 | tf_op jit(solution)/shard_map/pallas_call | solution.py:87
  91.5 1.7 %collective-permute-done.26.refs_1_ = bf16[80,2176]{1,0:T(8,128)(2,1)S(1)} collective-permute-done((bf16[80,2176]{1,0:T(8,128)(2,1)S(1)}, bf16[80,2176]{1,0:T(8,128)(2,1)S(1)}, u32[]{:S(2)}, u32[]{:S(2)}) %collective-permute-start.26) | collective-permute-done | bytes 348192 | tf_op jit(solution)/shard_map/ppermute | solution.py:28
  93.2 1.7 %shard_map.138 = (bf16[80,2048]{1,0:T(8,128)(2,1)S(1)}, bf16[80,2048]{1,0:T(8,128)(2,1)S(1)}, bf16[80,2048]{1,0:T(8,128)(2,1)S(1)}, bf16[80,2048]{1,0:T(8,128)(2,1)S(1)}, bf16[160,128]{1,0:T(8,128)(2,1)S(1)}) custom-call(s32[5]{0:T(128)S(1)} %stack.20.place, bf16[80,2176]{1,0:T(8,128)(2,1)S(1)} %collective-permute-done.24.refs_0_, ...), custom_call_target="tpu_custom_call" | custom-call | flops 209715200 | bytes 696340 | tf_op jit(solution)/shard_map/pallas_call | solution.py:87
  94.9 1.8 %collective-permute-start.27 = (bf16[80,2048]{1,0:T(8,128)(2,1)S(1)}, bf16[80,2048]{1,0:T(8,128)(2,1)S(1)}, u32[]{:S(2)}, u32[]{:S(2)}) collective-permute-start(bf16[80,2048]{1,0:T(8,128)(2,1)S(1)} %get-tuple-element.140), channel_id=1, source_target_pairs={{0,2},{1,3},{2,0},{3,1},{4,6},{5,7},{6,4},{7,5},{8,10},{9,11},{10,... | collective-permute-start | bytes 983048 | tf_op jit(solution)/shard_map/ppermute | solution.py:28
  96.6 1.1 collective-permute-start.28
  100.4 2.0 %collective-permute-done.25.refs_0_ = bf16[80,2176]{1,0:T(8,128)(2,1)S(1)} collective-permute-done((bf16[80,2176]{1,0:T(8,128)(2,1)S(1)}, bf16[80,2176]{1,0:T(8,128)(2,1)S(1)}, u32[]{:S(2)}, u32[]{:S(2)}) %collective-permute-start.25) | collective-permute-done | bytes 348192 | tf_op jit(solution)/shard_map/ppermute | solution.py:28
  102.4 1.5 shard_map.139
  104.9 1.8 %collective-permute-start.30 = (bf16[40,2048]{1,0:T(8,128)(2,1)S(1)}, bf16[40,2048]{1,0:T(8,128)(2,1)S(1)}, u32[]{:S(2)}, u32[]{:S(2)}) collective-permute-start(bf16[40,2048]{1,0:T(8,128)(2,1)S(1)} %get-tuple-element.157), channel_id=1, source_target_pairs={{0,2},{1,3},{2,0},{3,1},{4,6},{5,7},{6,4},{7,5},{8,10},{9,11},{10,... | collective-permute-start | bytes 491528 | tf_op jit(solution)/shard_map/ppermute | solution.py:28
  106.7 1.1 collective-permute-start.31
  108.4 5.7 %collective-permute-done.29.refs_3_ = bf16[80,2048]{1,0:T(8,128)(2,1)S(1)} collective-permute-done((bf16[80,2048]{1,0:T(8,128)(2,1)S(1)}, bf16[80,2048]{1,0:T(8,128)(2,1)S(1)}, u32[]{:S(2)}, u32[]{:S(2)}) %collective-permute-start.29) | collective-permute-done | bytes 327712 | tf_op jit(solution)/shard_map/ppermute | solution.py:28
  114.2 6.4 %shard_map.142 = (bf16[80,2048]{1,0:T(8,128)(2,1)S(1)}, bf16[80,2048]{1,0:T(8,128)(2,1)S(1)}, bf16[80,2048]{1,0:T(8,128)(2,1)S(1)}, bf16[80,2048]{1,0:T(8,128)(2,1)S(1)}) custom-call(bf16[80,2048]{1,0:T(8,128)(2,1)S(1)} %get-tuple-element.137.refs_0_, bf16[80,2048]{1,0:T(8,128)(2,1)S(1)} %collective-permute-done.27.refs_1_, ...), custom_call_target="tpu_custom_call" | custom-call | flops 5536481280 | bytes 18612224 | tf_op jit(solution)/shard_map/pallas_call | solution.py:87
  120.5 1.8 %collective-permute-start.33 = (bf16[80,2048]{1,0:T(8,128)(2,1)S(1)}, bf16[80,2048]{1,0:T(8,128)(2,1)S(1)}, u32[]{:S(2)}, u32[]{:S(2)}) collective-permute-start(bf16[80,2048]{1,0:T(8,128)(2,1)S(1)} %get-tuple-element.162), channel_id=1, source_target_pairs={{0,2},{1,3},{2,0},{3,1},{4,6},{5,7},{6,4},{7,5},{8,10},{9,11},{10,... | collective-permute-start | bytes 983048 | tf_op jit(solution)/shard_map/ppermute | solution.py:28
  122.3 1.1 collective-permute-start.34
  124.1 6.6 %shard_map.143 = (bf16[40,2048]{1,0:T(8,128)(2,1)S(1)}, bf16[40,2048]{1,0:T(8,128)(2,1)S(1)}, bf16[40,2048]{1,0:T(8,128)(2,1)S(1)}, bf16[40,2048]{1,0:T(8,128)(2...) custom-call(bf16[40,2048]{1,0:T(8,128)(2,1)S(1)} %get-tuple-element., ...), custom_call_target="tpu_custom_call" | custom-call | flops 5536481280 | bytes 18612224 | tf_op jit(solution)/shard_map/pallas_call | solution.py:87
  130.7 1.8 %collective-permute-start.41 = (bf16[40,2048]{1,0:T(8,128)(2,1)S(1)}, bf16[40,2048]{1,0:T(8,128)(2,1)S(1)}, u32[]{:S(2)}, u32[]{:S(2)}) collective-permute-start(bf16[40,2048]{1,0:T(8,128)(2,1)S(1)} %get-tuple-element.174), channel_id=1, source_target_pairs={{0,2},{1,3},{2,0},{3,1},{4,6},{5,7},{6,4},{7,5},{8,10},{9,11},{10,... | collective-permute-start | bytes 491528 | tf_op jit(solution)/shard_map/ppermute | solution.py:28
  132.5 1.1 collective-permute-start.42
  134.2 3.1 %collective-permute-done.35.refs_3_ = bf16[80,2048]{1,0:T(8,128)(2,1)S(1)} collective-permute-done((bf16[80,2048]{1,0:T(8,128)(2,1)S(1)}, bf16[80,2048]{1,0:T(8,128)(2,1)S(1)}, u32[]{:S(2)}, u32[]{:S(2)}) %collective-permute-start.35) | collective-permute-done | bytes 327712 | tf_op jit(solution)/shard_map/ppermute | solution.py:28
  137.4 1.5 shard_map.144
  138.8 3.7 %collective-permute-start.39 = (bf16[80,2048]{1,0:T(8,128)(2,1)S(1)}, bf16[80,2048]{1,0:T(8,128)(2,1)S(1)}, u32[]{:S(2)}, u32[]{:S(2)}) collective-permute-start(bf16[80,2048]{1,0:T(8,128)(2,1)S(1)} %get-tuple-element.165), channel_id=1, source_target_pairs={{0,24},{1,25},{2,26},{3,27},{4,28},{5,29},{6,30},{7,31},{8,0},{9,1... | collective-permute-start | bytes 983048 | tf_op jit(solution)/shard_map/ppermute | solution.py:28
  142.6 2.4 %collective-permute-start.38 = (bf16[40,2048]{1,0:T(8,128)(2,1)S(1)}, bf16[40,2048]{1,0:T(8,128)(2,1)S(1)}, u32[]{:S(2)}, u32[]{:S(2)}) collective-permute-start(bf16[40,2048]{1,0:T(8,128)(2,1)S(1)} %get-tuple-element.170), channel_id=1, source_target_pairs={{0,6},{1,7},{2,4},{3,5},{4,2},{5,3},{6,0},{7,1},{8,14},{9,15},{10,... | collective-permute-start | bytes 491528 | tf_op jit(solution)/shard_map/ppermute | solution.py:28
  145.8 2.2 %collective-permute-start.44 = (bf16[80,2048]{1,0:T(8,128)(2,1)S(1)}, bf16[80,2048]{1,0:T(8,128)(2,1)S(1)}, u32[]{:S(2)}, u32[]{:S(2)}) collective-permute-start(bf16[80,2048]{1,0:T(8,128)(2,1)S(1)} %shard_map.146), channel_id=1, source_target_pairs={{0,16},{1,17},{2,18},{3,19},{4,20},{5,21},{6,22},{7,23},{8,24},{9,... | collective-permute-start | bytes 983048 | tf_op jit(solution)/shard_map/ppermute | solution.py:28
  148.8 1.7 %collective-permute-start.36 = (bf16[40,2048]{1,0:T(8,128)(2,1)S(1)}, bf16[40,2048]{1,0:T(8,128)(2,1)S(1)}, u32[]{:S(2)}, u32[]{:S(2)}) collective-permute-start(bf16[40,2048]{1,0:T(8,128)(2,1)S(1)} %get-tuple-element.166), channel_id=1, source_target_pairs={{0,2},{1,3},{2,0},{3,1},{4,6},{5,7},{6,4},{7,5},{8,10},{9,11},{10,... | collective-permute-start | bytes 491528 | tf_op jit(solution)/shard_map/ppermute | solution.py:28
  150.4 2.8 %collective-permute-done.37.refs_2_ = bf16[40,2048]{1,0:T(8,128)(2,1)S(1)} collective-permute-done((bf16[40,2048]{1,0:T(8,128)(2,1)S(1)}, bf16[40,2048]{1,0:T(8,128)(2,1)S(1)}, u32[]{:S(2)}, u32[]{:S(2)}) %collective-permute-start.37) | collective-permute-done | bytes 163872 | tf_op jit(solution)/shard_map/ppermute | solution.py:28
  155.0 6.1 %collective-permute-done.44 = bf16[80,2048]{1,0:T(8,128)(2,1)S(1)} collective-permute-done((bf16[80,2048]{1,0:T(8,128)(2,1)S(1)}, bf16[80,2048]{1,0:T(8,128)(2,1)S(1)}, u32[]{:S(2)}, u32[]{:S(2)}) %collective-permute-start.44) | collective-permute-done | bytes 327712 | tf_op jit(solution)/shard_map/ppermute | solution.py:28
  (86 shorter events, 20.8 us)
Async XLA Ops:
  0.0 13.7 %collective-permute-start.3 = (bf16[1,2048,704]{1,2,0:T(8,128)(2,1)}, bf16[1,2048,704]{1,2,0:T(8,128)(2,1)}, u32[]{:S(2)}, u32[]{:S(2)}) collective-permute-start(bf16[1,2048,704]{1,2,0:T(8,128)(2,1)} %param.21), channel_id=1, source_target_pairs={{0,1},{1,0},{2,3},{3,2},{4,5},{5,4},{6,7},{7,6},{8,9},{9,8},{10,11... | collective-permute-start | bytes 8650760 | tf_op jit(solution)/shard_map/ppermute | solution.py:28
  0.5 13.3 %collective-permute-start.4 = (bf16[1,704,2048]{2,1,0:T(8,128)(2,1)}, bf16[1,704,2048]{2,1,0:T(8,128)(2,1)}, u32[]{:S(2)}, u32[]{:S(2)}) collective-permute-start(bf16[1,704,2048]{2,1,0:T(8,128)(2,1)} %param.23), channel_id=1, source_target_pairs={{0,1},{1,0},{2,3},{3,2},{4,5},{5,4},{6,7},{7,6},{8,9},{9,8},{10,11... | collective-permute-start | bytes 8650760 | tf_op jit(solution)/shard_map/ppermute | solution.py:28
  0.5 6.0 %collective-permute-start = (bf16[80,2048]{1,0:T(8,128)(2,1)}, bf16[80,2048]{1,0:T(8,128)(2,1)S(1)}, u32[]{:S(2)}, u32[]{:S(2)}) collective-permute-start(bf16[80,2048]{1,0:T(8,128)(2,1)} %inputs.1), channel_id=1, source_target_pairs={{0,1},{1,0},{2,3},{3,2},{4,5},{5,4},{6,7},{7,6},{8,9},{9,8},{10,11... | collective-permute-start | bytes 983048 | tf_op jit(solution)/shard_map/ppermute | solution.py:28
  1.0 11.1 %collective-permute-start.1 = (bf16[80,2048]{1,0:T(8,128)(2,1)}, bf16[80,2048]{1,0:T(8,128)(2,1)S(1)}, u32[]{:S(2)}, u32[]{:S(2)}) collective-permute-start(bf16[80,2048]{1,0:T(8,128)(2,1)} %inputs.1), channel_id=1, source_target_pairs={{0,2},{1,3},{2,0},{3,1},{4,6},{5,7},{6,4},{7,5},{8,10},{9,11},{10,... | collective-permute-start | bytes 983048 | tf_op jit(solution)/shard_map/ppermute | solution.py:28
  12.1 1.6 %collective-permute-start.2 = (bf16[80,2048]{1,0:T(8,128)(2,1)S(1)}, bf16[80,2048]{1,0:T(8,128)(2,1)S(1)}, u32[]{:S(2)}, u32[]{:S(2)}) collective-permute-start(bf16[80,2048]{1,0:T(8,128)(2,1)S(1)} %collective-permute-done.1.refs_3_), channel_id=1, source_target_pairs={{0,1},{1,0},{2,3},{3,2},{4,5},{5,4},{6,7},{7,6},{8,9},{9,8},{10,11... | collective-permute-start | bytes 983048 | tf_op jit(solution)/shard_map/ppermute | solution.py:28
  16.2 10.6 %collective-permute-start.6 = (bf16[336,384]{1,0:T(8,128)(2,1)S(1)}, bf16[336,384]{1,0:T(8,128)(2,1)S(1)}, u32[]{:S(2)}, u32[]{:S(2)}) collective-permute-start(bf16[336,384]{1,0:T(8,128)(2,1)S(1)} %get-tuple-element.98), channel_id=1, source_target_pairs={{0,8},{1,12},{2,10},{3,14},{4,9},{5,13},{6,11},{7,15},{8,16},{9,20... | collective-permute-start | bytes 774152 | tf_op jit(solution)/shard_map/ppermute | solution.py:28
  18.1 20.2 %collective-permute-start.7 = (bf16[336,384]{1,0:T(8,128)(2,1)S(1)}, bf16[336,384]{1,0:T(8,128)(2,1)S(1)}, u32[]{:S(2)}, u32[]{:S(2)}) collective-permute-start(bf16[336,384]{1,0:T(8,128)(2,1)S(1)} %get-tuple-element.99), channel_id=1, source_target_pairs={{0,16},{1,20},{2,18},{3,22},{4,17},{5,21},{6,19},{7,23},{8,24},{9,... | collective-permute-start | bytes 774152 | tf_op jit(solution)/shard_map/ppermute | solution.py:28
  20.7 17.9 %collective-permute-start.8 = (bf16[336,384]{1,0:T(8,128)(2,1)S(1)}, bf16[336,384]{1,0:T(8,128)(2,1)S(1)}, u32[]{:S(2)}, u32[]{:S(2)}) collective-permute-start(bf16[336,384]{1,0:T(8,128)(2,1)S(1)} %get-tuple-element.100), channel_id=1, source_target_pairs={{0,24},{1,28},{2,26},{3,30},{4,25},{5,29},{6,27},{7,31},{8,0},{9,4... | collective-permute-start | bytes 774152 | tf_op jit(solution)/shard_map/ppermute | solution.py:28
  22.0 38.3 %copy-start = (bf16[512,2048]{1,0:T(8,128)(2,1)S(1)}, bf16[512,2048]{1,0:T(8,128)(2,1)}, u32[]{:S(2)}) copy-start(bf16[512,2048]{1,0:T(8,128)(2,1)} %refs_4_.5) | copy-start | bytes 6291460
  22.0 16.8 %collective-permute-start.5 = (bf16[336,384]{1,0:T(8,128)(2,1)S(1)}, bf16[336,384]{1,0:T(8,128)(2,1)S(1)}, u32[]{:S(2)}, u32[]{:S(2)}) collective-permute-start(bf16[336,384]{1,0:T(8,128)(2,1)S(1)} %get-tuple-element.97), channel_id=1, source_target_pairs={{0,0},{1,4},{2,2},{3,6},{4,1},{5,5},{6,3},{7,7},{8,8},{9,12},{10,1... | collective-permute-start | bytes 774152 | tf_op jit(solution)/shard_map/ppermute | solution.py:28
  26.9 12.2 %collective-permute-start.10 = (bf16[336,384]{1,0:T(8,128)(2,1)S(1)}, bf16[336,384]{1,0:T(8,128)(2,1)S(1)}, u32[]{:S(2)}, u32[]{:S(2)}) collective-permute-start(bf16[336,384]{1,0:T(8,128)(2,1)S(1)} %collective-permute-done.6.refs_1_), channel_id=1, source_target_pairs={{0,1},{1,0},{2,3},{3,2},{4,5},{5,4},{6,7},{7,6},{8,9},{9,8},{10,11... | collective-permute-start | bytes 774152 | tf_op jit(solution)/shard_map/ppermute | solution.py:28
  38.3 1.5 collective-permute-start.11
  38.6 1.6 collective-permute-start.12
  38.8 1.8 %collective-permute-start.9 = (bf16[336,384]{1,0:T(8,128)(2,1)S(1)}, bf16[336,384]{1,0:T(8,128)(2,1)S(1)}, u32[]{:S(2)}, u32[]{:S(2)}) collective-permute-start(bf16[336,384]{1,0:T(8,128)(2,1)S(1)} %collective-permute-done.5.refs_0_), channel_id=1, source_target_pairs={{0,1},{1,0},{2,3},{3,2},{4,5},{5,4},{6,7},{7,6},{8,9},{9,8},{10,11... | collective-permute-start | bytes 774152 | tf_op jit(solution)/shard_map/ppermute | solution.py:28
  45.3 8.5 %collective-permute-start.13 = (bf16[320,128]{1,0:T(8,128)(2,1)S(1)}, bf16[320,128]{1,0:T(8,128)(2,1)S(1)}, u32[]{:S(2)}, u32[]{:S(2)}) collective-permute-start(bf16[320,128]{1,0:T(8,128)(2,1)S(1)} %get-tuple-element.101), channel_id=1, source_target_pairs={{0,0},{1,4},{2,2},{3,6},{4,1},{5,5},{6,3},{7,7},{8,8},{9,12},{10,1... | collective-permute-start | bytes 245768 | tf_op jit(solution)/shard_map/ppermute | solution.py:28
  45.9 9.3 %collective-permute-start.14 = (bf16[320,128]{1,0:T(8,128)(2,1)S(1)}, bf16[320,128]{1,0:T(8,128)(2,1)S(1)}, u32[]{:S(2)}, u32[]{:S(2)}) collective-permute-start(bf16[320,128]{1,0:T(8,128)(2,1)S(1)} %get-tuple-element.102), channel_id=1, source_target_pairs={{0,24},{1,28},{2,26},{3,30},{4,25},{5,29},{6,27},{7,31},{8,0},{9,4... | collective-permute-start | bytes 245768 | tf_op jit(solution)/shard_map/ppermute | solution.py:28
  53.2 7.1 %collective-permute-start.15 = (bf16[320,128]{1,0:T(8,128)(2,1)S(1)}, bf16[320,128]{1,0:T(8,128)(2,1)S(1)}, u32[]{:S(2)}, u32[]{:S(2)}) collective-permute-start(bf16[320,128]{1,0:T(8,128)(2,1)S(1)} %get-tuple-element.103), channel_id=1, source_target_pairs={{0,16},{1,20},{2,18},{3,22},{4,17},{5,21},{6,19},{7,23},{8,24},{9,... | collective-permute-start | bytes 245768 | tf_op jit(solution)/shard_map/ppermute | solution.py:28
  53.2 14.7 %copy-start.6 = (s32[80,6]{0,1:T(8,128)S(1)}, s32[80,6]{0,1:T(8,128)}, u32[]{:S(2)}) copy-start(s32[80,6]{0,1:T(8,128)} %param.24) | copy-start | bytes 5764
  53.2 14.7 %copy-start.5 = (f32[80,6]{0,1:T(8,128)S(1)}, f32[80,6]{0,1:T(8,128)}, u32[]{:S(2)}) copy-start(f32[80,6]{0,1:T(8,128)} %param.25) | copy-start | bytes 5764
  53.2 7.1 %collective-permute-start.16 = (bf16[320,128]{1,0:T(8,128)(2,1)S(1)}, bf16[320,128]{1,0:T(8,128)(2,1)S(1)}, u32[]{:S(2)}, u32[]{:S(2)}) collective-permute-start(bf16[320,128]{1,0:T(8,128)(2,1)S(1)} %get-tuple-element.104), channel_id=1, source_target_pairs={{0,8},{1,12},{2,10},{3,14},{4,9},{5,13},{6,11},{7,15},{8,16},{9,20... | collective-permute-start | bytes 245768 | tf_op jit(solution)/shard_map/ppermute | solution.py:28
  61.3 4.3 %collective-permute-start.17 = (bf16[80,2048]{1,0:T(8,128)(2,1)S(1)}, bf16[80,2048]{1,0:T(8,128)(2,1)S(1)}, u32[]{:S(2)}, u32[]{:S(2)}) collective-permute-start(bf16[80,2048]{1,0:T(8,128)(2,1)S(1)} %get-tuple-element.105), channel_id=1, source_target_pairs={{0,1},{1,0},{2,3},{3,2},{4,5},{5,4},{6,7},{7,6},{8,9},{9,8},{10,11... | collective-permute-start | bytes 983048 | tf_op jit(solution)/shard_map/ppermute | solution.py:28
  65.7 10.2 %collective-permute-start.20 = (bf16[1,2048,704]{1,2,0:T(8,128)(2,1)}, bf16[1,2048,704]{1,2,0:T(8,128)(2,1)}, u32[]{:S(2)}, u32[]{:S(2)}) collective-permute-start(bf16[1,2048,704]{1,2,0:T(8,128)(2,1)} %param.22), channel_id=1, source_target_pairs={{0,1},{1,0},{2,3},{3,2},{4,5},{5,4},{6,7},{7,6},{8,9},{9,8},{10,11... | collective-permute-start | bytes 8650760 | tf_op jit(solution)/shard_map/ppermute | solution.py:28
  66.1 9.8 %collective-permute-start.19 = (bf16[80,2048]{1,0:T(8,128)(2,1)S(1)}, bf16[80,2048]{1,0:T(8,128)(2,1)S(1)}, u32[]{:S(2)}, u32[]{:S(2)}) collective-permute-start(bf16[80,2048]{1,0:T(8,128)(2,1)S(1)} %shard_map.132), channel_id=1, source_target_pairs={{0,2},{1,3},{2,0},{3,1},{4,6},{5,7},{6,4},{7,5},{8,10},{9,11},{10,... | collective-permute-start | bytes 983048 | tf_op jit(solution)/shard_map/ppermute | solution.py:28
  67.8 8.0 %collective-permute-start.18 = (bf16[80,2048]{1,0:T(8,128)(2,1)S(1)}, bf16[80,2048]{1,0:T(8,128)(2,1)S(1)}, u32[]{:S(2)}, u32[]{:S(2)}) collective-permute-start(bf16[80,2048]{1,0:T(8,128)(2,1)S(1)} %get-tuple-element.111), channel_id=1, source_target_pairs={{0,1},{1,0},{2,3},{3,2},{4,5},{5,4},{6,7},{7,6},{8,9},{9,8},{10,11... | collective-permute-start | bytes 983048 | tf_op jit(solution)/shard_map/ppermute | solution.py:28
  76.3 12.9 %collective-permute-start.24 = (bf16[80,2176]{1,0:T(8,128)(2,1)S(1)}, bf16[80,2176]{1,0:T(8,128)(2,1)S(1)}, u32[]{:S(2)}, u32[]{:S(2)}) collective-permute-start(bf16[80,2176]{1,0:T(8,128)(2,1)S(1)} %get-tuple-element.126.refs_0_), channel_id=1, source_target_pairs={{0,8},{1,9},{2,10},{3,11},{4,12},{5,13},{6,14},{7,15},{8,16},{9,17... | collective-permute-start | bytes 1044488 | tf_op jit(solution)/shard_map/ppermute | solution.py:28
  76.3 16.9 %collective-permute-start.26 = (bf16[80,2176]{1,0:T(8,128)(2,1)S(1)}, bf16[80,2176]{1,0:T(8,128)(2,1)S(1)}, u32[]{:S(2)}, u32[]{:S(2)}) collective-permute-start(bf16[80,2176]{1,0:T(8,128)(2,1)S(1)} %get-tuple-element.126.refs_0_), channel_id=1, source_target_pairs={{0,24},{1,25},{2,26},{3,27},{4,28},{5,29},{6,30},{7,31},{8,0},{9,1... | collective-permute-start | bytes 1044488 | tf_op jit(solution)/shard_map/ppermute | solution.py:28
  81.6 9.4 %collective-permute-start.21 = (bf16[40,2048]{1,0:T(8,128)(2,1)S(1)}, bf16[40,2048]{1,0:T(8,128)(2,1)S(1)}, u32[]{:S(2)}, u32[]{:S(2)}) collective-permute-start(bf16[40,2048]{1,0:T(8,128)(2,1)S(1)} %get-tuple-element.131), channel_id=1, source_target_pairs={{0,2},{1,3},{2,0},{3,1},{4,6},{5,7},{6,4},{7,5},{8,10},{9,11},{10,... | collective-permute-start | bytes 491528 | tf_op jit(solution)/shard_map/ppermute | solution.py:28
  83.4 7.6 %collective-permute-start.22 = (bf16[40,2048]{1,0:T(8,128)(2,1)S(1)}, bf16[40,2048]{1,0:T(8,128)(2,1)S(1)}, u32[]{:S(2)}, u32[]{:S(2)}) collective-permute-start(bf16[40,2048]{1,0:T(8,128)(2,1)S(1)} %get-tuple-element.132), channel_id=1, source_target_pairs={{0,4},{1,5},{2,6},{3,7},{4,0},{5,1},{6,2},{7,3},{8,12},{9,13},{10,... | collective-permute-start | bytes 491528 | tf_op jit(solution)/shard_map/ppermute | solution.py:28
  84.3 7.2 %collective-permute-start.23 = (bf16[40,2048]{1,0:T(8,128)(2,1)S(1)}, bf16[40,2048]{1,0:T(8,128)(2,1)S(1)}, u32[]{:S(2)}, u32[]{:S(2)}) collective-permute-start(bf16[40,2048]{1,0:T(8,128)(2,1)S(1)} %get-tuple-element.133), channel_id=1, source_target_pairs={{0,6},{1,7},{2,4},{3,5},{4,2},{5,3},{6,0},{7,1},{8,14},{9,15},{10,... | collective-permute-start | bytes 491528 | tf_op jit(solution)/shard_map/ppermute | solution.py:28
  89.2 13.2 %collective-permute-start.25 = (bf16[80,2176]{1,0:T(8,128)(2,1)S(1)}, bf16[80,2176]{1,0:T(8,128)(2,1)S(1)}, u32[]{:S(2)}, u32[]{:S(2)}) collective-permute-start(bf16[80,2176]{1,0:T(8,128)(2,1)S(1)} %collective-permute-done.24.refs_0_), channel_id=1, source_target_pairs={{0,8},{1,9},{2,10},{3,11},{4,12},{5,13},{6,14},{7,15},{8,16},{9,17... | collective-permute-start | bytes 1044488 | tf_op jit(solution)/shard_map/ppermute | solution.py:28
  94.9 10.0 %collective-permute-start.27 = (bf16[80,2048]{1,0:T(8,128)(2,1)S(1)}, bf16[80,2048]{1,0:T(8,128)(2,1)S(1)}, u32[]{:S(2)}, u32[]{:S(2)}) collective-permute-start(bf16[80,2048]{1,0:T(8,128)(2,1)S(1)} %get-tuple-element.140), channel_id=1, source_target_pairs={{0,2},{1,3},{2,0},{3,1},{4,6},{5,7},{6,4},{7,5},{8,10},{9,11},{10,... | collective-permute-start | bytes 983048 | tf_op jit(solution)/shard_map/ppermute | solution.py:28
  96.6 11.8 %collective-permute-start.28 = (bf16[80,2048]{1,0:T(8,128)(2,1)S(1)}, bf16[80,2048]{1,0:T(8,128)(2,1)S(1)}, u32[]{:S(2)}, u32[]{:S(2)}) collective-permute-start(bf16[80,2048]{1,0:T(8,128)(2,1)S(1)} %get-tuple-element.148), channel_id=1, source_target_pairs={{0,4},{1,5},{2,6},{3,7},{4,0},{5,1},{6,2},{7,3},{8,12},{9,13},{10,... | collective-permute-start | bytes 983048 | tf_op jit(solution)/shard_map/ppermute | solution.py:28
  97.7 16.4 %collective-permute-start.29 = (bf16[80,2048]{1,0:T(8,128)(2,1)S(1)}, bf16[80,2048]{1,0:T(8,128)(2,1)S(1)}, u32[]{:S(2)}, u32[]{:S(2)}) collective-permute-start(bf16[80,2048]{1,0:T(8,128)(2,1)S(1)} %get-tuple-element.149), channel_id=1, source_target_pairs={{0,6},{1,7},{2,4},{3,5},{4,2},{5,3},{6,0},{7,1},{8,14},{9,15},{10,... | collective-permute-start | bytes 983048 | tf_op jit(solution)/shard_map/ppermute | solution.py:28
  104.9 18.5 %collective-permute-start.30 = (bf16[40,2048]{1,0:T(8,128)(2,1)S(1)}, bf16[40,2048]{1,0:T(8,128)(2,1)S(1)}, u32[]{:S(2)}, u32[]{:S(2)}) collective-permute-start(bf16[40,2048]{1,0:T(8,128)(2,1)S(1)} %get-tuple-element.157), channel_id=1, source_target_pairs={{0,2},{1,3},{2,0},{3,1},{4,6},{5,7},{6,4},{7,5},{8,10},{9,11},{10,... | collective-permute-start | bytes 491528 | tf_op jit(solution)/shard_map/ppermute | solution.py:28
  106.7 17.4 %collective-permute-start.31 = (bf16[40,2048]{1,0:T(8,128)(2,1)S(1)}, bf16[40,2048]{1,0:T(8,128)(2,1)S(1)}, u32[]{:S(2)}, u32[]{:S(2)}) collective-permute-start(bf16[40,2048]{1,0:T(8,128)(2,1)S(1)} %get-tuple-element.158), channel_id=1, source_target_pairs={{0,4},{1,5},{2,6},{3,7},{4,0},{5,1},{6,2},{7,3},{8,12},{9,13},{10,... | collective-permute-start | bytes 491528 | tf_op jit(solution)/shard_map/ppermute | solution.py:28
  107.8 16.3 %collective-permute-start.32 = (bf16[40,2048]{1,0:T(8,128)(2,1)S(1)}, bf16[40,2048]{1,0:T(8,128)(2,1)S(1)}, u32[]{:S(2)}, u32[]{:S(2)}) collective-permute-start(bf16[40,2048]{1,0:T(8,128)(2,1)S(1)} %get-tuple-element.159), channel_id=1, source_target_pairs={{0,6},{1,7},{2,4},{3,5},{4,2},{5,3},{6,0},{7,1},{8,14},{9,15},{10,... | collective-permute-start | bytes 491528 | tf_op jit(solution)/shard_map/ppermute | solution.py:28
  120.5 13.1 %collective-permute-start.33 = (bf16[80,2048]{1,0:T(8,128)(2,1)S(1)}, bf16[80,2048]{1,0:T(8,128)(2,1)S(1)}, u32[]{:S(2)}, u32[]{:S(2)}) collective-permute-start(bf16[80,2048]{1,0:T(8,128)(2,1)S(1)} %get-tuple-element.162), channel_id=1, source_target_pairs={{0,2},{1,3},{2,0},{3,1},{4,6},{5,7},{6,4},{7,5},{8,10},{9,11},{10,... | collective-permute-start | bytes 983048 | tf_op jit(solution)/shard_map/ppermute | solution.py:28
  122.3 11.9 %collective-permute-start.34 = (bf16[80,2048]{1,0:T(8,128)(2,1)S(1)}, bf16[80,2048]{1,0:T(8,128)(2,1)S(1)}, u32[]{:S(2)}, u32[]{:S(2)}) collective-permute-start(bf16[80,2048]{1,0:T(8,128)(2,1)S(1)} %get-tuple-element.163), channel_id=1, source_target_pairs={{0,4},{1,5},{2,6},{3,7},{4,0},{5,1},{6,2},{7,3},{8,12},{9,13},{10,... | collective-permute-start | bytes 983048 | tf_op jit(solution)/shard_map/ppermute | solution.py:28
  123.4 13.9 %collective-permute-start.35 = (bf16[80,2048]{1,0:T(8,128)(2,1)S(1)}, bf16[80,2048]{1,0:T(8,128)(2,1)S(1)}, u32[]{:S(2)}, u32[]{:S(2)}) collective-permute-start(bf16[80,2048]{1,0:T(8,128)(2,1)S(1)} %get-tuple-element.164), channel_id=1, source_target_pairs={{0,6},{1,7},{2,4},{3,5},{4,2},{5,3},{6,0},{7,1},{8,14},{9,15},{10,... | collective-permute-start | bytes 983048 | tf_op jit(solution)/shard_map/ppermute | solution.py:28
  130.7 14.3 %collective-permute-start.41 = (bf16[40,2048]{1,0:T(8,128)(2,1)S(1)}, bf16[40,2048]{1,0:T(8,128)(2,1)S(1)}, u32[]{:S(2)}, u32[]{:S(2)}) collective-permute-start(bf16[40,2048]{1,0:T(8,128)(2,1)S(1)} %get-tuple-element.174), channel_id=1, source_target_pairs={{0,2},{1,3},{2,0},{3,1},{4,6},{5,7},{6,4},{7,5},{8,10},{9,11},{10,... | collective-permute-start | bytes 491528 | tf_op jit(solution)/shard_map/ppermute | solution.py:28
  132.5 12.5 %collective-permute-start.42 = (bf16[40,2048]{1,0:T(8,128)(2,1)S(1)}, bf16[40,2048]{1,0:T(8,128)(2,1)S(1)}, u32[]{:S(2)}, u32[]{:S(2)}) collective-permute-start(bf16[40,2048]{1,0:T(8,128)(2,1)S(1)} %get-tuple-element.175), channel_id=1, source_target_pairs={{0,4},{1,5},{2,6},{3,7},{4,0},{5,1},{6,2},{7,3},{8,12},{9,13},{10,... | collective-permute-start | bytes 491528 | tf_op jit(solution)/shard_map/ppermute | solution.py:28
  133.6 11.4 %collective-permute-start.43 = (bf16[40,2048]{1,0:T(8,128)(2,1)S(1)}, bf16[40,2048]{1,0:T(8,128)(2,1)S(1)}, u32[]{:S(2)}, u32[]{:S(2)}) collective-permute-start(bf16[40,2048]{1,0:T(8,128)(2,1)S(1)} %get-tuple-element.176), channel_id=1, source_target_pairs={{0,6},{1,7},{2,4},{3,5},{4,2},{5,3},{6,0},{7,1},{8,14},{9,15},{10,... | collective-permute-start | bytes 491528 | tf_op jit(solution)/shard_map/ppermute | solution.py:28
  138.8 15.2 %collective-permute-start.39 = (bf16[80,2048]{1,0:T(8,128)(2,1)S(1)}, bf16[80,2048]{1,0:T(8,128)(2,1)S(1)}, u32[]{:S(2)}, u32[]{:S(2)}) collective-permute-start(bf16[80,2048]{1,0:T(8,128)(2,1)S(1)} %get-tuple-element.165), channel_id=1, source_target_pairs={{0,24},{1,25},{2,26},{3,27},{4,28},{5,29},{6,30},{7,31},{8,0},{9,1... | collective-permute-start | bytes 983048 | tf_op jit(solution)/shard_map/ppermute | solution.py:28
  142.6 6.2 %collective-permute-start.38 = (bf16[40,2048]{1,0:T(8,128)(2,1)S(1)}, bf16[40,2048]{1,0:T(8,128)(2,1)S(1)}, u32[]{:S(2)}, u32[]{:S(2)}) collective-permute-start(bf16[40,2048]{1,0:T(8,128)(2,1)S(1)} %get-tuple-element.170), channel_id=1, source_target_pairs={{0,6},{1,7},{2,4},{3,5},{4,2},{5,3},{6,0},{7,1},{8,14},{9,15},{10,... | collective-permute-start | bytes 491528 | tf_op jit(solution)/shard_map/ppermute | solution.py:28
  145.0 9.1 %collective-permute-start.40 = (bf16[80,2048]{1,0:T(8,128)(2,1)S(1)}, bf16[80,2048]{1,0:T(8,128)(2,1)S(1)}, u32[]{:S(2)}, u32[]{:S(2)}) collective-permute-start(bf16[80,2048]{1,0:T(8,128)(2,1)S(1)} %get-tuple-element.172), channel_id=1, source_target_pairs={{0,8},{1,9},{2,10},{3,11},{4,12},{5,13},{6,14},{7,15},{8,16},{9,17... | collective-permute-start | bytes 983048 | tf_op jit(solution)/shard_map/ppermute | solution.py:28
  145.8 15.3 %collective-permute-start.44 = (bf16[80,2048]{1,0:T(8,128)(2,1)S(1)}, bf16[80,2048]{1,0:T(8,128)(2,1)S(1)}, u32[]{:S(2)}, u32[]{:S(2)}) collective-permute-start(bf16[80,2048]{1,0:T(8,128)(2,1)S(1)} %shard_map.146), channel_id=1, source_target_pairs={{0,16},{1,17},{2,18},{3,19},{4,20},{5,21},{6,22},{7,23},{8,24},{9,... | collective-permute-start | bytes 983048 | tf_op jit(solution)/shard_map/ppermute | solution.py:28
  148.0 5.3 %collective-permute-start.37 = (bf16[40,2048]{1,0:T(8,128)(2,1)S(1)}, bf16[40,2048]{1,0:T(8,128)(2,1)S(1)}, u32[]{:S(2)}, u32[]{:S(2)}) collective-permute-start(bf16[40,2048]{1,0:T(8,128)(2,1)S(1)} %get-tuple-element.168), channel_id=1, source_target_pairs={{0,4},{1,5},{2,6},{3,7},{4,0},{5,1},{6,2},{7,3},{8,12},{9,13},{10,... | collective-permute-start | bytes 491528 | tf_op jit(solution)/shard_map/ppermute | solution.py:28
  148.8 5.3 %collective-permute-start.36 = (bf16[40,2048]{1,0:T(8,128)(2,1)S(1)}, bf16[40,2048]{1,0:T(8,128)(2,1)S(1)}, u32[]{:S(2)}, u32[]{:S(2)}) collective-permute-start(bf16[40,2048]{1,0:T(8,128)(2,1)S(1)} %get-tuple-element.166), channel_id=1, source_target_pairs={{0,2},{1,3},{2,0},{3,1},{4,6},{5,7},{6,4},{7,5},{8,10},{9,11},{10,... | collective-permute-start | bytes 491528 | tf_op jit(solution)/shard_map/ppermute | solution.py:28
  (4 other events, 28.6 us)

commit v10 on v9

--- a/solution.py
+++ b/solution.py
@@ -297,20 +297,13 @@
     summed[...] = (kept[...].astype(jnp.float32) + given[...].astype(jnp.float32)).astype(summed.dtype)
 
 
-def residual_kernel(top_count, inputs, kept, given, far, gain, noted, residual, ffn_in):
+def residual_kernel(inputs, kept, given, far, gain, noted, residual, ffn_in):
     summed = kept[...].astype(jnp.float32) + given[...].astype(jnp.float32) + far[...].astype(jnp.float32)
     rounded = (inputs[...].astype(jnp.float32) + summed).astype(jnp.bfloat16)
     residual[...] = rounded
     model_width = rounded.shape[1]
     ffn_in[:, 0:model_width] = normalize(rounded, gain[...])
-    lane = lax.broadcasted_iota(jnp.int32, noted.shape, 1)
-    left = noted[...]
-    upper = left.astype(jnp.bfloat16).astype(jnp.float32)
-    left = left - upper
-    middle = left.astype(jnp.bfloat16).astype(jnp.float32)
-    lower = left - middle
-    parts = jnp.where(lane < 2 * top_count, upper, jnp.where(lane < 3 * top_count, middle, lower))
-    ffn_in[:, model_width:] = parts.astype(jnp.bfloat16)
+    ffn_in[:, model_width:] = noted[...].astype(jnp.bfloat16)
 
 
 def pack_kernel(count, capacity, top_count, place, *refs):
@@ -364,13 +357,13 @@
             start += count
 
 
-def weigh_kernel(count, capacity, top_count, place, notes, upper, lower):
+def weigh_kernel(count, capacity, top_count, place, notes, shares):
     expert = place[4]
     total = notes.shape[0]
     tok_rows = total // count
     row = lax.broadcasted_iota(jnp.int32, (LANES, LANES), 0)
     lane = lax.broadcasted_iota(jnp.int32, (LANES, LANES), 1)
-    added = (lane < top_count) & (row >= top_count) & (row < 4 * top_count) & (row % top_count == lane)
+    added = (lane < top_count) & (row == lane + top_count)
     gates = f32_dot(notes[...], jnp.where(added, 1.0, 0.0).astype(jnp.bfloat16))
     routes = notes[...].astype(jnp.float32)
     routes = jnp.where(lax.broadcasted_iota(jnp.int32, routes.shape, 1) < top_count, routes, -1.0)
@@ -386,30 +379,28 @@
         place_in = f32_dot(before, jnp.broadcast_to(member, (total, LANES)).astype(jnp.bfloat16))[:, 0:1]
         target = jnp.where(member > 0.5, place_in.astype(jnp.int32) + first_slot, -1)
         placing = jnp.where(slot == target, factor, 0.0)
-        upper[hop] = placing.astype(jnp.bfloat16)
-        lower[hop] = (placing - upper[hop].astype(jnp.float32)).astype(jnp.bfloat16)
-
-
-def mix_slots(upper, lower, returned):
+        shares[hop] = placing.astype(jnp.bfloat16)
+
+
+def mix_slots(shares, returned):
     mixed = None
     for hop in range(4):
-        rows = returned[hop][...]
-        term = f32_dot(upper[hop], rows) + f32_dot(lower[hop], rows)
+        term = f32_dot(shares[hop], returned[hop][...])
         mixed = term if mixed is None else mixed + term
     return mixed
 
 
-def combine_kernel(count, upper, lower, *refs):
+def combine_kernel(count, shares, *refs):
     returned, outs = refs[:4], refs[4 : 4 + count]
-    tok_rows = upper.shape[1] // count
-    mixed = mix_slots(upper, lower, returned)
+    tok_rows = shares.shape[1] // count
+    mixed = mix_slots(shares, returned)
     for turn in range(count):
         outs[turn][...] = mixed[turn * tok_rows : (turn + 1) * tok_rows].astype(jnp.bfloat16)
 
 
-def finish_kernel(upper, lower, *refs):
+def finish_kernel(shares, *refs):
     returned, (residual, *others), out = refs[:4], refs[4:-1], refs[-1]
-    total = residual[...].astype(jnp.float32) + mix_slots(upper, lower, returned)
+    total = residual[...].astype(jnp.float32) + mix_slots(shares, returned)
     for other in others:
         total = total + other[...].astype(jnp.float32)
     out[...] = total
@@ -449,7 +440,7 @@
     weights = (w_gate, w_up, w_down)
     other_gate, other_up, other_down = swap_core(w_gate), None, swap_core(w_down)
     top_count = routes.shape[1]
-    noted = jnp.concatenate([routes.astype(jnp.float32)] + [gate_weights] * 3, axis=1)
+    noted = jnp.concatenate([routes.astype(jnp.float32), gate_weights], axis=1)
     noted = jnp.pad(noted, ((0, 0), (0, LANES - noted.shape[1])))
     if by_head:
         marks = jnp.sum(
@@ -534,7 +525,7 @@
     beyond = move(beyond, lambda z, x, y, c: (z, x, y ^ 1, c))
     beyond, expert_weights = lax.optimization_barrier((beyond, expert_weights))
     residual, ffn_in = call(
-        functools.partial(residual_kernel, top_count),
+        residual_kernel,
         [struct(tok_rows, model_width), struct(tok_rows, model_width + LANES)],
         [inputs, kept, given, beyond, ffn_gain.reshape(1, -1), noted],
         smem=0,
@@ -591,17 +582,17 @@
         shares.append(
             call(
                 functools.partial(weigh_kernel, count, capacity, top_count),
-                [struct(4, total, count * capacity)] * 2,
+                struct(4, total, count * capacity),
                 [place, note],
                 flops=8 * total * total * LANES,
                 limit=8 * MIB + 16 * total * total,
             )
         )
-    arrived[1][1] = after(arrived[1][1], *(part for share in shares for part in share))
-    results = [None, expert_rows(arrived[1]), None]
-    far_rows = [after(arrived[2][0], results[1][0])] + arrived[2][1:]
-    both = expert_rows(arrived[0] + far_rows)
-    results[0], results[2] = both[:4], both[4:]
+    arrived[1][1] = after(arrived[1][1], *shares)
+    own_results = expert_rows(arrived[0])
+    next_results = expert_rows([after(arrived[1][0], own_results[0])] + arrived[1][1:])
+    far_results = expert_rows([after(arrived[2][0], next_results[0])] + arrived[2][1:])
+    results = [own_results, next_results, far_results]
     sums = [None] * depth
     home = [None] * depth
     for index in (1, 2):
@@ -612,7 +603,7 @@
         parts = call(
             functools.partial(combine_kernel, count),
             [struct(tok_rows, model_width)] * count,
-            [*shares[index], *rows],
+            [shares[index], *rows],
             flops=16 * count * capacity * total * model_width,
             smem=0,
             limit=8 * MIB + 16 * total * model_width,
@@ -624,7 +615,7 @@
     layer_out = call(
         finish_kernel,
         struct(tok_rows, model_width, dtype=jnp.float32),
-        [*shares[0], *rows, residual, *(home[turn] for turn in groups[1])],
+        [shares[0], *rows, residual, *(home[turn] for turn in groups[1])],
         flops=16 * capacity * tok_rows * model_width,
         smem=0,
     )

time: 162 us -> 160 us (0.988)
  waiting for transfers between devices: 57.8 us -> 53.9 us
    ppermute x45, waiting for transfers between devices: 57.8 us -> 53.9 us  [move(): return lax.ppermute(block, AXES, route)]
    pallas_call x20 -> x21, Pallas kernels: 44.7 us -> 46.2 us  [call(): pl.pallas_call(kernel, out_shape=outs, in_specs=[SMEM] * smem + [VMEM] *...]
  transfers between devices with their start and end apart: 45 -> 45, of which waited for: 22 -> 21; matrix products, arithmetic and copies ran while one was open for 0% -> 0% of each run, Pallas kernels for 22% -> 23%
where the time goes in v10:
time: 160 us
  starting transfers between devices  58.7 us (37%)
  waiting for transfers between devices  53.9 us (34%)
  Pallas kernels  46.2 us (29%)
    ppermute x45, starting transfers between devices, move(): return lax.ppermute(block, AXES, route)  58.7 us
    ppermute x45, waiting for transfers between devices, move(): return lax.ppermute(block, AXES, route)  53.9 us
    pallas_call x21, Pallas kernels, call(): pl.pallas_call(kernel, out_shape=outs, in_specs=[SMEM] * smem + [VMEM] *...  46.2 us
  transfers between devices with their start and end apart: 45, of which 21 were waited for; matrix products, arithmetic and copies ran while one was open for 0% of the time, Pallas kernels for 23%

profile of v10, /device:TPU:0, one launch (start us, length us, event | category | flops | bytes accessed | tf_op | source)
XLA Modules:
  0.0 160.2 jit_solution(6656363278944172333)
XLA Ops:
  1.0 2.5 %collective-permute-start.1 = (bf16[80,2048]{1,0:T(8,128)(2,1)}, bf16[80,2048]{1,0:T(8,128)(2,1)S(1)}, u32[]{:S(2)}, u32[]{:S(2)}) collective-permute-start(bf16[80,2048]{1,0:T(8,128)(2,1)} %inputs.1), channel_id=1, source_target_pairs={{0,2},{1,3},{2,0},{3,1},{4,6},{5,7},{6,4},{7,5},{8,10},{9,11},{10,... | collective-permute-start | bytes 983048 | tf_op jit(solution)/shard_map/ppermute | solution.py:28
  3.6 2.9 %collective-permute-done.refs_0_ = bf16[80,2048]{1,0:T(8,128)(2,1)S(1)} collective-permute-done((bf16[80,2048]{1,0:T(8,128)(2,1)}, bf16[80,2048]{1,0:T(8,128)(2,1)S(1)}, u32[]{:S(2)}, u32[]{:S(2)}) %collective-permute-start) | collective-permute-done | bytes 327712 | tf_op jit(solution)/shard_map/ppermute | solution.py:28
  6.5 4.2 %shard_map.127 = (bf16[3,160,512]{2,1,0:T(8,128)(2,1)S(1)}, bf16[2048,512]{1,0:T(8,128)(2,1)S(1)}, bf16[2048,512]{1,0:T(8,128)(2,1)S(1)}, bf16[2048,512]{1,0:T(8,128)(2,1)S(1)}) custom-call(s32[5]{0:T(128)S(1)} %stack.20.place, bf16[80,2048]{1,0:T(8,128)(2,1)S(1)} %collective-permute-done.refs_0_, f32[1,2048]{1,0:T(1,128)} %bitcast.22, ...), custom_call_target="tpu_custom_call" | custom-call | flops 1006632960 | bytes 6955028 | tf_op jit(solution)/shard_map/pallas_call | solution.py:87
  10.7 1.3 collective-permute-done.1.refs_3_
  12.1 1.6 collective-permute-done.2.refs_4_
  13.7 2.5 %shard_map.128 = (bf16[336,384]{1,0:T(8,128)(2,1)S(1)}, bf16[336,384]{1,0:T(8,128)(2,1)S(1)}, bf16[336,384]{1,0:T(8,128)(2,1)S(1)}, bf16[336,384]{1,0:T(8,128)(2,1)S(1)}) custom-call(s32[5]{0:T(128)S(1)} %stack.20.place, bf16[4,16,384]{2,1,0:T(8,128)(2,1)S(1)} %broadcast_in_dim.11.marks, bf16[3,160,512]{2,1,0:T(8,128)(2,1)S(1)} %get-tuple-element.86.near_mixed, ...), custom_call_target="tpu_custom_call" | custom-call | flops 1006632960 | bytes 7495700 | tf_op jit(solution)/shard_map/pallas_call | solution.py:87
  16.2 1.9 %collective-permute-start.6 = (bf16[336,384]{1,0:T(8,128)(2,1)S(1)}, bf16[336,384]{1,0:T(8,128)(2,1)S(1)}, u32[]{:S(2)}, u32[]{:S(2)}) collective-permute-start(bf16[336,384]{1,0:T(8,128)(2,1)S(1)} %get-tuple-element.93), channel_id=1, source_target_pairs={{0,8},{1,12},{2,10},{3,14},{4,9},{5,13},{6,11},{7,15},{8,16},{9,20... | collective-permute-start | bytes 774152 | tf_op jit(solution)/shard_map/ppermute | solution.py:28
  18.1 2.6 %collective-permute-start.7 = (bf16[336,384]{1,0:T(8,128)(2,1)S(1)}, bf16[336,384]{1,0:T(8,128)(2,1)S(1)}, u32[]{:S(2)}, u32[]{:S(2)}) collective-permute-start(bf16[336,384]{1,0:T(8,128)(2,1)S(1)} %get-tuple-element.94), channel_id=1, source_target_pairs={{0,16},{1,20},{2,18},{3,22},{4,17},{5,21},{6,19},{7,23},{8,24},{9,... | collective-permute-start | bytes 774152 | tf_op jit(solution)/shard_map/ppermute | solution.py:28
  20.7 1.4 collective-permute-start.8
  22.8 4.0 %collective-permute-done.6.refs_1_ = bf16[336,384]{1,0:T(8,128)(2,1)S(1)} collective-permute-done((bf16[336,384]{1,0:T(8,128)(2,1)S(1)}, bf16[336,384]{1,0:T(8,128)(2,1)S(1)}, u32[]{:S(2)}, u32[]{:S(2)}) %collective-permute-start.6) | collective-permute-done | bytes 258080 | tf_op jit(solution)/shard_map/ppermute | solution.py:28
  26.8 1.1 collective-permute-start.10
  28.0 10.3 %collective-permute-done.7.refs_2_ = bf16[336,384]{1,0:T(8,128)(2,1)S(1)} collective-permute-done((bf16[336,384]{1,0:T(8,128)(2,1)S(1)}, bf16[336,384]{1,0:T(8,128)(2,1)S(1)}, u32[]{:S(2)}, u32[]{:S(2)}) %collective-permute-start.7) | collective-permute-done | bytes 258080 | tf_op jit(solution)/shard_map/ppermute | solution.py:28
  40.5 4.7 %shard_map.129 = (bf16[320,128]{1,0:T(8,128)(2,1)S(1)}, bf16[320,128]{1,0:T(8,128)(2,1)S(1)}, bf16[320,128]{1,0:T(8,128)(2,1)S(1)}, bf16[320,128]{1,0:T(8,128)(2,1)S(1)}) custom-call(s32[5]{0:T(128)S(1)} %stack.20.place, bf16[336,384]{1,0:T(8,128)(2,1)S(1)} %collective-permute-done.5.refs_0_, bf16[336,384]{1,0:T(8,128)(2,1)S(1)} %collective-permute-done.6.refs_1_, ...), custom_call_target="tpu_custom_call" | custom-call | flops 1677721600 | bytes 2064404 | tf_op jit(solution)/shard_map/pallas_call | solution.py:87
  45.9 7.2 %collective-permute-start.14 = (bf16[320,128]{1,0:T(8,128)(2,1)S(1)}, bf16[320,128]{1,0:T(8,128)(2,1)S(1)}, u32[]{:S(2)}, u32[]{:S(2)}) collective-permute-start(bf16[320,128]{1,0:T(8,128)(2,1)S(1)} %get-tuple-element.97), channel_id=1, source_target_pairs={{0,24},{1,28},{2,26},{3,30},{4,25},{5,29},{6,27},{7,31},{8,0},{9,4... | collective-permute-start | bytes 245768 | tf_op jit(solution)/shard_map/ppermute | solution.py:28
  53.8 1.4 collective-permute-done.14.refs_1_
  55.2 5.0 %collective-permute-done.15.refs_2_ = bf16[320,128]{1,0:T(8,128)(2,1)S(1)} collective-permute-done((bf16[320,128]{1,0:T(8,128)(2,1)S(1)}, bf16[320,128]{1,0:T(8,128)(2,1)S(1)}, u32[]{:S(2)}, u32[]{:S(2)}) %collective-permute-start.15) | collective-permute-done | bytes 81952 | tf_op jit(solution)/shard_map/ppermute | solution.py:28
  61.3 3.0 %collective-permute-start.17 = (bf16[80,2048]{1,0:T(8,128)(2,1)S(1)}, bf16[80,2048]{1,0:T(8,128)(2,1)S(1)}, u32[]{:S(2)}, u32[]{:S(2)}) collective-permute-start(bf16[80,2048]{1,0:T(8,128)(2,1)S(1)} %get-tuple-element.100), channel_id=1, source_target_pairs={{0,1},{1,0},{2,3},{3,2},{4,5},{5,4},{6,7},{7,6},{8,9},{9,8},{10,11... | collective-permute-start | bytes 983048 | tf_op jit(solution)/shard_map/ppermute | solution.py:28
  66.1 1.7 %collective-permute-start.19 = (bf16[80,2048]{1,0:T(8,128)(2,1)S(1)}, bf16[80,2048]{1,0:T(8,128)(2,1)S(1)}, u32[]{:S(2)}, u32[]{:S(2)}) collective-permute-start(bf16[80,2048]{1,0:T(8,128)(2,1)S(1)} %shard_map.132), channel_id=1, source_target_pairs={{0,2},{1,3},{2,0},{3,1},{4,6},{5,7},{6,4},{7,5},{8,10},{9,11},{10,... | collective-permute-start | bytes 983048 | tf_op jit(solution)/shard_map/ppermute | solution.py:28
  68.0 5.3 %shard_map.133 = (bf16[704,2048]{1,0:T(8,128)(2,1)S(1)}, bf16[704,2048]{1,0:T(8,128)(2,1)S(1)}, bf16[704,2048]{1,0:T(8,128)(2,1)S(1)}, bf16[704,2048]{1,0:T(8,128)(2,1)S(1)}, bf16[704,2048]{1,0:T(8,128)(2,1)S(1)}) custom-call(bf16[704,2048]{1,0:T(8,128)(2,1)} %bitcast.25, bf16[704,2048]{1,0:T(8,128)(2,1)} %bitcast.9.refs_1_, bf16[704,2048]{1,0:T(8,128)(2,1)} %bitcast.26, ...), custom_call_target="tpu_custom_call" | custom-call | bytes 14417920 | tf_op jit(solution)/shard_map/pallas_call | solution.py:87
  73.3 2.6 %collective-permute-done.19.far = bf16[80,2048]{1,0:T(8,128)(2,1)S(1)} collective-permute-done((bf16[80,2048]{1,0:T(8,128)(2,1)S(1)}, bf16[80,2048]{1,0:T(8,128)(2,1)S(1)}, u32[]{:S(2)}, u32[]{:S(2)}) %collective-permute-start.19) | collective-permute-done | bytes 327712 | tf_op jit(solution)/shard_map/ppermute | solution.py:28
  76.3 3.8 %collective-permute-start.25 = (bf16[80,2176]{1,0:T(8,128)(2,1)S(1)}, bf16[80,2176]{1,0:T(8,128)(2,1)S(1)}, u32[]{:S(2)}, u32[]{:S(2)}) collective-permute-start(bf16[80,2176]{1,0:T(8,128)(2,1)S(1)} %get-tuple-element.121.refs_0_), channel_id=1, source_target_pairs={{0,24},{1,25},{2,26},{3,27},{4,28},{5,29},{6,30},{7,31},{8,0},{9,1... | collective-permute-start | bytes 1044488 | tf_op jit(solution)/shard_map/ppermute | solution.py:28
  80.1 1.5 shard_map.135
  81.6 1.8 %collective-permute-start.21 = (bf16[40,2048]{1,0:T(8,128)(2,1)S(1)}, bf16[40,2048]{1,0:T(8,128)(2,1)S(1)}, u32[]{:S(2)}, u32[]{:S(2)}) collective-permute-start(bf16[40,2048]{1,0:T(8,128)(2,1)S(1)} %get-tuple-element.124), channel_id=1, source_target_pairs={{0,2},{1,3},{2,0},{3,1},{4,6},{5,7},{6,4},{7,5},{8,10},{9,11},{10,... | collective-permute-start | bytes 491528 | tf_op jit(solution)/shard_map/ppermute | solution.py:28
  85.2 4.0 %collective-permute-done.24.refs_0_ = bf16[80,2176]{1,0:T(8,128)(2,1)S(1)} collective-permute-done((bf16[80,2176]{1,0:T(8,128)(2,1)S(1)}, bf16[80,2176]{1,0:T(8,128)(2,1)S(1)}, u32[]{:S(2)}, u32[]{:S(2)}) %collective-permute-start.24) | collective-permute-done | bytes 348192 | tf_op jit(solution)/shard_map/ppermute | solution.py:28
  89.2 1.8 %shard_map.137.refs_8_ = bf16[704,2048]{1,0:T(8,128)(2,1)S(1)} custom-call(bf16[704,2048]{1,0:T(8,128)(2,1)} %bitcast.15.refs_0_), custom_call_target="tpu_custom_call" | custom-call | bytes 2883584 | tf_op jit(solution)/shard_map/pallas_call | solution.py:87
  91.4 1.8 %collective-permute-done.25.refs_1_ = bf16[80,2176]{1,0:T(8,128)(2,1)S(1)} collective-permute-done((bf16[80,2176]{1,0:T(8,128)(2,1)S(1)}, bf16[80,2176]{1,0:T(8,128)(2,1)S(1)}, u32[]{:S(2)}, u32[]{:S(2)}) %collective-permute-start.25) | collective-permute-done | bytes 348192 | tf_op jit(solution)/shard_map/ppermute | solution.py:28
  93.2 1.7 %shard_map.139 = (bf16[80,2048]{1,0:T(8,128)(2,1)S(1)}, bf16[80,2048]{1,0:T(8,128)(2,1)S(1)}, bf16[80,2048]{1,0:T(8,128)(2,1)S(1)}, bf16[80,2048]{1,0:T(8,128)(2,1)S(1)}, bf16[160,128]{1,0:T(8,128)(2,1)S(1)}) custom-call(s32[5]{0:T(128)S(1)} %stack.20.place, bf16[80,2176]{1,0:T(8,128)(2,1)S(1)} %collective-permute-done.24.refs_0_, ...), custom_call_target="tpu_custom_call" | custom-call | flops 209715200 | bytes 696340 | tf_op jit(solution)/shard_map/pallas_call | solution.py:87
  94.9 1.8 %collective-permute-start.26 = (bf16[80,2048]{1,0:T(8,128)(2,1)S(1)}, bf16[80,2048]{1,0:T(8,128)(2,1)S(1)}, u32[]{:S(2)}, u32[]{:S(2)}) collective-permute-start(bf16[80,2048]{1,0:T(8,128)(2,1)S(1)} %get-tuple-element.140), channel_id=1, source_target_pairs={{0,2},{1,3},{2,0},{3,1},{4,6},{5,7},{6,4},{7,5},{8,10},{9,11},{10,... | collective-permute-start | bytes 983048 | tf_op jit(solution)/shard_map/ppermute | solution.py:28
  99.3 4.7 %shard_map.138 = (bf16[40,2048]{1,0:T(8,128)(2,1)S(1)}, bf16[40,2048]{1,0:T(8,128)(2,1)S(1)}, bf16[40,2048]{1,0:T(8,128)(2,1)S(1)}, bf16[40,2048]{1,0:T(8,128)(2,1)S(1)}) custom-call(bf16[40,2048]{1,0:T(8,128)(2,1)S(1)} %get-tuple-element.123.refs_0_, bf16[40,2048]{1,0:T(8,128)(2,1)S(1)} %collective-permute-done.21.refs_1_, ...), custom_call_target="tpu_custom_call" | custom-call | flops 2768240640 | bytes 17956864 | tf_op jit(solution)/shard_map/pallas_call | solution.py:87
  105.0 1.5 shard_map.141
  107.4 1.8 %collective-permute-start.38 = (bf16[40,2048]{1,0:T(8,128)(2,1)S(1)}, bf16[40,2048]{1,0:T(8,128)(2,1)S(1)}, u32[]{:S(2)}, u32[]{:S(2)}) collective-permute-start(bf16[40,2048]{1,0:T(8,128)(2,1)S(1)} %get-tuple-element.160), channel_id=1, source_target_pairs={{0,2},{1,3},{2,0},{3,1},{4,6},{5,7},{6,4},{7,5},{8,10},{9,11},{10,... | collective-permute-start | bytes 491528 | tf_op jit(solution)/shard_map/ppermute | solution.py:28
  111.0 2.5 %collective-permute-done.29.refs_3_ = bf16[80,2048]{1,0:T(8,128)(2,1)S(1)} collective-permute-done((bf16[80,2048]{1,0:T(8,128)(2,1)S(1)}, bf16[80,2048]{1,0:T(8,128)(2,1)S(1)}, u32[]{:S(2)}, u32[]{:S(2)}) %collective-permute-start.29) | collective-permute-done | bytes 327712 | tf_op jit(solution)/shard_map/ppermute | solution.py:28
  113.5 6.3 %shard_map.143 = (bf16[80,2048]{1,0:T(8,128)(2,1)S(1)}, bf16[80,2048]{1,0:T(8,128)(2,1)S(1)}, bf16[80,2048]{1,0:T(8,128)(2,1)S(1)}, bf16[80,2048]{1,0:T(8,128)(2,1)S(1)}) custom-call(bf16[80,2048]{1,0:T(8,128)(2,1)S(1)} %get-tuple-element.139.refs_0_, bf16[80,2048]{1,0:T(8,128)(2,1)S(1)} %collective-permute-done.26.refs_1_, ...), custom_call_target="tpu_custom_call" | custom-call | flops 5536481280 | bytes 18612224 | tf_op jit(solution)/shard_map/pallas_call | solution.py:87
  119.8 1.7 %collective-permute-start.30 = (bf16[80,2048]{1,0:T(8,128)(2,1)S(1)}, bf16[80,2048]{1,0:T(8,128)(2,1)S(1)}, u32[]{:S(2)}, u32[]{:S(2)}) collective-permute-start(bf16[80,2048]{1,0:T(8,128)(2,1)S(1)} %get-tuple-element.147), channel_id=1, source_target_pairs={{0,2},{1,3},{2,0},{3,1},{4,6},{5,7},{6,4},{7,5},{8,10},{9,11},{10,... | collective-permute-start | bytes 983048 | tf_op jit(solution)/shard_map/ppermute | solution.py:28
  121.6 1.3 collective-permute-start.31
  123.4 4.9 %shard_map.146 = (bf16[40,2048]{1,0:T(8,128)(2,1)S(1)}, bf16[40,2048]{1,0:T(8,128)(2,1)S(1)}, bf16[40,2048]{1,0:T(8,128)(2,1)S(1)}, bf16[40,2048]{1,0:T(8,128)(2,1)S(1)}) custom-call(bf16[40,2048]{1,0:T(8,128)(2,1)S(1)} %get-tuple-element.159.refs_0_, bf16[40,2048]{1,0:T(8,128)(2,1)S(1)} %collective-permute-done.38.refs_1_, ...), custom_call_target="tpu_custom_call" | custom-call | flops 2768240640 | bytes 17956864 | tf_op jit(solution)/shard_map/pallas_call | solution.py:87
  128.3 1.7 %collective-permute-start.41 = (bf16[40,2048]{1,0:T(8,128)(2,1)S(1)}, bf16[40,2048]{1,0:T(8,128)(2,1)S(1)}, u32[]{:S(2)}, u32[]{:S(2)}) collective-permute-start(bf16[40,2048]{1,0:T(8,128)(2,1)S(1)} %get-tuple-element.164), channel_id=1, source_target_pairs={{0,2},{1,3},{2,0},{3,1},{4,6},{5,7},{6,4},{7,5},{8,10},{9,11},{10,... | collective-permute-start | bytes 491528 | tf_op jit(solution)/shard_map/ppermute | solution.py:28
  130.0 1.3 collective-permute-start.42
  132.0 2.4 %collective-permute-start.43 = (bf16[40,2048]{1,0:T(8,128)(2,1)S(1)}, bf16[40,2048]{1,0:T(8,128)(2,1)S(1)}, u32[]{:S(2)}, u32[]{:S(2)}) collective-permute-start(bf16[40,2048]{1,0:T(8,128)(2,1)S(1)} %get-tuple-element.166), channel_id=1, source_target_pairs={{0,6},{1,7},{2,4},{3,5},{4,2},{5,3},{6,0},{7,1},{8,14},{9,15},{10,... | collective-permute-start | bytes 491528 | tf_op jit(solution)/shard_map/ppermute | solution.py:28
  134.4 3.6 %collective-permute-done.32.refs_3_ = bf16[80,2048]{1,0:T(8,128)(2,1)S(1)} collective-permute-done((bf16[80,2048]{1,0:T(8,128)(2,1)S(1)}, bf16[80,2048]{1,0:T(8,128)(2,1)S(1)}, u32[]{:S(2)}, u32[]{:S(2)}) %collective-permute-start.32) | collective-permute-done | bytes 327712 | tf_op jit(solution)/shard_map/ppermute | solution.py:28
  138.8 2.0 %collective-permute-start.36 = (bf16[80,2048]{1,0:T(8,128)(2,1)S(1)}, bf16[80,2048]{1,0:T(8,128)(2,1)S(1)}, u32[]{:S(2)}, u32[]{:S(2)}) collective-permute-start(bf16[80,2048]{1,0:T(8,128)(2,1)S(1)} %get-tuple-element.150), channel_id=1, source_target_pairs={{0,24},{1,25},{2,26},{3,27},{4,28},{5,29},{6,30},{7,31},{8,0},{9,1... | collective-permute-start | bytes 983048 | tf_op jit(solution)/shard_map/ppermute | solution.py:28
  140.9 2.5 %collective-permute-start.35 = (bf16[40,2048]{1,0:T(8,128)(2,1)S(1)}, bf16[40,2048]{1,0:T(8,128)(2,1)S(1)}, u32[]{:S(2)}, u32[]{:S(2)}) collective-permute-start(bf16[40,2048]{1,0:T(8,128)(2,1)S(1)} %get-tuple-element.155), channel_id=1, source_target_pairs={{0,6},{1,7},{2,4},{3,5},{4,2},{5,3},{6,0},{7,1},{8,14},{9,15},{10,... | collective-permute-start | bytes 491528 | tf_op jit(solution)/shard_map/ppermute | solution.py:28
  144.9 1.5 collective-permute-start.44
  146.4 1.1 collective-permute-start.34
  147.5 1.3 collective-permute-start.33
  148.8 2.9 %collective-permute-done.34.refs_2_ = bf16[40,2048]{1,0:T(8,128)(2,1)S(1)} collective-permute-done((bf16[40,2048]{1,0:T(8,128)(2,1)S(1)}, bf16[40,2048]{1,0:T(8,128)(2,1)S(1)}, u32[]{:S(2)}, u32[]{:S(2)}) %collective-permute-start.34) | collective-permute-done | bytes 163872 | tf_op jit(solution)/shard_map/ppermute | solution.py:28
  151.7 1.1 collective-permute-done.33.refs_1_
  153.3 6.1 %collective-permute-done.44 = bf16[80,2048]{1,0:T(8,128)(2,1)S(1)} collective-permute-done((bf16[80,2048]{1,0:T(8,128)(2,1)S(1)}, bf16[80,2048]{1,0:T(8,128)(2,1)S(1)}, u32[]{:S(2)}, u32[]{:S(2)}) %collective-permute-start.44) | collective-permute-done | bytes 327712 | tf_op jit(solution)/shard_map/ppermute | solution.py:28
  (87 shorter events, 22.1 us)
Async XLA Ops:
  0.0 13.7 %collective-permute-start.3 = (bf16[1,2048,704]{1,2,0:T(8,128)(2,1)}, bf16[1,2048,704]{1,2,0:T(8,128)(2,1)}, u32[]{:S(2)}, u32[]{:S(2)}) collective-permute-start(bf16[1,2048,704]{1,2,0:T(8,128)(2,1)} %param.21), channel_id=1, source_target_pairs={{0,1},{1,0},{2,3},{3,2},{4,5},{5,4},{6,7},{7,6},{8,9},{9,8},{10,11... | collective-permute-start | bytes 8650760 | tf_op jit(solution)/shard_map/ppermute | solution.py:28
  0.5 13.3 %collective-permute-start.4 = (bf16[1,704,2048]{2,1,0:T(8,128)(2,1)}, bf16[1,704,2048]{2,1,0:T(8,128)(2,1)}, u32[]{:S(2)}, u32[]{:S(2)}) collective-permute-start(bf16[1,704,2048]{2,1,0:T(8,128)(2,1)} %param.23), channel_id=1, source_target_pairs={{0,1},{1,0},{2,3},{3,2},{4,5},{5,4},{6,7},{7,6},{8,9},{9,8},{10,11... | collective-permute-start | bytes 8650760 | tf_op jit(solution)/shard_map/ppermute | solution.py:28
  0.5 6.0 %collective-permute-start = (bf16[80,2048]{1,0:T(8,128)(2,1)}, bf16[80,2048]{1,0:T(8,128)(2,1)S(1)}, u32[]{:S(2)}, u32[]{:S(2)}) collective-permute-start(bf16[80,2048]{1,0:T(8,128)(2,1)} %inputs.1), channel_id=1, source_target_pairs={{0,1},{1,0},{2,3},{3,2},{4,5},{5,4},{6,7},{7,6},{8,9},{9,8},{10,11... | collective-permute-start | bytes 983048 | tf_op jit(solution)/shard_map/ppermute | solution.py:28
  1.0 11.1 %collective-permute-start.1 = (bf16[80,2048]{1,0:T(8,128)(2,1)}, bf16[80,2048]{1,0:T(8,128)(2,1)S(1)}, u32[]{:S(2)}, u32[]{:S(2)}) collective-permute-start(bf16[80,2048]{1,0:T(8,128)(2,1)} %inputs.1), channel_id=1, source_target_pairs={{0,2},{1,3},{2,0},{3,1},{4,6},{5,7},{6,4},{7,5},{8,10},{9,11},{10,... | collective-permute-start | bytes 983048 | tf_op jit(solution)/shard_map/ppermute | solution.py:28
  12.1 1.6 %collective-permute-start.2 = (bf16[80,2048]{1,0:T(8,128)(2,1)S(1)}, bf16[80,2048]{1,0:T(8,128)(2,1)S(1)}, u32[]{:S(2)}, u32[]{:S(2)}) collective-permute-start(bf16[80,2048]{1,0:T(8,128)(2,1)S(1)} %collective-permute-done.1.refs_3_), channel_id=1, source_target_pairs={{0,1},{1,0},{2,3},{3,2},{4,5},{5,4},{6,7},{7,6},{8,9},{9,8},{10,11... | collective-permute-start | bytes 983048 | tf_op jit(solution)/shard_map/ppermute | solution.py:28
  16.2 10.6 %collective-permute-start.6 = (bf16[336,384]{1,0:T(8,128)(2,1)S(1)}, bf16[336,384]{1,0:T(8,128)(2,1)S(1)}, u32[]{:S(2)}, u32[]{:S(2)}) collective-permute-start(bf16[336,384]{1,0:T(8,128)(2,1)S(1)} %get-tuple-element.93), channel_id=1, source_target_pairs={{0,8},{1,12},{2,10},{3,14},{4,9},{5,13},{6,11},{7,15},{8,16},{9,20... | collective-permute-start | bytes 774152 | tf_op jit(solution)/shard_map/ppermute | solution.py:28
  18.1 20.2 %collective-permute-start.7 = (bf16[336,384]{1,0:T(8,128)(2,1)S(1)}, bf16[336,384]{1,0:T(8,128)(2,1)S(1)}, u32[]{:S(2)}, u32[]{:S(2)}) collective-permute-start(bf16[336,384]{1,0:T(8,128)(2,1)S(1)} %get-tuple-element.94), channel_id=1, source_target_pairs={{0,16},{1,20},{2,18},{3,22},{4,17},{5,21},{6,19},{7,23},{8,24},{9,... | collective-permute-start | bytes 774152 | tf_op jit(solution)/shard_map/ppermute | solution.py:28
  20.7 17.9 %collective-permute-start.8 = (bf16[336,384]{1,0:T(8,128)(2,1)S(1)}, bf16[336,384]{1,0:T(8,128)(2,1)S(1)}, u32[]{:S(2)}, u32[]{:S(2)}) collective-permute-start(bf16[336,384]{1,0:T(8,128)(2,1)S(1)} %get-tuple-element.95), channel_id=1, source_target_pairs={{0,24},{1,28},{2,26},{3,30},{4,25},{5,29},{6,27},{7,31},{8,0},{9,4... | collective-permute-start | bytes 774152 | tf_op jit(solution)/shard_map/ppermute | solution.py:28
  22.0 38.2 %copy-start = (bf16[512,2048]{1,0:T(8,128)(2,1)S(1)}, bf16[512,2048]{1,0:T(8,128)(2,1)}, u32[]{:S(2)}) copy-start(bf16[512,2048]{1,0:T(8,128)(2,1)} %refs_4_.5) | copy-start | bytes 6291460
  22.0 16.8 %collective-permute-start.5 = (bf16[336,384]{1,0:T(8,128)(2,1)S(1)}, bf16[336,384]{1,0:T(8,128)(2,1)S(1)}, u32[]{:S(2)}, u32[]{:S(2)}) collective-permute-start(bf16[336,384]{1,0:T(8,128)(2,1)S(1)} %get-tuple-element.92), channel_id=1, source_target_pairs={{0,0},{1,4},{2,2},{3,6},{4,1},{5,5},{6,3},{7,7},{8,8},{9,12},{10,1... | collective-permute-start | bytes 774152 | tf_op jit(solution)/shard_map/ppermute | solution.py:28
  26.8 12.2 %collective-permute-start.10 = (bf16[336,384]{1,0:T(8,128)(2,1)S(1)}, bf16[336,384]{1,0:T(8,128)(2,1)S(1)}, u32[]{:S(2)}, u32[]{:S(2)}) collective-permute-start(bf16[336,384]{1,0:T(8,128)(2,1)S(1)} %collective-permute-done.6.refs_1_), channel_id=1, source_target_pairs={{0,1},{1,0},{2,3},{3,2},{4,5},{5,4},{6,7},{7,6},{8,9},{9,8},{10,11... | collective-permute-start | bytes 774152 | tf_op jit(solution)/shard_map/ppermute | solution.py:28
  38.3 1.5 collective-permute-start.11
  38.6 1.6 %collective-permute-start.12 = (bf16[336,384]{1,0:T(8,128)(2,1)S(1)}, bf16[336,384]{1,0:T(8,128)(2,1)S(1)}, u32[]{:S(2)}, u32[]{:S(2)}) collective-permute-start(bf16[336,384]{1,0:T(8,128)(2,1)S(1)} %collective-permute-done.8.refs_3_), channel_id=1, source_target_pairs={{0,1},{1,0},{2,3},{3,2},{4,5},{5,4},{6,7},{7,6},{8,9},{9,8},{10,11... | collective-permute-start | bytes 774152 | tf_op jit(solution)/shard_map/ppermute | solution.py:28
  38.8 1.8 %collective-permute-start.9 = (bf16[336,384]{1,0:T(8,128)(2,1)S(1)}, bf16[336,384]{1,0:T(8,128)(2,1)S(1)}, u32[]{:S(2)}, u32[]{:S(2)}) collective-permute-start(bf16[336,384]{1,0:T(8,128)(2,1)S(1)} %collective-permute-done.5.refs_0_), channel_id=1, source_target_pairs={{0,1},{1,0},{2,3},{3,2},{4,5},{5,4},{6,7},{7,6},{8,9},{9,8},{10,11... | collective-permute-start | bytes 774152 | tf_op jit(solution)/shard_map/ppermute | solution.py:28
  45.3 8.5 %collective-permute-start.13 = (bf16[320,128]{1,0:T(8,128)(2,1)S(1)}, bf16[320,128]{1,0:T(8,128)(2,1)S(1)}, u32[]{:S(2)}, u32[]{:S(2)}) collective-permute-start(bf16[320,128]{1,0:T(8,128)(2,1)S(1)} %get-tuple-element.96), channel_id=1, source_target_pairs={{0,0},{1,4},{2,2},{3,6},{4,1},{5,5},{6,3},{7,7},{8,8},{9,12},{10,1... | collective-permute-start | bytes 245768 | tf_op jit(solution)/shard_map/ppermute | solution.py:28
  45.9 9.2 %collective-permute-start.14 = (bf16[320,128]{1,0:T(8,128)(2,1)S(1)}, bf16[320,128]{1,0:T(8,128)(2,1)S(1)}, u32[]{:S(2)}, u32[]{:S(2)}) collective-permute-start(bf16[320,128]{1,0:T(8,128)(2,1)S(1)} %get-tuple-element.97), channel_id=1, source_target_pairs={{0,24},{1,28},{2,26},{3,30},{4,25},{5,29},{6,27},{7,31},{8,0},{9,4... | collective-permute-start | bytes 245768 | tf_op jit(solution)/shard_map/ppermute | solution.py:28
  53.1 7.1 %collective-permute-start.15 = (bf16[320,128]{1,0:T(8,128)(2,1)S(1)}, bf16[320,128]{1,0:T(8,128)(2,1)S(1)}, u32[]{:S(2)}, u32[]{:S(2)}) collective-permute-start(bf16[320,128]{1,0:T(8,128)(2,1)S(1)} %get-tuple-element.98), channel_id=1, source_target_pairs={{0,16},{1,20},{2,18},{3,22},{4,17},{5,21},{6,19},{7,23},{8,24},{9,... | collective-permute-start | bytes 245768 | tf_op jit(solution)/shard_map/ppermute | solution.py:28
  53.2 14.7 %copy-start.5 = (s32[80,6]{0,1:T(8,128)S(1)}, s32[80,6]{0,1:T(8,128)}, u32[]{:S(2)}) copy-start(s32[80,6]{0,1:T(8,128)} %param.24) | copy-start | bytes 5764
  53.2 14.7 %copy-start.6 = (f32[80,6]{0,1:T(8,128)S(1)}, f32[80,6]{0,1:T(8,128)}, u32[]{:S(2)}) copy-start(f32[80,6]{0,1:T(8,128)} %param.25) | copy-start | bytes 5764
  53.2 7.0 %collective-permute-start.16 = (bf16[320,128]{1,0:T(8,128)(2,1)S(1)}, bf16[320,128]{1,0:T(8,128)(2,1)S(1)}, u32[]{:S(2)}, u32[]{:S(2)}) collective-permute-start(bf16[320,128]{1,0:T(8,128)(2,1)S(1)} %get-tuple-element.99), channel_id=1, source_target_pairs={{0,8},{1,12},{2,10},{3,14},{4,9},{5,13},{6,11},{7,15},{8,16},{9,20... | collective-permute-start | bytes 245768 | tf_op jit(solution)/shard_map/ppermute | solution.py:28
  61.3 4.3 %collective-permute-start.17 = (bf16[80,2048]{1,0:T(8,128)(2,1)S(1)}, bf16[80,2048]{1,0:T(8,128)(2,1)S(1)}, u32[]{:S(2)}, u32[]{:S(2)}) collective-permute-start(bf16[80,2048]{1,0:T(8,128)(2,1)S(1)} %get-tuple-element.100), channel_id=1, source_target_pairs={{0,1},{1,0},{2,3},{3,2},{4,5},{5,4},{6,7},{7,6},{8,9},{9,8},{10,11... | collective-permute-start | bytes 983048 | tf_op jit(solution)/shard_map/ppermute | solution.py:28
  65.7 10.2 %collective-permute-start.20 = (bf16[1,2048,704]{1,2,0:T(8,128)(2,1)}, bf16[1,2048,704]{1,2,0:T(8,128)(2,1)}, u32[]{:S(2)}, u32[]{:S(2)}) collective-permute-start(bf16[1,2048,704]{1,2,0:T(8,128)(2,1)} %param.22), channel_id=1, source_target_pairs={{0,1},{1,0},{2,3},{3,2},{4,5},{5,4},{6,7},{7,6},{8,9},{9,8},{10,11... | collective-permute-start | bytes 8650760 | tf_op jit(solution)/shard_map/ppermute | solution.py:28
  66.1 9.8 %collective-permute-start.19 = (bf16[80,2048]{1,0:T(8,128)(2,1)S(1)}, bf16[80,2048]{1,0:T(8,128)(2,1)S(1)}, u32[]{:S(2)}, u32[]{:S(2)}) collective-permute-start(bf16[80,2048]{1,0:T(8,128)(2,1)S(1)} %shard_map.132), channel_id=1, source_target_pairs={{0,2},{1,3},{2,0},{3,1},{4,6},{5,7},{6,4},{7,5},{8,10},{9,11},{10,... | collective-permute-start | bytes 983048 | tf_op jit(solution)/shard_map/ppermute | solution.py:28
  67.9 8.0 %collective-permute-start.18 = (bf16[80,2048]{1,0:T(8,128)(2,1)S(1)}, bf16[80,2048]{1,0:T(8,128)(2,1)S(1)}, u32[]{:S(2)}, u32[]{:S(2)}) collective-permute-start(bf16[80,2048]{1,0:T(8,128)(2,1)S(1)} %get-tuple-element.106), channel_id=1, source_target_pairs={{0,1},{1,0},{2,3},{3,2},{4,5},{5,4},{6,7},{7,6},{8,9},{9,8},{10,11... | collective-permute-start | bytes 983048 | tf_op jit(solution)/shard_map/ppermute | solution.py:28
  76.3 12.9 %collective-permute-start.24 = (bf16[80,2176]{1,0:T(8,128)(2,1)S(1)}, bf16[80,2176]{1,0:T(8,128)(2,1)S(1)}, u32[]{:S(2)}, u32[]{:S(2)}) collective-permute-start(bf16[80,2176]{1,0:T(8,128)(2,1)S(1)} %get-tuple-element.121.refs_0_), channel_id=1, source_target_pairs={{0,8},{1,9},{2,10},{3,11},{4,12},{5,13},{6,14},{7,15},{8,16},{9,17... | collective-permute-start | bytes 1044488 | tf_op jit(solution)/shard_map/ppermute | solution.py:28
  76.3 16.9 %collective-permute-start.25 = (bf16[80,2176]{1,0:T(8,128)(2,1)S(1)}, bf16[80,2176]{1,0:T(8,128)(2,1)S(1)}, u32[]{:S(2)}, u32[]{:S(2)}) collective-permute-start(bf16[80,2176]{1,0:T(8,128)(2,1)S(1)} %get-tuple-element.121.refs_0_), channel_id=1, source_target_pairs={{0,24},{1,25},{2,26},{3,27},{4,28},{5,29},{6,30},{7,31},{8,0},{9,1... | collective-permute-start | bytes 1044488 | tf_op jit(solution)/shard_map/ppermute | solution.py:28
  81.6 9.4 %collective-permute-start.21 = (bf16[40,2048]{1,0:T(8,128)(2,1)S(1)}, bf16[40,2048]{1,0:T(8,128)(2,1)S(1)}, u32[]{:S(2)}, u32[]{:S(2)}) collective-permute-start(bf16[40,2048]{1,0:T(8,128)(2,1)S(1)} %get-tuple-element.124), channel_id=1, source_target_pairs={{0,2},{1,3},{2,0},{3,1},{4,6},{5,7},{6,4},{7,5},{8,10},{9,11},{10,... | collective-permute-start | bytes 491528 | tf_op jit(solution)/shard_map/ppermute | solution.py:28
  83.4 7.6 %collective-permute-start.22 = (bf16[40,2048]{1,0:T(8,128)(2,1)S(1)}, bf16[40,2048]{1,0:T(8,128)(2,1)S(1)}, u32[]{:S(2)}, u32[]{:S(2)}) collective-permute-start(bf16[40,2048]{1,0:T(8,128)(2,1)S(1)} %get-tuple-element.125), channel_id=1, source_target_pairs={{0,4},{1,5},{2,6},{3,7},{4,0},{5,1},{6,2},{7,3},{8,12},{9,13},{10,... | collective-permute-start | bytes 491528 | tf_op jit(solution)/shard_map/ppermute | solution.py:28
  84.2 7.2 %collective-permute-start.23 = (bf16[40,2048]{1,0:T(8,128)(2,1)S(1)}, bf16[40,2048]{1,0:T(8,128)(2,1)S(1)}, u32[]{:S(2)}, u32[]{:S(2)}) collective-permute-start(bf16[40,2048]{1,0:T(8,128)(2,1)S(1)} %get-tuple-element.126), channel_id=1, source_target_pairs={{0,6},{1,7},{2,4},{3,5},{4,2},{5,3},{6,0},{7,1},{8,14},{9,15},{10,... | collective-permute-start | bytes 491528 | tf_op jit(solution)/shard_map/ppermute | solution.py:28
  89.2 15.8 %collective-permute-start.27 = (bf16[80,2176]{1,0:T(8,128)(2,1)S(1)}, bf16[80,2176]{1,0:T(8,128)(2,1)S(1)}, u32[]{:S(2)}, u32[]{:S(2)}) collective-permute-start(bf16[80,2176]{1,0:T(8,128)(2,1)S(1)} %collective-permute-done.24.refs_0_), channel_id=1, source_target_pairs={{0,8},{1,9},{2,10},{3,11},{4,12},{5,13},{6,14},{7,15},{8,16},{9,17... | collective-permute-start | bytes 1044488 | tf_op jit(solution)/shard_map/ppermute | solution.py:28
  94.9 12.5 %collective-permute-start.26 = (bf16[80,2048]{1,0:T(8,128)(2,1)S(1)}, bf16[80,2048]{1,0:T(8,128)(2,1)S(1)}, u32[]{:S(2)}, u32[]{:S(2)}) collective-permute-start(bf16[80,2048]{1,0:T(8,128)(2,1)S(1)} %get-tuple-element.140), channel_id=1, source_target_pairs={{0,2},{1,3},{2,0},{3,1},{4,6},{5,7},{6,4},{7,5},{8,10},{9,11},{10,... | collective-permute-start | bytes 983048 | tf_op jit(solution)/shard_map/ppermute | solution.py:28
  96.7 14.3 %collective-permute-start.28 = (bf16[80,2048]{1,0:T(8,128)(2,1)S(1)}, bf16[80,2048]{1,0:T(8,128)(2,1)S(1)}, u32[]{:S(2)}, u32[]{:S(2)}) collective-permute-start(bf16[80,2048]{1,0:T(8,128)(2,1)S(1)} %get-tuple-element.144), channel_id=1, source_target_pairs={{0,4},{1,5},{2,6},{3,7},{4,0},{5,1},{6,2},{7,3},{8,12},{9,13},{10,... | collective-permute-start | bytes 983048 | tf_op jit(solution)/shard_map/ppermute | solution.py:28
  97.7 15.8 %collective-permute-start.29 = (bf16[80,2048]{1,0:T(8,128)(2,1)S(1)}, bf16[80,2048]{1,0:T(8,128)(2,1)S(1)}, u32[]{:S(2)}, u32[]{:S(2)}) collective-permute-start(bf16[80,2048]{1,0:T(8,128)(2,1)S(1)} %get-tuple-element.145), channel_id=1, source_target_pairs={{0,6},{1,7},{2,4},{3,5},{4,2},{5,3},{6,0},{7,1},{8,14},{9,15},{10,... | collective-permute-start | bytes 983048 | tf_op jit(solution)/shard_map/ppermute | solution.py:28
  107.4 15.5 %collective-permute-start.38 = (bf16[40,2048]{1,0:T(8,128)(2,1)S(1)}, bf16[40,2048]{1,0:T(8,128)(2,1)S(1)}, u32[]{:S(2)}, u32[]{:S(2)}) collective-permute-start(bf16[40,2048]{1,0:T(8,128)(2,1)S(1)} %get-tuple-element.160), channel_id=1, source_target_pairs={{0,2},{1,3},{2,0},{3,1},{4,6},{5,7},{6,4},{7,5},{8,10},{9,11},{10,... | collective-permute-start | bytes 491528 | tf_op jit(solution)/shard_map/ppermute | solution.py:28
  109.2 14.2 %collective-permute-start.39 = (bf16[40,2048]{1,0:T(8,128)(2,1)S(1)}, bf16[40,2048]{1,0:T(8,128)(2,1)S(1)}, u32[]{:S(2)}, u32[]{:S(2)}) collective-permute-start(bf16[40,2048]{1,0:T(8,128)(2,1)S(1)} %get-tuple-element.161), channel_id=1, source_target_pairs={{0,4},{1,5},{2,6},{3,7},{4,0},{5,1},{6,2},{7,3},{8,12},{9,13},{10,... | collective-permute-start | bytes 491528 | tf_op jit(solution)/shard_map/ppermute | solution.py:28
  110.3 13.1 %collective-permute-start.40 = (bf16[40,2048]{1,0:T(8,128)(2,1)S(1)}, bf16[40,2048]{1,0:T(8,128)(2,1)S(1)}, u32[]{:S(2)}, u32[]{:S(2)}) collective-permute-start(bf16[40,2048]{1,0:T(8,128)(2,1)S(1)} %get-tuple-element.162), channel_id=1, source_target_pairs={{0,6},{1,7},{2,4},{3,5},{4,2},{5,3},{6,0},{7,1},{8,14},{9,15},{10,... | collective-permute-start | bytes 491528 | tf_op jit(solution)/shard_map/ppermute | solution.py:28
  119.8 12.2 %collective-permute-start.30 = (bf16[80,2048]{1,0:T(8,128)(2,1)S(1)}, bf16[80,2048]{1,0:T(8,128)(2,1)S(1)}, u32[]{:S(2)}, u32[]{:S(2)}) collective-permute-start(bf16[80,2048]{1,0:T(8,128)(2,1)S(1)} %get-tuple-element.147), channel_id=1, source_target_pairs={{0,2},{1,3},{2,0},{3,1},{4,6},{5,7},{6,4},{7,5},{8,10},{9,11},{10,... | collective-permute-start | bytes 983048 | tf_op jit(solution)/shard_map/ppermute | solution.py:28
  121.6 12.9 %collective-permute-start.31 = (bf16[80,2048]{1,0:T(8,128)(2,1)S(1)}, bf16[80,2048]{1,0:T(8,128)(2,1)S(1)}, u32[]{:S(2)}, u32[]{:S(2)}) collective-permute-start(bf16[80,2048]{1,0:T(8,128)(2,1)S(1)} %get-tuple-element.148), channel_id=1, source_target_pairs={{0,4},{1,5},{2,6},{3,7},{4,0},{5,1},{6,2},{7,3},{8,12},{9,13},{10,... | collective-permute-start | bytes 983048 | tf_op jit(solution)/shard_map/ppermute | solution.py:28
  122.9 15.1 %collective-permute-start.32 = (bf16[80,2048]{1,0:T(8,128)(2,1)S(1)}, bf16[80,2048]{1,0:T(8,128)(2,1)S(1)}, u32[]{:S(2)}, u32[]{:S(2)}) collective-permute-start(bf16[80,2048]{1,0:T(8,128)(2,1)S(1)} %get-tuple-element.149), channel_id=1, source_target_pairs={{0,6},{1,7},{2,4},{3,5},{4,2},{5,3},{6,0},{7,1},{8,14},{9,15},{10,... | collective-permute-start | bytes 983048 | tf_op jit(solution)/shard_map/ppermute | solution.py:28
  128.3 15.0 %collective-permute-start.41 = (bf16[40,2048]{1,0:T(8,128)(2,1)S(1)}, bf16[40,2048]{1,0:T(8,128)(2,1)S(1)}, u32[]{:S(2)}, u32[]{:S(2)}) collective-permute-start(bf16[40,2048]{1,0:T(8,128)(2,1)S(1)} %get-tuple-element.164), channel_id=1, source_target_pairs={{0,2},{1,3},{2,0},{3,1},{4,6},{5,7},{6,4},{7,5},{8,10},{9,11},{10,... | collective-permute-start | bytes 491528 | tf_op jit(solution)/shard_map/ppermute | solution.py:28
  130.0 14.4 %collective-permute-start.42 = (bf16[40,2048]{1,0:T(8,128)(2,1)S(1)}, bf16[40,2048]{1,0:T(8,128)(2,1)S(1)}, u32[]{:S(2)}, u32[]{:S(2)}) collective-permute-start(bf16[40,2048]{1,0:T(8,128)(2,1)S(1)} %get-tuple-element.165), channel_id=1, source_target_pairs={{0,4},{1,5},{2,6},{3,7},{4,0},{5,1},{6,2},{7,3},{8,12},{9,13},{10,... | collective-permute-start | bytes 491528 | tf_op jit(solution)/shard_map/ppermute | solution.py:28
  132.0 12.4 %collective-permute-start.43 = (bf16[40,2048]{1,0:T(8,128)(2,1)S(1)}, bf16[40,2048]{1,0:T(8,128)(2,1)S(1)}, u32[]{:S(2)}, u32[]{:S(2)}) collective-permute-start(bf16[40,2048]{1,0:T(8,128)(2,1)S(1)} %get-tuple-element.166), channel_id=1, source_target_pairs={{0,6},{1,7},{2,4},{3,5},{4,2},{5,3},{6,0},{7,1},{8,14},{9,15},{10,... | collective-permute-start | bytes 491528 | tf_op jit(solution)/shard_map/ppermute | solution.py:28
  138.8 14.0 %collective-permute-start.36 = (bf16[80,2048]{1,0:T(8,128)(2,1)S(1)}, bf16[80,2048]{1,0:T(8,128)(2,1)S(1)}, u32[]{:S(2)}, u32[]{:S(2)}) collective-permute-start(bf16[80,2048]{1,0:T(8,128)(2,1)S(1)} %get-tuple-element.150), channel_id=1, source_target_pairs={{0,24},{1,25},{2,26},{3,27},{4,28},{5,29},{6,30},{7,31},{8,0},{9,1... | collective-permute-start | bytes 983048 | tf_op jit(solution)/shard_map/ppermute | solution.py:28
  140.9 6.6 %collective-permute-start.35 = (bf16[40,2048]{1,0:T(8,128)(2,1)S(1)}, bf16[40,2048]{1,0:T(8,128)(2,1)S(1)}, u32[]{:S(2)}, u32[]{:S(2)}) collective-permute-start(bf16[40,2048]{1,0:T(8,128)(2,1)S(1)} %get-tuple-element.155), channel_id=1, source_target_pairs={{0,6},{1,7},{2,4},{3,5},{4,2},{5,3},{6,0},{7,1},{8,14},{9,15},{10,... | collective-permute-start | bytes 491528 | tf_op jit(solution)/shard_map/ppermute | solution.py:28
  143.3 9.5 %collective-permute-start.37 = (bf16[80,2048]{1,0:T(8,128)(2,1)S(1)}, bf16[80,2048]{1,0:T(8,128)(2,1)S(1)}, u32[]{:S(2)}, u32[]{:S(2)}) collective-permute-start(bf16[80,2048]{1,0:T(8,128)(2,1)S(1)} %get-tuple-element.157), channel_id=1, source_target_pairs={{0,8},{1,9},{2,10},{3,11},{4,12},{5,13},{6,14},{7,15},{8,16},{9,17... | collective-permute-start | bytes 983048 | tf_op jit(solution)/shard_map/ppermute | solution.py:28
  144.9 14.5 %collective-permute-start.44 = (bf16[80,2048]{1,0:T(8,128)(2,1)S(1)}, bf16[80,2048]{1,0:T(8,128)(2,1)S(1)}, u32[]{:S(2)}, u32[]{:S(2)}) collective-permute-start(bf16[80,2048]{1,0:T(8,128)(2,1)S(1)} %shard_map.147), channel_id=1, source_target_pairs={{0,16},{1,17},{2,18},{3,19},{4,20},{5,21},{6,22},{7,23},{8,24},{9,... | collective-permute-start | bytes 983048 | tf_op jit(solution)/shard_map/ppermute | solution.py:28
  146.4 5.3 %collective-permute-start.34 = (bf16[40,2048]{1,0:T(8,128)(2,1)S(1)}, bf16[40,2048]{1,0:T(8,128)(2,1)S(1)}, u32[]{:S(2)}, u32[]{:S(2)}) collective-permute-start(bf16[40,2048]{1,0:T(8,128)(2,1)S(1)} %get-tuple-element.153), channel_id=1, source_target_pairs={{0,4},{1,5},{2,6},{3,7},{4,0},{5,1},{6,2},{7,3},{8,12},{9,13},{10,... | collective-permute-start | bytes 491528 | tf_op jit(solution)/shard_map/ppermute | solution.py:28
  147.5 5.3 %collective-permute-start.33 = (bf16[40,2048]{1,0:T(8,128)(2,1)S(1)}, bf16[40,2048]{1,0:T(8,128)(2,1)S(1)}, u32[]{:S(2)}, u32[]{:S(2)}) collective-permute-start(bf16[40,2048]{1,0:T(8,128)(2,1)S(1)} %get-tuple-element.151), channel_id=1, source_target_pairs={{0,2},{1,3},{2,0},{3,1},{4,6},{5,7},{6,4},{7,5},{8,10},{9,11},{10,... | collective-permute-start | bytes 491528 | tf_op jit(solution)/shard_map/ppermute | solution.py:28
  (4 other events, 28.5 us)
